TPU v7x, 32 devices: a whole 2x2x4 slice. The times are simulated.
32 devices in a mesh: gx: 8 (over z, x), gy: 4 (over y, core).
Axes of the slice: x: 2, y: 2, z: 4, core: 2. Of those that a mesh axis runs over, the one named last changes fastest.
Arguments:
- trans: float32 [13, 16, 4096], P(None, 'gx', 'gy'), may hold values from 0.1 to 1
- storage: float32 [16, 4096], P('gx', 'gy'), may hold values from 0.05 to 1
- fault_cells: int32 [8, 4, 512], P('gx', 'gy'), may hold values from 0 to 2047, as said below
- fault_count: int32 [8, 4], P('gx', 'gy'), may hold values from 0 to 512, as said below
- fault_trans: float32 [8, 4, 512], P('gx', 'gy'), may hold values from 0.1 to 1, as said below
Outputs:
- coarse_columns: float32 [125, 8, 1024], P(None, 'gx', 'gy')
Inputs may be any that keep to these rules, and one draw needn't show every extreme that they name: `fault_cells`: on a device with even gx index every slot's cell lies at x' = 1, on one with odd gx index at x' = 0; slot k of the partners with gx indices 2j and 2j + 1 (same gy index) has equal y' and layers z differing by at most 8. `fault_count`: equal on devices whose gx indices are 2j and 2j + 1 with the same gy index; some device has 512. `fault_trans`: equal slot by slot on devices whose gx indices are 2j and 2j + 1 with the same gy index.
All inputs are finite; a program needn't handle non-finite values.
Results may differ from a plain program's by a relative error of at most 0.0003.
Values sent between devices are 32-bit elements; how exact they have to be, the bound alone decides.
No kernel may reach another device: no remote copies, remote signals or barrier semaphores. Data moves between devices by JAX's collectives and lax.ppermute only.
A program may use at most 64 MiB of HBM per device.

v0:
```python
import jax
import jax.numpy as jnp
from jax import lax
from jax.sharding import PartitionSpec as P

NZ = 128
COLORS = 125


FORWARD = (
    (0, 0, 1),
    (0, 1, -1),
    (0, 1, 0),
    (0, 1, 1),
    (1, -1, -1),
    (1, -1, 0),
    (1, -1, 1),
    (1, 0, -1),
    (1, 0, 0),
    (1, 0, 1),
    (1, 1, -1),
    (1, 1, 0),
    (1, 1, 1),
)
damping = 2.0 / 3.0
tentative_value = 0.35355339059327373


def with_halo(value, sides, width):
    for axis, dim in sides:
        peers, length = (lax.axis_size(axis), value.shape[dim])
        up = [(i, (i + 1) % peers) for i in range(peers - 1)]
        down = [(j, i) for i, j in up]
        last = lax.slice_in_dim(value, length - width, length, axis=dim)
        leading = lax.slice_in_dim(value, 0, width, axis=dim)
        before = lax.ppermute(last, axis, up)
        after = lax.ppermute(leading, axis, down)
        value = jnp.concatenate([before, value, after], axis=dim)
    return value


def from_partner(value, axis, stride):
    mask = 2**stride
    pairs = [(source, source ^ mask) for source in range(lax.axis_size(axis))]
    return lax.ppermute(value, axis, pairs)


def build_probes(coord_x, coord_y, coord_z, grid_x, grid_y):
    colour = jnp.arange(COLORS, dtype=jnp.int32)[:, None, None, None]
    agrees = (
        (coord_x // 2 % 5 == colour // 25)
        & (coord_y // 2 % 5 == colour // 5 % 5)
        & (coord_z // 2 % 5 == colour % 5)
    )
    inside = (coord_x >= 0) & (coord_x < grid_x) & (coord_y >= 0) & (coord_y < grid_y)
    return jnp.where(agrees & inside, jnp.float32(tentative_value), jnp.float32(0.0))


def depth_pad(field):
    return jnp.pad(field, ((0, 0), (0, 0), (0, 0), (1, 1)))


def per_device(trans, storage, fault_cells, fault_count, fault_trans):
    layers = NZ
    cells_x = trans.shape[1]
    cells_y = trans.shape[2] // layers
    cell_count = cells_x * cells_y * layers
    grid_x = cells_x * lax.axis_size("gx")
    grid_y = cells_y * lax.axis_size("gy")
    start_x = lax.axis_index("gx") * cells_x
    start_y = lax.axis_index("gy") * cells_y
    coord_x = start_x + jnp.arange(cells_x, dtype=jnp.int32)[:, None, None]
    coord_y = start_y + jnp.arange(cells_y, dtype=jnp.int32)[None, :, None]
    coord_z = jnp.arange(layers, dtype=jnp.int32)[None, None, :]
    weights = trans.reshape(13, cells_x, cells_y, layers)
    pieces = []
    for offset, step in enumerate(FORWARD):
        inside = (
            (coord_x + step[0] >= 0)
            & (coord_x + step[0] < grid_x)
            & (coord_y + step[1] >= 0)
            & (coord_y + step[1] < grid_y)
            & (coord_z + step[2] >= 0)
            & (coord_z + step[2] < layers)
        )
        pieces.append(jnp.where(inside, weights[offset], jnp.float32(0.0)))
    masked = jnp.stack(pieces)
    rim_depth = 1
    widened = with_halo(masked, (("gx", 1), ("gy", 2)), rim_depth)
    widened = depth_pad(widened)

    def window(array, margin, step_x, step_y, step_z, edge):
        low_x = margin - edge + step_x
        low_y = margin - edge + step_y
        return array[
            ...,
            low_x : low_x + cells_x + 2 * edge,
            low_y : low_y + cells_y + 2 * edge,
            1 + step_z : 1 + step_z + layers,
        ]

    behind_sum = jnp.zeros((cells_x, cells_y, layers), jnp.float32)
    for offset, step in enumerate(FORWARD):
        behind_sum = behind_sum + window(
            widened[offset], rim_depth, -step[0], -step[1], -step[2], 0
        )
    fault_flat = fault_cells.reshape(-1)
    slots = jnp.arange(fault_flat.shape[0], dtype=jnp.int32)
    live_trans = jnp.where(
        slots < fault_count.reshape(()), fault_trans.reshape(-1), jnp.float32(0.0)
    )
    one_hot = (fault_flat[:, None] == jnp.arange(cell_count, dtype=jnp.int32)[None, :]).astype(
        jnp.float32
    )
    fault_diag = jnp.dot(live_trans, one_hot, precision=lax.Precision.HIGHEST).reshape(
        cells_x, cells_y, layers
    )
    diagonal = (
        storage.reshape(cells_x, cells_y, layers) + jnp.sum(masked, 0) + behind_sum + fault_diag
    )

    def stencil(padded, margin, edge, diag_region):
        summed = diag_region * window(padded, margin, 0, 0, 0, edge)
        for offset, step in enumerate(FORWARD):
            summed = (
                summed
                - window(widened[offset], rim_depth, 0, 0, 0, edge)
                * window(padded, margin, step[0], step[1], step[2], edge)
                - window(widened[offset], rim_depth, -step[0], -step[1], -step[2], edge)
                * window(padded, margin, -step[0], -step[1], -step[2], edge)
            )
        return summed

    def fault_term(center):
        own_values = jnp.take(center.reshape(center.shape[0], cell_count), fault_flat, axis=1)
        partner_values = from_partner(own_values, "gx", 0)
        across = jnp.dot(
            partner_values * live_trans[None, :], one_hot, precision=lax.Precision.HIGHEST
        )
        return across.reshape(center.shape)

    def extend(field):
        return with_halo(field, (("gx", 1), ("gy", 2)), 1)

    probes = build_probes(coord_x, coord_y, coord_z, grid_x, grid_y)
    outer_x = start_x - 1 + jnp.arange(cells_x + 2, dtype=jnp.int32)[:, None, None]
    outer_y = start_y - 1 + jnp.arange(cells_y + 2, dtype=jnp.int32)[None, :, None]
    extended = build_probes(outer_x, outer_y, coord_z, grid_x, grid_y)
    first = stencil(depth_pad(extended), 1, 0, diagonal) - fault_term(probes)
    smoothed = probes - damping * first / diagonal
    across_smooth = fault_term(smoothed)
    applied = stencil(depth_pad(extend(smoothed)), 1, 0, diagonal) - across_smooth
    scaled = applied / diagonal
    image = stencil(depth_pad(extend(scaled)), 1, 0, diagonal) - fault_term(scaled)
    result = applied - damping * image
    coarse = result.reshape(COLORS, cells_x // 2, 2, cells_y // 2, 2, layers // 2, 2).sum((2, 4, 6))
    return (tentative_value * coarse).reshape(COLORS, cells_x // 2, cells_y // 2 * (layers // 2))


def solution(mesh):
    placed = (
        P(None, "gx", "gy"),
        P("gx", "gy"),
        P("gx", "gy", None),
        P("gx", "gy"),
        P("gx", "gy", None),
    )
    return jax.shard_map(
        per_device, mesh=mesh, in_specs=placed, out_specs=P(None, "gx", "gy"), check_vma=False
    )
```

profile of v0, /device:TPU:1, one launch (start us, length us, event | category | flops | bytes accessed | tf_op | source)
XLA Modules:
  0.0 145.4 jit_solution(10880205714512439072)
XLA Ops:
  0.1 0.9 slice_bitcast_fusion.25
  2.1 3.9 %collective-permute-start = (f32[13,1,8,128]{3,2,1,0:T(8,128)S(1)}, f32[13,1,8,128]{3,2,1,0:T(8,128)S(1)}, u32[]{:S(2)}, u32[]{:S(2)}) collective-permute-start(f32[13,1,8,128]{3,2,1,0:T(8,128)S(1)} %get-tuple-element.31), channel_id=1, source_target_pairs={{0,4},{4,8},{8,12},{12,16},{16,20},{20,24},{24,28},{1,5},{5,9},{9,... | collective-permute-start | bytes 159752 | tf_op jit(solution)/shard_map/ppermute | solution.py:36
  6.0 1.3 collective-permute-start.1
  7.5 0.7 compare_and_fusion
  8.2 0.7 compare_select_fusion.1
  9.2 0.2 broadcast_and_fusion.2
  9.4 0.3 broadcast_and_fusion
  9.7 0.7 copy.13
  10.4 0.3 fusion.11
  10.8 1.0 gather_fusion
  11.8 0.1 select_bitcast_fusion.2
  11.9 2.1 %collective-permute-start.4 = (f32[125,512]{0,1:T(8,128)S(1)}, f32[125,512]{0,1:T(8,128)S(1)}, u32[]{:S(2)}, u32[]{:S(2)}) collective-permute-start(f32[125,512]{0,1:T(8,128)S(1)} %select_bitcast_fusion.2), channel_id=1, source_target_pairs={{0,4},{4,0},{8,12},{12,8},{16,20},{20,16},{24,28},{28,24},{1,5},{5... | collective-permute-start | bytes 768008 | tf_op jit(solution)/shard_map/ppermute | solution.py:45
  15.0 0.2 broadcast_and_fusion.1
  15.3 1.3 and_select_fusion
  16.6 1.9 %fusion.4 = f32[1,2,8,128]{3,0,2,1:T(1,128)S(1)} fusion(s32[2,8,128]{2,1,0:T(8,128)S(1)} %multiply_add_fusion, s32[512]{0:T(512)S(1)} %bitcast.305, f32[1,1,512]{2,1,0:T(1,128)S(1)} %copy-done.25, s32[]{:T(128)} %bitcast.291), kind=kOutput, calls=%fused_computation.36 | convolution fusion | flops 13632512 | bytes 20484 | tf_op jit(solution)/shard_map/dot_general | solution.py:115
  18.6 4.5 %collective-permute-start.2 = (f32[13,4,1,128]{3,2,1,0:T(1,128)S(1)}, f32[13,4,1,128]{3,2,1,0:T(1,128)S(1)}, u32[]{:S(2)}, u32[]{:S(2)}) collective-permute-start(f32[13,4,1,128]{3,2,1,0:T(1,128)S(1)} %get-tuple-element.29), channel_id=1, source_target_pairs={{0,1},{1,2},{2,3},{4,5},{5,6},{6,7},{8,9},{9,10},{10,11},{12,13},{... | collective-permute-start | bytes 79880 | tf_op jit(solution)/shard_map/ppermute | solution.py:36
  23.1 1.9 %collective-permute-start.3 = (f32[13,4,1,128]{3,2,1,0:T(1,128)S(1)}, f32[13,4,1,128]{3,2,1,0:T(1,128)S(1)}, u32[]{:S(2)}, u32[]{:S(2)}) collective-permute-start(f32[13,4,1,128]{3,2,1,0:T(1,128)S(1)} %get-tuple-element.30), channel_id=1, source_target_pairs={{1,0},{2,1},{3,2},{5,4},{6,5},{7,6},{9,8},{10,9},{11,10},{13,12},{... | collective-permute-start | bytes 79880 | tf_op jit(solution)/shard_map/ppermute | solution.py:37
  25.1 3.2 %collective-permute-done.3 = f32[13,4,1,128]{3,2,1,0:T(1,128)S(1)} collective-permute-done((f32[13,4,1,128]{3,2,1,0:T(1,128)S(1)}, f32[13,4,1,128]{3,2,1,0:T(1,128)S(1)}, u32[]{:S(2)}, u32[]{:S(2)}) %collective-permute-start.3) | collective-permute-done | bytes 26656 | tf_op jit(solution)/shard_map/ppermute | solution.py:37
  28.3 0.5 select_maximum_fusion.8
  29.4 0.7 fusion.175
  30.1 0.7 fusion.176
  30.8 0.7 fusion.177
  31.4 0.7 fusion.178
  32.1 0.7 fusion.179
  32.8 0.7 fusion.180
  33.4 0.7 fusion.130
  34.1 1.7 %fusion.3 = f32[125,2048]{1,0:T(8,128)S(1)} fusion(s32[512]{0:T(512)S(1)} %bitcast.306, f32[125,512]{0,1:T(8,128)S(1)} %collective-permute-done.4, f32[512]{0:T(512)S(1)} %fusion.145), kind=kOutput, calls=%fused_computation.35 | convolution fusion | flops 1573976576 | bytes 1284096 | tf_op jit(solution)/shard_map/dot_general | solution.py:137
  35.8 0.2 copy.47
  36.0 6.5 %divide_subtract_fusion = f32[125,2,8,128]{3,2,1,0:T(8,128)S(1)} fusion(f32[128,16,128]{2,1,0:T(8,128)S(1)} %bitcast.296, f32[125,4,10,128]{3,2,1,0:T(8,128)S(1)} %and_select_fusion, f32[2,8,128]{2,1,0:T(8,128)} %get-tuple-element.71, f32[2,8,128]{2,1,0:T(8,128)} %get-tuple-element.70, f32[2,8,128]{2,1,0:T(8,128)} %get-tuple-element.69, ...), kind=kLoop, calls=%fused_computation.227 | loop fusion | flops 15360000 | bytes 15661584 | tf_op jit(solution)/shard_map/sub | solution.py:150
  42.5 1.1 fusion.166
  43.6 1.7 %collective-permute-start.5 = (f32[125,1,8,128]{3,2,1,0:T(8,128)}, f32[125,1,8,128]{3,2,1,0:T(8,128)S(1)}, u32[]{:S(2)}, u32[]{:S(2)}) collective-permute-start(f32[125,1,8,128]{3,2,1,0:T(8,128)} %get-tuple-element.14), channel_id=1, source_target_pairs={{0,4},{4,8},{8,12},{12,16},{16,20},{20,24},{24,28},{1,5},{5,9},{9,... | collective-permute-start | bytes 1536008 | tf_op jit(solution)/shard_map/ppermute | solution.py:36
  45.3 1.3 collective-permute-start.6
  46.6 0.4 copy.14
  47.0 1.6 %gather_fusion.1 = f32[512,125]{1,0:T(8,128)} fusion(f32[125,2048]{0,1:T(8,128)S(1)} %bitcast.294, s32[1024]{0:T(1024)S(1)} %pad_clamp_fusion), kind=kCustom, calls=%fused_computation.1.clone | custom fusion | bytes 514048 | tf_op jit(solution)/shard_map/jit(_take)/gather | solution.py:135
  48.6 1.1 select_bitcast_fusion.1
  49.9 3.4 %collective-permute-start.9 = (f32[125,512]{0,1:T(8,128)S(1)}, f32[125,512]{0,1:T(8,128)S(1)}, u32[]{:S(2)}, u32[]{:S(2)}) collective-permute-start(f32[125,512]{0,1:T(8,128)S(1)} %select_bitcast_fusion.1), channel_id=1, source_target_pairs={{0,4},{4,0},{8,12},{12,8},{16,20},{20,16},{24,28},{28,24},{1,5},{5... | collective-permute-start | bytes 768008 | tf_op jit(solution)/shard_map/ppermute | solution.py:45
  53.3 14.8 %collective-permute-done.5 = f32[125,1,8,128]{3,2,1,0:T(8,128)S(1)} collective-permute-done((f32[125,1,8,128]{3,2,1,0:T(8,128)}, f32[125,1,8,128]{3,2,1,0:T(8,128)S(1)}, u32[]{:S(2)}, u32[]{:S(2)}) %collective-permute-start.5) | collective-permute-done | bytes 512032 | tf_op jit(solution)/shard_map/ppermute | solution.py:36
  68.0 0.3 pad_maximum_fusion.21
  68.4 2.6 %collective-permute-start.7 = (f32[125,4,1,128]{3,2,1,0:T(1,128)S(1)}, f32[125,4,1,128]{3,2,1,0:T(1,128)S(1)}, u32[]{:S(2)}, u32[]{:S(2)}) collective-permute-start(f32[125,4,1,128]{3,2,1,0:T(1,128)S(1)} %get-tuple-element.10), channel_id=1, source_target_pairs={{0,1},{1,2},{2,3},{4,5},{5,6},{6,7},{8,9},{9,10},{10,11},{12,13},{... | collective-permute-start | bytes 768008 | tf_op jit(solution)/shard_map/ppermute | solution.py:36
  71.0 2.1 %collective-permute-start.8 = (f32[125,4,1,128]{3,2,1,0:T(1,128)S(1)}, f32[125,4,1,128]{3,2,1,0:T(1,128)S(1)}, u32[]{:S(2)}, u32[]{:S(2)}) collective-permute-start(f32[125,4,1,128]{3,2,1,0:T(1,128)S(1)} %get-tuple-element.11), channel_id=1, source_target_pairs={{1,0},{2,1},{3,2},{5,4},{6,5},{7,6},{9,8},{10,9},{11,10},{13,12},{... | collective-permute-start | bytes 768008 | tf_op jit(solution)/shard_map/ppermute | solution.py:37
  73.2 1.7 %fusion.2 = f32[125,2048]{1,0:T(8,128)S(1)} fusion(s32[512]{0:T(512)S(1)} %bitcast.307, f32[125,512]{0,1:T(8,128)S(1)} %collective-permute-done.9, f32[512]{0:T(512)S(1)} %copy-done.27), kind=kOutput, calls=%fused_computation.34 | convolution fusion | flops 1573976576 | bytes 1284096 | tf_op jit(solution)/shard_map/dot_general | solution.py:137
  74.9 0.2 copy.48
  75.1 3.6 %collective-permute-done.8 = f32[125,4,1,128]{3,2,1,0:T(1,128)S(1)} collective-permute-done((f32[125,4,1,128]{3,2,1,0:T(1,128)S(1)}, f32[125,4,1,128]{3,2,1,0:T(1,128)S(1)}, u32[]{:S(2)}, u32[]{:S(2)}) %collective-permute-start.8) | collective-permute-done | bytes 256032 | tf_op jit(solution)/shard_map/ppermute | solution.py:37
  78.7 6.2 %select_maximum_fusion.4 = f32[125,4,10,130]{3,2,1,0:T(8,128)S(1)} fusion(f32[125,4,1,128]{3,2,1,0:T(1,128)S(1)} %collective-permute-done.8, f32[125,4,1,128]{3,2,1,0:T(1,128)S(1)} %collective-permute-done.7, f32[125,1,8,128]{3,2,1,0:T(8,128)S(1)} %collective-permute-done.6, f32[125,2,8,128]{3,2,1,0:T(8,128)S(1)} %divide_subtract_fusion, ...), kind=kLoop, calls=%fused_computation.27 | loop fusion | flops 7800000 | bytes 5160000 | tf_op jit(solution)/shard_map/concatenate | solution.py:38
  85.1 6.9 %broadcast_divide_fusion = (f32[125,2,8,128]{3,2,1,0:T(8,128)S(1)}, f32[125,2,8,128]{3,2,1,0:T(8,128)}) fusion(f32[2,8,128]{2,1,0:T(8,128)S(1)} %copy-done.16, f32[128,16,128]{2,1,0:T(8,128)S(1)} %bitcast.297, f32[125,4,10,130]{3,2,1,0:T(8,128)S(1)} %select_maximum_fusion.4, f32[2,8,128]{2,1,0:T(8,128)S(1)} %copy-done.15, f32[2,8,128]{2,1,0:T(8,128)S(1)} %copy-done.14, ...), kind=kLoop, calls=%fused_computation.233 | loop fusion | flops 19200000 | bytes 24285184 | tf_op jit(solution)/shard_map/div | solution.py:153
  91.9 1.0 fusion.165
  93.0 4.0 %collective-permute-start.10 = (f32[125,1,8,128]{3,2,1,0:T(8,128)}, f32[125,1,8,128]{3,2,1,0:T(8,128)S(1)}, u32[]{:S(2)}, u32[]{:S(2)}) collective-permute-start(f32[125,1,8,128]{3,2,1,0:T(8,128)} %get-tuple-element.12), channel_id=1, source_target_pairs={{0,4},{4,8},{8,12},{12,16},{16,20},{20,24},{24,28},{1,5},{5,9},{9,... | collective-permute-start | bytes 1536008 | tf_op jit(solution)/shard_map/ppermute | solution.py:36
  97.0 1.3 collective-permute-start.11
  98.3 0.4 copy.15
  98.7 1.6 %gather_fusion.2 = f32[512,125]{1,0:T(8,128)} fusion(f32[125,2048]{0,1:T(8,128)S(1)} %bitcast.293, s32[1024]{0:T(1024)S(1)} %pad_clamp_fusion), kind=kCustom, calls=%fused_computation.2.clone | custom fusion | bytes 514048 | tf_op jit(solution)/shard_map/jit(_take)/gather | solution.py:135
  100.4 1.1 select_bitcast_fusion
  101.5 2.5 %collective-permute-start.14 = (f32[125,512]{0,1:T(8,128)S(1)}, f32[125,512]{0,1:T(8,128)S(1)}, u32[]{:S(2)}, u32[]{:S(2)}) collective-permute-start(f32[125,512]{0,1:T(8,128)S(1)} %select_bitcast_fusion), channel_id=1, source_target_pairs={{0,4},{4,0},{8,12},{12,8},{16,20},{20,16},{24,28},{28,24},{1,5},{5... | collective-permute-start | bytes 768008 | tf_op jit(solution)/shard_map/ppermute | solution.py:45
  103.9 14.9 %collective-permute-done.10 = f32[125,1,8,128]{3,2,1,0:T(8,128)S(1)} collective-permute-done((f32[125,1,8,128]{3,2,1,0:T(8,128)}, f32[125,1,8,128]{3,2,1,0:T(8,128)S(1)}, u32[]{:S(2)}, u32[]{:S(2)}) %collective-permute-start.10) | collective-permute-done | bytes 512032 | tf_op jit(solution)/shard_map/ppermute | solution.py:36
  118.8 0.3 pad_maximum_fusion.18
  119.1 2.5 %collective-permute-start.12 = (f32[125,4,1,128]{3,2,1,0:T(1,128)S(1)}, f32[125,4,1,128]{3,2,1,0:T(1,128)S(1)}, u32[]{:S(2)}, u32[]{:S(2)}) collective-permute-start(f32[125,4,1,128]{3,2,1,0:T(1,128)S(1)} %get-tuple-element.8), channel_id=1, source_target_pairs={{0,1},{1,2},{2,3},{4,5},{5,6},{6,7},{8,9},{9,10},{10,11},{12,13},{... | collective-permute-start | bytes 768008 | tf_op jit(solution)/shard_map/ppermute | solution.py:36
  121.6 2.1 %collective-permute-start.13 = (f32[125,4,1,128]{3,2,1,0:T(1,128)S(1)}, f32[125,4,1,128]{3,2,1,0:T(1,128)S(1)}, u32[]{:S(2)}, u32[]{:S(2)}) collective-permute-start(f32[125,4,1,128]{3,2,1,0:T(1,128)S(1)} %get-tuple-element.9), channel_id=1, source_target_pairs={{1,0},{2,1},{3,2},{5,4},{6,5},{7,6},{9,8},{10,9},{11,10},{13,12},{... | collective-permute-start | bytes 768008 | tf_op jit(solution)/shard_map/ppermute | solution.py:37
  123.8 1.7 %fusion.1 = f32[125,2048]{1,0:T(8,128)S(1)} fusion(s32[512]{0:T(512)S(1)} %bitcast.308, f32[125,512]{0,1:T(8,128)S(1)} %collective-permute-done.14, f32[512]{0:T(512)S(1)} %copy-done.28), kind=kOutput, calls=%fused_computation.33 | convolution fusion | flops 1573976576 | bytes 1284096 | tf_op jit(solution)/shard_map/dot_general | solution.py:137
  125.5 0.2 copy.49
  125.7 3.6 %collective-permute-done.13 = f32[125,4,1,128]{3,2,1,0:T(1,128)S(1)} collective-permute-done((f32[125,4,1,128]{3,2,1,0:T(1,128)S(1)}, f32[125,4,1,128]{3,2,1,0:T(1,128)S(1)}, u32[]{:S(2)}, u32[]{:S(2)}) %collective-permute-start.13) | collective-permute-done | bytes 256032 | tf_op jit(solution)/shard_map/ppermute | solution.py:37
  129.3 6.2 %select_maximum_fusion = f32[125,4,10,130]{3,2,1,0:T(8,128)S(1)} fusion(f32[125,4,1,128]{3,2,1,0:T(1,128)S(1)} %collective-permute-done.13, f32[125,4,1,128]{3,2,1,0:T(1,128)S(1)} %collective-permute-done.12, f32[125,1,8,128]{3,2,1,0:T(8,128)S(1)} %collective-permute-done.11, f32[125,2,8,128]{3,2,1,0:T(8,128)S(1)} %get-tuple-element.6, ...), kind=kLoop, calls=%fused_computation.23 | loop fusion | flops 7800000 | bytes 5160000 | tf_op jit(solution)/shard_map/concatenate | solution.py:38
  135.5 7.4 %fusion.57 = f32[125,8,128]{2,1,0:T(8,128)} fusion(f32[125,2,8,128]{3,2,1,0:T(8,128)} %get-tuple-element.7, f32[128,16,128]{2,1,0:T(8,128)S(1)} %bitcast.295, f32[125,4,10,130]{3,2,1,0:T(8,128)S(1)} %select_maximum_fusion, f32[125,4,1,128]{3,2,1,0:T(1,128)} %copy-done, f32[125,1,8,128]{3,2,1,0:T(8,128)S(1)} %collective-permute-done.11, ...), kind=kLoop, calls=%fused_computation.94 | loop fusion | flops 19584000 | bytes 23773184 | tf_op jit(solution)/shard_map/reduce_sum | solution.py:156
  142.9 1.2 copy.16
  144.2 0.4 reduce_sum.70
  144.6 0.8 copy.17
  (120 shorter events, 2.7 us)
Async XLA Ops:
  0.0 16.6 %copy-start.21 = (s32[1,1,512]{2,1,0:T(1,128)S(1)}, s32[1,1,512]{2,1,0:T(1,128)}, u32[]{:S(2)}) copy-start(s32[1,1,512]{2,1,0:T(1,128)} %param.9) | copy-start | bytes 6148
  0.0 16.6 %copy-start.25 = (f32[1,1,512]{2,1,0:T(1,128)S(1)}, f32[1,1,512]{2,1,0:T(1,128)}, u32[]{:S(2)}) copy-start(f32[1,1,512]{2,1,0:T(1,128)} %param.11) | copy-start | bytes 6148
  0.0 33.4 %copy-start.24 = (f32[2,1024]{1,0:T(2,128)S(1)}, f32[2,1024]{1,0:T(2,128)}, u32[]{:S(2)}) copy-start(f32[2,1024]{1,0:T(2,128)} %param.8) | copy-start | bytes 24580
  1.1 34.8 %copy-start.17 = (pred[2,8]{1,0:T(4,128)(4,1)}, pred[2,8]{1,0:T(4,128)(4,1)S(1)}, u32[]{:S(2)}) copy-start(pred[2,8]{1,0:T(4,128)(4,1)S(1)} %get-tuple-element.77) | copy-start | bytes 52
  2.1 16.4 %collective-permute-start = (f32[13,1,8,128]{3,2,1,0:T(8,128)S(1)}, f32[13,1,8,128]{3,2,1,0:T(8,128)S(1)}, u32[]{:S(2)}, u32[]{:S(2)}) collective-permute-start(f32[13,1,8,128]{3,2,1,0:T(8,128)S(1)} %get-tuple-element.31), channel_id=1, source_target_pairs={{0,4},{4,8},{8,12},{12,16},{16,20},{20,24},{24,28},{1,5},{5,9},{9,... | collective-permute-start | bytes 159752 | tf_op jit(solution)/shard_map/ppermute | solution.py:36
  6.0 12.5 %collective-permute-start.1 = (f32[13,1,8,128]{3,2,1,0:T(8,128)S(1)}, f32[13,1,8,128]{3,2,1,0:T(8,128)S(1)}, u32[]{:S(2)}, u32[]{:S(2)}) collective-permute-start(f32[13,1,8,128]{3,2,1,0:T(8,128)S(1)} %get-tuple-element.32), channel_id=1, source_target_pairs={{4,0},{8,4},{12,8},{16,12},{20,16},{24,20},{28,24},{5,1},{9,5},{13... | collective-permute-start | bytes 159752 | tf_op jit(solution)/shard_map/ppermute | solution.py:37
  8.2 6.0 %copy-start.18 = (pred[512]{0:T(512)(128)(4,1)}, pred[512]{0:T(512)(128)(4,1)S(1)}, u32[]{:S(2)}) copy-start(pred[512]{0:T(512)(128)(4,1)S(1)} %compare_and_fusion) | copy-start | bytes 1540
  11.9 22.2 %collective-permute-start.4 = (f32[125,512]{0,1:T(8,128)S(1)}, f32[125,512]{0,1:T(8,128)S(1)}, u32[]{:S(2)}, u32[]{:S(2)}) collective-permute-start(f32[125,512]{0,1:T(8,128)S(1)} %select_bitcast_fusion.2), channel_id=1, source_target_pairs={{0,4},{4,0},{8,12},{12,8},{16,20},{20,16},{24,28},{28,24},{1,5},{5... | collective-permute-start | bytes 768008 | tf_op jit(solution)/shard_map/ppermute | solution.py:45
  18.6 6.5 %collective-permute-start.2 = (f32[13,4,1,128]{3,2,1,0:T(1,128)S(1)}, f32[13,4,1,128]{3,2,1,0:T(1,128)S(1)}, u32[]{:S(2)}, u32[]{:S(2)}) collective-permute-start(f32[13,4,1,128]{3,2,1,0:T(1,128)S(1)} %get-tuple-element.29), channel_id=1, source_target_pairs={{0,1},{1,2},{2,3},{4,5},{5,6},{6,7},{8,9},{9,10},{10,11},{12,13},{... | collective-permute-start | bytes 79880 | tf_op jit(solution)/shard_map/ppermute | solution.py:36
  23.1 5.2 %collective-permute-start.3 = (f32[13,4,1,128]{3,2,1,0:T(1,128)S(1)}, f32[13,4,1,128]{3,2,1,0:T(1,128)S(1)}, u32[]{:S(2)}, u32[]{:S(2)}) collective-permute-start(f32[13,4,1,128]{3,2,1,0:T(1,128)S(1)} %get-tuple-element.30), channel_id=1, source_target_pairs={{1,0},{2,1},{3,2},{5,4},{6,5},{7,6},{9,8},{10,9},{11,10},{13,12},{... | collective-permute-start | bytes 79880 | tf_op jit(solution)/shard_map/ppermute | solution.py:37
  25.1 11.0 %copy-start.26 = (f32[512]{0:T(512)}, f32[512]{0:T(512)S(1)}, u32[]{:S(2)}) copy-start(f32[512]{0:T(512)S(1)} %fusion.145) | copy-start | bytes 6148
  36.0 12.6 %copy-start.19 = (pred[512]{0:T(512)(128)(4,1)S(1)}, pred[512]{0:T(512)(128)(4,1)}, u32[]{:S(2)}) copy-start(pred[512]{0:T(512)(128)(4,1)} %copy-done.18) | copy-start | bytes 1540
  42.5 30.7 %copy-start.22 = (s32[1,1,512]{2,1,0:T(1,128)S(1)}, s32[1,1,512]{2,1,0:T(1,128)}, u32[]{:S(2)}) copy-start(s32[1,1,512]{2,1,0:T(1,128)} %param.9) | copy-start | bytes 6148
  42.5 30.7 %copy-start.27 = (f32[512]{0:T(512)S(1)}, f32[512]{0:T(512)}, u32[]{:S(2)}) copy-start(f32[512]{0:T(512)} %copy-done.26) | copy-start | bytes 6148
  43.6 24.4 %collective-permute-start.5 = (f32[125,1,8,128]{3,2,1,0:T(8,128)}, f32[125,1,8,128]{3,2,1,0:T(8,128)S(1)}, u32[]{:S(2)}, u32[]{:S(2)}) collective-permute-start(f32[125,1,8,128]{3,2,1,0:T(8,128)} %get-tuple-element.14), channel_id=1, source_target_pairs={{0,4},{4,8},{8,12},{12,16},{16,20},{20,24},{24,28},{1,5},{5,9},{9,... | collective-permute-start | bytes 1536008 | tf_op jit(solution)/shard_map/ppermute | solution.py:36
  45.3 22.8 %collective-permute-start.6 = (f32[125,1,8,128]{3,2,1,0:T(8,128)}, f32[125,1,8,128]{3,2,1,0:T(8,128)S(1)}, u32[]{:S(2)}, u32[]{:S(2)}) collective-permute-start(f32[125,1,8,128]{3,2,1,0:T(8,128)} %get-tuple-element.15), channel_id=1, source_target_pairs={{4,0},{8,4},{12,8},{16,12},{20,16},{24,20},{28,24},{5,1},{9,5},{13... | collective-permute-start | bytes 1536008 | tf_op jit(solution)/shard_map/ppermute | solution.py:37
  49.7 35.2 %copy-start.4 = (f32[2,8,128]{2,1,0:T(8,128)S(1)}, f32[2,8,128]{2,1,0:T(8,128)}, u32[]{:S(2)}) copy-start(f32[2,8,128]{2,1,0:T(8,128)} %get-tuple-element.60) | copy-start | bytes 24580
  49.7 35.2 %copy-start.5 = (f32[2,8,128]{2,1,0:T(8,128)S(1)}, f32[2,8,128]{2,1,0:T(8,128)}, u32[]{:S(2)}) copy-start(f32[2,8,128]{2,1,0:T(8,128)} %get-tuple-element.61) | copy-start | bytes 24580
  49.8 35.2 %copy-start.6 = (f32[2,8,128]{2,1,0:T(8,128)S(1)}, f32[2,8,128]{2,1,0:T(8,128)}, u32[]{:S(2)}) copy-start(f32[2,8,128]{2,1,0:T(8,128)} %get-tuple-element.62) | copy-start | bytes 24580
  49.8 35.2 %copy-start.7 = (f32[2,8,128]{2,1,0:T(8,128)S(1)}, f32[2,8,128]{2,1,0:T(8,128)}, u32[]{:S(2)}) copy-start(f32[2,8,128]{2,1,0:T(8,128)} %get-tuple-element.63) | copy-start | bytes 24580
  49.8 35.2 %copy-start.8 = (f32[2,8,128]{2,1,0:T(8,128)S(1)}, f32[2,8,128]{2,1,0:T(8,128)}, u32[]{:S(2)}) copy-start(f32[2,8,128]{2,1,0:T(8,128)} %get-tuple-element.64) | copy-start | bytes 24580
  49.8 35.2 %copy-start.9 = (f32[2,8,128]{2,1,0:T(8,128)S(1)}, f32[2,8,128]{2,1,0:T(8,128)}, u32[]{:S(2)}) copy-start(f32[2,8,128]{2,1,0:T(8,128)} %get-tuple-element.65) | copy-start | bytes 24580
  49.8 35.2 %copy-start.10 = (f32[2,8,128]{2,1,0:T(8,128)S(1)}, f32[2,8,128]{2,1,0:T(8,128)}, u32[]{:S(2)}) copy-start(f32[2,8,128]{2,1,0:T(8,128)} %get-tuple-element.66) | copy-start | bytes 24580
  49.8 35.2 %copy-start.11 = (f32[2,8,128]{2,1,0:T(8,128)S(1)}, f32[2,8,128]{2,1,0:T(8,128)}, u32[]{:S(2)}) copy-start(f32[2,8,128]{2,1,0:T(8,128)} %get-tuple-element.67) | copy-start | bytes 24580
  49.8 35.2 %copy-start.12 = (f32[2,8,128]{2,1,0:T(8,128)S(1)}, f32[2,8,128]{2,1,0:T(8,128)}, u32[]{:S(2)}) copy-start(f32[2,8,128]{2,1,0:T(8,128)} %get-tuple-element.68) | copy-start | bytes 24580
  49.8 35.2 %copy-start.13 = (f32[2,8,128]{2,1,0:T(8,128)S(1)}, f32[2,8,128]{2,1,0:T(8,128)}, u32[]{:S(2)}) copy-start(f32[2,8,128]{2,1,0:T(8,128)} %get-tuple-element.69) | copy-start | bytes 24580
  49.8 35.2 %copy-start.14 = (f32[2,8,128]{2,1,0:T(8,128)S(1)}, f32[2,8,128]{2,1,0:T(8,128)}, u32[]{:S(2)}) copy-start(f32[2,8,128]{2,1,0:T(8,128)} %get-tuple-element.70) | copy-start | bytes 24580
  49.8 35.2 %copy-start.15 = (f32[2,8,128]{2,1,0:T(8,128)S(1)}, f32[2,8,128]{2,1,0:T(8,128)}, u32[]{:S(2)}) copy-start(f32[2,8,128]{2,1,0:T(8,128)} %get-tuple-element.71) | copy-start | bytes 24580
  49.9 35.2 %copy-start.16 = (f32[2,8,128]{2,1,0:T(8,128)S(1)}, f32[2,8,128]{2,1,0:T(8,128)}, u32[]{:S(2)}) copy-start(f32[2,8,128]{2,1,0:T(8,128)} %fusion.130) | copy-start | bytes 24580
  49.9 23.3 %collective-permute-start.9 = (f32[125,512]{0,1:T(8,128)S(1)}, f32[125,512]{0,1:T(8,128)S(1)}, u32[]{:S(2)}, u32[]{:S(2)}) collective-permute-start(f32[125,512]{0,1:T(8,128)S(1)} %select_bitcast_fusion.1), channel_id=1, source_target_pairs={{0,4},{4,0},{8,12},{12,8},{16,20},{20,16},{24,28},{28,24},{1,5},{5... | collective-permute-start | bytes 768008 | tf_op jit(solution)/shard_map/ppermute | solution.py:45
  68.4 6.7 %collective-permute-start.7 = (f32[125,4,1,128]{3,2,1,0:T(1,128)S(1)}, f32[125,4,1,128]{3,2,1,0:T(1,128)S(1)}, u32[]{:S(2)}, u32[]{:S(2)}) collective-permute-start(f32[125,4,1,128]{3,2,1,0:T(1,128)S(1)} %get-tuple-element.10), channel_id=1, source_target_pairs={{0,1},{1,2},{2,3},{4,5},{5,6},{6,7},{8,9},{9,10},{10,11},{12,13},{... | collective-permute-start | bytes 768008 | tf_op jit(solution)/shard_map/ppermute | solution.py:36
  71.0 7.6 %collective-permute-start.8 = (f32[125,4,1,128]{3,2,1,0:T(1,128)S(1)}, f32[125,4,1,128]{3,2,1,0:T(1,128)S(1)}, u32[]{:S(2)}, u32[]{:S(2)}) collective-permute-start(f32[125,4,1,128]{3,2,1,0:T(1,128)S(1)} %get-tuple-element.11), channel_id=1, source_target_pairs={{1,0},{2,1},{3,2},{5,4},{6,5},{7,6},{9,8},{10,9},{11,10},{13,12},{... | collective-permute-start | bytes 768008 | tf_op jit(solution)/shard_map/ppermute | solution.py:37
  75.1 9.8 %copy-start.2 = (f32[125,4,1,128]{3,2,1,0:T(1,128)}, f32[125,4,1,128]{3,2,1,0:T(1,128)S(1)}, u32[]{:S(2)}) copy-start(f32[125,4,1,128]{3,2,1,0:T(1,128)S(1)} %collective-permute-done.7) | copy-start | bytes 768004
  78.7 6.2 %copy-start.3 = (f32[125,4,1,128]{3,2,1,0:T(1,128)}, f32[125,4,1,128]{3,2,1,0:T(1,128)S(1)}, u32[]{:S(2)}) copy-start(f32[125,4,1,128]{3,2,1,0:T(1,128)S(1)} %collective-permute-done.8) | copy-start | bytes 768004
  85.0 15.3 %copy-start.20 = (pred[512]{0:T(512)(128)(4,1)S(1)}, pred[512]{0:T(512)(128)(4,1)}, u32[]{:S(2)}) copy-start(pred[512]{0:T(512)(128)(4,1)} %copy-done.18) | copy-start | bytes 1540
  91.9 31.9 %copy-start.23 = (s32[1,1,512]{2,1,0:T(1,128)S(1)}, s32[1,1,512]{2,1,0:T(1,128)}, u32[]{:S(2)}) copy-start(s32[1,1,512]{2,1,0:T(1,128)} %param.9) | copy-start | bytes 6148
  91.9 31.9 %copy-start.28 = (f32[512]{0:T(512)S(1)}, f32[512]{0:T(512)}, u32[]{:S(2)}) copy-start(f32[512]{0:T(512)} %copy-done.26) | copy-start | bytes 6148
  93.0 25.8 %collective-permute-start.10 = (f32[125,1,8,128]{3,2,1,0:T(8,128)}, f32[125,1,8,128]{3,2,1,0:T(8,128)S(1)}, u32[]{:S(2)}, u32[]{:S(2)}) collective-permute-start(f32[125,1,8,128]{3,2,1,0:T(8,128)} %get-tuple-element.12), channel_id=1, source_target_pairs={{0,4},{4,8},{8,12},{12,16},{16,20},{20,24},{24,28},{1,5},{5,9},{9,... | collective-permute-start | bytes 1536008 | tf_op jit(solution)/shard_map/ppermute | solution.py:36
  97.0 21.8 %collective-permute-start.11 = (f32[125,1,8,128]{3,2,1,0:T(8,128)}, f32[125,1,8,128]{3,2,1,0:T(8,128)S(1)}, u32[]{:S(2)}, u32[]{:S(2)}) collective-permute-start(f32[125,1,8,128]{3,2,1,0:T(8,128)} %get-tuple-element.13), channel_id=1, source_target_pairs={{4,0},{8,4},{12,8},{16,12},{20,16},{24,20},{28,24},{5,1},{9,5},{13... | collective-permute-start | bytes 1536008 | tf_op jit(solution)/shard_map/ppermute | solution.py:37
  101.5 22.3 %collective-permute-start.14 = (f32[125,512]{0,1:T(8,128)S(1)}, f32[125,512]{0,1:T(8,128)S(1)}, u32[]{:S(2)}, u32[]{:S(2)}) collective-permute-start(f32[125,512]{0,1:T(8,128)S(1)} %select_bitcast_fusion), channel_id=1, source_target_pairs={{0,4},{4,0},{8,12},{12,8},{16,20},{20,16},{24,28},{28,24},{1,5},{5... | collective-permute-start | bytes 768008 | tf_op jit(solution)/shard_map/ppermute | solution.py:45
  119.1 6.5 %collective-permute-start.12 = (f32[125,4,1,128]{3,2,1,0:T(1,128)S(1)}, f32[125,4,1,128]{3,2,1,0:T(1,128)S(1)}, u32[]{:S(2)}, u32[]{:S(2)}) collective-permute-start(f32[125,4,1,128]{3,2,1,0:T(1,128)S(1)} %get-tuple-element.8), channel_id=1, source_target_pairs={{0,1},{1,2},{2,3},{4,5},{5,6},{6,7},{8,9},{9,10},{10,11},{12,13},{... | collective-permute-start | bytes 768008 | tf_op jit(solution)/shard_map/ppermute | solution.py:36
  121.6 7.6 %collective-permute-start.13 = (f32[125,4,1,128]{3,2,1,0:T(1,128)S(1)}, f32[125,4,1,128]{3,2,1,0:T(1,128)S(1)}, u32[]{:S(2)}, u32[]{:S(2)}) collective-permute-start(f32[125,4,1,128]{3,2,1,0:T(1,128)S(1)} %get-tuple-element.9), channel_id=1, source_target_pairs={{1,0},{2,1},{3,2},{5,4},{6,5},{7,6},{9,8},{10,9},{11,10},{13,12},{... | collective-permute-start | bytes 768008 | tf_op jit(solution)/shard_map/ppermute | solution.py:37
  125.7 3.6 %copy-start = (f32[125,4,1,128]{3,2,1,0:T(1,128)}, f32[125,4,1,128]{3,2,1,0:T(1,128)S(1)}, u32[]{:S(2)}) copy-start(f32[125,4,1,128]{3,2,1,0:T(1,128)S(1)} %collective-permute-done.12) | copy-start | bytes 768004
  129.3 6.2 %copy-start.1 = (f32[125,4,1,128]{3,2,1,0:T(1,128)}, f32[125,4,1,128]{3,2,1,0:T(1,128)S(1)}, u32[]{:S(2)}) copy-start(f32[125,4,1,128]{3,2,1,0:T(1,128)S(1)} %collective-permute-done.13) | copy-start | bytes 768004
where the time goes:
time: 148 us; the launch traced here: 145 us
  other arithmetic  43.4 us (29%)
  waiting for transfers between devices  40 us (27%)
  starting transfers between devices  37.4 us (25%)
  local copies, waits for them, and re-layouts  16.2 us (11%)
  matrix products  6.88 us (5%)
  between operations  1.53 us (1%)
    ppermute x6, waiting for transfers between devices, with_halo(): before = lax.ppermute(last, axis, up)  29.6 us
    ppermute x6, starting transfers between devices, with_halo(): before = lax.ppermute(last, axis, up)  19.3 us
    concatenate x3, other arithmetic, with_halo(): value = jnp.concatenate([before, value, after], axis=dim)  12.9 us
    ppermute x6, waiting for transfers between devices, with_halo(): after = lax.ppermute(leading, axis, down)  10.4 us
    ppermute x6, starting transfers between devices, with_halo(): after = lax.ppermute(leading, axis, down)  10 us
    ppermute x3, starting transfers between devices, from_partner(): return lax.ppermute(value, axis, pairs)  8.02 us
    reduce_sum x2, other arithmetic, per_device(): result.reshape(COLORS, cells_x // 2, 2, cells_y // 2, 2, layers // 2, 2)  7.85 us
    div x1, other arithmetic, per_device(): scaled = applied / diagonal  6.86 us
  transfers between devices with their start and end apart: 15, of which 5 were waited for; matrix products, arithmetic and copies ran while one was open for 17% of the time, Pallas kernels for 0%

commit v1 on v0

v1 whole, which is shorter than its diff:
```python
import functools

import jax
import jax.numpy as jnp
from jax import lax
from jax.experimental import pallas as pl
from jax.experimental.pallas import tpu as pltpu
from jax.sharding import PartitionSpec as P

NZ = 128
CY = 8
SLOTS = 512

FORWARD = (
    (0, 0, 1),
    (0, 1, -1),
    (0, 1, 0),
    (0, 1, 1),
    (1, -1, -1),
    (1, -1, 0),
    (1, -1, 1),
    (1, 0, -1),
    (1, 0, 0),
    (1, 0, 1),
    (1, 1, -1),
    (1, 1, 0),
    (1, 1, 1),
)
OFFSET = {step: k for k, step in enumerate(FORWARD)}
damping = 2.0 / 3.0

ROWS = 24
PER = 14
COLBLOCK = 93
FAULT_ROW = 280
YROWS = 320

f32 = jnp.float32
bf16 = jnp.bfloat16


def dot_nt(a, b):
    return lax.dot_general(a, b, (((1,), (1,)), ((), ())), preferred_element_type=f32)


def dot_nn(a, b):
    return lax.dot_general(a, b, (((1,), (0,)), ((), ())), preferred_element_type=f32)


def split(value):
    high = value.astype(bf16)
    return high, (value - high.astype(f32)).astype(bf16)


def pack_kernel(peers, trans, storage, cells, count, ftrans, block, plane, far_cells):
    last_x = lax.axis_index("gx") == peers[0] - 1
    first_y = lax.axis_index("gy") == 0
    last_y = lax.axis_index("gy") == peers[1] - 1
    depth = lax.broadcasted_iota(jnp.int32, (8, NZ), 1)
    row = lax.broadcasted_iota(jnp.int32, (8, NZ), 0)
    for x in range(2):
        for o in range(PER):
            base = (x * PER + o) * 8
            for y in range(CY):
                lanes = slice(y * NZ, (y + 1) * NZ)
                if o < 13:
                    value = trans[o, x : x + 1, lanes]
                else:
                    value = storage[x : x + 1, lanes]
                block[base + y : base + y + 1, :] = value
            if o == 13:
                continue
            step = FORWARD[o]
            keep = None
            if step[2] == 1:
                keep = depth < NZ - 1
            if step[2] == -1:
                keep = depth > 0
            if step[1] == 1:
                inside = (row < CY - 1) | jnp.logical_not(last_y)
                keep = inside if keep is None else keep & inside
            if step[1] == -1:
                inside = (row > 0) | jnp.logical_not(first_y)
                keep = inside if keep is None else keep & inside
            if step[0] == 1 and x == 1:
                inside = (row >= 0) & jnp.logical_not(last_x)
                keep = inside if keep is None else keep & inside
            if keep is not None:
                block[base : base + 8, :] = jnp.where(keep, block[base : base + 8, :], 0.0)
    live = count[0, 0]
    lane = lax.broadcasted_iota(jnp.int32, (1, NZ), 1)
    base = 2 * PER * 8
    for r in range(4):
        lanes = slice(r * NZ, (r + 1) * NZ)
        block[base + r : base + r + 1, :] = cells[0, :, lanes].astype(f32)
        block[base + 4 + r : base + 5 + r, :] = jnp.where(
            lane + r * NZ < live, ftrans[0, :, lanes], 0.0
        )
    plane[0:72, :] = block[(PER + 4) * 8 : (PER + 13) * 8, :]
    plane[72:80, :] = block[base : base + 8, :]
    far_cells[...] = block[base : base + 8, :]


def column_kernel(own, lo, hi, lo2, hi2, up, down):
    for out, first in ((up, CY - 3), (down, 0)):
        for c in range(3):
            y = first + c
            base = c * COLBLOCK
            out[base : base + 9, :] = lo2[pl.ds(y, 9, stride=8), :]
            for k, ref in enumerate((lo, own, hi)):
                start = base + 9 + 28 * k
                out[start : start + 28, :] = ref[pl.ds(y, 28, stride=8), :]
        for k, (ref, start) in enumerate(((own, 224), (lo, 224), (hi, 224), (lo2, 72), (hi2, 0))):
            out[FAULT_ROW + 8 * k : FAULT_ROW + 8 * k + 8, :] = ref[start : start + 8, :]


def lists_of(even, read):
    own, lo, hi, lo2, hi2 = (read(k) for k in range(5))
    partner = jnp.where(even, hi, lo)
    other = jnp.where(even, lo, hi)
    beyond = jnp.where(even, lo2, hi2)

    def flat(tile, start):
        return jnp.concatenate([tile[start + r : start + r + 1, :] for r in range(4)], axis=1)

    def whole(tile):
        return flat(tile, 0).astype(jnp.int32)

    return (whole(own), whole(partner), flat(own, 4)), (whole(other), whole(beyond), flat(other, 4))


def main_kernel(
    peers,
    own,
    lo,
    hi,
    lo2,
    hi2,
    yl,
    yh,
    out,
    w,
    wr,
    qc,
    inv,
    diag,
    fd,
    rf,
    qe,
    ap,
    tt,
    fh,
    fl,
):
    gx = lax.axis_index("gx")
    gy = lax.axis_index("gy")
    par = lax.rem(gx, 2)
    even = par == 0
    sgn = 1 - 2 * par
    p_own = jnp.where(even, 3, 2)
    p_far = jnp.where(even, 4, 1)
    p_third = jnp.where(even, 0, 5)

    def place(ref, count, first):
        for k in range(count):
            base = (first + k) * ROWS
            w[base + 3 : base + 11, :] = ref[8 * k : 8 * k + 8, :]

    place(lo2, 9, 4)
    for k, ref in enumerate((lo, own, hi)):
        place(ref, 28, PER * (1 + 2 * k))
    for ref, row in ((yl, 0), (yh, 11)):
        for c in range(3):
            base = c * COLBLOCK
            w[pl.ds(4 * ROWS + row + c, 9, stride=ROWS), :] = ref[base : base + 9, :]
            w[pl.ds(PER * ROWS + row + c, 84, stride=ROWS), :] = ref[base + 9 : base + 93, :]
    for p in range(7):
        for o, step in enumerate(FORWARD):
            if step[2] == 0 or (p == 0 and o < 4):
                continue
            base = (p * PER + o) * ROWS
            shift = 1 if step[2] == 1 else NZ - 1
            wr[base : base + ROWS, :] = pltpu.roll(w[base : base + ROWS, :], shift, 1)

    z128 = lax.broadcasted_iota(jnp.int32, (NZ, SLOTS), 0)
    z8 = lax.broadcasted_iota(jnp.int32, (8, NZ), 1)
    e8 = lax.broadcasted_iota(jnp.int32, (8, NZ), 0)

    def colour(z):
        half = z >> 1
        return half - 5 * ((half * 205) >> 10)

    one_all = jnp.where((e8 == colour(z8)) | (e8 == 5), 1.0, 0.0).astype(bf16)
    es = lax.broadcasted_iota(jnp.int32, (8, SLOTS), 0)

    fd[...] = jnp.zeros_like(fd)

    def prepare(lists):
        (c_own, c_far, live), (c_other, c_beyond, live_o) = lists
        live_h = live.astype(bf16).astype(f32)
        live_l = live - live_h
        match = (c_far & 127) == z128
        far2 = jnp.concatenate(
            [jnp.where(match, live_h, 0.0), jnp.where(match, live_l, 0.0)], axis=0
        ).astype(bf16)
        lo_h = live_o.astype(bf16).astype(f32)
        lo_l = live_o - lo_h
        same = (es == colour(c_beyond & 127)) | (es == 5)
        other2 = jnp.concatenate(
            [jnp.where(same, lo_h, 0.0), jnp.where(same, lo_l, 0.0)], axis=0
        ).astype(bf16)
        return c_own & 1023, far2, c_other & 1023, other2

    def build(column, y, ready):
        at_own, far2, at_other, other2 = ready
        hot = jnp.where(at_own == z128 + y * NZ, 1.0, 0.0).astype(bf16)
        both = dot_nt(hot, far2)
        f_h, f_l = split(both[:, :NZ] + both[:, NZ:])
        fh[column] = f_h
        fl[column] = f_l
        to_own = dot_nt(one_all, f_h) + dot_nt(one_all, f_l)
        to_far = dot_nn(one_all, f_h) + dot_nn(one_all, f_l)
        hot_o = jnp.where(at_other == z128 + y * NZ, 1.0, 0.0).astype(bf16)
        pieces = dot_nt(other2, hot_o)
        to_third = pieces[:8] + pieces[8:]
        for k, (plane, value) in enumerate(((p_own, to_own), (p_far, to_far), (p_third, to_third))):
            rf[k, column] = value
            fd[pl.ds(plane * 16 + column, 1), :] = value[5:6, :]

    tiles = ((own, 224), (lo, 224), (hi, 224), (lo2, 72), (hi2, 0))
    ready = prepare(lists_of(even, lambda k: tiles[k][0][tiles[k][1] : tiles[k][1] + 8, :]))

    def build_own(y, carry):
        build(y + 2, y, ready)
        return carry

    lax.fori_loop(0, CY, build_own, 0)
    for ref, columns in ((yl, ((0, 6), (1, 7))), (yh, ((10, 0), (11, 1)))):
        ready_y = prepare(
            lists_of(even, lambda k: ref[FAULT_ROW + 8 * k : FAULT_ROW + 8 * k + 8, :])
        )
        for column, y in columns:
            build(column, y, ready_y)

    r16 = lax.broadcasted_iota(jnp.int32, (16, NZ), 0)
    z16 = lax.broadcasted_iota(jnp.int32, (16, NZ), 1)
    even_y = (r16 & 1) == 0
    even_z = (z16 & 1) == 0
    for p in range(6):
        base = p + 1

        def weight(dx, dy, dz):
            if (dx, dy, dz) in OFFSET:
                start = (base * PER + OFFSET[dx, dy, dz]) * ROWS + 1
                return w[start : start + 16, :]
            o = OFFSET[-dx, -dy, -dz]
            start = ((base + dx) * PER + o) * ROWS + 1 + dy
            return (w if dz == 0 else wr)[start : start + 16, :]

        near = 1 if p % 2 == 0 else -1
        sums = {}
        for dz in (-1, 0, 1):
            got = {}
            for dx in (-1, 0, 1):
                below, above = weight(dx, -1, dz), weight(dx, 1, dz)
                got[dx, 0] = jnp.where(even_y, above, below)
                if (dx, dz) != (0, 0):
                    got[dx, 0] = got[dx, 0] + weight(dx, 0, dz)
                got[dx, 1] = jnp.where(even_y, below, above)
            for sy in range(2):
                sums[0, sy, dz] = got[0, sy] + got[near, sy]
                sums[1, sy, dz] = got[-near, sy]
        total = w[(base * PER + 13) * ROWS + 1 : (base * PER + 13) * ROWS + 17, :]
        total = total + fd[p * 16 : p * 16 + 16, :]
        r = []
        for sx in range(2):
            for sy in range(2):
                down, same, up = (sums[sx, sy, dz] for dz in (-1, 0, 1))
                r.append(same + jnp.where(even_z, up, down))
                r.append(jnp.where(even_z, down, up))
        for value in r:
            total = total + value
        total = jnp.where(total == 0.0, 1.0, total)
        scale = damping / total
        diag[p * 16 : p * 16 + 16, :] = total
        inv[p * 16 : p * 16 + 16, :] = scale
        for k, value in enumerate(r):
            value = value * scale
            if k == 0:
                value = value + (1.0 - damping)
            qc[(p * 8 + k) * 16 : (p * 8 + k) * 16 + 16, :] = value

    beside = jnp.where((z8 & 1) == 0, z8 - 1, z8 + 1)
    mask_own = jnp.where(e8 == colour(z8), 1.0, 0.0)
    mask_oth = jnp.where(e8 == colour(beside + 10), 1.0, 0.0)
    rows5 = jnp.where(e8 < 5, 1.0, 0.0)

    def spread(c, carry):
        for p in range(6):
            for lat in range(4):
                at = (p * 8 + 2 * lat) * 16 + c
                qe[p, c, lat] = (
                    qc[pl.ds(at, 1), :] * mask_own + qc[pl.ds(at + 16, 1), :] * mask_oth
                )
        for k, plane in enumerate((p_own, p_far, p_third)):
            qe[plane, c, 2] = qe[plane, c, 2] + rf[k, c] * (
                inv[pl.ds(plane * 16 + c, 1), :] * rows5
            )
        return carry

    lax.fori_loop(0, 12, spread, 0)

    def apply_column(p, y, odd_y):
        odd_x = p % 2
        acc = {}
        for dx in (-1, 0, 1):
            for dy in (-1, 0, 1):
                q = [qe[p + dx, y + dy, lat] for lat in range(4)]
                own_x = dx if (dx == 1 and odd_x) or (dx == -1 and not odd_x) else 0
                own_y = dy if (dy == 1 and odd_y) or (dy == -1 and not odd_y) else 0
                oth_x = own_x + (1 if (p + dx) % 2 else -1)
                oth_y = own_y + (1 if (odd_y + dy) % 2 else -1)
                for dz in (-1, 0, 1):
                    if (dx, dy, dz) == (0, 0, 0):
                        continue
                    if (dx, dy, dz) in OFFSET:
                        at = ((p + 1) * PER + OFFSET[dx, dy, dz]) * ROWS + y + 1
                        ref = w if dz == 0 else wr
                    else:
                        at = ((p + 1 + dx) * PER + OFFSET[-dx, -dy, -dz]) * ROWS + y + 1 + dy
                        ref = w
                    wt = ref[pl.ds(at, 1), :]
                    for lat in range(4):
                        lx = oth_x if lat >= 2 else own_x
                        ly = oth_y if lat % 2 else own_y
                        value = wt * q[lat]
                        key = (lx, ly, dz)
                        acc[key] = acc[key] + value if key in acc else value
        centre = diag[pl.ds(p * 16 + y, 1), :]
        for lx in (-1, 0, 1):
            for ly in (-1, 0, 1):
                total = acc[lx, ly, 0]
                total = total + pltpu.roll(acc[lx, ly, 1], NZ - 1, 1)
                total = total + pltpu.roll(acc[lx, ly, -1], 1, 1)
                own_lat = None
                sx = {0: 0, (1 if odd_x else -1): 1}.get(lx)
                sy = {0: 0, (1 if odd_y else -1): 1}.get(ly)
                if sx is not None and sy is not None:
                    own_lat = 2 * sx + sy
                if own_lat is None:
                    total = -total
                else:
                    total = centre * qe[p, y, own_lat] - total
                ap[p - 1, y - 1, lx + 1, ly + 1] = total

    def apply_pair(k, carry):
        for p in range(1, 5):
            apply_column(p, 2 * k + 1, 1)
            apply_column(p, 2 * k + 2, 0)
        return carry

    lax.fori_loop(0, 5, apply_pair, 0)

    def fault_apply(c, carry):
        both = jnp.concatenate([fh[c], fl[c]], axis=0)
        ly_oth = 2 * lax.rem(c, 2)
        for plane, source, x_own, forward in (
            (p_own, p_far, 1 + sgn, True),
            (p_far, p_own, 1 - sgn, False),
        ):
            high, low = split(qe[source, c].reshape(32, NZ))
            if forward:
                got = dot_nt(jnp.concatenate([high, low], axis=0), both)
                total = got[:32, :NZ] + got[:32, NZ:] + got[32:, :NZ]
            else:
                total = dot_nn(high, fh[c]) + dot_nn(high, fl[c]) + dot_nn(low, fh[c])
            for lat in range(4):
                lx = 1 if lat >= 2 else x_own
                ly = ly_oth if lat % 2 else 1
                ap[plane - 1, c - 1, lx, ly] = ap[plane - 1, c - 1, lx, ly] - total[8 * lat : 8 * lat + 8]
        return carry

    lax.fori_loop(1, 11, fault_apply, 0)

    x_coarse = lax.rem(gx, 5) + 5
    a_of = [lax.rem(x_coarse + d, 5) for d in range(-2, 3)]

    def b_of(coarse_y, d):
        return lax.rem(gy * (CY // 2) + coarse_y + d + 5, 5)

    def gather(pair, carry):
        for half in range(2):
            coarse_y = 2 * pair + half
            columns = []
            for x in range(-1, 3):
                for y in range(-1, 3):
                    sx = 0 if x in (0, 1) else 1
                    sy = 0 if y in (0, 1) else 1
                    columns.append((x, y, 2 * sx + sy, (-1, 0, 0, 1)[x + 1], (-1, 0, 0, 1)[y + 1]))
            for zk in range(2):
                acc = {}
                for x, y, lat, ax, ay in columns:
                    c = 2 * coarse_y + y + 2
                    q = qc[pl.ds(((x + 2) * 8 + 2 * lat + zk) * 16 + c, 1), :]
                    for lx in range(3):
                        for ly in range(3):
                            value = q * ap[x + 1, c - 1, lx, ly]
                            key = (ax + lx - 1, ay + ly - 1)
                            acc[key] = acc[key] + value if key in acc else value
                lane = half * 256 + zk * NZ
                for (dx, dy), value in acc.items():
                    tt[pair, a_of[dx + 2], b_of(coarse_y, dy), :, lane : lane + NZ] = value
        return carry

    lax.fori_loop(0, 2, gather, 0)

    for y in range(CY):
        c = y + 2
        coarse_y = y // 2
        lane = (coarse_y % 2) * 256
        both = jnp.concatenate([fh[c], fl[c]], axis=0)
        value = ap[p_far - 1, c - 1].reshape(72, NZ) * inv[pl.ds(p_far * 16 + c, 1), :]
        high, low = split(value)

        def add(total):
            for lx in range(3):
                a = lax.rem(x_coarse + lx - 1 + sgn, 5)
                for ly in range(3):
                    b = b_of(coarse_y, ly - 1)
                    at = 8 * (3 * lx + ly)
                    place_at = tt.at[coarse_y // 2, a, b, :, lane : lane + NZ]
                    place_at[...] = place_at[...] + total[at : at + 8]

        got = dot_nt(jnp.concatenate([high, low], axis=0), both)
        add(got[:72, :NZ] + got[:72, NZ:] + got[72:, :NZ])

    kz = lax.broadcasted_iota(jnp.int32, (512, NZ), 0)
    kout = lax.broadcasted_iota(jnp.int32, (512, NZ), 1)
    z_in = kz & 127
    is_oth = ((kz >> 7) & 1) == 1
    target = jnp.where(
        is_oth, (z_in >> 1) + jnp.where((z_in & 1) == 0, -1, 1), z_in >> 1
    )
    fits = (target == (kout & 63)) & ((kz >> 8) == (kout >> 6))
    collect = jnp.where(fits, 1.0, 0.0).astype(bf16)
    for pair in range(2):
        high, low = split(tt[pair].reshape(200, 512))
        got = (dot_nn(high, collect) + dot_nn(low, collect)) * 0.125
        for k in range(25):
            out[5 * k : 5 * k + 5, 0, pair * NZ : (pair + 1) * NZ] = got[8 * k : 8 * k + 5]


def shift(value, axis, distance):
    peers = lax.axis_size(axis)
    pairs = [(i, i + distance) for i in range(peers) if 0 <= i + distance < peers]
    return lax.ppermute(value, axis, pairs)


VMEM = pl.BlockSpec(memory_space=pltpu.VMEM)
SMEM = pl.BlockSpec(memory_space=pltpu.SMEM)
PARAMS = pltpu.CompilerParams(vmem_limit_bytes=48 * 1024 * 1024)


def sds(*shape):
    return jax.ShapeDtypeStruct(shape, f32)


def per_device(trans, storage, fault_cells, fault_count, fault_trans):
    peers = (lax.axis_size("gx"), lax.axis_size("gy"))
    own, plane, cells = pl.pallas_call(
        functools.partial(pack_kernel, peers),
        out_shape=(sds(232, NZ), sds(80, NZ), sds(8, NZ)),
        in_specs=[VMEM, VMEM, VMEM, SMEM, VMEM],
        out_specs=(VMEM, VMEM, VMEM),
        compiler_params=PARAMS,
        name="pack",
    )(trans, storage, fault_cells, fault_count, fault_trans)
    lo = shift(own, "gx", 1)
    hi = shift(own, "gx", -1)
    lo2 = shift(plane, "gx", 2)
    hi2 = shift(cells, "gx", -2)
    up, down = pl.pallas_call(
        column_kernel,
        out_shape=(sds(YROWS, NZ), sds(YROWS, NZ)),
        in_specs=[VMEM] * 5,
        out_specs=(VMEM, VMEM),
        compiler_params=PARAMS,
        name="columns",
    )(own, lo, hi, lo2, hi2)
    yl = shift(up, "gy", 1)
    yh = shift(down, "gy", -1)
    return pl.pallas_call(
        functools.partial(main_kernel, peers),
        out_shape=sds(125, 1, 256),
        in_specs=[VMEM] * 7,
        out_specs=VMEM,
        scratch_shapes=[
            pltpu.VMEM((7 * PER * ROWS, NZ), f32),
            pltpu.VMEM((7 * PER * ROWS, NZ), f32),
            pltpu.VMEM((6 * 8 * 16, NZ), f32),
            pltpu.VMEM((6 * 16, NZ), f32),
            pltpu.VMEM((6 * 16, NZ), f32),
            pltpu.VMEM((6 * 16, NZ), f32),
            pltpu.VMEM((3, 12, 8, NZ), f32),
            pltpu.VMEM((6, 12, 4, 8, NZ), f32),
            pltpu.VMEM((4, 10, 3, 3, 8, NZ), f32),
            pltpu.VMEM((2, 5, 5, 8, 512), f32),
            pltpu.VMEM((12, NZ, NZ), bf16),
            pltpu.VMEM((12, NZ, NZ), bf16),
        ],
        compiler_params=PARAMS,
        name="galerkin",
    )(own, lo, hi, lo2, hi2, yl, yh)


def solution(mesh):
    placed = (
        P(None, "gx", "gy"),
        P("gx", "gy"),
        P("gx", "gy", None),
        P("gx", "gy"),
        P("gx", "gy", None),
    )
    return jax.shard_map(
        per_device, mesh=mesh, in_specs=placed, out_specs=P(None, "gx", "gy"), check_vma=False
    )
```

time: 148 us -> 41.9 us (0.28); the launches traced: 145 us -> 41.5 us
  other arithmetic: 43.4 us -> 0 us
  waiting for transfers between devices: 40 us -> 7.77 us
  starting transfers between devices: 37.4 us -> 18.2 us
  local copies, waits for them, and re-layouts: 16.2 us -> 2.95 us
  Pallas kernels: 0 us -> 11.8 us
  matrix products: 6.88 us -> 0 us
    ppermute x15 -> x6, waiting for transfers between devices: 40 us -> 7.77 us  [shift(): return lax.ppermute(value, axis, pairs)]
    ppermute x15 -> x6, starting transfers between devices: 37.4 us -> 18.2 us  [shift(): return lax.ppermute(value, axis, pairs)]
    concatenate x3 -> x0, other arithmetic: 12.9 us -> none  [with_halo(): value = jnp.concatenate([before, value, after], axis=dim)]
    pallas_call x0 -> x3, Pallas kernels: none -> 11.8 us  [the longest x1 11.6 us: per_device(): pl.pallas_call(functools.partial(main_kernel, peers), out_shape=sds(125,...]
    reduce_sum x2 -> x0, other arithmetic: 7.85 us -> none  [per_device(): result.reshape(COLORS, cells_x // 2, 2, cells_y // 2, 2, layers // 2, 2)]
    dot_general x4 -> x0, matrix products: 6.88 us -> none  [the longest x3 5 us: fault_term(): jnp.dot(partner_values * live_trans[None, :], one_hot, precision=lax.Prec...]
    div x1 -> x0, other arithmetic: 6.86 us -> none  [per_device(): scaled = applied / diagonal]
    slice x16 -> x0, local copies, waits for them, and re-layouts: 6.66 us -> none  [the longest x13 4.54 us: window(): array[..., low_x:low_x + cells_x + 2 * edge, low_y:low_y + cells_y + 2 *...]
  transfers between devices with their start and end apart: 15 -> 6, of which waited for: 5 -> 3; matrix products, arithmetic and copies ran while one was open for 17% -> 0% of each run, Pallas kernels for 0% -> 0%
where the time goes in v1:
time: 41.9 us; the launch traced here: 41.5 us
  starting transfers between devices  18.2 us (43%)
  Pallas kernels  11.8 us (28%)
  waiting for transfers between devices  7.77 us (19%)
  local copies, waits for them, and re-layouts  2.95 us (7%)
  between operations  0.73 us (2%)
    ppermute x6, starting transfers between devices, shift(): return lax.ppermute(value, axis, pairs)  18.2 us
    pallas_call x1, Pallas kernels, per_device(): pl.pallas_call(functools.partial(main_kernel, peers), out_shape=sds(125,...  11.6 us
    ppermute x6, waiting for transfers between devices, shift(): return lax.ppermute(value, axis, pairs)  7.77 us
    unnamed x8, local copies, waits for them, and re-layouts  2.95 us
  transfers between devices with their start and end apart: 6, of which 3 were waited for; matrix products, arithmetic and copies ran while one was open for 0% of the time, Pallas kernels for 0%

profile of v1, /device:TPU:1, one launch (start us, length us, event | category | flops | bytes accessed | tf_op | source)
XLA Modules:
  0.0 41.5 jit_solution(16685484118538154004)
XLA Ops:
  0.7 0.0 copy-start
  0.7 0.9 %copy-done = f32[13,2,1024]{2,1,0:T(2,128)S(1)} copy-done((f32[13,2,1024]{2,1,0:T(2,128)S(1)}, f32[13,2,1024]{2,1,0:T(2,128)}, u32[]{:S(2)}) %copy-start) | copy-done | bytes 106520
  1.5 0.0 copy-start.1
  1.6 0.7 %copy-done.1 = f32[2,1024]{1,0:T(2,128)S(1)} copy-done((f32[2,1024]{1,0:T(2,128)S(1)}, f32[2,1024]{1,0:T(2,128)}, u32[]{:S(2)}) %copy-start.1) | copy-done | bytes 8216
  2.2 0.0 copy-start.2
  2.2 0.7 %copy-done.2 = s32[1,1,512]{2,1,0:T(1,128)S(1)} copy-done((s32[1,1,512]{2,1,0:T(1,128)S(1)}, s32[1,1,512]{2,1,0:T(1,128)}, u32[]{:S(2)}) %copy-start.2) | copy-done | bytes 2072
  2.9 0.0 copy-start.3
  2.9 0.7 %copy-done.3 = f32[1,1,512]{2,1,0:T(1,128)S(1)} copy-done((f32[1,1,512]{2,1,0:T(1,128)S(1)}, f32[1,1,512]{2,1,0:T(1,128)}, u32[]{:S(2)}) %copy-start.3) | copy-done | bytes 2072
  3.6 0.1 pack.1
  3.7 1.3 %collective-permute-start.1 = (f32[232,128]{1,0:T(8,128)S(1)}, f32[232,128]{1,0:T(8,128)S(1)}, u32[]{:S(2)}, u32[]{:S(2)}) collective-permute-start(f32[232,128]{1,0:T(8,128)S(1)} %get-tuple-element.10.own), channel_id=1, source_target_pairs={{4,0},{8,4},{12,8},{16,12},{20,16},{24,20},{28,24},{5,1},{9,5},{13... | collective-permute-start | bytes 356360 | tf_op jit(solution)/shard_map/ppermute | solution.py:456
  5.0 4.6 %collective-permute-start = (f32[232,128]{1,0:T(8,128)S(1)}, f32[232,128]{1,0:T(8,128)S(1)}, u32[]{:S(2)}, u32[]{:S(2)}) collective-permute-start(f32[232,128]{1,0:T(8,128)S(1)} %get-tuple-element.10.own), channel_id=1, source_target_pairs={{0,4},{4,8},{8,12},{12,16},{16,20},{20,24},{24,28},{1,5},{5,9},{9,... | collective-permute-start | bytes 356360 | tf_op jit(solution)/shard_map/ppermute | solution.py:456
  9.6 3.4 %collective-permute-start.2 = (f32[80,128]{1,0:T(8,128)S(1)}, f32[80,128]{1,0:T(8,128)S(1)}, u32[]{:S(2)}, u32[]{:S(2)}) collective-permute-start(f32[80,128]{1,0:T(8,128)S(1)} %get-tuple-element.11), channel_id=1, source_target_pairs={{0,8},{4,12},{8,16},{12,20},{16,24},{20,28},{1,9},{5,13},{9,17},{1... | collective-permute-start | bytes 122888 | tf_op jit(solution)/shard_map/ppermute | solution.py:456
  13.1 1.3 %collective-permute-start.3 = (f32[8,128]{1,0:T(8,128)S(1)}, f32[8,128]{1,0:T(8,128)S(1)}, u32[]{:S(2)}, u32[]{:S(2)}) collective-permute-start(f32[8,128]{1,0:T(8,128)S(1)} %get-tuple-element.12), channel_id=1, source_target_pairs={{8,0},{12,4},{16,8},{20,12},{24,16},{28,20},{9,1},{13,5},{17,9},{2... | collective-permute-start | bytes 12296 | tf_op jit(solution)/shard_map/ppermute | solution.py:456
  14.4 3.1 %collective-permute-done.3.hi2 = f32[8,128]{1,0:T(8,128)S(1)} collective-permute-done((f32[8,128]{1,0:T(8,128)S(1)}, f32[8,128]{1,0:T(8,128)S(1)}, u32[]{:S(2)}, u32[]{:S(2)}) %collective-permute-start.3) | collective-permute-done | bytes 4128 | tf_op jit(solution)/shard_map/ppermute | solution.py:456
  17.4 0.0 collective-permute-done.2.lo2
  17.4 0.0 collective-permute-done.1.hi
  17.4 0.0 collective-permute-done.lo
  17.4 0.1 columns.1
  17.5 5.7 %collective-permute-start.4 = (f32[320,128]{1,0:T(8,128)S(1)}, f32[320,128]{1,0:T(8,128)S(1)}, u32[]{:S(2)}, u32[]{:S(2)}) collective-permute-start(f32[320,128]{1,0:T(8,128)S(1)} %get-tuple-element.13), channel_id=1, source_target_pairs={{0,1},{1,2},{2,3},{4,5},{5,6},{6,7},{8,9},{9,10},{10,11},{12,13},{... | collective-permute-start | bytes 491528 | tf_op jit(solution)/shard_map/ppermute | solution.py:456
  23.2 1.9 %collective-permute-start.5 = (f32[320,128]{1,0:T(8,128)S(1)}, f32[320,128]{1,0:T(8,128)S(1)}, u32[]{:S(2)}, u32[]{:S(2)}) collective-permute-start(f32[320,128]{1,0:T(8,128)S(1)} %get-tuple-element.14), channel_id=1, source_target_pairs={{1,0},{2,1},{3,2},{5,4},{6,5},{7,6},{9,8},{10,9},{11,10},{13,12},{... | collective-permute-start | bytes 491528 | tf_op jit(solution)/shard_map/ppermute | solution.py:456
  25.1 0.3 collective-permute-done.4.yl
  25.4 4.4 %collective-permute-done.5.yh = f32[320,128]{1,0:T(8,128)S(1)} collective-permute-done((f32[320,128]{1,0:T(8,128)S(1)}, f32[320,128]{1,0:T(8,128)S(1)}, u32[]{:S(2)}, u32[]{:S(2)}) %collective-permute-start.5) | collective-permute-done | bytes 163872 | tf_op jit(solution)/shard_map/ppermute | solution.py:456
  29.8 11.6 %galerkin.1 = f32[125,1,256]{2,1,0:T(1,128)} custom-call(f32[232,128]{1,0:T(8,128)S(1)} %get-tuple-element.10.own, f32[232,128]{1,0:T(8,128)S(1)} %collective-permute-done.lo, f32[232,128]{1,0:T(8,128)S(1)} %collective-permute-done.1.hi, f32[80,128]{1,0:T(8,128)S(1)} %collective-permute-done.2.lo2, f32[8,128]{1,0:T(8,128)S(1)} %collective-permute-done.3.hi2, ...), custom_call_target="tpu_custom_call" | custom-call | tf_op jit(solution)/shard_map/galerkin/pallas_call | solution.py:492
Async XLA Ops:
  0.7 0.9 %copy-start = (f32[13,2,1024]{2,1,0:T(2,128)S(1)}, f32[13,2,1024]{2,1,0:T(2,128)}, u32[]{:S(2)}) copy-start(f32[13,2,1024]{2,1,0:T(2,128)} %trans.1) | copy-start | bytes 319492
  1.5 0.7 %copy-start.1 = (f32[2,1024]{1,0:T(2,128)S(1)}, f32[2,1024]{1,0:T(2,128)}, u32[]{:S(2)}) copy-start(f32[2,1024]{1,0:T(2,128)} %storage.1) | copy-start | bytes 24580
  2.2 0.7 %copy-start.2 = (s32[1,1,512]{2,1,0:T(1,128)S(1)}, s32[1,1,512]{2,1,0:T(1,128)}, u32[]{:S(2)}) copy-start(s32[1,1,512]{2,1,0:T(1,128)} %cells.1) | copy-start | bytes 6148
  2.9 0.7 %copy-start.3 = (f32[1,1,512]{2,1,0:T(1,128)S(1)}, f32[1,1,512]{2,1,0:T(1,128)}, u32[]{:S(2)}) copy-start(f32[1,1,512]{2,1,0:T(1,128)} %ftrans.1) | copy-start | bytes 6148
  3.7 13.7 %collective-permute-start.1 = (f32[232,128]{1,0:T(8,128)S(1)}, f32[232,128]{1,0:T(8,128)S(1)}, u32[]{:S(2)}, u32[]{:S(2)}) collective-permute-start(f32[232,128]{1,0:T(8,128)S(1)} %get-tuple-element.10.own), channel_id=1, source_target_pairs={{4,0},{8,4},{12,8},{16,12},{20,16},{24,20},{28,24},{5,1},{9,5},{13... | collective-permute-start | bytes 356360 | tf_op jit(solution)/shard_map/ppermute | solution.py:456
  5.0 12.4 %collective-permute-start = (f32[232,128]{1,0:T(8,128)S(1)}, f32[232,128]{1,0:T(8,128)S(1)}, u32[]{:S(2)}, u32[]{:S(2)}) collective-permute-start(f32[232,128]{1,0:T(8,128)S(1)} %get-tuple-element.10.own), channel_id=1, source_target_pairs={{0,4},{4,8},{8,12},{12,16},{16,20},{20,24},{24,28},{1,5},{5,9},{9,... | collective-permute-start | bytes 356360 | tf_op jit(solution)/shard_map/ppermute | solution.py:456
  9.6 7.8 %collective-permute-start.2 = (f32[80,128]{1,0:T(8,128)S(1)}, f32[80,128]{1,0:T(8,128)S(1)}, u32[]{:S(2)}, u32[]{:S(2)}) collective-permute-start(f32[80,128]{1,0:T(8,128)S(1)} %get-tuple-element.11), channel_id=1, source_target_pairs={{0,8},{4,12},{8,16},{12,20},{16,24},{20,28},{1,9},{5,13},{9,17},{1... | collective-permute-start | bytes 122888 | tf_op jit(solution)/shard_map/ppermute | solution.py:456
  13.1 4.4 %collective-permute-start.3 = (f32[8,128]{1,0:T(8,128)S(1)}, f32[8,128]{1,0:T(8,128)S(1)}, u32[]{:S(2)}, u32[]{:S(2)}) collective-permute-start(f32[8,128]{1,0:T(8,128)S(1)} %get-tuple-element.12), channel_id=1, source_target_pairs={{8,0},{12,4},{16,8},{20,12},{24,16},{28,20},{9,1},{13,5},{17,9},{2... | collective-permute-start | bytes 12296 | tf_op jit(solution)/shard_map/ppermute | solution.py:456
  17.5 7.9 %collective-permute-start.4 = (f32[320,128]{1,0:T(8,128)S(1)}, f32[320,128]{1,0:T(8,128)S(1)}, u32[]{:S(2)}, u32[]{:S(2)}) collective-permute-start(f32[320,128]{1,0:T(8,128)S(1)} %get-tuple-element.13), channel_id=1, source_target_pairs={{0,1},{1,2},{2,3},{4,5},{5,6},{6,7},{8,9},{9,10},{10,11},{12,13},{... | collective-permute-start | bytes 491528 | tf_op jit(solution)/shard_map/ppermute | solution.py:456
  23.2 6.6 %collective-permute-start.5 = (f32[320,128]{1,0:T(8,128)S(1)}, f32[320,128]{1,0:T(8,128)S(1)}, u32[]{:S(2)}, u32[]{:S(2)}) collective-permute-start(f32[320,128]{1,0:T(8,128)S(1)} %get-tuple-element.14), channel_id=1, source_target_pairs={{1,0},{2,1},{3,2},{5,4},{6,5},{7,6},{9,8},{10,9},{11,10},{13,12},{... | collective-permute-start | bytes 491528 | tf_op jit(solution)/shard_map/ppermute | solution.py:456

commit v2 on v1

--- a/solution.py
+++ b/solution.py
@@ -32,8 +32,9 @@
 ROWS = 24
 PER = 14
 COLBLOCK = 93
-FAULT_ROW = 280
-YROWS = 320
+THIRD = 2 * COLBLOCK
+UP_FAULT, UP_ROWS = 232, 256
+DOWN_FAULT, DOWN_ROWS = 208, 232
 
 f32 = jnp.float32
 bf16 = jnp.bfloat16
@@ -52,7 +53,17 @@
     return high, (value - high.astype(f32)).astype(bf16)
 
 
-def pack_kernel(peers, trans, storage, cells, count, ftrans, block, plane, far_cells):
+def pack_kernel(peers, count, *refs):
+    sources, (block, plane), targets, sems = refs[:4], refs[4:6], refs[6:10], refs[10]
+    copies = [
+        pltpu.make_async_copy(src, dst, sems.at[k])
+        for k, (src, dst) in enumerate(zip(sources, targets))
+    ]
+    for copy in copies:
+        copy.start()
+    for copy in copies:
+        copy.wait()
+    trans, storage, cells, ftrans = targets
     last_x = lax.axis_index("gx") == peers[0] - 1
     first_y = lax.axis_index("gy") == 0
     last_y = lax.axis_index("gy") == peers[1] - 1
@@ -98,35 +109,108 @@
         )
     plane[0:72, :] = block[(PER + 4) * 8 : (PER + 13) * 8, :]
     plane[72:80, :] = block[base : base + 8, :]
-    far_cells[...] = block[base : base + 8, :]
-
-
-def column_kernel(own, lo, hi, lo2, hi2, up, down):
-    for out, first in ((up, CY - 3), (down, 0)):
-        for c in range(3):
+
+
+def column_kernel(own, lo, hi, lo2, hi2, up, down, fb):
+    even = lax.rem(lax.axis_index("gx"), 2) == 0
+    tile_own, tile_lo, tile_hi = (ref[224:232, :] for ref in (own, lo, hi))
+    partner = jnp.where(even, tile_hi, tile_lo)
+    other = jnp.where(even, tile_lo, tile_hi)
+    fb[0:4, :] = tile_own[0:4]
+    fb[4:8, :] = partner[0:4]
+    fb[8:12, :] = tile_own[4:8]
+    fb[12:16, :] = other[0:4]
+    for r in range(4):
+        beyond = hi2[0, :, r * NZ : (r + 1) * NZ].astype(f32)
+        fb[16 + r : 17 + r, :] = jnp.where(even, lo2[72 + r : 73 + r, :], beyond)
+    fb[20:24, :] = other[4:8]
+    up[UP_FAULT : UP_FAULT + 24, :] = fb[...]
+    down[DOWN_FAULT : DOWN_FAULT + 24, :] = fb[...]
+    for out, first, third, runs in ((up, CY - 2, CY - 3, (1, 10)), (down, 0, 2, (4,))):
+        for c in range(2):
             y = first + c
             base = c * COLBLOCK
             out[base : base + 9, :] = lo2[pl.ds(y, 9, stride=8), :]
             for k, ref in enumerate((lo, own, hi)):
                 start = base + 9 + 28 * k
                 out[start : start + 28, :] = ref[pl.ds(y, 28, stride=8), :]
-        for k, (ref, start) in enumerate(((own, 224), (lo, 224), (hi, 224), (lo2, 72), (hi2, 0))):
-            out[FAULT_ROW + 8 * k : FAULT_ROW + 8 * k + 8, :] = ref[start : start + 8, :]
-
-
-def lists_of(even, read):
-    own, lo, hi, lo2, hi2 = (read(k) for k in range(5))
-    partner = jnp.where(even, hi, lo)
-    other = jnp.where(even, lo, hi)
-    beyond = jnp.where(even, lo2, hi2)
-
-    def flat(tile, start):
-        return jnp.concatenate([tile[start + r : start + r + 1, :] for r in range(4)], axis=1)
-
-    def whole(tile):
-        return flat(tile, 0).astype(jnp.int32)
-
-    return (whole(own), whole(partner), flat(own, 4)), (whole(other), whole(beyond), flat(other, 4))
+        at = THIRD
+        out[at : at + 3, :] = lo2[pl.ds((runs[-1] - 4) * 8 + third, 3, stride=8), :]
+        at += 3
+        for ref in (lo, own, hi):
+            for x in range(2):
+                for o in runs:
+                    out[at : at + 3, :] = ref[pl.ds((x * PER + o) * 8 + third, 3, stride=8), :]
+                    at += 3
+
+
+def colour(z):
+    half = z >> 1
+    return half - 5 * ((half * 205) >> 10)
+
+
+def prepare(tile, far2, eo):
+    columns = jnp.transpose(tile)
+    lane = lax.broadcasted_iota(jnp.int32, (NZ, NZ), 1)
+    for r in range(4):
+        rows = slice(r * NZ, (r + 1) * NZ)
+
+        def column(k):
+            return columns[:, 4 * k + r : 4 * k + r + 1]
+
+        match = (column(1).astype(jnp.int32) & 127) == lane
+        high = column(2).astype(bf16).astype(f32)
+        far2[rows, 0:NZ] = jnp.where(match, high, 0.0).astype(bf16)
+        far2[rows, NZ : 2 * NZ] = jnp.where(match, column(2) - high, 0.0).astype(bf16)
+        tint = colour(column(4).astype(jnp.int32) & 127)
+        high = column(5).astype(bf16).astype(f32)
+        value = jnp.where((lane == tint) | (lane == 5), high, 0.0)
+        value = jnp.where((lane == tint + 8) | (lane == 13), column(5) - high, value)
+        eo[rows, :] = value.astype(bf16)
+
+    def flat(k):
+        row = jnp.concatenate([tile[4 * k + r : 4 * k + r + 1, :] for r in range(4)], axis=1)
+        return row.astype(jnp.int32) & 1023
+
+    return flat(0), flat(3)
+
+
+def build(y, at_own, at_other, far2, eo):
+    z128 = lax.broadcasted_iota(jnp.int32, (NZ, SLOTS), 0)
+    z8 = lax.broadcasted_iota(jnp.int32, (8, NZ), 1)
+    e8 = lax.broadcasted_iota(jnp.int32, (8, NZ), 0)
+    one = jnp.where((e8 == colour(z8)) | (e8 == 5), 1.0, 0.0).astype(bf16)
+    one2 = jnp.concatenate([one, one], axis=1)
+    hot = jnp.where(at_own == z128 + y * NZ, 1.0, 0.0).astype(bf16)
+    both = dot_nn(hot, far2[...])
+    matrix = both[:, :NZ] + both[:, NZ:]
+    f2 = jnp.concatenate(split(matrix), axis=0)
+    ft2 = jnp.concatenate(split(jnp.transpose(matrix)), axis=0)
+    hot_o = jnp.where(at_other == z128 + y * NZ, 1.0, 0.0).astype(bf16)
+    pieces = jnp.transpose(dot_nn(hot_o, eo[...]))
+    return f2, ft2, (dot_nn(one2, ft2), dot_nn(one2, f2), pieces[:8] + pieces[8:16])
+
+
+def fault_kernel(fb, f2, ft2, rf, far2, eo):
+    at_own, at_other = prepare(fb[...], far2, eo)
+
+    def column(y, carry):
+        f2[y], ft2[y], sums = build(y, at_own, at_other, far2, eo)
+        for k in range(3):
+            rf[k, y] = sums[k]
+        return carry
+
+    lax.fori_loop(0, CY, column, 0)
+
+
+def through(value, matrix2):
+    rows = value.shape[0]
+    high, low = split(value)
+    left = jnp.concatenate(
+        [jnp.concatenate([high, high], axis=1), jnp.concatenate([low, low], axis=1)], axis=0
+    )
+    got = dot_nn(left, matrix2)
+    return got[:rows] + got[rows:]
 
 
 def main_kernel(
@@ -135,9 +219,11 @@
     lo,
     hi,
     lo2,
-    hi2,
     yl,
     yh,
+    f2,
+    ft2,
+    rf_in,
     out,
     w,
     wr,
@@ -149,8 +235,10 @@
     qe,
     ap,
     tt,
-    fh,
-    fl,
+    f2h,
+    ft2h,
+    far2,
+    eo,
 ):
     gx = lax.axis_index("gx")
     gy = lax.axis_index("gy")
@@ -160,6 +248,9 @@
     p_own = jnp.where(even, 3, 2)
     p_far = jnp.where(even, 4, 1)
     p_third = jnp.where(even, 0, 5)
+    p_fault = (p_own, p_far, p_third)
+    z8 = lax.broadcasted_iota(jnp.int32, (8, NZ), 1)
+    e8 = lax.broadcasted_iota(jnp.int32, (8, NZ), 0)
 
     def place(ref, count, first):
         for k in range(count):
@@ -169,11 +260,17 @@
     place(lo2, 9, 4)
     for k, ref in enumerate((lo, own, hi)):
         place(ref, 28, PER * (1 + 2 * k))
-    for ref, row in ((yl, 0), (yh, 11)):
-        for c in range(3):
+    for ref, row, third, runs in ((yl, 1, 0, (1, 10)), (yh, 11, 13, (4,))):
+        for c in range(2):
             base = c * COLBLOCK
             w[pl.ds(4 * ROWS + row + c, 9, stride=ROWS), :] = ref[base : base + 9, :]
             w[pl.ds(PER * ROWS + row + c, 84, stride=ROWS), :] = ref[base + 9 : base + 93, :]
+        at = THIRD
+        for plane in range(7):
+            for o in runs[-1:] if plane == 0 else runs:
+                start = (plane * PER + o) * ROWS + third
+                w[pl.ds(start, 3, stride=ROWS), :] = ref[at : at + 3, :]
+                at += 3
     for p in range(7):
         for o, step in enumerate(FORWARD):
             if step[2] == 0 or (p == 0 and o < 4):
@@ -182,65 +279,24 @@
             shift = 1 if step[2] == 1 else NZ - 1
             wr[base : base + ROWS, :] = pltpu.roll(w[base : base + ROWS, :], shift, 1)
 
-    z128 = lax.broadcasted_iota(jnp.int32, (NZ, SLOTS), 0)
-    z8 = lax.broadcasted_iota(jnp.int32, (8, NZ), 1)
-    e8 = lax.broadcasted_iota(jnp.int32, (8, NZ), 0)
-
-    def colour(z):
-        half = z >> 1
-        return half - 5 * ((half * 205) >> 10)
-
-    one_all = jnp.where((e8 == colour(z8)) | (e8 == 5), 1.0, 0.0).astype(bf16)
-    es = lax.broadcasted_iota(jnp.int32, (8, SLOTS), 0)
-
     fd[...] = jnp.zeros_like(fd)
 
-    def prepare(lists):
-        (c_own, c_far, live), (c_other, c_beyond, live_o) = lists
-        live_h = live.astype(bf16).astype(f32)
-        live_l = live - live_h
-        match = (c_far & 127) == z128
-        far2 = jnp.concatenate(
-            [jnp.where(match, live_h, 0.0), jnp.where(match, live_l, 0.0)], axis=0
-        ).astype(bf16)
-        lo_h = live_o.astype(bf16).astype(f32)
-        lo_l = live_o - lo_h
-        same = (es == colour(c_beyond & 127)) | (es == 5)
-        other2 = jnp.concatenate(
-            [jnp.where(same, lo_h, 0.0), jnp.where(same, lo_l, 0.0)], axis=0
-        ).astype(bf16)
-        return c_own & 1023, far2, c_other & 1023, other2
-
-    def build(column, y, ready):
-        at_own, far2, at_other, other2 = ready
-        hot = jnp.where(at_own == z128 + y * NZ, 1.0, 0.0).astype(bf16)
-        both = dot_nt(hot, far2)
-        f_h, f_l = split(both[:, :NZ] + both[:, NZ:])
-        fh[column] = f_h
-        fl[column] = f_l
-        to_own = dot_nt(one_all, f_h) + dot_nt(one_all, f_l)
-        to_far = dot_nn(one_all, f_h) + dot_nn(one_all, f_l)
-        hot_o = jnp.where(at_other == z128 + y * NZ, 1.0, 0.0).astype(bf16)
-        pieces = dot_nt(other2, hot_o)
-        to_third = pieces[:8] + pieces[8:]
-        for k, (plane, value) in enumerate(((p_own, to_own), (p_far, to_far), (p_third, to_third))):
-            rf[k, column] = value
-            fd[pl.ds(plane * 16 + column, 1), :] = value[5:6, :]
-
-    tiles = ((own, 224), (lo, 224), (hi, 224), (lo2, 72), (hi2, 0))
-    ready = prepare(lists_of(even, lambda k: tiles[k][0][tiles[k][1] : tiles[k][1] + 8, :]))
-
-    def build_own(y, carry):
-        build(y + 2, y, ready)
-        return carry
-
-    lax.fori_loop(0, CY, build_own, 0)
-    for ref, columns in ((yl, ((0, 6), (1, 7))), (yh, ((10, 0), (11, 1)))):
-        ready_y = prepare(
-            lists_of(even, lambda k: ref[FAULT_ROW + 8 * k : FAULT_ROW + 8 * k + 8, :])
-        )
+    def put(column, k, value):
+        rf[k, column] = value
+        fd[pl.ds(p_fault[k] * 16 + column, 1), :] = value[5:6, :]
+
+    for y in range(CY):
+        for k in range(3):
+            put(y + 2, k, rf_in[k, y])
+    for ref, start, columns in ((yl, UP_FAULT, ((0, 6), (1, 7))), (yh, DOWN_FAULT, ((10, 0), (11, 1)))):
+        at_own, at_other = prepare(ref[start : start + 24, :], far2, eo)
         for column, y in columns:
-            build(column, y, ready_y)
+            near, near_t, values = build(y, at_own, at_other, far2, eo)
+            if column in (1, 10):
+                f2h[column // 10] = near
+                ft2h[column // 10] = near_t
+            for k in range(3):
+                put(column, k, values[k])
 
     r16 = lax.broadcasted_iota(jnp.int32, (16, NZ), 0)
     z16 = lax.broadcasted_iota(jnp.int32, (16, NZ), 1)
@@ -302,7 +358,7 @@
                 qe[p, c, lat] = (
                     qc[pl.ds(at, 1), :] * mask_own + qc[pl.ds(at + 16, 1), :] * mask_oth
                 )
-        for k, plane in enumerate((p_own, p_far, p_third)):
+        for k, plane in enumerate(p_fault):
             qe[plane, c, 2] = qe[plane, c, 2] + rf[k, c] * (
                 inv[pl.ds(plane * 16 + c, 1), :] * rows5
             )
@@ -361,26 +417,25 @@
 
     lax.fori_loop(0, 5, apply_pair, 0)
 
-    def fault_apply(c, carry):
-        both = jnp.concatenate([fh[c], fl[c]], axis=0)
+    def fault_apply(c, f2c, ft2c):
         ly_oth = 2 * lax.rem(c, 2)
-        for plane, source, x_own, forward in (
-            (p_own, p_far, 1 + sgn, True),
-            (p_far, p_own, 1 - sgn, False),
+        for plane, source, x_own, matrix in (
+            (p_own, p_far, 1 + sgn, ft2c),
+            (p_far, p_own, 1 - sgn, f2c),
         ):
-            high, low = split(qe[source, c].reshape(32, NZ))
-            if forward:
-                got = dot_nt(jnp.concatenate([high, low], axis=0), both)
-                total = got[:32, :NZ] + got[:32, NZ:] + got[32:, :NZ]
-            else:
-                total = dot_nn(high, fh[c]) + dot_nn(high, fl[c]) + dot_nn(low, fh[c])
+            total = through(qe[source, c].reshape(32, NZ), matrix)
             for lat in range(4):
                 lx = 1 if lat >= 2 else x_own
                 ly = ly_oth if lat % 2 else 1
                 ap[plane - 1, c - 1, lx, ly] = ap[plane - 1, c - 1, lx, ly] - total[8 * lat : 8 * lat + 8]
+
+    def fault_own(y, carry):
+        fault_apply(y + 2, f2[y], ft2[y])
         return carry
 
-    lax.fori_loop(1, 11, fault_apply, 0)
+    lax.fori_loop(0, CY, fault_own, 0)
+    fault_apply(1, f2h[0], ft2h[0])
+    fault_apply(10, f2h[1], ft2h[1])
 
     x_coarse = lax.rem(gx, 5) + 5
     a_of = [lax.rem(x_coarse + d, 5) for d in range(-2, 3)]
@@ -418,21 +473,15 @@
         c = y + 2
         coarse_y = y // 2
         lane = (coarse_y % 2) * 256
-        both = jnp.concatenate([fh[c], fl[c]], axis=0)
         value = ap[p_far - 1, c - 1].reshape(72, NZ) * inv[pl.ds(p_far * 16 + c, 1), :]
-        high, low = split(value)
-
-        def add(total):
-            for lx in range(3):
-                a = lax.rem(x_coarse + lx - 1 + sgn, 5)
-                for ly in range(3):
-                    b = b_of(coarse_y, ly - 1)
-                    at = 8 * (3 * lx + ly)
-                    place_at = tt.at[coarse_y // 2, a, b, :, lane : lane + NZ]
-                    place_at[...] = place_at[...] + total[at : at + 8]
-
-        got = dot_nt(jnp.concatenate([high, low], axis=0), both)
-        add(got[:72, :NZ] + got[:72, NZ:] + got[72:, :NZ])
+        total = through(value, ft2[y])
+        for lx in range(3):
+            a = lax.rem(x_coarse + lx - 1 + sgn, 5)
+            for ly in range(3):
+                b = b_of(coarse_y, ly - 1)
+                at = 8 * (3 * lx + ly)
+                place_at = tt.at[coarse_y // 2, a, b, :, lane : lane + NZ]
+                place_at[...] = place_at[...] + total[at : at + 8]
 
     kz = lax.broadcasted_iota(jnp.int32, (512, NZ), 0)
     kout = lax.broadcasted_iota(jnp.int32, (512, NZ), 1)
@@ -457,42 +506,62 @@
 
 
 VMEM = pl.BlockSpec(memory_space=pltpu.VMEM)
-SMEM = pl.BlockSpec(memory_space=pltpu.SMEM)
-PARAMS = pltpu.CompilerParams(vmem_limit_bytes=48 * 1024 * 1024)
-
-
-def sds(*shape):
-    return jax.ShapeDtypeStruct(shape, f32)
+HBM = pl.BlockSpec(memory_space=pltpu.HBM)
+
+
+def params(mib):
+    return pltpu.CompilerParams(vmem_limit_bytes=mib * 1024 * 1024)
+
+
+def sds(*shape, dtype=f32):
+    return jax.ShapeDtypeStruct(shape, dtype)
 
 
 def per_device(trans, storage, fault_cells, fault_count, fault_trans):
     peers = (lax.axis_size("gx"), lax.axis_size("gy"))
-    own, plane, cells = pl.pallas_call(
+    hi2 = shift(fault_cells, "gx", -2)
+    sources = [
+        pltpu.with_memory_space_constraint(array, pltpu.HBM)
+        for array in (trans, storage, fault_cells, fault_trans)
+    ]
+    own, plane = pl.pallas_call(
         functools.partial(pack_kernel, peers),
-        out_shape=(sds(232, NZ), sds(80, NZ), sds(8, NZ)),
-        in_specs=[VMEM, VMEM, VMEM, SMEM, VMEM],
-        out_specs=(VMEM, VMEM, VMEM),
-        compiler_params=PARAMS,
+        out_shape=(sds(232, NZ), sds(80, NZ)),
+        in_specs=[pl.BlockSpec(memory_space=pltpu.SMEM)] + [HBM] * 4,
+        out_specs=(VMEM, VMEM),
+        scratch_shapes=[pltpu.VMEM(array.shape, array.dtype) for array in sources]
+        + [pltpu.SemaphoreType.DMA((4,))],
+        compiler_params=params(16),
         name="pack",
-    )(trans, storage, fault_cells, fault_count, fault_trans)
+    )(fault_count, *sources)
+    lo2 = shift(plane, "gx", 2)
     lo = shift(own, "gx", 1)
     hi = shift(own, "gx", -1)
-    lo2 = shift(plane, "gx", 2)
-    hi2 = shift(cells, "gx", -2)
-    up, down = pl.pallas_call(
+    up, down, fb = pl.pallas_call(
         column_kernel,
-        out_shape=(sds(YROWS, NZ), sds(YROWS, NZ)),
+        out_shape=(sds(UP_ROWS, NZ), sds(DOWN_ROWS, NZ), sds(24, NZ)),
         in_specs=[VMEM] * 5,
-        out_specs=(VMEM, VMEM),
-        compiler_params=PARAMS,
+        out_specs=(VMEM,) * 3,
+        compiler_params=params(16),
         name="columns",
     )(own, lo, hi, lo2, hi2)
     yl = shift(up, "gy", 1)
     yh = shift(down, "gy", -1)
+    pieces = sds(CY, 2 * NZ, NZ, dtype=bf16)
+    f2, ft2, rf = pl.pallas_call(
+        fault_kernel,
+        out_shape=(pieces, pieces, sds(3, CY, 8, NZ)),
+        in_specs=[VMEM],
+        out_specs=(VMEM,) * 3,
+        scratch_shapes=[pltpu.VMEM((SLOTS, 2 * NZ), bf16), pltpu.VMEM((SLOTS, NZ), bf16)],
+        compiler_params=params(16),
+        cost_estimate=pl.CostEstimate(flops=2 * 10**9, bytes_accessed=2**21, transcendentals=0),
+        name="faults",
+    )(fb)
     return pl.pallas_call(
         functools.partial(main_kernel, peers),
         out_shape=sds(125, 1, 256),
-        in_specs=[VMEM] * 7,
+        in_specs=[VMEM] * 9,
         out_specs=VMEM,
         scratch_shapes=[
             pltpu.VMEM((7 * PER * ROWS, NZ), f32),
@@ -505,12 +574,14 @@
             pltpu.VMEM((6, 12, 4, 8, NZ), f32),
             pltpu.VMEM((4, 10, 3, 3, 8, NZ), f32),
             pltpu.VMEM((2, 5, 5, 8, 512), f32),
-            pltpu.VMEM((12, NZ, NZ), bf16),
-            pltpu.VMEM((12, NZ, NZ), bf16),
+            pltpu.VMEM((2, 2 * NZ, NZ), bf16),
+            pltpu.VMEM((2, 2 * NZ, NZ), bf16),
+            pltpu.VMEM((SLOTS, 2 * NZ), bf16),
+            pltpu.VMEM((SLOTS, NZ), bf16),
         ],
-        compiler_params=PARAMS,
+        compiler_params=params(24),
         name="galerkin",
-    )(own, lo, hi, lo2, hi2, yl, yh)
+    )(own, lo, hi, lo2, yl, yh, f2, ft2, rf)
 
 
 def solution(mesh):

time: 41.9 us -> 35 us (0.84)
  waiting for transfers between devices: 7.77 us -> 3.04 us
  local copies, waits for them, and re-layouts: 2.95 us -> 0.01 us
  Pallas kernels: 11.8 us -> 12.6 us
    ppermute x6, waiting for transfers between devices: 7.77 us -> 3.04 us  [shift(): return lax.ppermute(value, axis, pairs)]
    pallas_call x1, Pallas kernels: 11.6 us -> 7.61 us  [per_device(): pl.pallas_call(functools.partial(main_kernel, peers), out_shape=sds(125,...]
    pallas_call x1 -> x2, Pallas kernels: 0.06 us -> 3.97 us  [the longest x1 3.92 us: per_device(): pl.pallas_call(fault_kernel, out_shape=(pieces, pieces, sds(3, CY, 8, NZ)...]
    unnamed x8 -> x2, local copies, waits for them, and re-layouts: 2.95 us -> 0.01 us
    pallas_call x1, Pallas kernels: 0.11 us -> 1.05 us  [per_device(): pl.pallas_call(functools.partial(pack_kernel, peers), out_shape=(sds(232,...]
  transfers between devices with their start and end apart: 6 -> 6, of which waited for: 3 -> 1; matrix products, arithmetic and copies ran while one was open for 0% -> 0% of each run, Pallas kernels for 0% -> 11%
where the time goes in v2:
time: 35 us; the launch traced here: 34.6 us
  starting transfers between devices  18.2 us (52%)
  Pallas kernels  12.6 us (36%)
  waiting for transfers between devices  3.04 us (9%)
  between operations  0.74 us (2%)
    ppermute x6, starting transfers between devices, shift(): return lax.ppermute(value, axis, pairs)  18.2 us
    pallas_call x1, Pallas kernels, per_device(): pl.pallas_call(functools.partial(main_kernel, peers), out_shape=sds(125,...  7.61 us
    pallas_call x1, Pallas kernels, per_device(): pl.pallas_call(fault_kernel, out_shape=(pieces, pieces, sds(3, CY, 8, NZ)...  3.92 us
    ppermute x6, waiting for transfers between devices, shift(): return lax.ppermute(value, axis, pairs)  3.04 us
    pallas_call x1, Pallas kernels, per_device(): pl.pallas_call(functools.partial(pack_kernel, peers), out_shape=(sds(232,...  1.05 us
  transfers between devices with their start and end apart: 6, of which 1 were waited for; matrix products, arithmetic and copies ran while one was open for 0% of the time, Pallas kernels for 11%

profile of v2, /device:TPU:1, one launch (start us, length us, event | category | flops | bytes accessed | tf_op | source)
XLA Modules:
  0.0 34.6 jit_solution(16967192498392270088)
XLA Ops:
  0.7 1.0 %pack.1 = (f32[232,128]{1,0:T(8,128)S(1)}, f32[80,128]{1,0:T(8,128)S(1)}) custom-call(s32[1,1]{1,0:T(1,128)S(6)} %copy.6.count, f32[13,2,1024]{2,1,0:T(2,128)} %refs_0_.1, f32[2,1024]{1,0:T(2,128)} %refs_1_.1, s32[1,1,512]{2,1,0:T(1,128)} %refs_2_.1, f32[1,1,512]{2,1,0:T(1,128)} %refs_3_.1), custom_call_target="tpu_custom_call" | custom-call | tf_op jit(solution)/shard_map/pack/pallas_call | solution.py:527
  1.7 0.0 copy-start
  1.7 1.3 %collective-permute-start.1 = (f32[232,128]{1,0:T(8,128)S(1)}, f32[232,128]{1,0:T(8,128)S(1)}, u32[]{:S(2)}, u32[]{:S(2)}) collective-permute-start(f32[232,128]{1,0:T(8,128)S(1)} %get-tuple-element.13.own), channel_id=1, source_target_pairs={{4,0},{8,4},{12,8},{16,12},{20,16},{24,20},{28,24},{5,1},{9,5},{13... | collective-permute-start | bytes 356360 | tf_op jit(solution)/shard_map/ppermute | solution.py:505
  3.0 4.6 %collective-permute-start = (f32[232,128]{1,0:T(8,128)S(1)}, f32[232,128]{1,0:T(8,128)S(1)}, u32[]{:S(2)}, u32[]{:S(2)}) collective-permute-start(f32[232,128]{1,0:T(8,128)S(1)} %get-tuple-element.13.own), channel_id=1, source_target_pairs={{0,4},{4,8},{8,12},{12,16},{16,20},{20,24},{24,28},{1,5},{5,9},{9,... | collective-permute-start | bytes 356360 | tf_op jit(solution)/shard_map/ppermute | solution.py:505
  7.6 3.4 %collective-permute-start.2 = (f32[80,128]{1,0:T(8,128)S(1)}, f32[80,128]{1,0:T(8,128)S(1)}, u32[]{:S(2)}, u32[]{:S(2)}) collective-permute-start(f32[80,128]{1,0:T(8,128)S(1)} %get-tuple-element.14), channel_id=1, source_target_pairs={{0,8},{4,12},{8,16},{12,20},{16,24},{20,28},{1,9},{5,13},{9,17},{1... | collective-permute-start | bytes 122888 | tf_op jit(solution)/shard_map/ppermute | solution.py:505
  11.1 0.0 copy-done
  11.1 1.3 %collective-permute-start.3 = (s32[1,1,512]{2,1,0:T(1,128)S(1)}, s32[1,1,512]{2,1,0:T(1,128)S(1)}, u32[]{:S(2)}, u32[]{:S(2)}) collective-permute-start(s32[1,1,512]{2,1,0:T(1,128)S(1)} %copy-done), channel_id=1, source_target_pairs={{8,0},{12,4},{16,8},{20,12},{24,16},{28,20},{9,1},{13,5},{17,9},{2... | collective-permute-start | bytes 6152 | tf_op jit(solution)/shard_map/ppermute | solution.py:505
  12.4 3.0 %collective-permute-done.3.hi2 = s32[1,1,512]{2,1,0:T(1,128)S(1)} collective-permute-done((s32[1,1,512]{2,1,0:T(1,128)S(1)}, s32[1,1,512]{2,1,0:T(1,128)S(1)}, u32[]{:S(2)}, u32[]{:S(2)}) %collective-permute-start.3) | collective-permute-done | bytes 2080 | tf_op jit(solution)/shard_map/ppermute | solution.py:505
  15.4 0.0 collective-permute-done.2.lo2
  15.4 0.0 collective-permute-done.1.hi
  15.4 0.0 collective-permute-done.lo
  15.4 0.1 columns.1
  15.5 4.6 %collective-permute-start.5 = (f32[232,128]{1,0:T(8,128)S(1)}, f32[232,128]{1,0:T(8,128)S(1)}, u32[]{:S(2)}, u32[]{:S(2)}) collective-permute-start(f32[232,128]{1,0:T(8,128)S(1)} %get-tuple-element.16), channel_id=1, source_target_pairs={{1,0},{2,1},{3,2},{5,4},{6,5},{7,6},{9,8},{10,9},{11,10},{13,12},{... | collective-permute-start | bytes 356360 | tf_op jit(solution)/shard_map/ppermute | solution.py:505
  20.1 3.0 %collective-permute-start.4 = (f32[256,128]{1,0:T(8,128)S(1)}, f32[256,128]{1,0:T(8,128)S(1)}, u32[]{:S(2)}, u32[]{:S(2)}) collective-permute-start(f32[256,128]{1,0:T(8,128)S(1)} %get-tuple-element.15), channel_id=1, source_target_pairs={{0,1},{1,2},{2,3},{4,5},{5,6},{6,7},{8,9},{9,10},{10,11},{12,13},{... | collective-permute-start | bytes 393224 | tf_op jit(solution)/shard_map/ppermute | solution.py:505
  23.1 3.9 %faults.1 = (bf16[8,256,128]{2,1,0:T(8,128)(2,1)S(1)}, bf16[8,256,128]{2,1,0:T(8,128)(2,1)S(1)}, f32[3,8,8,128]{3,2,1,0:T(8,128)S(1)}) custom-call(f32[24,128]{1,0:T(8,128)S(1)} %get-tuple-element.17.fb), custom_call_target="tpu_custom_call" | custom-call | flops 2000000000 | bytes 2097152 | tf_op jit(solution)/shard_map/faults/pallas_call | solution.py:551
  27.0 0.0 collective-permute-done.5.yh
  27.0 0.0 collective-permute-done.4.yl
  27.0 7.6 %galerkin.1 = f32[125,1,256]{2,1,0:T(1,128)} custom-call(f32[232,128]{1,0:T(8,128)S(1)} %get-tuple-element.13.own, f32[232,128]{1,0:T(8,128)S(1)} %collective-permute-done.lo, f32[232,128]{1,0:T(8,128)S(1)} %collective-permute-done.1.hi, f32[80,128]{1,0:T(8,128)S(1)} %collective-permute-done.2.lo2, f32[256,128]{1,0:T(8,128)S(1)} %collective-permute-done.4.yl, ...), custom_call_target="tpu_custom_call" | custom-call | tf_op jit(solution)/shard_map/galerkin/pallas_call | solution.py:561
Async XLA Ops:
  1.7 9.4 %copy-start = (s32[1,1,512]{2,1,0:T(1,128)S(1)}, s32[1,1,512]{2,1,0:T(1,128)}, u32[]{:S(2)}) copy-start(s32[1,1,512]{2,1,0:T(1,128)} %refs_2_.1) | copy-start | bytes 6148
  1.7 13.7 %collective-permute-start.1 = (f32[232,128]{1,0:T(8,128)S(1)}, f32[232,128]{1,0:T(8,128)S(1)}, u32[]{:S(2)}, u32[]{:S(2)}) collective-permute-start(f32[232,128]{1,0:T(8,128)S(1)} %get-tuple-element.13.own), channel_id=1, source_target_pairs={{4,0},{8,4},{12,8},{16,12},{20,16},{24,20},{28,24},{5,1},{9,5},{13... | collective-permute-start | bytes 356360 | tf_op jit(solution)/shard_map/ppermute | solution.py:505
  3.0 12.4 %collective-permute-start = (f32[232,128]{1,0:T(8,128)S(1)}, f32[232,128]{1,0:T(8,128)S(1)}, u32[]{:S(2)}, u32[]{:S(2)}) collective-permute-start(f32[232,128]{1,0:T(8,128)S(1)} %get-tuple-element.13.own), channel_id=1, source_target_pairs={{0,4},{4,8},{8,12},{12,16},{16,20},{20,24},{24,28},{1,5},{5,9},{9,... | collective-permute-start | bytes 356360 | tf_op jit(solution)/shard_map/ppermute | solution.py:505
  7.6 7.8 %collective-permute-start.2 = (f32[80,128]{1,0:T(8,128)S(1)}, f32[80,128]{1,0:T(8,128)S(1)}, u32[]{:S(2)}, u32[]{:S(2)}) collective-permute-start(f32[80,128]{1,0:T(8,128)S(1)} %get-tuple-element.14), channel_id=1, source_target_pairs={{0,8},{4,12},{8,16},{12,20},{16,24},{20,28},{1,9},{5,13},{9,17},{1... | collective-permute-start | bytes 122888 | tf_op jit(solution)/shard_map/ppermute | solution.py:505
  11.1 4.3 %collective-permute-start.3 = (s32[1,1,512]{2,1,0:T(1,128)S(1)}, s32[1,1,512]{2,1,0:T(1,128)S(1)}, u32[]{:S(2)}, u32[]{:S(2)}) collective-permute-start(s32[1,1,512]{2,1,0:T(1,128)S(1)} %copy-done), channel_id=1, source_target_pairs={{8,0},{12,4},{16,8},{20,12},{24,16},{28,20},{9,1},{13,5},{17,9},{2... | collective-permute-start | bytes 6152 | tf_op jit(solution)/shard_map/ppermute | solution.py:505
  15.5 11.6 %collective-permute-start.5 = (f32[232,128]{1,0:T(8,128)S(1)}, f32[232,128]{1,0:T(8,128)S(1)}, u32[]{:S(2)}, u32[]{:S(2)}) collective-permute-start(f32[232,128]{1,0:T(8,128)S(1)} %get-tuple-element.16), channel_id=1, source_target_pairs={{1,0},{2,1},{3,2},{5,4},{6,5},{7,6},{9,8},{10,9},{11,10},{13,12},{... | collective-permute-start | bytes 356360 | tf_op jit(solution)/shard_map/ppermute | solution.py:505
  20.1 7.0 %collective-permute-start.4 = (f32[256,128]{1,0:T(8,128)S(1)}, f32[256,128]{1,0:T(8,128)S(1)}, u32[]{:S(2)}, u32[]{:S(2)}) collective-permute-start(f32[256,128]{1,0:T(8,128)S(1)} %get-tuple-element.15), channel_id=1, source_target_pairs={{0,1},{1,2},{2,3},{4,5},{5,6},{6,7},{8,9},{9,10},{10,11},{12,13},{... | collective-permute-start | bytes 393224 | tf_op jit(solution)/shard_map/ppermute | solution.py:505

commit v3 on v2

--- a/solution.py
+++ b/solution.py
@@ -33,15 +33,10 @@
 PER = 14
 COLBLOCK = 93
 THIRD = 2 * COLBLOCK
-UP_FAULT, UP_ROWS = 232, 256
-DOWN_FAULT, DOWN_ROWS = 208, 232
+FAULT_ROW, Y_ROWS = 232, 256
 
 f32 = jnp.float32
 bf16 = jnp.bfloat16
-
-
-def dot_nt(a, b):
-    return lax.dot_general(a, b, (((1,), (1,)), ((), ())), preferred_element_type=f32)
 
 
 def dot_nn(a, b):
@@ -111,22 +106,21 @@
     plane[72:80, :] = block[base : base + 8, :]
 
 
-def column_kernel(own, lo, hi, lo2, hi2, up, down, fb):
-    even = lax.rem(lax.axis_index("gx"), 2) == 0
-    tile_own, tile_lo, tile_hi = (ref[224:232, :] for ref in (own, lo, hi))
-    partner = jnp.where(even, tile_hi, tile_lo)
-    other = jnp.where(even, tile_lo, tile_hi)
-    fb[0:4, :] = tile_own[0:4]
-    fb[4:8, :] = partner[0:4]
-    fb[8:12, :] = tile_own[4:8]
-    fb[12:16, :] = other[0:4]
-    for r in range(4):
-        beyond = hi2[0, :, r * NZ : (r + 1) * NZ].astype(f32)
-        fb[16 + r : 17 + r, :] = jnp.where(even, lo2[72 + r : 73 + r, :], beyond)
-    fb[20:24, :] = other[4:8]
-    up[UP_FAULT : UP_FAULT + 24, :] = fb[...]
-    down[DOWN_FAULT : DOWN_FAULT + 24, :] = fb[...]
-    for out, first, third, runs in ((up, CY - 2, CY - 3, (1, 10)), (down, 0, 2, (4,))):
+def by_parity(axis, body):
+    odd = lax.rem(lax.axis_index(axis), 2)
+    for k in range(2):
+        pl.when(odd == k)(functools.partial(body, k))
+
+
+def column_kernel(own, rp, ro, rd, re, to_core, to_chip):
+    tile = own[224:232, :]
+    other = ro[224:232, :]
+    parts = (tile[0:4], rp[224:228, :], tile[4:8], other[0:4], rd[72:76, :], other[4:8])
+    for out in (to_core, to_chip):
+        for k, part in enumerate(parts):
+            out[FAULT_ROW + 4 * k : FAULT_ROW + 4 * k + 4, :] = part
+
+    def fill(out, lo, hi, lo2, first, third, runs):
         for c in range(2):
             y = first + c
             base = c * COLBLOCK
@@ -143,64 +137,89 @@
                     out[at : at + 3, :] = ref[pl.ds((x * PER + o) * 8 + third, 3, stride=8), :]
                     at += 3
 
+    def for_x(odd_x):
+        lo, hi, lo2 = (rp, ro, re) if odd_x else (ro, rp, rd)
+
+        def for_y(odd_y):
+            up, down = (to_chip, to_core) if odd_y else (to_core, to_chip)
+            fill(up, lo, hi, lo2, CY - 2, CY - 3, (1, 10))
+            fill(down, lo, hi, lo2, 0, 2, (4,))
+
+        by_parity("gy", for_y)
+
+    by_parity("gx", for_x)
+
 
 def colour(z):
     half = z >> 1
     return half - 5 * ((half * 205) >> 10)
 
 
-def prepare(tile, far2, eo):
-    columns = jnp.transpose(tile)
+def slot_columns(rows):
+    tall = jnp.transpose(jnp.concatenate(rows, axis=0))
+    return [[tall[:, 4 * k + r : 4 * k + r + 1] for r in range(4)] for k in range(len(rows))]
+
+
+def flat_cells(rows):
+    row = jnp.concatenate([rows[r : r + 1] for r in range(4)], axis=1)
+    return row.astype(jnp.int32) & 1023
+
+
+def fill_far(far2, partner, live):
     lane = lax.broadcasted_iota(jnp.int32, (NZ, NZ), 1)
     for r in range(4):
         rows = slice(r * NZ, (r + 1) * NZ)
-
-        def column(k):
-            return columns[:, 4 * k + r : 4 * k + r + 1]
-
-        match = (column(1).astype(jnp.int32) & 127) == lane
-        high = column(2).astype(bf16).astype(f32)
+        match = (partner[r].astype(jnp.int32) & 127) == lane
+        high = live[r].astype(bf16).astype(f32)
         far2[rows, 0:NZ] = jnp.where(match, high, 0.0).astype(bf16)
-        far2[rows, NZ : 2 * NZ] = jnp.where(match, column(2) - high, 0.0).astype(bf16)
-        tint = colour(column(4).astype(jnp.int32) & 127)
-        high = column(5).astype(bf16).astype(f32)
+        far2[rows, NZ : 2 * NZ] = jnp.where(match, live[r] - high, 0.0).astype(bf16)
+
+
+def fill_tint(eo, beyond, live):
+    lane = lax.broadcasted_iota(jnp.int32, (NZ, NZ), 1)
+    for r in range(4):
+        tint = colour(beyond[r].astype(jnp.int32) & 127)
+        high = live[r].astype(bf16).astype(f32)
         value = jnp.where((lane == tint) | (lane == 5), high, 0.0)
-        value = jnp.where((lane == tint + 8) | (lane == 13), column(5) - high, value)
-        eo[rows, :] = value.astype(bf16)
-
-    def flat(k):
-        row = jnp.concatenate([tile[4 * k + r : 4 * k + r + 1, :] for r in range(4)], axis=1)
-        return row.astype(jnp.int32) & 1023
-
-    return flat(0), flat(3)
-
-
-def build(y, at_own, at_other, far2, eo):
+        value = jnp.where((lane == tint + 8) | (lane == 13), live[r] - high, value)
+        eo[r * NZ : (r + 1) * NZ, :] = value.astype(bf16)
+
+
+def fill_hot(hot, cells, columns):
     z128 = lax.broadcasted_iota(jnp.int32, (NZ, SLOTS), 0)
+    for k, y in enumerate(columns):
+        value = jnp.where(cells == z128 + y * NZ, 1.0, 0.0)
+        hot[k * NZ : (k + 1) * NZ, :] = value.astype(bf16)
+
+
+def pair_matrix(both):
     z8 = lax.broadcasted_iota(jnp.int32, (8, NZ), 1)
     e8 = lax.broadcasted_iota(jnp.int32, (8, NZ), 0)
     one = jnp.where((e8 == colour(z8)) | (e8 == 5), 1.0, 0.0).astype(bf16)
     one2 = jnp.concatenate([one, one], axis=1)
-    hot = jnp.where(at_own == z128 + y * NZ, 1.0, 0.0).astype(bf16)
-    both = dot_nn(hot, far2[...])
     matrix = both[:, :NZ] + both[:, NZ:]
     f2 = jnp.concatenate(split(matrix), axis=0)
     ft2 = jnp.concatenate(split(jnp.transpose(matrix)), axis=0)
-    hot_o = jnp.where(at_other == z128 + y * NZ, 1.0, 0.0).astype(bf16)
-    pieces = jnp.transpose(dot_nn(hot_o, eo[...]))
-    return f2, ft2, (dot_nn(one2, ft2), dot_nn(one2, f2), pieces[:8] + pieces[8:16])
-
-
-def fault_kernel(fb, f2, ft2, rf, far2, eo):
-    at_own, at_other = prepare(fb[...], far2, eo)
-
-    def column(y, carry):
-        f2[y], ft2[y], sums = build(y, at_own, at_other, far2, eo)
-        for k in range(3):
-            rf[k, y] = sums[k]
-        return carry
-
-    lax.fori_loop(0, CY, column, 0)
+    return f2, ft2, dot_nn(one2, ft2), dot_nn(one2, f2)
+
+
+def fault_kernel(own, rp, f2, ft2, rf, far2, hot, both):
+    partner, live = slot_columns([rp[224:228, :], own[228:232, :]])
+    fill_far(far2, partner, live)
+    fill_hot(hot, flat_cells(own[224:228, :]), range(CY))
+    both[...] = dot_nn(hot[...], far2[...])
+    for y in range(CY):
+        f2[y], ft2[y], rf[0, y], rf[1, y] = pair_matrix(both[y * NZ : (y + 1) * NZ, :])
+
+
+def third_kernel(ro, rd, rf, eo, hot, both):
+    beyond, live = slot_columns([rd[72:76, :], ro[228:232, :]])
+    fill_tint(eo, beyond, live)
+    fill_hot(hot, flat_cells(ro[224:228, :]), range(CY))
+    both[...] = dot_nn(hot[...], eo[...])
+    for y in range(CY):
+        pieces = jnp.transpose(both[y * NZ : (y + 1) * NZ, :])
+        rf[y] = pieces[:8] + pieces[8:16]
 
 
 def through(value, matrix2):
@@ -214,16 +233,17 @@
 
 
 def main_kernel(
-    peers,
     own,
-    lo,
-    hi,
-    lo2,
-    yl,
-    yh,
+    rp,
+    ro,
+    rd,
+    re,
+    from_core,
+    from_chip,
     f2,
     ft2,
-    rf_in,
+    rf_pair,
+    rf_third,
     out,
     w,
     wr,
@@ -239,6 +259,7 @@
     ft2h,
     far2,
     eo,
+    hot,
 ):
     gx = lax.axis_index("gx")
     gy = lax.axis_index("gy")
@@ -257,20 +278,30 @@
             base = (first + k) * ROWS
             w[base + 3 : base + 11, :] = ref[8 * k : 8 * k + 8, :]
 
-    place(lo2, 9, 4)
-    for k, ref in enumerate((lo, own, hi)):
-        place(ref, 28, PER * (1 + 2 * k))
-    for ref, row, third, runs in ((yl, 1, 0, (1, 10)), (yh, 11, 13, (4,))):
-        for c in range(2):
-            base = c * COLBLOCK
-            w[pl.ds(4 * ROWS + row + c, 9, stride=ROWS), :] = ref[base : base + 9, :]
-            w[pl.ds(PER * ROWS + row + c, 84, stride=ROWS), :] = ref[base + 9 : base + 93, :]
-        at = THIRD
-        for plane in range(7):
-            for o in runs[-1:] if plane == 0 else runs:
-                start = (plane * PER + o) * ROWS + third
-                w[pl.ds(start, 3, stride=ROWS), :] = ref[at : at + 3, :]
-                at += 3
+    def place_x(odd):
+        lo, hi, lo2 = (rp, ro, re) if odd else (ro, rp, rd)
+        place(lo2, 9, 4)
+        place(lo, 28, PER)
+        place(hi, 28, 5 * PER)
+
+    place(own, 28, 3 * PER)
+    by_parity("gx", place_x)
+
+    def place_y(odd):
+        yl, yh = (from_core, from_chip) if odd else (from_chip, from_core)
+        for ref, row, third, runs in ((yl, 1, 0, (1, 10)), (yh, 11, 13, (4,))):
+            for c in range(2):
+                base = c * COLBLOCK
+                w[pl.ds(4 * ROWS + row + c, 9, stride=ROWS), :] = ref[base : base + 9, :]
+                w[pl.ds(PER * ROWS + row + c, 84, stride=ROWS), :] = ref[base + 9 : base + 93, :]
+            at = THIRD
+            for plane in range(7):
+                for o in runs[-1:] if plane == 0 else runs:
+                    start = (plane * PER + o) * ROWS + third
+                    w[pl.ds(start, 3, stride=ROWS), :] = ref[at : at + 3, :]
+                    at += 3
+
+    by_parity("gy", place_y)
     for p in range(7):
         for o, step in enumerate(FORWARD):
             if step[2] == 0 or (p == 0 and o < 4):
@@ -286,17 +317,35 @@
         fd[pl.ds(p_fault[k] * 16 + column, 1), :] = value[5:6, :]
 
     for y in range(CY):
-        for k in range(3):
-            put(y + 2, k, rf_in[k, y])
-    for ref, start, columns in ((yl, UP_FAULT, ((0, 6), (1, 7))), (yh, DOWN_FAULT, ((10, 0), (11, 1)))):
-        at_own, at_other = prepare(ref[start : start + 24, :], far2, eo)
-        for column, y in columns:
-            near, near_t, values = build(y, at_own, at_other, far2, eo)
+        put(y + 2, 0, rf_pair[0, y])
+        put(y + 2, 1, rf_pair[1, y])
+        put(y + 2, 2, rf_third[y])
+    core_rows = from_core[FAULT_ROW : FAULT_ROW + 24, :]
+    chip_rows = from_chip[FAULT_ROW : FAULT_ROW + 24, :]
+    odd_y = lax.rem(gy, 2) == 1
+    for side, first, second, columns in (
+        (0, core_rows, chip_rows, ((0, 6), (1, 7))),
+        (1, chip_rows, core_rows, ((10, 0), (11, 1))),
+    ):
+        rows = jnp.where(odd_y, first, second)
+        cells, far, weight, cells_o, far_o, weight_o = (rows[4 * k : 4 * k + 4] for k in range(6))
+        partner, live, beyond, live_o = slot_columns([far, weight, far_o, weight_o])
+        fill_far(far2.at[side], partner, live)
+        fill_tint(eo.at[side], beyond, live_o)
+        ys = [y for _, y in columns]
+        fill_hot(hot.at[side, 0], flat_cells(cells), ys)
+        fill_hot(hot.at[side, 1], flat_cells(cells_o), ys)
+        pair = dot_nn(hot[side, 0], far2[side])
+        third = dot_nn(hot[side, 1], eo[side])
+        for k, (column, y) in enumerate(columns):
+            near, near_t, at_own, at_far = pair_matrix(pair[k * NZ : (k + 1) * NZ])
             if column in (1, 10):
-                f2h[column // 10] = near
-                ft2h[column // 10] = near_t
-            for k in range(3):
-                put(column, k, values[k])
+                f2h[side] = near
+                ft2h[side] = near_t
+            put(column, 0, at_own)
+            put(column, 1, at_far)
+            pieces = jnp.transpose(third[k * NZ : (k + 1) * NZ])
+            put(column, 2, pieces[:8] + pieces[8:16])
 
     r16 = lax.broadcasted_iota(jnp.int32, (16, NZ), 0)
     z16 = lax.broadcasted_iota(jnp.int32, (16, NZ), 1)
@@ -418,7 +467,7 @@
     lax.fori_loop(0, 5, apply_pair, 0)
 
     def fault_apply(c, f2c, ft2c):
-        ly_oth = 2 * lax.rem(c, 2)
+        ly_oth = 2 * (c % 2)
         for plane, source, x_own, matrix in (
             (p_own, p_far, 1 + sgn, ft2c),
             (p_far, p_own, 1 - sgn, f2c),
@@ -429,11 +478,8 @@
                 ly = ly_oth if lat % 2 else 1
                 ap[plane - 1, c - 1, lx, ly] = ap[plane - 1, c - 1, lx, ly] - total[8 * lat : 8 * lat + 8]
 
-    def fault_own(y, carry):
+    for y in range(CY):
         fault_apply(y + 2, f2[y], ft2[y])
-        return carry
-
-    lax.fori_loop(0, CY, fault_own, 0)
     fault_apply(1, f2h[0], ft2h[0])
     fault_apply(10, f2h[1], ft2h[1])
 
@@ -499,10 +545,26 @@
             out[5 * k : 5 * k + 5, 0, pair * NZ : (pair + 1) * NZ] = got[8 * k : 8 * k + 5]
 
 
-def shift(value, axis, distance):
+def send(value, axis, target):
     peers = lax.axis_size(axis)
-    pairs = [(i, i + distance) for i in range(peers) if 0 <= i + distance < peers]
-    return lax.ppermute(value, axis, pairs)
+    pairs = [(i, target(i)) for i in range(peers) if target(i) is not None]
+    return lax.ppermute(value, axis, [(i, j) for i, j in pairs if 0 <= j < peers])
+
+
+def partner_of(i):
+    return i ^ 1
+
+
+def other_of(i):
+    return i + 1 if i % 2 else i - 1
+
+
+def beyond_of(i):
+    return i - 2 if i % 2 else i + 2
+
+
+def odd_after(i):
+    return i + 2 if i % 2 else None
 
 
 VMEM = pl.BlockSpec(memory_space=pltpu.VMEM)
@@ -519,7 +581,6 @@
 
 def per_device(trans, storage, fault_cells, fault_count, fault_trans):
     peers = (lax.axis_size("gx"), lax.axis_size("gy"))
-    hi2 = shift(fault_cells, "gx", -2)
     sources = [
         pltpu.with_memory_space_constraint(array, pltpu.HBM)
         for array in (trans, storage, fault_cells, fault_trans)
@@ -534,34 +595,53 @@
         compiler_params=params(16),
         name="pack",
     )(fault_count, *sources)
-    lo2 = shift(plane, "gx", 2)
-    lo = shift(own, "gx", 1)
-    hi = shift(own, "gx", -1)
-    up, down, fb = pl.pallas_call(
-        column_kernel,
-        out_shape=(sds(UP_ROWS, NZ), sds(DOWN_ROWS, NZ), sds(24, NZ)),
-        in_specs=[VMEM] * 5,
+    rp = send(own, "gx", partner_of)
+    rd = send(plane, "gx", beyond_of)
+    re = send(plane, "gx", odd_after)
+    ro = send(own, "gx", other_of)
+    pieces = sds(CY, 2 * NZ, NZ, dtype=bf16)
+    f2, ft2, rf_pair = pl.pallas_call(
+        fault_kernel,
+        out_shape=(pieces, pieces, sds(2, CY, 8, NZ)),
+        in_specs=[VMEM] * 2,
         out_specs=(VMEM,) * 3,
-        compiler_params=params(16),
-        name="columns",
-    )(own, lo, hi, lo2, hi2)
-    yl = shift(up, "gy", 1)
-    yh = shift(down, "gy", -1)
-    pieces = sds(CY, 2 * NZ, NZ, dtype=bf16)
-    f2, ft2, rf = pl.pallas_call(
-        fault_kernel,
-        out_shape=(pieces, pieces, sds(3, CY, 8, NZ)),
-        in_specs=[VMEM],
-        out_specs=(VMEM,) * 3,
-        scratch_shapes=[pltpu.VMEM((SLOTS, 2 * NZ), bf16), pltpu.VMEM((SLOTS, NZ), bf16)],
+        scratch_shapes=[
+            pltpu.VMEM((SLOTS, 2 * NZ), bf16),
+            pltpu.VMEM((CY * NZ, SLOTS), bf16),
+            pltpu.VMEM((CY * NZ, 2 * NZ), f32),
+        ],
         compiler_params=params(16),
         cost_estimate=pl.CostEstimate(flops=2 * 10**9, bytes_accessed=2**21, transcendentals=0),
         name="faults",
-    )(fb)
+    )(own, rp)
+    to_core, to_chip = pl.pallas_call(
+        column_kernel,
+        out_shape=(sds(Y_ROWS, NZ), sds(Y_ROWS, NZ)),
+        in_specs=[VMEM] * 5,
+        out_specs=(VMEM,) * 2,
+        compiler_params=params(16),
+        name="columns",
+    )(own, rp, ro, rd, re)
+    from_chip = send(to_chip, "gy", other_of)
+    from_core = send(to_core, "gy", partner_of)
+    rf_third = pl.pallas_call(
+        third_kernel,
+        out_shape=sds(CY, 8, NZ),
+        in_specs=[VMEM] * 2,
+        out_specs=VMEM,
+        scratch_shapes=[
+            pltpu.VMEM((SLOTS, NZ), bf16),
+            pltpu.VMEM((CY * NZ, SLOTS), bf16),
+            pltpu.VMEM((CY * NZ, NZ), f32),
+        ],
+        compiler_params=params(16),
+        cost_estimate=pl.CostEstimate(flops=10**9, bytes_accessed=2**20, transcendentals=0),
+        name="third",
+    )(ro, rd)
     return pl.pallas_call(
-        functools.partial(main_kernel, peers),
+        main_kernel,
         out_shape=sds(125, 1, 256),
-        in_specs=[VMEM] * 9,
+        in_specs=[VMEM] * 11,
         out_specs=VMEM,
         scratch_shapes=[
             pltpu.VMEM((7 * PER * ROWS, NZ), f32),
@@ -576,12 +656,13 @@
             pltpu.VMEM((2, 5, 5, 8, 512), f32),
             pltpu.VMEM((2, 2 * NZ, NZ), bf16),
             pltpu.VMEM((2, 2 * NZ, NZ), bf16),
-            pltpu.VMEM((SLOTS, 2 * NZ), bf16),
-            pltpu.VMEM((SLOTS, NZ), bf16),
+            pltpu.VMEM((2, SLOTS, 2 * NZ), bf16),
+            pltpu.VMEM((2, SLOTS, NZ), bf16),
+            pltpu.VMEM((2, 2, 2 * NZ, SLOTS), bf16),
         ],
         compiler_params=params(24),
         name="galerkin",
-    )(own, lo, hi, lo2, yl, yh, f2, ft2, rf)
+    )(own, rp, ro, rd, re, from_core, from_chip, f2, ft2, rf_pair, rf_third)
 
 
 def solution(mesh):

time: 35 us -> 28 us (0.80)
  the two profiles are of different devices: /device:TPU:1 before, /device:TPU:19 now
where the time goes in v3:
time: 28 us; the launch traced here: 27.8 us
  starting transfers between devices  14.4 us (51%)
  Pallas kernels  8.82 us (32%)
  waiting for transfers between devices  3.88 us (14%)
  between operations  0.71 us (3%)
    ppermute x6, starting transfers between devices, send(): lax.ppermute(value, axis, [(i, j) for i, j in pairs if 0 <= j < peers])  14.4 us
    pallas_call x1, Pallas kernels, per_device(): pl.pallas_call(main_kernel, out_shape=sds(125, 1, 256), in_specs=[VMEM] *...  5.71 us
    ppermute x6, waiting for transfers between devices, send(): lax.ppermute(value, axis, [(i, j) for i, j in pairs if 0 <= j < peers])  3.88 us
    pallas_call x1, Pallas kernels, per_device(): pl.pallas_call(functools.partial(pack_kernel, peers), out_shape=(sds(232,...  1.05 us
    pallas_call x1, Pallas kernels, per_device(): pl.pallas_call(fault_kernel, out_shape=(pieces, pieces, sds(2, CY, 8, NZ)...  1.03 us
    pallas_call x1, Pallas kernels, per_device(): pl.pallas_call(third_kernel, out_shape=sds(CY, 8, NZ), in_specs=[VMEM] *...  0.96 us
  transfers between devices with their start and end apart: 6, of which 2 were waited for; matrix products, arithmetic and copies ran while one was open for 0% of the time, Pallas kernels for 7%

profile of v3, /device:TPU:19, one launch (start us, length us, event | category | flops | bytes accessed | tf_op | source)
XLA Modules:
  0.0 27.8 jit_solution(2992362761323684838)
XLA Ops:
  0.7 1.0 %pack.1 = (f32[232,128]{1,0:T(8,128)S(1)}, f32[80,128]{1,0:T(8,128)S(1)}) custom-call(s32[1,1]{1,0:T(1,128)S(6)} %copy.6.count, f32[13,2,1024]{2,1,0:T(2,128)} %refs_0_.1, f32[2,1024]{1,0:T(2,128)} %refs_1_.1, s32[1,1,512]{2,1,0:T(1,128)} %refs_2_.1, f32[1,1,512]{2,1,0:T(1,128)} %refs_3_.1), custom_call_target="tpu_custom_call" | custom-call | tf_op jit(solution)/shard_map/pack/pallas_call | solution.py:588
  1.7 3.2 %collective-permute-start.1 = (f32[232,128]{1,0:T(8,128)S(1)}, f32[232,128]{1,0:T(8,128)S(1)}, u32[]{:S(2)}, u32[]{:S(2)}) collective-permute-start(f32[232,128]{1,0:T(8,128)S(1)} %get-tuple-element.12.own), channel_id=1, source_target_pairs={{4,8},{8,4},{12,16},{16,12},{20,24},{24,20},{5,9},{9,5},{13,17},{1... | collective-permute-start | bytes 356360 | tf_op jit(solution)/shard_map/ppermute | solution.py:551
  4.9 0.1 collective-permute-start
  5.0 3.2 %collective-permute-start.3 = (f32[80,128]{1,0:T(8,128)S(1)}, f32[80,128]{1,0:T(8,128)S(1)}, u32[]{:S(2)}, u32[]{:S(2)}) collective-permute-start(f32[80,128]{1,0:T(8,128)S(1)} %get-tuple-element.13), channel_id=1, source_target_pairs={{4,12},{12,20},{20,28},{5,13},{13,21},{21,29},{6,14},{14,22},{22,3... | collective-permute-start | bytes 122888 | tf_op jit(solution)/shard_map/ppermute | solution.py:551
  8.2 2.1 %collective-permute-start.2 = (f32[80,128]{1,0:T(8,128)S(1)}, f32[80,128]{1,0:T(8,128)S(1)}, u32[]{:S(2)}, u32[]{:S(2)}) collective-permute-start(f32[80,128]{1,0:T(8,128)S(1)} %get-tuple-element.13), channel_id=1, source_target_pairs={{0,8},{8,16},{12,4},{16,24},{20,12},{28,20},{1,9},{9,17},{13,5},{1... | collective-permute-start | bytes 122888 | tf_op jit(solution)/shard_map/ppermute | solution.py:551
  10.3 0.0 collective-permute-done.3.re
  10.3 2.6 %collective-permute-done.2.rd = f32[80,128]{1,0:T(8,128)S(1)} collective-permute-done((f32[80,128]{1,0:T(8,128)S(1)}, f32[80,128]{1,0:T(8,128)S(1)}, u32[]{:S(2)}, u32[]{:S(2)}) %collective-permute-start.2) | collective-permute-done | bytes 40992 | tf_op jit(solution)/shard_map/ppermute | solution.py:551
  13.0 0.0 collective-permute-done.1.ro
  13.0 0.0 collective-permute-done.rp
  13.0 0.1 columns.1
  13.1 2.7 %collective-permute-start.4 = (f32[256,128]{1,0:T(8,128)S(1)}, f32[256,128]{1,0:T(8,128)S(1)}, u32[]{:S(2)}, u32[]{:S(2)}) collective-permute-start(f32[256,128]{1,0:T(8,128)S(1)} %get-tuple-element.14), channel_id=1, source_target_pairs={{0,1},{1,0},{2,3},{3,2},{4,5},{5,4},{6,7},{7,6},{8,9},{9,8},{10,11... | collective-permute-start | bytes 393224 | tf_op jit(solution)/shard_map/ppermute | solution.py:551
  15.8 3.0 %collective-permute-start.5 = (f32[256,128]{1,0:T(8,128)S(1)}, f32[256,128]{1,0:T(8,128)S(1)}, u32[]{:S(2)}, u32[]{:S(2)}) collective-permute-start(f32[256,128]{1,0:T(8,128)S(1)} %get-tuple-element.15), channel_id=1, source_target_pairs={{1,2},{2,1},{5,6},{6,5},{9,10},{10,9},{13,14},{14,13},{17,18},{18,... | collective-permute-start | bytes 393224 | tf_op jit(solution)/shard_map/ppermute | solution.py:551
  18.9 1.0 %faults.1 = (bf16[8,256,128]{2,1,0:T(8,128)(2,1)S(1)}, bf16[8,256,128]{2,1,0:T(8,128)(2,1)S(1)}, f32[2,8,8,128]{3,2,1,0:T(8,128)S(1)}) custom-call(f32[232,128]{1,0:T(8,128)S(1)} %get-tuple-element.12.own, f32[232,128]{1,0:T(8,128)S(1)} %collective-permute-done.rp), custom_call_target="tpu_custom_call" | custom-call | flops 2000000000 | bytes 2097152 | tf_op jit(solution)/shard_map/faults/pallas_call | solution.py:603
  19.9 1.0 %third.1.rf_third = f32[8,8,128]{2,1,0:T(8,128)S(1)} custom-call(f32[232,128]{1,0:T(8,128)S(1)} %collective-permute-done.1.ro, f32[80,128]{1,0:T(8,128)S(1)} %collective-permute-done.2.rd), custom_call_target="tpu_custom_call" | custom-call | flops 1000000000 | bytes 1048576 | tf_op jit(solution)/shard_map/third/pallas_call | solution.py:627
  20.9 0.0 collective-permute-done.4.from_core
  20.9 1.2 %collective-permute-done.5.from_chip = f32[256,128]{1,0:T(8,128)S(1)} collective-permute-done((f32[256,128]{1,0:T(8,128)S(1)}, f32[256,128]{1,0:T(8,128)S(1)}, u32[]{:S(2)}, u32[]{:S(2)}) %collective-permute-start.5) | collective-permute-done | bytes 131104 | tf_op jit(solution)/shard_map/ppermute | solution.py:551
  22.1 5.7 %galerkin.1 = f32[125,1,256]{2,1,0:T(1,128)} custom-call(f32[232,128]{1,0:T(8,128)S(1)} %get-tuple-element.12.own, f32[232,128]{1,0:T(8,128)S(1)} %collective-permute-done.rp, f32[232,128]{1,0:T(8,128)S(1)} %collective-permute-done.1.ro, f32[80,128]{1,0:T(8,128)S(1)} %collective-permute-done.2.rd, f32[80,128]{1,0:T(8,128)S(1)} %collective-permute-done.3.re, ...), custom_call_target="tpu_custom_call" | custom-call | tf_op jit(solution)/shard_map/galerkin/pallas_call | solution.py:641
Async XLA Ops:
  1.7 11.3 %collective-permute-start.1 = (f32[232,128]{1,0:T(8,128)S(1)}, f32[232,128]{1,0:T(8,128)S(1)}, u32[]{:S(2)}, u32[]{:S(2)}) collective-permute-start(f32[232,128]{1,0:T(8,128)S(1)} %get-tuple-element.12.own), channel_id=1, source_target_pairs={{4,8},{8,4},{12,16},{16,12},{20,24},{24,20},{5,9},{9,5},{13,17},{1... | collective-permute-start | bytes 356360 | tf_op jit(solution)/shard_map/ppermute | solution.py:551
  4.9 8.1 %collective-permute-start = (f32[232,128]{1,0:T(8,128)S(1)}, f32[232,128]{1,0:T(8,128)S(1)}, u32[]{:S(2)}, u32[]{:S(2)}) collective-permute-start(f32[232,128]{1,0:T(8,128)S(1)} %get-tuple-element.12.own), channel_id=1, source_target_pairs={{0,4},{4,0},{8,12},{12,8},{16,20},{20,16},{24,28},{28,24},{1,5},{5... | collective-permute-start | bytes 356360 | tf_op jit(solution)/shard_map/ppermute | solution.py:551
  5.0 5.3 %collective-permute-start.3 = (f32[80,128]{1,0:T(8,128)S(1)}, f32[80,128]{1,0:T(8,128)S(1)}, u32[]{:S(2)}, u32[]{:S(2)}) collective-permute-start(f32[80,128]{1,0:T(8,128)S(1)} %get-tuple-element.13), channel_id=1, source_target_pairs={{4,12},{12,20},{20,28},{5,13},{13,21},{21,29},{6,14},{14,22},{22,3... | collective-permute-start | bytes 122888 | tf_op jit(solution)/shard_map/ppermute | solution.py:551
  8.2 4.7 %collective-permute-start.2 = (f32[80,128]{1,0:T(8,128)S(1)}, f32[80,128]{1,0:T(8,128)S(1)}, u32[]{:S(2)}, u32[]{:S(2)}) collective-permute-start(f32[80,128]{1,0:T(8,128)S(1)} %get-tuple-element.13), channel_id=1, source_target_pairs={{0,8},{8,16},{12,4},{16,24},{20,12},{28,20},{1,9},{9,17},{13,5},{1... | collective-permute-start | bytes 122888 | tf_op jit(solution)/shard_map/ppermute | solution.py:551
  13.1 7.8 %collective-permute-start.4 = (f32[256,128]{1,0:T(8,128)S(1)}, f32[256,128]{1,0:T(8,128)S(1)}, u32[]{:S(2)}, u32[]{:S(2)}) collective-permute-start(f32[256,128]{1,0:T(8,128)S(1)} %get-tuple-element.14), channel_id=1, source_target_pairs={{0,1},{1,0},{2,3},{3,2},{4,5},{5,4},{6,7},{7,6},{8,9},{9,8},{10,11... | collective-permute-start | bytes 393224 | tf_op jit(solution)/shard_map/ppermute | solution.py:551
  15.8 6.3 %collective-permute-start.5 = (f32[256,128]{1,0:T(8,128)S(1)}, f32[256,128]{1,0:T(8,128)S(1)}, u32[]{:S(2)}, u32[]{:S(2)}) collective-permute-start(f32[256,128]{1,0:T(8,128)S(1)} %get-tuple-element.15), channel_id=1, source_target_pairs={{1,2},{2,1},{5,6},{6,5},{9,10},{10,9},{13,14},{14,13},{17,18},{18,... | collective-permute-start | bytes 393224 | tf_op jit(solution)/shard_map/ppermute | solution.py:551

commit v4 on v3

--- a/solution.py
+++ b/solution.py
@@ -103,7 +103,6 @@
             lane + r * NZ < live, ftrans[0, :, lanes], 0.0
         )
     plane[0:72, :] = block[(PER + 4) * 8 : (PER + 13) * 8, :]
-    plane[72:80, :] = block[base : base + 8, :]
 
 
 def by_parity(axis, body):
@@ -112,24 +111,44 @@
         pl.when(odd == k)(functools.partial(body, k))
 
 
-def column_kernel(own, rp, ro, rd, re, to_core, to_chip):
+def cells_at(cells, device):
+    at = jnp.clip(device, 0, cells.shape[0] - 1)
+    row = cells[at]
+    return jnp.concatenate([row[:, r * NZ : (r + 1) * NZ] for r in range(4)], axis=0).astype(f32)
+
+
+def partner_cells(cells):
+    gx = lax.axis_index("gx")
+    return cells_at(cells, gx + 1 - 2 * lax.rem(gx, 2))
+
+
+def beyond_cells(cells):
+    gx = lax.axis_index("gx")
+    return cells_at(cells, gx - 2 + 4 * lax.rem(gx, 2))
+
+
+def column_kernel(own, rp, ro, planes, cells, to_core, to_chip):
+    gx = lax.axis_index("gx")
+    lo2_base = jnp.maximum(gx // 2 - 1, 0) * 72
+    has_lo2 = gx >= 2
     tile = own[224:232, :]
     other = ro[224:232, :]
-    parts = (tile[0:4], rp[224:228, :], tile[4:8], other[0:4], rd[72:76, :], other[4:8])
+    parts = (tile[0:4], partner_cells(cells), tile[4:8], other[0:4], beyond_cells(cells), other[4:8])
     for out in (to_core, to_chip):
         for k, part in enumerate(parts):
             out[FAULT_ROW + 4 * k : FAULT_ROW + 4 * k + 4, :] = part
 
-    def fill(out, lo, hi, lo2, first, third, runs):
+    def fill(out, lo, hi, first, third, runs):
         for c in range(2):
             y = first + c
             base = c * COLBLOCK
-            out[base : base + 9, :] = lo2[pl.ds(y, 9, stride=8), :]
+            out[base : base + 9, :] = jnp.where(has_lo2, planes[pl.ds(lo2_base + y, 9, stride=8), :], 0.0)
             for k, ref in enumerate((lo, own, hi)):
                 start = base + 9 + 28 * k
                 out[start : start + 28, :] = ref[pl.ds(y, 28, stride=8), :]
         at = THIRD
-        out[at : at + 3, :] = lo2[pl.ds((runs[-1] - 4) * 8 + third, 3, stride=8), :]
+        start = lo2_base + (runs[-1] - 4) * 8 + third
+        out[at : at + 3, :] = jnp.where(has_lo2, planes[pl.ds(start, 3, stride=8), :], 0.0)
         at += 3
         for ref in (lo, own, hi):
             for x in range(2):
@@ -138,12 +157,12 @@
                     at += 3
 
     def for_x(odd_x):
-        lo, hi, lo2 = (rp, ro, re) if odd_x else (ro, rp, rd)
+        lo, hi = (rp, ro) if odd_x else (ro, rp)
 
         def for_y(odd_y):
             up, down = (to_chip, to_core) if odd_y else (to_core, to_chip)
-            fill(up, lo, hi, lo2, CY - 2, CY - 3, (1, 10))
-            fill(down, lo, hi, lo2, 0, 2, (4,))
+            fill(up, lo, hi, CY - 2, CY - 3, (1, 10))
+            fill(down, lo, hi, 0, 2, (4,))
 
         by_parity("gy", for_y)
 
@@ -203,8 +222,8 @@
     return f2, ft2, dot_nn(one2, ft2), dot_nn(one2, f2)
 
 
-def fault_kernel(own, rp, f2, ft2, rf, far2, hot, both):
-    partner, live = slot_columns([rp[224:228, :], own[228:232, :]])
+def fault_kernel(own, cells, f2, ft2, rf, far2, hot, both):
+    partner, live = slot_columns([partner_cells(cells), own[228:232, :]])
     fill_far(far2, partner, live)
     fill_hot(hot, flat_cells(own[224:228, :]), range(CY))
     both[...] = dot_nn(hot[...], far2[...])
@@ -212,8 +231,8 @@
         f2[y], ft2[y], rf[0, y], rf[1, y] = pair_matrix(both[y * NZ : (y + 1) * NZ, :])
 
 
-def third_kernel(ro, rd, rf, eo, hot, both):
-    beyond, live = slot_columns([rd[72:76, :], ro[228:232, :]])
+def third_kernel(ro, cells, rf, eo, hot, both):
+    beyond, live = slot_columns([beyond_cells(cells), ro[228:232, :]])
     fill_tint(eo, beyond, live)
     fill_hot(hot, flat_cells(ro[224:228, :]), range(CY))
     both[...] = dot_nn(hot[...], eo[...])
@@ -236,8 +255,7 @@
     own,
     rp,
     ro,
-    rd,
-    re,
+    planes,
     from_core,
     from_chip,
     f2,
@@ -279,11 +297,15 @@
             w[base + 3 : base + 11, :] = ref[8 * k : 8 * k + 8, :]
 
     def place_x(odd):
-        lo, hi, lo2 = (rp, ro, re) if odd else (ro, rp, rd)
-        place(lo2, 9, 4)
+        lo, hi = (rp, ro) if odd else (ro, rp)
         place(lo, 28, PER)
         place(hi, 28, 5 * PER)
 
+    lo2_base = jnp.maximum(gx // 2 - 1, 0) * 72
+    for k in range(9):
+        base = (4 + k) * ROWS
+        value = planes[pl.ds(pl.multiple_of(lo2_base + 8 * k, 8), 8), :]
+        w[base + 3 : base + 11, :] = jnp.where(gx >= 2, value, 0.0)
     place(own, 28, 3 * PER)
     by_parity("gx", place_x)
 
@@ -559,14 +581,6 @@
     return i + 1 if i % 2 else i - 1
 
 
-def beyond_of(i):
-    return i - 2 if i % 2 else i + 2
-
-
-def odd_after(i):
-    return i + 2 if i % 2 else None
-
-
 VMEM = pl.BlockSpec(memory_space=pltpu.VMEM)
 HBM = pl.BlockSpec(memory_space=pltpu.HBM)
 
@@ -581,13 +595,14 @@
 
 def per_device(trans, storage, fault_cells, fault_count, fault_trans):
     peers = (lax.axis_size("gx"), lax.axis_size("gy"))
+    cells = lax.all_gather(fault_cells, "gx", tiled=True)
     sources = [
         pltpu.with_memory_space_constraint(array, pltpu.HBM)
         for array in (trans, storage, fault_cells, fault_trans)
     ]
     own, plane = pl.pallas_call(
         functools.partial(pack_kernel, peers),
-        out_shape=(sds(232, NZ), sds(80, NZ)),
+        out_shape=(sds(232, NZ), sds(72, NZ)),
         in_specs=[pl.BlockSpec(memory_space=pltpu.SMEM)] + [HBM] * 4,
         out_specs=(VMEM, VMEM),
         scratch_shapes=[pltpu.VMEM(array.shape, array.dtype) for array in sources]
@@ -595,9 +610,9 @@
         compiler_params=params(16),
         name="pack",
     )(fault_count, *sources)
+    groups = [list(range(k, peers[0], 2)) for k in range(2)]
+    planes = lax.all_gather(plane, "gx", axis_index_groups=groups, tiled=True)
     rp = send(own, "gx", partner_of)
-    rd = send(plane, "gx", beyond_of)
-    re = send(plane, "gx", odd_after)
     ro = send(own, "gx", other_of)
     pieces = sds(CY, 2 * NZ, NZ, dtype=bf16)
     f2, ft2, rf_pair = pl.pallas_call(
@@ -613,7 +628,7 @@
         compiler_params=params(16),
         cost_estimate=pl.CostEstimate(flops=2 * 10**9, bytes_accessed=2**21, transcendentals=0),
         name="faults",
-    )(own, rp)
+    )(own, cells)
     to_core, to_chip = pl.pallas_call(
         column_kernel,
         out_shape=(sds(Y_ROWS, NZ), sds(Y_ROWS, NZ)),
@@ -621,7 +636,7 @@
         out_specs=(VMEM,) * 2,
         compiler_params=params(16),
         name="columns",
-    )(own, rp, ro, rd, re)
+    )(own, rp, ro, planes, cells)
     from_chip = send(to_chip, "gy", other_of)
     from_core = send(to_core, "gy", partner_of)
     rf_third = pl.pallas_call(
@@ -637,11 +652,11 @@
         compiler_params=params(16),
         cost_estimate=pl.CostEstimate(flops=10**9, bytes_accessed=2**20, transcendentals=0),
         name="third",
-    )(ro, rd)
+    )(ro, cells)
     return pl.pallas_call(
         main_kernel,
         out_shape=sds(125, 1, 256),
-        in_specs=[VMEM] * 11,
+        in_specs=[VMEM] * 10,
         out_specs=VMEM,
         scratch_shapes=[
             pltpu.VMEM((7 * PER * ROWS, NZ), f32),
@@ -662,7 +677,7 @@
         ],
         compiler_params=params(24),
         name="galerkin",
-    )(own, rp, ro, rd, re, from_core, from_chip, f2, ft2, rf_pair, rf_third)
+    )(own, rp, ro, planes, from_core, from_chip, f2, ft2, rf_pair, rf_third)
 
 
 def solution(mesh):

time: 28 us -> 60.3 us (2.15)
  the two profiles are of different devices: /device:TPU:19 before, /device:TPU:1 now
where the time goes in v4:
time: 60.3 us; the launch traced here: 60.1 us
  blocking collectives  33.5 us (56%)
  starting transfers between devices  15.8 us (26%)
  Pallas kernels  8.86 us (15%)
  waiting for transfers between devices  1.21 us (2%)
  between operations  0.7 us (1%)
    all_gather x1, blocking collectives, per_device(): cells = lax.all_gather(fault_cells, 'gx', tiled=True)  23 us
    ppermute x4, starting transfers between devices, send(): lax.ppermute(value, axis, [(i, j) for i, j in pairs if 0 <= j < peers])  15.8 us
    all_gather x1, blocking collectives, per_device(): planes = lax.all_gather(plane, 'gx', axis_index_groups=groups, tiled=True)  10.6 us
    pallas_call x1, Pallas kernels, per_device(): pl.pallas_call(main_kernel, out_shape=sds(125, 1, 256), in_specs=[VMEM] *...  5.71 us
  transfers between devices with their start and end apart: 4, of which 1 were waited for; matrix products, arithmetic and copies ran while one was open for 0% of the time, Pallas kernels for 3%

profile of v4, /device:TPU:1, one launch (start us, length us, event | category | flops | bytes accessed | tf_op | source)
XLA Modules:
  0.0 60.1 jit_solution(16305940504953266899)
XLA Ops:
  0.7 0.0 copy-start
  0.7 1.0 %pack.1 = (f32[232,128]{1,0:T(8,128)S(1)}, f32[72,128]{1,0:T(8,128)S(1)}) custom-call(s32[1,1]{1,0:T(1,128)S(6)} %copy.6.count, f32[13,2,1024]{2,1,0:T(2,128)} %refs_0_.1, f32[2,1024]{1,0:T(2,128)} %refs_1_.1, s32[1,1,512]{2,1,0:T(1,128)} %refs_2_.1, f32[1,1,512]{2,1,0:T(1,128)} %refs_3_.1), custom_call_target="tpu_custom_call" | custom-call | tf_op jit(solution)/shard_map/pack/pallas_call | solution.py:603
  1.7 0.7 %collective-permute-start.1 = (f32[232,128]{1,0:T(8,128)S(1)}, f32[232,128]{1,0:T(8,128)S(1)}, u32[]{:S(2)}, u32[]{:S(2)}) collective-permute-start(f32[232,128]{1,0:T(8,128)S(1)} %get-tuple-element.12.own), channel_id=1, source_target_pairs={{4,8},{8,4},{12,16},{16,12},{20,24},{24,20},{5,9},{9,5},{13,17},{1... | collective-permute-start | bytes 356360 | tf_op jit(solution)/shard_map/ppermute | solution.py:573
  2.4 4.6 %collective-permute-start = (f32[232,128]{1,0:T(8,128)S(1)}, f32[232,128]{1,0:T(8,128)S(1)}, u32[]{:S(2)}, u32[]{:S(2)}) collective-permute-start(f32[232,128]{1,0:T(8,128)S(1)} %get-tuple-element.12.own), channel_id=1, source_target_pairs={{0,4},{4,0},{8,12},{12,8},{16,20},{20,16},{24,28},{28,24},{1,5},{5... | collective-permute-start | bytes 356360 | tf_op jit(solution)/shard_map/ppermute | solution.py:573
  7.0 0.0 copy-done
  7.0 23.0 %all_gather.7.cells = s32[8,1,512]{2,1,0:T(1,128)S(1)} all-gather(s32[1,1,512]{2,1,0:T(1,128)S(1)} %copy-done), channel_id=1, replica_groups=mesh['gx'=8,'gy'=4] {'gx'}, dimensions={0}, use_global_device_ids=true | all-gather | bytes 18432 | tf_op jit(solution)/shard_map/all_gather | solution.py:598
  30.0 10.6 %all_gather.6.planes = f32[288,128]{1,0:T(8,128)S(1)} all-gather(f32[72,128]{1,0:T(8,128)S(1)} %get-tuple-element.13), channel_id=1, replica_groups={{0,8,16,24},{4,12,20,28},{1,9,17,25},{5,13,21,29},{2,10,18,26},{6,14,22..., dimensions={0}, use_global_device_ids=true | all-gather | bytes 184320 | tf_op jit(solution)/shard_map/all_gather | solution.py:614
  40.6 0.0 collective-permute-done.1.ro
  40.6 0.0 collective-permute-done.rp
  40.6 0.1 columns.1
  40.7 7.4 %collective-permute-start.2 = (f32[256,128]{1,0:T(8,128)S(1)}, f32[256,128]{1,0:T(8,128)S(1)}, u32[]{:S(2)}, u32[]{:S(2)}) collective-permute-start(f32[256,128]{1,0:T(8,128)S(1)} %get-tuple-element.14), channel_id=1, source_target_pairs={{0,1},{1,0},{2,3},{3,2},{4,5},{5,4},{6,7},{7,6},{8,9},{9,8},{10,11... | collective-permute-start | bytes 393224 | tf_op jit(solution)/shard_map/ppermute | solution.py:573
  48.1 3.0 %collective-permute-start.3 = (f32[256,128]{1,0:T(8,128)S(1)}, f32[256,128]{1,0:T(8,128)S(1)}, u32[]{:S(2)}, u32[]{:S(2)}) collective-permute-start(f32[256,128]{1,0:T(8,128)S(1)} %get-tuple-element.15), channel_id=1, source_target_pairs={{1,2},{2,1},{5,6},{6,5},{9,10},{10,9},{13,14},{14,13},{17,18},{18,... | collective-permute-start | bytes 393224 | tf_op jit(solution)/shard_map/ppermute | solution.py:573
  51.2 1.0 %faults.1 = (bf16[8,256,128]{2,1,0:T(8,128)(2,1)S(1)}, bf16[8,256,128]{2,1,0:T(8,128)(2,1)S(1)}, f32[2,8,8,128]{3,2,1,0:T(8,128)S(1)}) custom-call(f32[232,128]{1,0:T(8,128)S(1)} %get-tuple-element.12.own, s32[8,1,512]{2,1,0:T(1,128)S(1)} %all_gather.7.cells), custom_call_target="tpu_custom_call" | custom-call | flops 2000000000 | bytes 2097152 | tf_op jit(solution)/shard_map/faults/pallas_call | solution.py:618
  52.2 1.0 %third.1.rf_third = f32[8,8,128]{2,1,0:T(8,128)S(1)} custom-call(f32[232,128]{1,0:T(8,128)S(1)} %collective-permute-done.1.ro, s32[8,1,512]{2,1,0:T(1,128)S(1)} %all_gather.7.cells), custom_call_target="tpu_custom_call" | custom-call | flops 1000000000 | bytes 1048576 | tf_op jit(solution)/shard_map/third/pallas_call | solution.py:642
  53.2 0.0 collective-permute-done.2.from_core
  53.2 1.2 %collective-permute-done.3.from_chip = f32[256,128]{1,0:T(8,128)S(1)} collective-permute-done((f32[256,128]{1,0:T(8,128)S(1)}, f32[256,128]{1,0:T(8,128)S(1)}, u32[]{:S(2)}, u32[]{:S(2)}) %collective-permute-start.3) | collective-permute-done | bytes 131104 | tf_op jit(solution)/shard_map/ppermute | solution.py:573
  54.4 5.7 %galerkin.1 = f32[125,1,256]{2,1,0:T(1,128)} custom-call(f32[232,128]{1,0:T(8,128)S(1)} %get-tuple-element.12.own, f32[232,128]{1,0:T(8,128)S(1)} %collective-permute-done.rp, f32[232,128]{1,0:T(8,128)S(1)} %collective-permute-done.1.ro, f32[288,128]{1,0:T(8,128)S(1)} %all_gather.6.planes, f32[256,128]{1,0:T(8,128)S(1)} %collective-permute-done.2.from_core, ...), custom_call_target="tpu_custom_call" | custom-call | tf_op jit(solution)/shard_map/galerkin/pallas_call | solution.py:656
Async XLA Ops:
  0.7 6.4 %copy-start = (s32[1,1,512]{2,1,0:T(1,128)S(1)}, s32[1,1,512]{2,1,0:T(1,128)}, u32[]{:S(2)}) copy-start(s32[1,1,512]{2,1,0:T(1,128)} %refs_2_.1) | copy-start | bytes 6148
  1.7 38.8 %collective-permute-start.1 = (f32[232,128]{1,0:T(8,128)S(1)}, f32[232,128]{1,0:T(8,128)S(1)}, u32[]{:S(2)}, u32[]{:S(2)}) collective-permute-start(f32[232,128]{1,0:T(8,128)S(1)} %get-tuple-element.12.own), channel_id=1, source_target_pairs={{4,8},{8,4},{12,16},{16,12},{20,24},{24,20},{5,9},{9,5},{13,17},{1... | collective-permute-start | bytes 356360 | tf_op jit(solution)/shard_map/ppermute | solution.py:573
  2.4 38.2 %collective-permute-start = (f32[232,128]{1,0:T(8,128)S(1)}, f32[232,128]{1,0:T(8,128)S(1)}, u32[]{:S(2)}, u32[]{:S(2)}) collective-permute-start(f32[232,128]{1,0:T(8,128)S(1)} %get-tuple-element.12.own), channel_id=1, source_target_pairs={{0,4},{4,0},{8,12},{12,8},{16,20},{20,16},{24,28},{28,24},{1,5},{5... | collective-permute-start | bytes 356360 | tf_op jit(solution)/shard_map/ppermute | solution.py:573
  40.7 12.5 %collective-permute-start.2 = (f32[256,128]{1,0:T(8,128)S(1)}, f32[256,128]{1,0:T(8,128)S(1)}, u32[]{:S(2)}, u32[]{:S(2)}) collective-permute-start(f32[256,128]{1,0:T(8,128)S(1)} %get-tuple-element.14), channel_id=1, source_target_pairs={{0,1},{1,0},{2,3},{3,2},{4,5},{5,4},{6,7},{7,6},{8,9},{9,8},{10,11... | collective-permute-start | bytes 393224 | tf_op jit(solution)/shard_map/ppermute | solution.py:573
  48.1 6.3 %collective-permute-start.3 = (f32[256,128]{1,0:T(8,128)S(1)}, f32[256,128]{1,0:T(8,128)S(1)}, u32[]{:S(2)}, u32[]{:S(2)}) collective-permute-start(f32[256,128]{1,0:T(8,128)S(1)} %get-tuple-element.15), channel_id=1, source_target_pairs={{1,2},{2,1},{5,6},{6,5},{9,10},{10,9},{13,14},{14,13},{17,18},{18,... | collective-permute-start | bytes 393224 | tf_op jit(solution)/shard_map/ppermute | solution.py:573

commit v5 on v3

--- a/solution.py
+++ b/solution.py
@@ -49,7 +49,7 @@
 
 
 def pack_kernel(peers, count, *refs):
-    sources, (block, plane), targets, sems = refs[:4], refs[4:6], refs[6:10], refs[10]
+    sources, (block, plane, tile), targets, sems = refs[:4], refs[4:7], refs[7:11], refs[11]
     copies = [
         pltpu.make_async_copy(src, dst, sems.at[k])
         for k, (src, dst) in enumerate(zip(sources, targets))
@@ -104,6 +104,7 @@
         )
     plane[0:72, :] = block[(PER + 4) * 8 : (PER + 13) * 8, :]
     plane[72:80, :] = block[base : base + 8, :]
+    tile[...] = block[base : base + 8, :]
 
 
 def by_parity(axis, body):
@@ -112,15 +113,30 @@
         pl.when(odd == k)(functools.partial(body, k))
 
 
-def column_kernel(own, rp, ro, rd, re, to_core, to_chip):
+class Masked:
+    def __init__(self, ref, due):
+        self.ref, self.due = ref, due
+
+    def __getitem__(self, index):
+        return jnp.where(self.due, self.ref[index], 0.0)
+
+
+def has_other(axis, peers):
+    at = lax.axis_index(axis)
+    return jnp.where(lax.rem(at, 2) == 0, at > 0, at < peers - 1)
+
+
+def column_kernel(peers, own, rp, ro, rs, rt, to_core, to_chip):
+    ro = Masked(ro, has_other("gx", peers[0]))
+    lo2 = Masked(rs, lax.axis_index("gx") >= 2)
     tile = own[224:232, :]
     other = ro[224:232, :]
-    parts = (tile[0:4], rp[224:228, :], tile[4:8], other[0:4], rd[72:76, :], other[4:8])
+    parts = (tile[0:4], rp[224:228, :], tile[4:8], other[0:4], beyond_cells(rs, rt), other[4:8])
     for out in (to_core, to_chip):
         for k, part in enumerate(parts):
             out[FAULT_ROW + 4 * k : FAULT_ROW + 4 * k + 4, :] = part
 
-    def fill(out, lo, hi, lo2, first, third, runs):
+    def fill(out, lo, hi, first, third, runs):
         for c in range(2):
             y = first + c
             base = c * COLBLOCK
@@ -138,12 +154,12 @@
                     at += 3
 
     def for_x(odd_x):
-        lo, hi, lo2 = (rp, ro, re) if odd_x else (ro, rp, rd)
+        lo, hi = (rp, ro) if odd_x else (ro, rp)
 
         def for_y(odd_y):
             up, down = (to_chip, to_core) if odd_y else (to_core, to_chip)
-            fill(up, lo, hi, lo2, CY - 2, CY - 3, (1, 10))
-            fill(down, lo, hi, lo2, 0, 2, (4,))
+            fill(up, lo, hi, CY - 2, CY - 3, (1, 10))
+            fill(down, lo, hi, 0, 2, (4,))
 
         by_parity("gy", for_y)
 
@@ -212,8 +228,13 @@
         f2[y], ft2[y], rf[0, y], rf[1, y] = pair_matrix(both[y * NZ : (y + 1) * NZ, :])
 
 
-def third_kernel(ro, rd, rf, eo, hot, both):
-    beyond, live = slot_columns([rd[72:76, :], ro[228:232, :]])
+def beyond_cells(rs, rt):
+    return jnp.where(lax.rem(lax.axis_index("gx"), 2) == 0, rs[72:76, :], rt[0:4, :])
+
+
+def third_kernel(peers, ro, rs, rt, rf, eo, hot, both):
+    ro = Masked(ro, has_other("gx", peers[0]))
+    beyond, live = slot_columns([beyond_cells(rs, rt), ro[228:232, :]])
     fill_tint(eo, beyond, live)
     fill_hot(hot, flat_cells(ro[224:228, :]), range(CY))
     both[...] = dot_nn(hot[...], eo[...])
@@ -233,11 +254,11 @@
 
 
 def main_kernel(
+    peers,
     own,
     rp,
     ro,
-    rd,
-    re,
+    rs,
     from_core,
     from_chip,
     f2,
@@ -263,6 +284,8 @@
 ):
     gx = lax.axis_index("gx")
     gy = lax.axis_index("gy")
+    ro = Masked(ro, has_other("gx", peers[0]))
+    from_chip = Masked(from_chip, has_other("gy", peers[1]))
     par = lax.rem(gx, 2)
     even = par == 0
     sgn = 1 - 2 * par
@@ -279,11 +302,11 @@
             w[base + 3 : base + 11, :] = ref[8 * k : 8 * k + 8, :]
 
     def place_x(odd):
-        lo, hi, lo2 = (rp, ro, re) if odd else (ro, rp, rd)
-        place(lo2, 9, 4)
+        lo, hi = (rp, ro) if odd else (ro, rp)
         place(lo, 28, PER)
         place(hi, 28, 5 * PER)
 
+    place(Masked(rs, gx >= 2), 9, 4)
     place(own, 28, 3 * PER)
     by_parity("gx", place_x)
 
@@ -547,24 +570,24 @@
 
 def send(value, axis, target):
     peers = lax.axis_size(axis)
-    pairs = [(i, target(i)) for i in range(peers) if target(i) is not None]
-    return lax.ppermute(value, axis, [(i, j) for i, j in pairs if 0 <= j < peers])
-
-
-def partner_of(i):
+    return lax.ppermute(value, axis, [(i, target(i, peers)) for i in range(peers)])
+
+
+def partner_of(i, peers):
     return i ^ 1
 
 
-def other_of(i):
-    return i + 1 if i % 2 else i - 1
-
-
-def beyond_of(i):
-    return i - 2 if i % 2 else i + 2
-
-
-def odd_after(i):
-    return i + 2 if i % 2 else None
+def other_of(i, peers):
+    j = i + 1 if i % 2 else i - 1
+    return j if 0 <= j < peers else i
+
+
+def ahead_of(i, peers):
+    return (i + 2) % peers
+
+
+def odd_behind(i, peers):
+    return (i - 2) % peers if i % 2 else i
 
 
 VMEM = pl.BlockSpec(memory_space=pltpu.VMEM)
@@ -585,19 +608,19 @@
         pltpu.with_memory_space_constraint(array, pltpu.HBM)
         for array in (trans, storage, fault_cells, fault_trans)
     ]
-    own, plane = pl.pallas_call(
+    own, plane, tile = pl.pallas_call(
         functools.partial(pack_kernel, peers),
-        out_shape=(sds(232, NZ), sds(80, NZ)),
+        out_shape=(sds(232, NZ), sds(80, NZ), sds(8, NZ)),
         in_specs=[pl.BlockSpec(memory_space=pltpu.SMEM)] + [HBM] * 4,
-        out_specs=(VMEM, VMEM),
+        out_specs=(VMEM,) * 3,
         scratch_shapes=[pltpu.VMEM(array.shape, array.dtype) for array in sources]
         + [pltpu.SemaphoreType.DMA((4,))],
         compiler_params=params(16),
         name="pack",
     )(fault_count, *sources)
     rp = send(own, "gx", partner_of)
-    rd = send(plane, "gx", beyond_of)
-    re = send(plane, "gx", odd_after)
+    rs = send(plane, "gx", ahead_of)
+    rt = send(tile, "gx", odd_behind)
     ro = send(own, "gx", other_of)
     pieces = sds(CY, 2 * NZ, NZ, dtype=bf16)
     f2, ft2, rf_pair = pl.pallas_call(
@@ -615,19 +638,19 @@
         name="faults",
     )(own, rp)
     to_core, to_chip = pl.pallas_call(
-        column_kernel,
+        functools.partial(column_kernel, peers),
         out_shape=(sds(Y_ROWS, NZ), sds(Y_ROWS, NZ)),
         in_specs=[VMEM] * 5,
         out_specs=(VMEM,) * 2,
         compiler_params=params(16),
         name="columns",
-    )(own, rp, ro, rd, re)
+    )(own, rp, ro, rs, rt)
     from_chip = send(to_chip, "gy", other_of)
     from_core = send(to_core, "gy", partner_of)
     rf_third = pl.pallas_call(
-        third_kernel,
+        functools.partial(third_kernel, peers),
         out_shape=sds(CY, 8, NZ),
-        in_specs=[VMEM] * 2,
+        in_specs=[VMEM] * 3,
         out_specs=VMEM,
         scratch_shapes=[
             pltpu.VMEM((SLOTS, NZ), bf16),
@@ -637,11 +660,11 @@
         compiler_params=params(16),
         cost_estimate=pl.CostEstimate(flops=10**9, bytes_accessed=2**20, transcendentals=0),
         name="third",
-    )(ro, rd)
+    )(ro, rs, rt)
     return pl.pallas_call(
-        main_kernel,
+        functools.partial(main_kernel, peers),
         out_shape=sds(125, 1, 256),
-        in_specs=[VMEM] * 11,
+        in_specs=[VMEM] * 10,
         out_specs=VMEM,
         scratch_shapes=[
             pltpu.VMEM((7 * PER * ROWS, NZ), f32),
@@ -662,7 +685,7 @@
         ],
         compiler_params=params(24),
         name="galerkin",
-    )(own, rp, ro, rd, re, from_core, from_chip, f2, ft2, rf_pair, rf_third)
+    )(own, rp, ro, rs, from_core, from_chip, f2, ft2, rf_pair, rf_third)
 
 
 def solution(mesh):

time: 28 us -> 26.4 us (0.943)
  the two profiles are of different devices: /device:TPU:19 before, /device:TPU:1 now
where the time goes in v5:
time: 26.4 us; the launch traced here: 26.2 us
  starting transfers between devices  12.3 us (47%)
  Pallas kernels  8.84 us (33%)
  waiting for transfers between devices  4.35 us (16%)
  between operations  0.7 us (3%)
    ppermute x6, starting transfers between devices, send(): lax.ppermute(value, axis, [(i, target(i, peers)) for i in range(peers)])  12.3 us
    pallas_call x1, Pallas kernels, per_device(): pl.pallas_call(functools.partial(main_kernel, peers), out_shape=sds(125,...  5.71 us
    ppermute x6, waiting for transfers between devices, send(): lax.ppermute(value, axis, [(i, target(i, peers)) for i in range(peers)])  4.35 us
    pallas_call x1, Pallas kernels, per_device(): pl.pallas_call(functools.partial(pack_kernel, peers), out_shape=(sds(232,...  1.05 us
    pallas_call x1, Pallas kernels, per_device(): pl.pallas_call(fault_kernel, out_shape=(pieces, pieces, sds(2, CY, 8, NZ)...  1.03 us
    pallas_call x1, Pallas kernels, per_device(): pl.pallas_call(functools.partial(third_kernel, peers), out_shape=sds(CY,...  0.97 us
  transfers between devices with their start and end apart: 6, of which 2 were waited for; matrix products, arithmetic and copies ran while one was open for 0% of the time, Pallas kernels for 8%

profile of v5, /device:TPU:1, one launch (start us, length us, event | category | flops | bytes accessed | tf_op | source)
XLA Modules:
  0.0 26.2 jit_solution(16001016050029536316)
XLA Ops:
  0.7 1.1 %pack.1 = (f32[232,128]{1,0:T(8,128)S(1)}, f32[80,128]{1,0:T(8,128)S(1)}, f32[8,128]{1,0:T(8,128)S(1)}) custom-call(s32[1,1]{1,0:T(1,128)S(6)} %copy.6.count, f32[13,2,1024]{2,1,0:T(2,128)} %refs_0_.1, f32[2,1024]{1,0:T(2,128)} %refs_1_.1, s32[1,1,512]{2,1,0:T(1,128)} %refs_2_.1, f32[1,1,512]{2,1,0:T(1,128)} %refs_3_.1), custom_call_target="tpu_custom_call" | custom-call | tf_op jit(solution)/shard_map/pack/pallas_call | solution.py:611
  1.7 0.7 %collective-permute-start.1 = (f32[232,128]{1,0:T(8,128)S(1)}, f32[232,128]{1,0:T(8,128)S(1)}, u32[]{:S(2)}, u32[]{:S(2)}) collective-permute-start(f32[232,128]{1,0:T(8,128)S(1)} %get-tuple-element.13.own), channel_id=1, source_target_pairs={{0,0},{4,8},{8,4},{12,16},{16,12},{20,24},{24,20},{28,28},{1,1},{5... | collective-permute-start | bytes 356360 | tf_op jit(solution)/shard_map/ppermute | solution.py:573
  2.4 4.6 %collective-permute-start = (f32[232,128]{1,0:T(8,128)S(1)}, f32[232,128]{1,0:T(8,128)S(1)}, u32[]{:S(2)}, u32[]{:S(2)}) collective-permute-start(f32[232,128]{1,0:T(8,128)S(1)} %get-tuple-element.13.own), channel_id=1, source_target_pairs={{0,4},{4,0},{8,12},{12,8},{16,20},{20,16},{24,28},{28,24},{1,5},{5... | collective-permute-start | bytes 356360 | tf_op jit(solution)/shard_map/ppermute | solution.py:573
  7.0 1.3 %collective-permute-start.2 = (f32[80,128]{1,0:T(8,128)S(1)}, f32[80,128]{1,0:T(8,128)S(1)}, u32[]{:S(2)}, u32[]{:S(2)}) collective-permute-start(f32[80,128]{1,0:T(8,128)S(1)} %get-tuple-element.14), channel_id=1, source_target_pairs={{0,8},{4,12},{8,16},{12,20},{16,24},{20,28},{24,0},{28,4},{1,9},{5... | collective-permute-start | bytes 122888 | tf_op jit(solution)/shard_map/ppermute | solution.py:573
  8.3 0.6 %collective-permute-start.3 = (f32[8,128]{1,0:T(8,128)S(1)}, f32[8,128]{1,0:T(8,128)S(1)}, u32[]{:S(2)}, u32[]{:S(2)}) collective-permute-start(f32[8,128]{1,0:T(8,128)S(1)} %get-tuple-element.15), channel_id=1, source_target_pairs={{0,0},{4,28},{8,8},{12,4},{16,16},{20,12},{24,24},{28,20},{1,1},{5... | collective-permute-start | bytes 12296 | tf_op jit(solution)/shard_map/ppermute | solution.py:573
  9.0 0.0 collective-permute-done.3.rt
  9.0 3.1 %collective-permute-done.2.rs = f32[80,128]{1,0:T(8,128)S(1)} collective-permute-done((f32[80,128]{1,0:T(8,128)S(1)}, f32[80,128]{1,0:T(8,128)S(1)}, u32[]{:S(2)}, u32[]{:S(2)}) %collective-permute-start.2) | collective-permute-done | bytes 40992 | tf_op jit(solution)/shard_map/ppermute | solution.py:573
  12.1 0.0 collective-permute-done.1.ro
  12.1 0.0 collective-permute-done.rp
  12.1 0.1 columns.1
  12.2 2.0 %collective-permute-start.4 = (f32[256,128]{1,0:T(8,128)S(1)}, f32[256,128]{1,0:T(8,128)S(1)}, u32[]{:S(2)}, u32[]{:S(2)}) collective-permute-start(f32[256,128]{1,0:T(8,128)S(1)} %get-tuple-element.16), channel_id=1, source_target_pairs={{0,1},{1,0},{2,3},{3,2},{4,5},{5,4},{6,7},{7,6},{8,9},{9,8},{10,11... | collective-permute-start | bytes 393224 | tf_op jit(solution)/shard_map/ppermute | solution.py:573
  14.2 3.0 %collective-permute-start.5 = (f32[256,128]{1,0:T(8,128)S(1)}, f32[256,128]{1,0:T(8,128)S(1)}, u32[]{:S(2)}, u32[]{:S(2)}) collective-permute-start(f32[256,128]{1,0:T(8,128)S(1)} %get-tuple-element.17), channel_id=1, source_target_pairs={{0,0},{1,2},{2,1},{3,3},{4,4},{5,6},{6,5},{7,7},{8,8},{9,10},{10,9... | collective-permute-start | bytes 393224 | tf_op jit(solution)/shard_map/ppermute | solution.py:573
  17.2 1.0 %faults.1 = (bf16[8,256,128]{2,1,0:T(8,128)(2,1)S(1)}, bf16[8,256,128]{2,1,0:T(8,128)(2,1)S(1)}, f32[2,8,8,128]{3,2,1,0:T(8,128)S(1)}) custom-call(f32[232,128]{1,0:T(8,128)S(1)} %get-tuple-element.13.own, f32[232,128]{1,0:T(8,128)S(1)} %collective-permute-done.rp), custom_call_target="tpu_custom_call" | custom-call | flops 2000000000 | bytes 2097152 | tf_op jit(solution)/shard_map/faults/pallas_call | solution.py:626
  18.3 1.0 %third.1.rf_third = f32[8,8,128]{2,1,0:T(8,128)S(1)} custom-call(f32[232,128]{1,0:T(8,128)S(1)} %collective-permute-done.1.ro, f32[80,128]{1,0:T(8,128)S(1)} %collective-permute-done.2.rs, f32[8,128]{1,0:T(8,128)S(1)} %collective-permute-done.3.rt), custom_call_target="tpu_custom_call" | custom-call | flops 1000000000 | bytes 1048576 | tf_op jit(solution)/shard_map/third/pallas_call | solution.py:650
  19.3 0.0 collective-permute-done.4.from_core
  19.3 1.2 %collective-permute-done.5.from_chip = f32[256,128]{1,0:T(8,128)S(1)} collective-permute-done((f32[256,128]{1,0:T(8,128)S(1)}, f32[256,128]{1,0:T(8,128)S(1)}, u32[]{:S(2)}, u32[]{:S(2)}) %collective-permute-start.5) | collective-permute-done | bytes 131104 | tf_op jit(solution)/shard_map/ppermute | solution.py:573
  20.5 5.7 %galerkin.1 = f32[125,1,256]{2,1,0:T(1,128)} custom-call(f32[232,128]{1,0:T(8,128)S(1)} %get-tuple-element.13.own, f32[232,128]{1,0:T(8,128)S(1)} %collective-permute-done.rp, f32[232,128]{1,0:T(8,128)S(1)} %collective-permute-done.1.ro, f32[80,128]{1,0:T(8,128)S(1)} %collective-permute-done.2.rs, f32[256,128]{1,0:T(8,128)S(1)} %collective-permute-done.4.from_core, ...), custom_call_target="tpu_custom_call" | custom-call | tf_op jit(solution)/shard_map/galerkin/pallas_call | solution.py:664
Async XLA Ops:
  1.7 10.4 %collective-permute-start.1 = (f32[232,128]{1,0:T(8,128)S(1)}, f32[232,128]{1,0:T(8,128)S(1)}, u32[]{:S(2)}, u32[]{:S(2)}) collective-permute-start(f32[232,128]{1,0:T(8,128)S(1)} %get-tuple-element.13.own), channel_id=1, source_target_pairs={{0,0},{4,8},{8,4},{12,16},{16,12},{20,24},{24,20},{28,28},{1,1},{5... | collective-permute-start | bytes 356360 | tf_op jit(solution)/shard_map/ppermute | solution.py:573
  2.4 9.7 %collective-permute-start = (f32[232,128]{1,0:T(8,128)S(1)}, f32[232,128]{1,0:T(8,128)S(1)}, u32[]{:S(2)}, u32[]{:S(2)}) collective-permute-start(f32[232,128]{1,0:T(8,128)S(1)} %get-tuple-element.13.own), channel_id=1, source_target_pairs={{0,4},{4,0},{8,12},{12,8},{16,20},{20,16},{24,28},{28,24},{1,5},{5... | collective-permute-start | bytes 356360 | tf_op jit(solution)/shard_map/ppermute | solution.py:573
  7.0 5.1 %collective-permute-start.2 = (f32[80,128]{1,0:T(8,128)S(1)}, f32[80,128]{1,0:T(8,128)S(1)}, u32[]{:S(2)}, u32[]{:S(2)}) collective-permute-start(f32[80,128]{1,0:T(8,128)S(1)} %get-tuple-element.14), channel_id=1, source_target_pairs={{0,8},{4,12},{8,16},{12,20},{16,24},{20,28},{24,0},{28,4},{1,9},{5... | collective-permute-start | bytes 122888 | tf_op jit(solution)/shard_map/ppermute | solution.py:573
  8.3 0.7 %collective-permute-start.3 = (f32[8,128]{1,0:T(8,128)S(1)}, f32[8,128]{1,0:T(8,128)S(1)}, u32[]{:S(2)}, u32[]{:S(2)}) collective-permute-start(f32[8,128]{1,0:T(8,128)S(1)} %get-tuple-element.15), channel_id=1, source_target_pairs={{0,0},{4,28},{8,8},{12,4},{16,16},{20,12},{24,24},{28,20},{1,1},{5... | collective-permute-start | bytes 12296 | tf_op jit(solution)/shard_map/ppermute | solution.py:573
  12.2 7.1 %collective-permute-start.4 = (f32[256,128]{1,0:T(8,128)S(1)}, f32[256,128]{1,0:T(8,128)S(1)}, u32[]{:S(2)}, u32[]{:S(2)}) collective-permute-start(f32[256,128]{1,0:T(8,128)S(1)} %get-tuple-element.16), channel_id=1, source_target_pairs={{0,1},{1,0},{2,3},{3,2},{4,5},{5,4},{6,7},{7,6},{8,9},{9,8},{10,11... | collective-permute-start | bytes 393224 | tf_op jit(solution)/shard_map/ppermute | solution.py:573
  14.2 6.3 %collective-permute-start.5 = (f32[256,128]{1,0:T(8,128)S(1)}, f32[256,128]{1,0:T(8,128)S(1)}, u32[]{:S(2)}, u32[]{:S(2)}) collective-permute-start(f32[256,128]{1,0:T(8,128)S(1)} %get-tuple-element.17), channel_id=1, source_target_pairs={{0,0},{1,2},{2,1},{3,3},{4,4},{5,6},{6,5},{7,7},{8,8},{9,10},{10,9... | collective-permute-start | bytes 393224 | tf_op jit(solution)/shard_map/ppermute | solution.py:573

commit v6 on v5

--- a/solution.py
+++ b/solution.py
@@ -126,7 +126,8 @@
     return jnp.where(lax.rem(at, 2) == 0, at > 0, at < peers - 1)
 
 
-def column_kernel(peers, own, rp, ro, rs, rt, to_core, to_chip):
+def column_kernel(peers, own, rp, ro, rs, rt, after, to_core, to_chip):
+    del after
     ro = Masked(ro, has_other("gx", peers[0]))
     lo2 = Masked(rs, lax.axis_index("gx") >= 2)
     tile = own[224:232, :]
@@ -618,10 +619,10 @@
         compiler_params=params(16),
         name="pack",
     )(fault_count, *sources)
+    ro = send(own, "gx", other_of)
+    rt = send(tile, "gx", odd_behind)
+    rs = send(plane, "gx", ahead_of)
     rp = send(own, "gx", partner_of)
-    rs = send(plane, "gx", ahead_of)
-    rt = send(tile, "gx", odd_behind)
-    ro = send(own, "gx", other_of)
     pieces = sds(CY, 2 * NZ, NZ, dtype=bf16)
     f2, ft2, rf_pair = pl.pallas_call(
         fault_kernel,
@@ -640,11 +641,11 @@
     to_core, to_chip = pl.pallas_call(
         functools.partial(column_kernel, peers),
         out_shape=(sds(Y_ROWS, NZ), sds(Y_ROWS, NZ)),
-        in_specs=[VMEM] * 5,
+        in_specs=[VMEM] * 6,
         out_specs=(VMEM,) * 2,
         compiler_params=params(16),
         name="columns",
-    )(own, rp, ro, rs, rt)
+    )(own, rp, ro, rs, rt, rf_pair)
     from_chip = send(to_chip, "gy", other_of)
     from_core = send(to_core, "gy", partner_of)
     rf_third = pl.pallas_call(

time: 26.4 us -> 27.3 us (1.034)
  the two profiles are of different devices: /device:TPU:1 before, /device:TPU:27 now
where the time goes in v6:
time: 27.3 us; the launch traced here: 27.1 us
  starting transfers between devices  12.4 us (45%)
  Pallas kernels  8.84 us (32%)
  waiting for transfers between devices  5.21 us (19%)
  between operations  0.7 us (3%)
    ppermute x6, starting transfers between devices, send(): lax.ppermute(value, axis, [(i, target(i, peers)) for i in range(peers)])  12.4 us
    pallas_call x1, Pallas kernels, per_device(): pl.pallas_call(functools.partial(main_kernel, peers), out_shape=sds(125,...  5.72 us
    ppermute x6, waiting for transfers between devices, send(): lax.ppermute(value, axis, [(i, target(i, peers)) for i in range(peers)])  5.21 us
    pallas_call x1, Pallas kernels, per_device(): pl.pallas_call(functools.partial(pack_kernel, peers), out_shape=(sds(232,...  1.04 us
    pallas_call x1, Pallas kernels, per_device(): pl.pallas_call(fault_kernel, out_shape=(pieces, pieces, sds(2, CY, 8, NZ)...  1.03 us
    pallas_call x1, Pallas kernels, per_device(): pl.pallas_call(functools.partial(third_kernel, peers), out_shape=sds(CY,...  0.97 us
  transfers between devices with their start and end apart: 6, of which 2 were waited for; matrix products, arithmetic and copies ran while one was open for 0% of the time, Pallas kernels for 7%

profile of v6, /device:TPU:27, one launch (start us, length us, event | category | flops | bytes accessed | tf_op | source)
XLA Modules:
  0.0 27.1 jit_solution(9619460377829381704)
XLA Ops:
  0.7 1.0 %pack.1 = (f32[232,128]{1,0:T(8,128)S(1)}, f32[80,128]{1,0:T(8,128)S(1)}, f32[8,128]{1,0:T(8,128)S(1)}) custom-call(s32[1,1]{1,0:T(1,128)S(6)} %copy.6.count, f32[13,2,1024]{2,1,0:T(2,128)} %refs_0_.1, f32[2,1024]{1,0:T(2,128)} %refs_1_.1, s32[1,1,512]{2,1,0:T(1,128)} %refs_2_.1, f32[1,1,512]{2,1,0:T(1,128)} %refs_3_.1), custom_call_target="tpu_custom_call" | custom-call | tf_op jit(solution)/shard_map/pack/pallas_call | solution.py:612
  1.7 0.3 %collective-permute-start = (f32[232,128]{1,0:T(8,128)S(1)}, f32[232,128]{1,0:T(8,128)S(1)}, u32[]{:S(2)}, u32[]{:S(2)}) collective-permute-start(f32[232,128]{1,0:T(8,128)S(1)} %get-tuple-element.13.own), channel_id=1, source_target_pairs={{0,4},{4,0},{8,12},{12,8},{16,20},{20,16},{24,28},{28,24},{1,5},{5... | collective-permute-start | bytes 356360 | tf_op jit(solution)/shard_map/ppermute | solution.py:574
  2.0 0.7 %collective-permute-start.1 = (f32[232,128]{1,0:T(8,128)S(1)}, f32[232,128]{1,0:T(8,128)S(1)}, u32[]{:S(2)}, u32[]{:S(2)}) collective-permute-start(f32[232,128]{1,0:T(8,128)S(1)} %get-tuple-element.13.own), channel_id=1, source_target_pairs={{0,0},{4,8},{8,4},{12,16},{16,12},{20,24},{24,20},{28,28},{1,1},{5... | collective-permute-start | bytes 356360 | tf_op jit(solution)/shard_map/ppermute | solution.py:574
  2.7 3.5 %collective-permute-start.2 = (f32[80,128]{1,0:T(8,128)S(1)}, f32[80,128]{1,0:T(8,128)S(1)}, u32[]{:S(2)}, u32[]{:S(2)}) collective-permute-start(f32[80,128]{1,0:T(8,128)S(1)} %get-tuple-element.14), channel_id=1, source_target_pairs={{0,8},{4,12},{8,16},{12,20},{16,24},{20,28},{24,0},{28,4},{1,9},{5... | collective-permute-start | bytes 122888 | tf_op jit(solution)/shard_map/ppermute | solution.py:574
  6.2 2.1 %collective-permute-start.3 = (f32[8,128]{1,0:T(8,128)S(1)}, f32[8,128]{1,0:T(8,128)S(1)}, u32[]{:S(2)}, u32[]{:S(2)}) collective-permute-start(f32[8,128]{1,0:T(8,128)S(1)} %get-tuple-element.15), channel_id=1, source_target_pairs={{0,0},{4,28},{8,8},{12,4},{16,16},{20,12},{24,24},{28,20},{1,1},{5... | collective-permute-start | bytes 12296 | tf_op jit(solution)/shard_map/ppermute | solution.py:574
  8.3 0.0 collective-permute-done.rp
  8.3 1.0 %faults.1 = (bf16[8,256,128]{2,1,0:T(8,128)(2,1)S(1)}, bf16[8,256,128]{2,1,0:T(8,128)(2,1)S(1)}, f32[2,8,8,128]{3,2,1,0:T(8,128)S(1)}) custom-call(f32[232,128]{1,0:T(8,128)S(1)} %get-tuple-element.13.own, f32[232,128]{1,0:T(8,128)S(1)} %collective-permute-done.rp), custom_call_target="tpu_custom_call" | custom-call | flops 2000000000 | bytes 2097152 | tf_op jit(solution)/shard_map/faults/pallas_call | solution.py:627
  9.3 2.9 %collective-permute-done.3.rt = f32[8,128]{1,0:T(8,128)S(1)} collective-permute-done((f32[8,128]{1,0:T(8,128)S(1)}, f32[8,128]{1,0:T(8,128)S(1)}, u32[]{:S(2)}, u32[]{:S(2)}) %collective-permute-start.3) | collective-permute-done | bytes 4128 | tf_op jit(solution)/shard_map/ppermute | solution.py:574
  12.3 0.0 collective-permute-done.2.rs
  12.3 0.0 collective-permute-done.1.ro
  12.3 0.1 columns.1
  12.4 2.7 %collective-permute-start.4 = (f32[256,128]{1,0:T(8,128)S(1)}, f32[256,128]{1,0:T(8,128)S(1)}, u32[]{:S(2)}, u32[]{:S(2)}) collective-permute-start(f32[256,128]{1,0:T(8,128)S(1)} %get-tuple-element.17), channel_id=1, source_target_pairs={{0,1},{1,0},{2,3},{3,2},{4,5},{5,4},{6,7},{7,6},{8,9},{9,8},{10,11... | collective-permute-start | bytes 393224 | tf_op jit(solution)/shard_map/ppermute | solution.py:574
  15.1 3.0 %collective-permute-start.5 = (f32[256,128]{1,0:T(8,128)S(1)}, f32[256,128]{1,0:T(8,128)S(1)}, u32[]{:S(2)}, u32[]{:S(2)}) collective-permute-start(f32[256,128]{1,0:T(8,128)S(1)} %get-tuple-element.18), channel_id=1, source_target_pairs={{0,0},{1,2},{2,1},{3,3},{4,4},{5,6},{6,5},{7,7},{8,8},{9,10},{10,9... | collective-permute-start | bytes 393224 | tf_op jit(solution)/shard_map/ppermute | solution.py:574
  18.2 1.0 %third.1.rf_third = f32[8,8,128]{2,1,0:T(8,128)S(1)} custom-call(f32[232,128]{1,0:T(8,128)S(1)} %collective-permute-done.1.ro, f32[80,128]{1,0:T(8,128)S(1)} %collective-permute-done.2.rs, f32[8,128]{1,0:T(8,128)S(1)} %collective-permute-done.3.rt), custom_call_target="tpu_custom_call" | custom-call | flops 1000000000 | bytes 1048576 | tf_op jit(solution)/shard_map/third/pallas_call | solution.py:651
  19.1 0.0 collective-permute-done.4.from_core
  19.1 2.3 %collective-permute-done.5.from_chip = f32[256,128]{1,0:T(8,128)S(1)} collective-permute-done((f32[256,128]{1,0:T(8,128)S(1)}, f32[256,128]{1,0:T(8,128)S(1)}, u32[]{:S(2)}, u32[]{:S(2)}) %collective-permute-start.5) | collective-permute-done | bytes 131104 | tf_op jit(solution)/shard_map/ppermute | solution.py:574
  21.4 5.7 %galerkin.1 = f32[125,1,256]{2,1,0:T(1,128)} custom-call(f32[232,128]{1,0:T(8,128)S(1)} %get-tuple-element.13.own, f32[232,128]{1,0:T(8,128)S(1)} %collective-permute-done.rp, f32[232,128]{1,0:T(8,128)S(1)} %collective-permute-done.1.ro, f32[80,128]{1,0:T(8,128)S(1)} %collective-permute-done.2.rs, f32[256,128]{1,0:T(8,128)S(1)} %collective-permute-done.4.from_core, ...), custom_call_target="tpu_custom_call" | custom-call | tf_op jit(solution)/shard_map/galerkin/pallas_call | solution.py:665
Async XLA Ops:
  1.7 6.6 %collective-permute-start = (f32[232,128]{1,0:T(8,128)S(1)}, f32[232,128]{1,0:T(8,128)S(1)}, u32[]{:S(2)}, u32[]{:S(2)}) collective-permute-start(f32[232,128]{1,0:T(8,128)S(1)} %get-tuple-element.13.own), channel_id=1, source_target_pairs={{0,4},{4,0},{8,12},{12,8},{16,20},{20,16},{24,28},{28,24},{1,5},{5... | collective-permute-start | bytes 356360 | tf_op jit(solution)/shard_map/ppermute | solution.py:574
  2.0 10.3 %collective-permute-start.1 = (f32[232,128]{1,0:T(8,128)S(1)}, f32[232,128]{1,0:T(8,128)S(1)}, u32[]{:S(2)}, u32[]{:S(2)}) collective-permute-start(f32[232,128]{1,0:T(8,128)S(1)} %get-tuple-element.13.own), channel_id=1, source_target_pairs={{0,0},{4,8},{8,4},{12,16},{16,12},{20,24},{24,20},{28,28},{1,1},{5... | collective-permute-start | bytes 356360 | tf_op jit(solution)/shard_map/ppermute | solution.py:574
  2.7 9.6 %collective-permute-start.2 = (f32[80,128]{1,0:T(8,128)S(1)}, f32[80,128]{1,0:T(8,128)S(1)}, u32[]{:S(2)}, u32[]{:S(2)}) collective-permute-start(f32[80,128]{1,0:T(8,128)S(1)} %get-tuple-element.14), channel_id=1, source_target_pairs={{0,8},{4,12},{8,16},{12,20},{16,24},{20,28},{24,0},{28,4},{1,9},{5... | collective-permute-start | bytes 122888 | tf_op jit(solution)/shard_map/ppermute | solution.py:574
  6.2 6.1 %collective-permute-start.3 = (f32[8,128]{1,0:T(8,128)S(1)}, f32[8,128]{1,0:T(8,128)S(1)}, u32[]{:S(2)}, u32[]{:S(2)}) collective-permute-start(f32[8,128]{1,0:T(8,128)S(1)} %get-tuple-element.15), channel_id=1, source_target_pairs={{0,0},{4,28},{8,8},{12,4},{16,16},{20,12},{24,24},{28,20},{1,1},{5... | collective-permute-start | bytes 12296 | tf_op jit(solution)/shard_map/ppermute | solution.py:574
  12.4 6.8 %collective-permute-start.4 = (f32[256,128]{1,0:T(8,128)S(1)}, f32[256,128]{1,0:T(8,128)S(1)}, u32[]{:S(2)}, u32[]{:S(2)}) collective-permute-start(f32[256,128]{1,0:T(8,128)S(1)} %get-tuple-element.17), channel_id=1, source_target_pairs={{0,1},{1,0},{2,3},{3,2},{4,5},{5,4},{6,7},{7,6},{8,9},{9,8},{10,11... | collective-permute-start | bytes 393224 | tf_op jit(solution)/shard_map/ppermute | solution.py:574
  15.1 6.3 %collective-permute-start.5 = (f32[256,128]{1,0:T(8,128)S(1)}, f32[256,128]{1,0:T(8,128)S(1)}, u32[]{:S(2)}, u32[]{:S(2)}) collective-permute-start(f32[256,128]{1,0:T(8,128)S(1)} %get-tuple-element.18), channel_id=1, source_target_pairs={{0,0},{1,2},{2,1},{3,3},{4,4},{5,6},{6,5},{7,7},{8,8},{9,10},{10,9... | collective-permute-start | bytes 393224 | tf_op jit(solution)/shard_map/ppermute | solution.py:574

commit v7 on v6

--- a/solution.py
+++ b/solution.py
@@ -49,7 +49,7 @@
 
 
 def pack_kernel(peers, count, *refs):
-    sources, (block, plane, tile), targets, sems = refs[:4], refs[4:7], refs[7:11], refs[11]
+    sources, (block, plane), targets, sems = refs[:4], refs[4:6], refs[6:10], refs[10]
     copies = [
         pltpu.make_async_copy(src, dst, sems.at[k])
         for k, (src, dst) in enumerate(zip(sources, targets))
@@ -102,9 +102,19 @@
         block[base + 4 + r : base + 5 + r, :] = jnp.where(
             lane + r * NZ < live, ftrans[0, :, lanes], 0.0
         )
-    plane[0:72, :] = block[(PER + 4) * 8 : (PER + 13) * 8, :]
-    plane[72:80, :] = block[base : base + 8, :]
-    tile[...] = block[base : base + 8, :]
+    plane[...] = block[(PER + 4) * 8 : (PER + 13) * 8, :]
+
+
+def partner_rows(cells):
+    return jnp.concatenate(
+        [cells[0, :, r * NZ : (r + 1) * NZ] for r in range(4)], axis=0
+    ).astype(f32)
+
+
+def join_kernel(own, cells, joined):
+    joined[0:232, :] = own[...]
+    joined[232:236, :] = partner_rows(cells)
+    joined[236:240, :] = jnp.zeros((4, NZ), f32)
 
 
 def by_parity(axis, body):
@@ -126,13 +136,13 @@
     return jnp.where(lax.rem(at, 2) == 0, at > 0, at < peers - 1)
 
 
-def column_kernel(peers, own, rp, ro, rs, rt, after, to_core, to_chip):
+def column_kernel(peers, own, rp, ro, rs, cells, after, to_core, to_chip):
     del after
     ro = Masked(ro, has_other("gx", peers[0]))
     lo2 = Masked(rs, lax.axis_index("gx") >= 2)
     tile = own[224:232, :]
     other = ro[224:232, :]
-    parts = (tile[0:4], rp[224:228, :], tile[4:8], other[0:4], beyond_cells(rs, rt), other[4:8])
+    parts = (tile[0:4], partner_rows(cells), tile[4:8], other[0:4], ro[232:236, :], other[4:8])
     for out in (to_core, to_chip):
         for k, part in enumerate(parts):
             out[FAULT_ROW + 4 * k : FAULT_ROW + 4 * k + 4, :] = part
@@ -220,8 +230,8 @@
     return f2, ft2, dot_nn(one2, ft2), dot_nn(one2, f2)
 
 
-def fault_kernel(own, rp, f2, ft2, rf, far2, hot, both):
-    partner, live = slot_columns([rp[224:228, :], own[228:232, :]])
+def fault_kernel(own, cells, f2, ft2, rf, far2, hot, both):
+    partner, live = slot_columns([partner_rows(cells), own[228:232, :]])
     fill_far(far2, partner, live)
     fill_hot(hot, flat_cells(own[224:228, :]), range(CY))
     both[...] = dot_nn(hot[...], far2[...])
@@ -229,13 +239,9 @@
         f2[y], ft2[y], rf[0, y], rf[1, y] = pair_matrix(both[y * NZ : (y + 1) * NZ, :])
 
 
-def beyond_cells(rs, rt):
-    return jnp.where(lax.rem(lax.axis_index("gx"), 2) == 0, rs[72:76, :], rt[0:4, :])
-
-
-def third_kernel(peers, ro, rs, rt, rf, eo, hot, both):
+def third_kernel(peers, ro, rf, eo, hot, both):
     ro = Masked(ro, has_other("gx", peers[0]))
-    beyond, live = slot_columns([beyond_cells(rs, rt), ro[228:232, :]])
+    beyond, live = slot_columns([ro[232:236, :], ro[228:232, :]])
     fill_tint(eo, beyond, live)
     fill_hot(hot, flat_cells(ro[224:228, :]), range(CY))
     both[...] = dot_nn(hot[...], eo[...])
@@ -587,10 +593,6 @@
     return (i + 2) % peers
 
 
-def odd_behind(i, peers):
-    return (i - 2) % peers if i % 2 else i
-
-
 VMEM = pl.BlockSpec(memory_space=pltpu.VMEM)
 HBM = pl.BlockSpec(memory_space=pltpu.HBM)
 
@@ -605,22 +607,30 @@
 
 def per_device(trans, storage, fault_cells, fault_count, fault_trans):
     peers = (lax.axis_size("gx"), lax.axis_size("gy"))
+    cells = send(fault_cells, "gx", partner_of)
     sources = [
         pltpu.with_memory_space_constraint(array, pltpu.HBM)
         for array in (trans, storage, fault_cells, fault_trans)
     ]
-    own, plane, tile = pl.pallas_call(
+    own, plane = pl.pallas_call(
         functools.partial(pack_kernel, peers),
-        out_shape=(sds(232, NZ), sds(80, NZ), sds(8, NZ)),
+        out_shape=(sds(232, NZ), sds(72, NZ)),
         in_specs=[pl.BlockSpec(memory_space=pltpu.SMEM)] + [HBM] * 4,
-        out_specs=(VMEM,) * 3,
+        out_specs=(VMEM,) * 2,
         scratch_shapes=[pltpu.VMEM(array.shape, array.dtype) for array in sources]
         + [pltpu.SemaphoreType.DMA((4,))],
         compiler_params=params(16),
         name="pack",
     )(fault_count, *sources)
-    ro = send(own, "gx", other_of)
-    rt = send(tile, "gx", odd_behind)
+    joined = pl.pallas_call(
+        join_kernel,
+        out_shape=sds(240, NZ),
+        in_specs=[VMEM] * 2,
+        out_specs=VMEM,
+        compiler_params=params(16),
+        name="join",
+    )(own, cells)
+    ro = send(joined, "gx", other_of)
     rs = send(plane, "gx", ahead_of)
     rp = send(own, "gx", partner_of)
     pieces = sds(CY, 2 * NZ, NZ, dtype=bf16)
@@ -637,7 +647,7 @@
         compiler_params=params(16),
         cost_estimate=pl.CostEstimate(flops=2 * 10**9, bytes_accessed=2**21, transcendentals=0),
         name="faults",
-    )(own, rp)
+    )(own, cells)
     to_core, to_chip = pl.pallas_call(
         functools.partial(column_kernel, peers),
         out_shape=(sds(Y_ROWS, NZ), sds(Y_ROWS, NZ)),
@@ -645,13 +655,13 @@
         out_specs=(VMEM,) * 2,
         compiler_params=params(16),
         name="columns",
-    )(own, rp, ro, rs, rt, rf_pair)
+    )(own, rp, ro, rs, cells, rf_pair)
     from_chip = send(to_chip, "gy", other_of)
     from_core = send(to_core, "gy", partner_of)
     rf_third = pl.pallas_call(
         functools.partial(third_kernel, peers),
         out_shape=sds(CY, 8, NZ),
-        in_specs=[VMEM] * 3,
+        in_specs=[VMEM],
         out_specs=VMEM,
         scratch_shapes=[
             pltpu.VMEM((SLOTS, NZ), bf16),
@@ -661,7 +671,7 @@
         compiler_params=params(16),
         cost_estimate=pl.CostEstimate(flops=10**9, bytes_accessed=2**20, transcendentals=0),
         name="third",
-    )(ro, rs, rt)
+    )(ro)
     return pl.pallas_call(
         functools.partial(main_kernel, peers),
         out_shape=sds(125, 1, 256),

time: 27.3 us -> 26.1 us (0.956)
  the two profiles are of different devices: /device:TPU:27 before, /device:TPU:9 now
where the time goes in v7:
time: 26.1 us; the launch traced here: 25.9 us
  starting transfers between devices  11.6 us (44%)
  Pallas kernels  8.84 us (34%)
  waiting for transfers between devices  4.73 us (18%)
  between operations  0.7 us (3%)
    ppermute x6, starting transfers between devices, send(): lax.ppermute(value, axis, [(i, target(i, peers)) for i in range(peers)])  11.6 us
    pallas_call x1, Pallas kernels, per_device(): pl.pallas_call(functools.partial(main_kernel, peers), out_shape=sds(125,...  5.72 us
    ppermute x6, waiting for transfers between devices, send(): lax.ppermute(value, axis, [(i, target(i, peers)) for i in range(peers)])  4.73 us
    pallas_call x1, Pallas kernels, per_device(): pl.pallas_call(functools.partial(pack_kernel, peers), out_shape=(sds(232,...  1.05 us
    pallas_call x1, Pallas kernels, per_device(): pl.pallas_call(fault_kernel, out_shape=(pieces, pieces, sds(2, CY, 8, NZ)...  1.03 us
    pallas_call x1, Pallas kernels, per_device(): pl.pallas_call(functools.partial(third_kernel, peers), out_shape=sds(CY,...  0.96 us
  transfers between devices with their start and end apart: 6, of which 2 were waited for; matrix products, arithmetic and copies ran while one was open for 0% of the time, Pallas kernels for 12%

profile of v7, /device:TPU:9, one launch (start us, length us, event | category | flops | bytes accessed | tf_op | source)
XLA Modules:
  0.0 25.9 jit_solution(17110025950653031059)
XLA Ops:
  0.0 1.2 %collective-permute-start.1 = (s32[1,1,512]{2,1,0:T(1,128)}, s32[1,1,512]{2,1,0:T(1,128)S(1)}, u32[]{:S(2)}, u32[]{:S(2)}) collective-permute-start(s32[1,1,512]{2,1,0:T(1,128)} %refs_2_.1), channel_id=1, source_target_pairs={{0,4},{4,0},{8,12},{12,8},{16,20},{20,16},{24,28},{28,24},{1,5},{5... | collective-permute-start | bytes 6152 | tf_op jit(solution)/shard_map/ppermute | solution.py:580
  1.9 1.0 %pack.1 = (f32[232,128]{1,0:T(8,128)S(1)}, f32[72,128]{1,0:T(8,128)S(1)}) custom-call(s32[1,1]{1,0:T(1,128)S(6)} %copy.6.count, f32[13,2,1024]{2,1,0:T(2,128)} %refs_0_.1, f32[2,1024]{1,0:T(2,128)} %refs_1_.1, s32[1,1,512]{2,1,0:T(1,128)} %refs_2_.1, f32[1,1,512]{2,1,0:T(1,128)} %refs_3_.1), custom_call_target="tpu_custom_call" | custom-call | tf_op jit(solution)/shard_map/pack/pallas_call | solution.py:615
  2.9 0.3 %collective-permute-start = (f32[232,128]{1,0:T(8,128)S(1)}, f32[232,128]{1,0:T(8,128)S(1)}, u32[]{:S(2)}, u32[]{:S(2)}) collective-permute-start(f32[232,128]{1,0:T(8,128)S(1)} %get-tuple-element.12.own), channel_id=1, source_target_pairs={{0,4},{4,0},{8,12},{12,8},{16,20},{20,16},{24,28},{28,24},{1,5},{5... | collective-permute-start | bytes 356360 | tf_op jit(solution)/shard_map/ppermute | solution.py:580
  3.2 1.3 %collective-permute-start.3 = (f32[72,128]{1,0:T(8,128)S(1)}, f32[72,128]{1,0:T(8,128)S(1)}, u32[]{:S(2)}, u32[]{:S(2)}) collective-permute-start(f32[72,128]{1,0:T(8,128)S(1)} %get-tuple-element.13), channel_id=1, source_target_pairs={{0,8},{4,12},{8,16},{12,20},{16,24},{20,28},{24,0},{28,4},{1,9},{5... | collective-permute-start | bytes 110600 | tf_op jit(solution)/shard_map/ppermute | solution.py:580
  4.5 0.0 collective-permute-done.1.cells
  4.6 3.0 %collective-permute-start.2 = (f32[240,128]{1,0:T(8,128)S(1)}, f32[240,128]{1,0:T(8,128)S(1)}, u32[]{:S(2)}, u32[]{:S(2)}) collective-permute-start(f32[240,128]{1,0:T(8,128)S(1)} %join.1), channel_id=1, source_target_pairs={{0,0},{4,8},{8,4},{12,16},{16,12},{20,24},{24,20},{28,28},{1,1},{5... | collective-permute-start | bytes 368648 | tf_op jit(solution)/shard_map/ppermute | solution.py:580
  7.6 1.0 %faults.1 = (bf16[8,256,128]{2,1,0:T(8,128)(2,1)S(1)}, bf16[8,256,128]{2,1,0:T(8,128)(2,1)S(1)}, f32[2,8,8,128]{3,2,1,0:T(8,128)S(1)}) custom-call(f32[232,128]{1,0:T(8,128)S(1)} %get-tuple-element.12.own, s32[1,1,512]{2,1,0:T(1,128)S(1)} %collective-permute-done.1.cells), custom_call_target="tpu_custom_call" | custom-call | flops 2000000000 | bytes 2097152 | tf_op jit(solution)/shard_map/faults/pallas_call | solution.py:637
  8.6 0.0 collective-permute-done.3.rs
  8.6 0.0 collective-permute-done.rp
  8.6 2.5 %collective-permute-done.2.ro = f32[240,128]{1,0:T(8,128)S(1)} collective-permute-done((f32[240,128]{1,0:T(8,128)S(1)}, f32[240,128]{1,0:T(8,128)S(1)}, u32[]{:S(2)}, u32[]{:S(2)}) %collective-permute-start.2) | collective-permute-done | bytes 122912 | tf_op jit(solution)/shard_map/ppermute | solution.py:580
  11.1 0.1 columns.1
  11.2 2.7 %collective-permute-start.4 = (f32[256,128]{1,0:T(8,128)S(1)}, f32[256,128]{1,0:T(8,128)S(1)}, u32[]{:S(2)}, u32[]{:S(2)}) collective-permute-start(f32[256,128]{1,0:T(8,128)S(1)} %get-tuple-element.15), channel_id=1, source_target_pairs={{0,1},{1,0},{2,3},{3,2},{4,5},{5,4},{6,7},{7,6},{8,9},{9,8},{10,11... | collective-permute-start | bytes 393224 | tf_op jit(solution)/shard_map/ppermute | solution.py:580
  13.9 3.0 %collective-permute-start.5 = (f32[256,128]{1,0:T(8,128)S(1)}, f32[256,128]{1,0:T(8,128)S(1)}, u32[]{:S(2)}, u32[]{:S(2)}) collective-permute-start(f32[256,128]{1,0:T(8,128)S(1)} %get-tuple-element.16), channel_id=1, source_target_pairs={{0,0},{1,2},{2,1},{3,3},{4,4},{5,6},{6,5},{7,7},{8,8},{9,10},{10,9... | collective-permute-start | bytes 393224 | tf_op jit(solution)/shard_map/ppermute | solution.py:580
  16.9 1.0 %third.1.rf_third = f32[8,8,128]{2,1,0:T(8,128)S(1)} custom-call(f32[240,128]{1,0:T(8,128)S(1)} %collective-permute-done.2.ro), custom_call_target="tpu_custom_call" | custom-call | flops 1000000000 | bytes 1048576 | tf_op jit(solution)/shard_map/third/pallas_call | solution.py:661
  17.9 0.0 collective-permute-done.4.from_core
  17.9 2.3 %collective-permute-done.5.from_chip = f32[256,128]{1,0:T(8,128)S(1)} collective-permute-done((f32[256,128]{1,0:T(8,128)S(1)}, f32[256,128]{1,0:T(8,128)S(1)}, u32[]{:S(2)}, u32[]{:S(2)}) %collective-permute-start.5) | collective-permute-done | bytes 131104 | tf_op jit(solution)/shard_map/ppermute | solution.py:580
  20.2 5.7 %galerkin.1 = f32[125,1,256]{2,1,0:T(1,128)} custom-call(f32[232,128]{1,0:T(8,128)S(1)} %get-tuple-element.12.own, f32[232,128]{1,0:T(8,128)S(1)} %collective-permute-done.rp, f32[240,128]{1,0:T(8,128)S(1)} %collective-permute-done.2.ro, f32[72,128]{1,0:T(8,128)S(1)} %collective-permute-done.3.rs, f32[256,128]{1,0:T(8,128)S(1)} %collective-permute-done.4.from_core, ...), custom_call_target="tpu_custom_call" | custom-call | tf_op jit(solution)/shard_map/galerkin/pallas_call | solution.py:675
  (1 shorter events, 0.0 us)
Async XLA Ops:
  0.0 4.5 %collective-permute-start.1 = (s32[1,1,512]{2,1,0:T(1,128)}, s32[1,1,512]{2,1,0:T(1,128)S(1)}, u32[]{:S(2)}, u32[]{:S(2)}) collective-permute-start(s32[1,1,512]{2,1,0:T(1,128)} %refs_2_.1), channel_id=1, source_target_pairs={{0,4},{4,0},{8,12},{12,8},{16,20},{20,16},{24,28},{28,24},{1,5},{5... | collective-permute-start | bytes 6152 | tf_op jit(solution)/shard_map/ppermute | solution.py:580
  2.9 5.7 %collective-permute-start = (f32[232,128]{1,0:T(8,128)S(1)}, f32[232,128]{1,0:T(8,128)S(1)}, u32[]{:S(2)}, u32[]{:S(2)}) collective-permute-start(f32[232,128]{1,0:T(8,128)S(1)} %get-tuple-element.12.own), channel_id=1, source_target_pairs={{0,4},{4,0},{8,12},{12,8},{16,20},{20,16},{24,28},{28,24},{1,5},{5... | collective-permute-start | bytes 356360 | tf_op jit(solution)/shard_map/ppermute | solution.py:580
  3.2 5.4 %collective-permute-start.3 = (f32[72,128]{1,0:T(8,128)S(1)}, f32[72,128]{1,0:T(8,128)S(1)}, u32[]{:S(2)}, u32[]{:S(2)}) collective-permute-start(f32[72,128]{1,0:T(8,128)S(1)} %get-tuple-element.13), channel_id=1, source_target_pairs={{0,8},{4,12},{8,16},{12,20},{16,24},{20,28},{24,0},{28,4},{1,9},{5... | collective-permute-start | bytes 110600 | tf_op jit(solution)/shard_map/ppermute | solution.py:580
  4.6 6.5 %collective-permute-start.2 = (f32[240,128]{1,0:T(8,128)S(1)}, f32[240,128]{1,0:T(8,128)S(1)}, u32[]{:S(2)}, u32[]{:S(2)}) collective-permute-start(f32[240,128]{1,0:T(8,128)S(1)} %join.1), channel_id=1, source_target_pairs={{0,0},{4,8},{8,4},{12,16},{16,12},{20,24},{24,20},{28,28},{1,1},{5... | collective-permute-start | bytes 368648 | tf_op jit(solution)/shard_map/ppermute | solution.py:580
  11.2 6.8 %collective-permute-start.4 = (f32[256,128]{1,0:T(8,128)S(1)}, f32[256,128]{1,0:T(8,128)S(1)}, u32[]{:S(2)}, u32[]{:S(2)}) collective-permute-start(f32[256,128]{1,0:T(8,128)S(1)} %get-tuple-element.15), channel_id=1, source_target_pairs={{0,1},{1,0},{2,3},{3,2},{4,5},{5,4},{6,7},{7,6},{8,9},{9,8},{10,11... | collective-permute-start | bytes 393224 | tf_op jit(solution)/shard_map/ppermute | solution.py:580
  13.9 6.3 %collective-permute-start.5 = (f32[256,128]{1,0:T(8,128)S(1)}, f32[256,128]{1,0:T(8,128)S(1)}, u32[]{:S(2)}, u32[]{:S(2)}) collective-permute-start(f32[256,128]{1,0:T(8,128)S(1)} %get-tuple-element.16), channel_id=1, source_target_pairs={{0,0},{1,2},{2,1},{3,3},{4,4},{5,6},{6,5},{7,7},{8,8},{9,10},{10,9... | collective-permute-start | bytes 393224 | tf_op jit(solution)/shard_map/ppermute | solution.py:580

commit v8 on v7

--- a/solution.py
+++ b/solution.py
@@ -230,24 +230,14 @@
     return f2, ft2, dot_nn(one2, ft2), dot_nn(one2, f2)
 
 
-def fault_kernel(own, cells, f2, ft2, rf, far2, hot, both):
+def fault_kernel(own, plane, cells, f2, ft2, rf, plane_out, far2, hot, both):
+    plane_out[...] = plane[...]
     partner, live = slot_columns([partner_rows(cells), own[228:232, :]])
     fill_far(far2, partner, live)
     fill_hot(hot, flat_cells(own[224:228, :]), range(CY))
     both[...] = dot_nn(hot[...], far2[...])
     for y in range(CY):
         f2[y], ft2[y], rf[0, y], rf[1, y] = pair_matrix(both[y * NZ : (y + 1) * NZ, :])
-
-
-def third_kernel(peers, ro, rf, eo, hot, both):
-    ro = Masked(ro, has_other("gx", peers[0]))
-    beyond, live = slot_columns([ro[232:236, :], ro[228:232, :]])
-    fill_tint(eo, beyond, live)
-    fill_hot(hot, flat_cells(ro[224:228, :]), range(CY))
-    both[...] = dot_nn(hot[...], eo[...])
-    for y in range(CY):
-        pieces = jnp.transpose(both[y * NZ : (y + 1) * NZ, :])
-        rf[y] = pieces[:8] + pieces[8:16]
 
 
 def through(value, matrix2):
@@ -260,62 +250,296 @@
     return got[:rows] + got[rows:]
 
 
+class Place:
+    def __init__(self):
+        self.gx = lax.axis_index("gx")
+        self.gy = lax.axis_index("gy")
+        par = lax.rem(self.gx, 2)
+        even = par == 0
+        self.sgn = 1 - 2 * par
+        self.p_own = jnp.where(even, 3, 2)
+        self.p_far = jnp.where(even, 4, 1)
+        self.p_third = jnp.where(even, 0, 5)
+        self.p_fault = (self.p_own, self.p_far, self.p_third)
+        self.x_coarse = lax.rem(self.gx, 5) + 5
+
+    def a_of(self, d):
+        return lax.rem(self.x_coarse + d, 5)
+
+    def b_of(self, coarse_y, d):
+        return lax.rem(self.gy * (CY // 2) + coarse_y + d + 5, 5)
+
+
+def roll_weights(w, wr, first, count):
+    for p in range(7):
+        for o, step in enumerate(FORWARD):
+            if step[2] == 0 or (p == 0 and o < 4):
+                continue
+            at = (p * PER + o) * ROWS + first
+            distance = 1 if step[2] == 1 else NZ - 1
+            wr[at : at + count, :] = pltpu.roll(w[at : at + count, :], distance, 1)
+
+
+def smooth(w, wr, fd, qc, inv, diag, first, count):
+    even_y = (lax.broadcasted_iota(jnp.int32, (count, NZ), 0) & 1) == 0
+    even_z = (lax.broadcasted_iota(jnp.int32, (count, NZ), 1) & 1) == 0
+    for p in range(6):
+        base = p + 1
+
+        def weight(dx, dy, dz):
+            if (dx, dy, dz) in OFFSET:
+                start = (base * PER + OFFSET[dx, dy, dz]) * ROWS + 1 + first
+                return w[start : start + count, :]
+            o = OFFSET[-dx, -dy, -dz]
+            start = ((base + dx) * PER + o) * ROWS + 1 + first + dy
+            return (w if dz == 0 else wr)[start : start + count, :]
+
+        near = 1 if p % 2 == 0 else -1
+        sums = {}
+        for dz in (-1, 0, 1):
+            got = {}
+            for dx in (-1, 0, 1):
+                below, above = weight(dx, -1, dz), weight(dx, 1, dz)
+                got[dx, 0] = jnp.where(even_y, above, below)
+                if (dx, dz) != (0, 0):
+                    got[dx, 0] = got[dx, 0] + weight(dx, 0, dz)
+                got[dx, 1] = jnp.where(even_y, below, above)
+            for sy in range(2):
+                sums[0, sy, dz] = got[0, sy] + got[near, sy]
+                sums[1, sy, dz] = got[-near, sy]
+        start = (base * PER + 13) * ROWS + 1 + first
+        at = p * 16 + first
+        total = w[start : start + count, :] + fd[at : at + count, :]
+        r = []
+        for sx in range(2):
+            for sy in range(2):
+                down, same, up = (sums[sx, sy, dz] for dz in (-1, 0, 1))
+                r.append(same + jnp.where(even_z, up, down))
+                r.append(jnp.where(even_z, down, up))
+        for value in r:
+            total = total + value
+        total = jnp.where(total == 0.0, 1.0, total)
+        scale = damping / total
+        diag[at : at + count, :] = total
+        inv[at : at + count, :] = scale
+        for k, value in enumerate(r):
+            value = value * scale
+            if k == 0:
+                value = value + (1.0 - damping)
+            at = (p * 8 + k) * 16 + first
+            qc[at : at + count, :] = value
+
+
+def spread(here, qc, inv, qe, rf_at, columns, count):
+    z8 = lax.broadcasted_iota(jnp.int32, (8, NZ), 1)
+    e8 = lax.broadcasted_iota(jnp.int32, (8, NZ), 0)
+    beside = jnp.where((z8 & 1) == 0, z8 - 1, z8 + 1)
+    mask_own = jnp.where(e8 == colour(z8), 1.0, 0.0)
+    mask_oth = jnp.where(e8 == colour(beside + 10), 1.0, 0.0)
+    rows5 = jnp.where(e8 < 5, 1.0, 0.0)
+
+    def one(k, carry):
+        c = columns(k)
+        for p in range(6):
+            for lat in range(4):
+                at = (p * 8 + 2 * lat) * 16 + c
+                qe[p, c, lat] = (
+                    qc[pl.ds(at, 1), :] * mask_own + qc[pl.ds(at + 16, 1), :] * mask_oth
+                )
+        for k, plane in enumerate(here.p_fault):
+            qe[plane, c, 2] = qe[plane, c, 2] + rf_at(k, c) * (
+                inv[pl.ds(plane * 16 + c, 1), :] * rows5
+            )
+        return carry
+
+    lax.fori_loop(0, count, one, 0)
+
+
+def apply_column(w, wr, diag, qe, ap, p, y, odd_y):
+    odd_x = p % 2
+    acc = {}
+    for dx in (-1, 0, 1):
+        for dy in (-1, 0, 1):
+            q = [qe[p + dx, y + dy, lat] for lat in range(4)]
+            own_x = dx if (dx == 1 and odd_x) or (dx == -1 and not odd_x) else 0
+            own_y = dy if (dy == 1 and odd_y) or (dy == -1 and not odd_y) else 0
+            oth_x = own_x + (1 if (p + dx) % 2 else -1)
+            oth_y = own_y + (1 if (odd_y + dy) % 2 else -1)
+            for dz in (-1, 0, 1):
+                if (dx, dy, dz) == (0, 0, 0):
+                    continue
+                if (dx, dy, dz) in OFFSET:
+                    at = ((p + 1) * PER + OFFSET[dx, dy, dz]) * ROWS + y + 1
+                    ref = w if dz == 0 else wr
+                else:
+                    at = ((p + 1 + dx) * PER + OFFSET[-dx, -dy, -dz]) * ROWS + y + 1 + dy
+                    ref = w
+                wt = ref[pl.ds(at, 1), :]
+                for lat in range(4):
+                    lx = oth_x if lat >= 2 else own_x
+                    ly = oth_y if lat % 2 else own_y
+                    value = wt * q[lat]
+                    key = (lx, ly, dz)
+                    acc[key] = acc[key] + value if key in acc else value
+    centre = diag[pl.ds(p * 16 + y, 1), :]
+    for lx in (-1, 0, 1):
+        for ly in (-1, 0, 1):
+            total = acc[lx, ly, 0]
+            total = total + pltpu.roll(acc[lx, ly, 1], NZ - 1, 1)
+            total = total + pltpu.roll(acc[lx, ly, -1], 1, 1)
+            own_lat = None
+            sx = {0: 0, (1 if odd_x else -1): 1}.get(lx)
+            sy = {0: 0, (1 if odd_y else -1): 1}.get(ly)
+            if sx is not None and sy is not None:
+                own_lat = 2 * sx + sy
+            if own_lat is None:
+                total = -total
+            else:
+                total = centre * qe[p, y, own_lat] - total
+            ap[p - 1, y - 1, lx + 1, ly + 1] = total
+
+
+def fault_apply(here, qe, ap, c, f2c, ft2c):
+    ly_oth = 2 * (c % 2)
+    for plane, source, x_own, matrix in (
+        (here.p_own, here.p_far, 1 + here.sgn, ft2c),
+        (here.p_far, here.p_own, 1 - here.sgn, f2c),
+    ):
+        total = through(qe[source, c].reshape(32, NZ), matrix)
+        for lat in range(4):
+            lx = 1 if lat >= 2 else x_own
+            ly = ly_oth if lat % 2 else 1
+            ap[plane - 1, c - 1, lx, ly] = ap[plane - 1, c - 1, lx, ly] - total[8 * lat : 8 * lat + 8]
+
+
+def gather(here, qc, ap, tt, coarse_y, rows, add):
+    shift = (-1, 0, 0, 1)
+    for zk in range(2):
+        acc = {}
+        for x in range(-1, 3):
+            for y in rows:
+                lat = 2 * (x not in (0, 1)) + (y not in (0, 1))
+                c = 2 * coarse_y + y + 2
+                at = ((x + 2) * 8 + 2 * lat + zk) * 16 + c
+                q = qc[at : at + 1, :]
+                for lx in range(3):
+                    for ly in range(3):
+                        value = q * ap[x + 1, c - 1, lx, ly]
+                        key = (shift[x + 1] + lx - 1, shift[y + 1] + ly - 1)
+                        acc[key] = acc[key] + value if key in acc else value
+        lane = (coarse_y % 2) * 256 + zk * NZ
+        for (dx, dy), value in acc.items():
+            at = (coarse_y // 2, here.a_of(dx), here.b_of(coarse_y, dy), slice(None), slice(lane, lane + NZ))
+            tt[at] = tt[at] + value if add else value
+
+
+def gather_fault(here, inv, ap, tt, y, ft2c):
+    c = y + 2
+    coarse_y = y // 2
+    lane = (coarse_y % 2) * 256
+    value = ap[here.p_far - 1, c - 1].reshape(72, NZ) * inv[pl.ds(here.p_far * 16 + c, 1), :]
+    total = through(value, ft2c)
+    for lx in range(3):
+        a = here.a_of(lx - 1 + here.sgn)
+        for ly in range(3):
+            at = (coarse_y // 2, a, here.b_of(coarse_y, ly - 1), slice(None), slice(lane, lane + NZ))
+            row = 8 * (3 * lx + ly)
+            tt[at] = tt[at] + total[row : row + 8]
+
+
+INNER = (2, 3, 4, 5)
+
+
+def rows_of(coarse_y, inner):
+    return [y for y in range(-1, 3) if (2 * coarse_y + y in INNER) == inner]
+
+
+def inner_kernel(
+    peers, own, rp, ro, rs, f2, ft2, rf_pair, w, wr, qe, ap, tt, rf_third, qc, inv, diag, fd, eo, hot, both
+):
+    here = Place()
+    ro = Masked(ro, has_other("gx", peers[0]))
+
+    def place(ref, count, first):
+        for k in range(count):
+            base = (first + k) * ROWS
+            w[base + 3 : base + 11, :] = ref[8 * k : 8 * k + 8, :]
+
+    def place_x(odd):
+        lo, hi = (rp, ro) if odd else (ro, rp)
+        place(lo, 28, PER)
+        place(hi, 28, 5 * PER)
+
+    by_parity("gx", place_x)
+    place(Masked(rs, here.gx >= 2), 9, 4)
+    place(own, 28, 3 * PER)
+
+    beyond, live = slot_columns([ro[232:236, :], ro[228:232, :]])
+    fill_tint(eo, beyond, live)
+    fill_hot(hot, flat_cells(ro[224:228, :]), range(CY))
+    both[...] = dot_nn(hot[...], eo[...])
+    fd[...] = jnp.zeros_like(fd)
+    for y in range(CY):
+        pieces = jnp.transpose(both[y * NZ : (y + 1) * NZ, :])
+        rf_third[y] = pieces[:8] + pieces[8:16]
+        for plane, value in zip(here.p_fault, (rf_pair[0, y], rf_pair[1, y], rf_third[y])):
+            fd[pl.ds(plane * 16 + y + 2, 1), :] = value[5:6, :]
+
+    roll_weights(w, wr, 3, 8)
+    smooth(w, wr, fd, qc, inv, diag, 2, 8)
+    spread(
+        here, qc, inv, qe, lambda k, c: rf_third[c - 2] if k == 2 else rf_pair[k, c - 2], lambda k: k + 3, 6
+    )
+
+    def pair(k, carry):
+        for p in range(1, 5):
+            apply_column(w, wr, diag, qe, ap, p, 2 * k + 4, 0)
+            apply_column(w, wr, diag, qe, ap, p, 2 * k + 5, 1)
+        return carry
+
+    lax.fori_loop(0, 2, pair, 0)
+    for y in INNER:
+        fault_apply(here, qe, ap, y + 2, f2[y], ft2[y])
+    tt[...] = jnp.zeros_like(tt)
+    for coarse_y in range(CY // 2):
+        gather(here, qc, ap, tt, coarse_y, rows_of(coarse_y, True), False)
+    for y in INNER:
+        gather_fault(here, inv, ap, tt, y, ft2[y])
+
+
 def main_kernel(
     peers,
-    own,
-    rp,
-    ro,
-    rs,
     from_core,
     from_chip,
     f2,
     ft2,
     rf_pair,
     rf_third,
+    w_in,
+    wr_in,
+    qe_in,
+    ap_in,
+    tt_in,
     out,
     w,
     wr,
+    qe,
+    ap,
+    tt,
     qc,
     inv,
     diag,
     fd,
     rf,
-    qe,
-    ap,
-    tt,
     f2h,
     ft2h,
     far2,
     eo,
     hot,
 ):
-    gx = lax.axis_index("gx")
-    gy = lax.axis_index("gy")
-    ro = Masked(ro, has_other("gx", peers[0]))
+    del w_in, wr_in, qe_in, ap_in, tt_in
+    here = Place()
     from_chip = Masked(from_chip, has_other("gy", peers[1]))
-    par = lax.rem(gx, 2)
-    even = par == 0
-    sgn = 1 - 2 * par
-    p_own = jnp.where(even, 3, 2)
-    p_far = jnp.where(even, 4, 1)
-    p_third = jnp.where(even, 0, 5)
-    p_fault = (p_own, p_far, p_third)
-    z8 = lax.broadcasted_iota(jnp.int32, (8, NZ), 1)
-    e8 = lax.broadcasted_iota(jnp.int32, (8, NZ), 0)
-
-    def place(ref, count, first):
-        for k in range(count):
-            base = (first + k) * ROWS
-            w[base + 3 : base + 11, :] = ref[8 * k : 8 * k + 8, :]
-
-    def place_x(odd):
-        lo, hi = (rp, ro) if odd else (ro, rp)
-        place(lo, 28, PER)
-        place(hi, 28, 5 * PER)
-
-    place(Masked(rs, gx >= 2), 9, 4)
-    place(own, 28, 3 * PER)
-    by_parity("gx", place_x)
 
     def place_y(odd):
         yl, yh = (from_core, from_chip) if odd else (from_chip, from_core)
@@ -332,19 +556,13 @@
                     at += 3
 
     by_parity("gy", place_y)
-    for p in range(7):
-        for o, step in enumerate(FORWARD):
-            if step[2] == 0 or (p == 0 and o < 4):
-                continue
-            base = (p * PER + o) * ROWS
-            shift = 1 if step[2] == 1 else NZ - 1
-            wr[base : base + ROWS, :] = pltpu.roll(w[base : base + ROWS, :], shift, 1)
+    roll_weights(w, wr, 0, 16)
 
     fd[...] = jnp.zeros_like(fd)
 
     def put(column, k, value):
         rf[k, column] = value
-        fd[pl.ds(p_fault[k] * 16 + column, 1), :] = value[5:6, :]
+        fd[pl.ds(here.p_fault[k] * 16 + column, 1), :] = value[5:6, :]
 
     for y in range(CY):
         put(y + 2, 0, rf_pair[0, y])
@@ -352,7 +570,7 @@
         put(y + 2, 2, rf_third[y])
     core_rows = from_core[FAULT_ROW : FAULT_ROW + 24, :]
     chip_rows = from_chip[FAULT_ROW : FAULT_ROW + 24, :]
-    odd_y = lax.rem(gy, 2) == 1
+    odd_y = lax.rem(here.gy, 2) == 1
     for side, first, second, columns in (
         (0, core_rows, chip_rows, ((0, 6), (1, 7))),
         (1, chip_rows, core_rows, ((10, 0), (11, 1))),
@@ -377,187 +595,29 @@
             pieces = jnp.transpose(third[k * NZ : (k + 1) * NZ])
             put(column, 2, pieces[:8] + pieces[8:16])
 
-    r16 = lax.broadcasted_iota(jnp.int32, (16, NZ), 0)
-    z16 = lax.broadcasted_iota(jnp.int32, (16, NZ), 1)
-    even_y = (r16 & 1) == 0
-    even_z = (z16 & 1) == 0
-    for p in range(6):
-        base = p + 1
-
-        def weight(dx, dy, dz):
-            if (dx, dy, dz) in OFFSET:
-                start = (base * PER + OFFSET[dx, dy, dz]) * ROWS + 1
-                return w[start : start + 16, :]
-            o = OFFSET[-dx, -dy, -dz]
-            start = ((base + dx) * PER + o) * ROWS + 1 + dy
-            return (w if dz == 0 else wr)[start : start + 16, :]
-
-        near = 1 if p % 2 == 0 else -1
-        sums = {}
-        for dz in (-1, 0, 1):
-            got = {}
-            for dx in (-1, 0, 1):
-                below, above = weight(dx, -1, dz), weight(dx, 1, dz)
-                got[dx, 0] = jnp.where(even_y, above, below)
-                if (dx, dz) != (0, 0):
-                    got[dx, 0] = got[dx, 0] + weight(dx, 0, dz)
-                got[dx, 1] = jnp.where(even_y, below, above)
-            for sy in range(2):
-                sums[0, sy, dz] = got[0, sy] + got[near, sy]
-                sums[1, sy, dz] = got[-near, sy]
-        total = w[(base * PER + 13) * ROWS + 1 : (base * PER + 13) * ROWS + 17, :]
-        total = total + fd[p * 16 : p * 16 + 16, :]
-        r = []
-        for sx in range(2):
-            for sy in range(2):
-                down, same, up = (sums[sx, sy, dz] for dz in (-1, 0, 1))
-                r.append(same + jnp.where(even_z, up, down))
-                r.append(jnp.where(even_z, down, up))
-        for value in r:
-            total = total + value
-        total = jnp.where(total == 0.0, 1.0, total)
-        scale = damping / total
-        diag[p * 16 : p * 16 + 16, :] = total
-        inv[p * 16 : p * 16 + 16, :] = scale
-        for k, value in enumerate(r):
-            value = value * scale
-            if k == 0:
-                value = value + (1.0 - damping)
-            qc[(p * 8 + k) * 16 : (p * 8 + k) * 16 + 16, :] = value
-
-    beside = jnp.where((z8 & 1) == 0, z8 - 1, z8 + 1)
-    mask_own = jnp.where(e8 == colour(z8), 1.0, 0.0)
-    mask_oth = jnp.where(e8 == colour(beside + 10), 1.0, 0.0)
-    rows5 = jnp.where(e8 < 5, 1.0, 0.0)
-
-    def spread(c, carry):
-        for p in range(6):
-            for lat in range(4):
-                at = (p * 8 + 2 * lat) * 16 + c
-                qe[p, c, lat] = (
-                    qc[pl.ds(at, 1), :] * mask_own + qc[pl.ds(at + 16, 1), :] * mask_oth
-                )
-        for k, plane in enumerate(p_fault):
-            qe[plane, c, 2] = qe[plane, c, 2] + rf[k, c] * (
-                inv[pl.ds(plane * 16 + c, 1), :] * rows5
-            )
+    smooth(w, wr, fd, qc, inv, diag, 0, 16)
+    spread(
+        here, qc, inv, qe, lambda k, c: rf[k, c], lambda k: jnp.where(k < 3, k, k + 6), 6
+    )
+
+    def outer_pair(k, carry):
+        odd_y = 1 + 2 * k + 4 * (k // 2)
+        even_y = 2 + 6 * jnp.minimum(k, 1) + 2 * (k // 2)
+        for p in range(1, 5):
+            apply_column(w, wr, diag, qe, ap, p, odd_y, 1)
+            apply_column(w, wr, diag, qe, ap, p, even_y, 0)
         return carry
 
-    lax.fori_loop(0, 12, spread, 0)
-
-    def apply_column(p, y, odd_y):
-        odd_x = p % 2
-        acc = {}
-        for dx in (-1, 0, 1):
-            for dy in (-1, 0, 1):
-                q = [qe[p + dx, y + dy, lat] for lat in range(4)]
-                own_x = dx if (dx == 1 and odd_x) or (dx == -1 and not odd_x) else 0
-                own_y = dy if (dy == 1 and odd_y) or (dy == -1 and not odd_y) else 0
-                oth_x = own_x + (1 if (p + dx) % 2 else -1)
-                oth_y = own_y + (1 if (odd_y + dy) % 2 else -1)
-                for dz in (-1, 0, 1):
-                    if (dx, dy, dz) == (0, 0, 0):
-                        continue
-                    if (dx, dy, dz) in OFFSET:
-                        at = ((p + 1) * PER + OFFSET[dx, dy, dz]) * ROWS + y + 1
-                        ref = w if dz == 0 else wr
-                    else:
-                        at = ((p + 1 + dx) * PER + OFFSET[-dx, -dy, -dz]) * ROWS + y + 1 + dy
-                        ref = w
-                    wt = ref[pl.ds(at, 1), :]
-                    for lat in range(4):
-                        lx = oth_x if lat >= 2 else own_x
-                        ly = oth_y if lat % 2 else own_y
-                        value = wt * q[lat]
-                        key = (lx, ly, dz)
-                        acc[key] = acc[key] + value if key in acc else value
-        centre = diag[pl.ds(p * 16 + y, 1), :]
-        for lx in (-1, 0, 1):
-            for ly in (-1, 0, 1):
-                total = acc[lx, ly, 0]
-                total = total + pltpu.roll(acc[lx, ly, 1], NZ - 1, 1)
-                total = total + pltpu.roll(acc[lx, ly, -1], 1, 1)
-                own_lat = None
-                sx = {0: 0, (1 if odd_x else -1): 1}.get(lx)
-                sy = {0: 0, (1 if odd_y else -1): 1}.get(ly)
-                if sx is not None and sy is not None:
-                    own_lat = 2 * sx + sy
-                if own_lat is None:
-                    total = -total
-                else:
-                    total = centre * qe[p, y, own_lat] - total
-                ap[p - 1, y - 1, lx + 1, ly + 1] = total
-
-    def apply_pair(k, carry):
-        for p in range(1, 5):
-            apply_column(p, 2 * k + 1, 1)
-            apply_column(p, 2 * k + 2, 0)
-        return carry
-
-    lax.fori_loop(0, 5, apply_pair, 0)
-
-    def fault_apply(c, f2c, ft2c):
-        ly_oth = 2 * (c % 2)
-        for plane, source, x_own, matrix in (
-            (p_own, p_far, 1 + sgn, ft2c),
-            (p_far, p_own, 1 - sgn, f2c),
-        ):
-            total = through(qe[source, c].reshape(32, NZ), matrix)
-            for lat in range(4):
-                lx = 1 if lat >= 2 else x_own
-                ly = ly_oth if lat % 2 else 1
-                ap[plane - 1, c - 1, lx, ly] = ap[plane - 1, c - 1, lx, ly] - total[8 * lat : 8 * lat + 8]
-
-    for y in range(CY):
-        fault_apply(y + 2, f2[y], ft2[y])
-    fault_apply(1, f2h[0], ft2h[0])
-    fault_apply(10, f2h[1], ft2h[1])
-
-    x_coarse = lax.rem(gx, 5) + 5
-    a_of = [lax.rem(x_coarse + d, 5) for d in range(-2, 3)]
-
-    def b_of(coarse_y, d):
-        return lax.rem(gy * (CY // 2) + coarse_y + d + 5, 5)
-
-    def gather(pair, carry):
-        for half in range(2):
-            coarse_y = 2 * pair + half
-            columns = []
-            for x in range(-1, 3):
-                for y in range(-1, 3):
-                    sx = 0 if x in (0, 1) else 1
-                    sy = 0 if y in (0, 1) else 1
-                    columns.append((x, y, 2 * sx + sy, (-1, 0, 0, 1)[x + 1], (-1, 0, 0, 1)[y + 1]))
-            for zk in range(2):
-                acc = {}
-                for x, y, lat, ax, ay in columns:
-                    c = 2 * coarse_y + y + 2
-                    q = qc[pl.ds(((x + 2) * 8 + 2 * lat + zk) * 16 + c, 1), :]
-                    for lx in range(3):
-                        for ly in range(3):
-                            value = q * ap[x + 1, c - 1, lx, ly]
-                            key = (ax + lx - 1, ay + ly - 1)
-                            acc[key] = acc[key] + value if key in acc else value
-                lane = half * 256 + zk * NZ
-                for (dx, dy), value in acc.items():
-                    tt[pair, a_of[dx + 2], b_of(coarse_y, dy), :, lane : lane + NZ] = value
-        return carry
-
-    lax.fori_loop(0, 2, gather, 0)
-
-    for y in range(CY):
-        c = y + 2
-        coarse_y = y // 2
-        lane = (coarse_y % 2) * 256
-        value = ap[p_far - 1, c - 1].reshape(72, NZ) * inv[pl.ds(p_far * 16 + c, 1), :]
-        total = through(value, ft2[y])
-        for lx in range(3):
-            a = lax.rem(x_coarse + lx - 1 + sgn, 5)
-            for ly in range(3):
-                b = b_of(coarse_y, ly - 1)
-                at = 8 * (3 * lx + ly)
-                place_at = tt.at[coarse_y // 2, a, b, :, lane : lane + NZ]
-                place_at[...] = place_at[...] + total[at : at + 8]
+    lax.fori_loop(0, 3, outer_pair, 0)
+    outer = [y for y in range(CY) if y not in INNER]
+    for y in outer:
+        fault_apply(here, qe, ap, y + 2, f2[y], ft2[y])
+    fault_apply(here, qe, ap, 1, f2h[0], ft2h[0])
+    fault_apply(here, qe, ap, 10, f2h[1], ft2h[1])
+    for coarse_y in range(CY // 2):
+        gather(here, qc, ap, tt, coarse_y, rows_of(coarse_y, False), True)
+    for y in outer:
+        gather_fault(here, inv, ap, tt, y, ft2[y])
 
     kz = lax.broadcasted_iota(jnp.int32, (512, NZ), 0)
     kout = lax.broadcasted_iota(jnp.int32, (512, NZ), 1)
@@ -631,14 +691,13 @@
         name="join",
     )(own, cells)
     ro = send(joined, "gx", other_of)
-    rs = send(plane, "gx", ahead_of)
     rp = send(own, "gx", partner_of)
     pieces = sds(CY, 2 * NZ, NZ, dtype=bf16)
-    f2, ft2, rf_pair = pl.pallas_call(
+    f2, ft2, rf_pair, plane = pl.pallas_call(
         fault_kernel,
-        out_shape=(pieces, pieces, sds(2, CY, 8, NZ)),
-        in_specs=[VMEM] * 2,
-        out_specs=(VMEM,) * 3,
+        out_shape=(pieces, pieces, sds(2, CY, 8, NZ), sds(72, NZ)),
+        in_specs=[VMEM] * 3,
+        out_specs=(VMEM,) * 4,
         scratch_shapes=[
             pltpu.VMEM((SLOTS, 2 * NZ), bf16),
             pltpu.VMEM((CY * NZ, SLOTS), bf16),
@@ -647,7 +706,8 @@
         compiler_params=params(16),
         cost_estimate=pl.CostEstimate(flops=2 * 10**9, bytes_accessed=2**21, transcendentals=0),
         name="faults",
-    )(own, cells)
+    )(own, plane, cells)
+    rs = send(plane, "gx", ahead_of)
     to_core, to_chip = pl.pallas_call(
         functools.partial(column_kernel, peers),
         out_shape=(sds(Y_ROWS, NZ), sds(Y_ROWS, NZ)),
@@ -658,45 +718,53 @@
     )(own, rp, ro, rs, cells, rf_pair)
     from_chip = send(to_chip, "gy", other_of)
     from_core = send(to_core, "gy", partner_of)
-    rf_third = pl.pallas_call(
-        functools.partial(third_kernel, peers),
-        out_shape=sds(CY, 8, NZ),
-        in_specs=[VMEM],
-        out_specs=VMEM,
-        scratch_shapes=[
+    work = (
+        sds(7 * PER * ROWS, NZ),
+        sds(7 * PER * ROWS, NZ),
+        sds(6, 12, 4, 8, NZ),
+        sds(4, 10, 3, 3, 8, NZ),
+        sds(2, 5, 5, 8, 512),
+    )
+    fields = [
+        pltpu.VMEM((6 * 8 * 16, NZ), f32),
+        pltpu.VMEM((6 * 16, NZ), f32),
+        pltpu.VMEM((6 * 16, NZ), f32),
+        pltpu.VMEM((6 * 16, NZ), f32),
+    ]
+    *work_in, rf_third = pl.pallas_call(
+        functools.partial(inner_kernel, peers),
+        out_shape=work + (sds(CY, 8, NZ),),
+        in_specs=[VMEM] * 7,
+        out_specs=(VMEM,) * 6,
+        scratch_shapes=fields
+        + [
             pltpu.VMEM((SLOTS, NZ), bf16),
             pltpu.VMEM((CY * NZ, SLOTS), bf16),
             pltpu.VMEM((CY * NZ, NZ), f32),
         ],
         compiler_params=params(16),
-        cost_estimate=pl.CostEstimate(flops=10**9, bytes_accessed=2**20, transcendentals=0),
-        name="third",
-    )(ro)
-    return pl.pallas_call(
+        cost_estimate=pl.CostEstimate(flops=4 * 10**9, bytes_accessed=2**21, transcendentals=0),
+        name="inner",
+    )(own, rp, ro, rs, f2, ft2, rf_pair)
+    result, *_ = pl.pallas_call(
         functools.partial(main_kernel, peers),
-        out_shape=sds(125, 1, 256),
-        in_specs=[VMEM] * 10,
-        out_specs=VMEM,
-        scratch_shapes=[
-            pltpu.VMEM((7 * PER * ROWS, NZ), f32),
-            pltpu.VMEM((7 * PER * ROWS, NZ), f32),
-            pltpu.VMEM((6 * 8 * 16, NZ), f32),
-            pltpu.VMEM((6 * 16, NZ), f32),
-            pltpu.VMEM((6 * 16, NZ), f32),
-            pltpu.VMEM((6 * 16, NZ), f32),
+        out_shape=(sds(125, 1, 256),) + work,
+        in_specs=[VMEM] * 11,
+        out_specs=(VMEM,) * 6,
+        scratch_shapes=fields
+        + [
             pltpu.VMEM((3, 12, 8, NZ), f32),
-            pltpu.VMEM((6, 12, 4, 8, NZ), f32),
-            pltpu.VMEM((4, 10, 3, 3, 8, NZ), f32),
-            pltpu.VMEM((2, 5, 5, 8, 512), f32),
             pltpu.VMEM((2, 2 * NZ, NZ), bf16),
             pltpu.VMEM((2, 2 * NZ, NZ), bf16),
             pltpu.VMEM((2, SLOTS, 2 * NZ), bf16),
             pltpu.VMEM((2, SLOTS, NZ), bf16),
             pltpu.VMEM((2, 2, 2 * NZ, SLOTS), bf16),
         ],
-        compiler_params=params(24),
+        input_output_aliases={6 + k: 1 + k for k in range(5)},
+        compiler_params=params(16),
         name="galerkin",
-    )(own, rp, ro, rs, from_core, from_chip, f2, ft2, rf_pair, rf_third)
+    )(from_core, from_chip, f2, ft2, rf_pair, rf_third, *work_in)
+    return result
 
 
 def solution(mesh):

time: 26.1 us -> 26.9 us (1.031)
  the two profiles are of different devices: /device:TPU:9 before, /device:TPU:1 now
where the time goes in v8:
time: 26.9 us; the launch traced here: 26.7 us
  starting transfers between devices  12.1 us (45%)
  Pallas kernels  9.35 us (35%)
  waiting for transfers between devices  4.54 us (17%)
  between operations  0.73 us (3%)
    ppermute x6, starting transfers between devices, send(): lax.ppermute(value, axis, [(i, target(i, peers)) for i in range(peers)])  12.1 us
    pallas_call x1, Pallas kernels, per_device(): pl.pallas_call(functools.partial(main_kernel, peers), out_shape=(sds(125,...  4.81 us
    ppermute x6, waiting for transfers between devices, send(): lax.ppermute(value, axis, [(i, target(i, peers)) for i in range(peers)])  4.54 us
    pallas_call x1, Pallas kernels, per_device(): pl.pallas_call(functools.partial(inner_kernel, peers), out_shape=work + (...  2.37 us
    pallas_call x1, Pallas kernels, per_device(): pl.pallas_call(functools.partial(pack_kernel, peers), out_shape=(sds(232,...  1.04 us
    pallas_call x1, Pallas kernels, per_device(): pl.pallas_call(fault_kernel, out_shape=(pieces, pieces, sds(2, CY, 8, NZ)...  1.03 us
  transfers between devices with their start and end apart: 6, of which 2 were waited for; matrix products, arithmetic and copies ran while one was open for 0% of the time, Pallas kernels for 17%

profile of v8, /device:TPU:1, one launch (start us, length us, event | category | flops | bytes accessed | tf_op | source)
XLA Modules:
  0.0 26.7 jit_solution(9531073995859705263)
XLA Ops:
  0.0 2.0 %collective-permute-start.1 = (s32[1,1,512]{2,1,0:T(1,128)}, s32[1,1,512]{2,1,0:T(1,128)S(1)}, u32[]{:S(2)}, u32[]{:S(2)}) collective-permute-start(s32[1,1,512]{2,1,0:T(1,128)} %refs_2_.1), channel_id=1, source_target_pairs={{0,4},{4,0},{8,12},{12,8},{16,20},{20,16},{24,28},{28,24},{1,5},{5... | collective-permute-start | bytes 6152 | tf_op jit(solution)/shard_map/ppermute | solution.py:640
  2.7 1.0 %pack.1 = (f32[232,128]{1,0:T(8,128)S(1)}, f32[72,128]{1,0:T(8,128)S(1)}) custom-call(s32[1,1]{1,0:T(1,128)S(6)} %copy.16.count, f32[13,2,1024]{2,1,0:T(2,128)} %refs_0_.1, f32[2,1024]{1,0:T(2,128)} %refs_1_.1, s32[1,1,512]{2,1,0:T(1,128)} %refs_2_.1, f32[1,1,512]{2,1,0:T(1,128)} %refs_3_.1), custom_call_target="tpu_custom_call" | custom-call | tf_op jit(solution)/shard_map/pack/pallas_call | solution.py:675
  3.7 0.1 collective-permute-start
  3.8 0.0 collective-permute-done.1.cells
  3.9 0.7 %collective-permute-start.2 = (f32[240,128]{1,0:T(8,128)S(1)}, f32[240,128]{1,0:T(8,128)S(1)}, u32[]{:S(2)}, u32[]{:S(2)}) collective-permute-start(f32[240,128]{1,0:T(8,128)S(1)} %join.1), channel_id=1, source_target_pairs={{0,0},{4,8},{8,4},{12,16},{16,12},{20,24},{24,20},{28,28},{1,1},{5... | collective-permute-start | bytes 368648 | tf_op jit(solution)/shard_map/ppermute | solution.py:640
  4.5 1.0 %faults.1 = (bf16[8,256,128]{2,1,0:T(8,128)(2,1)S(1)}, bf16[8,256,128]{2,1,0:T(8,128)(2,1)S(1)}, f32[2,8,8,128]{3,2,1,0:T(8,128)S(1)}, f32[72,128]{1,0:T(8,128)S(1)}) custom-call(f32[232,128]{1,0:T(8,128)S(1)} %get-tuple-element.20.own, f32[72,128]{1,0:T(8,128)S(1)} %get-tuple-element.21.plane, s32[1,1,512]{2,1,0:T(1,128)S(1)} %collective-permute-done.1.cells), custom_call_target="tpu_custom_call" | custom-call | flops 2000000000 | bytes 2097152 | tf_op jit(solution)/shard_map/faults/pallas_call | solution.py:696
  5.6 3.9 %collective-permute-start.3 = (f32[72,128]{1,0:T(8,128)S(1)}, f32[72,128]{1,0:T(8,128)S(1)}, u32[]{:S(2)}, u32[]{:S(2)}) collective-permute-start(f32[72,128]{1,0:T(8,128)S(1)} %get-tuple-element.22), channel_id=1, source_target_pairs={{0,8},{4,12},{8,16},{12,20},{16,24},{20,28},{24,0},{28,4},{1,9},{5... | collective-permute-start | bytes 110600 | tf_op jit(solution)/shard_map/ppermute | solution.py:640
  9.5 3.7 %collective-permute-done.3.rs = f32[72,128]{1,0:T(8,128)S(1)} collective-permute-done((f32[72,128]{1,0:T(8,128)S(1)}, f32[72,128]{1,0:T(8,128)S(1)}, u32[]{:S(2)}, u32[]{:S(2)}) %collective-permute-start.3) | collective-permute-done | bytes 36896 | tf_op jit(solution)/shard_map/ppermute | solution.py:640
  13.2 0.0 collective-permute-done.rp
  13.2 0.0 collective-permute-done.2.ro
  13.2 0.1 columns.1
  13.2 2.4 %collective-permute-start.4 = (f32[256,128]{1,0:T(8,128)S(1)}, f32[256,128]{1,0:T(8,128)S(1)}, u32[]{:S(2)}, u32[]{:S(2)}) collective-permute-start(f32[256,128]{1,0:T(8,128)S(1)} %get-tuple-element.24), channel_id=1, source_target_pairs={{0,1},{1,0},{2,3},{3,2},{4,5},{5,4},{6,7},{7,6},{8,9},{9,8},{10,11... | collective-permute-start | bytes 393224 | tf_op jit(solution)/shard_map/ppermute | solution.py:640
  15.6 3.0 %collective-permute-start.5 = (f32[256,128]{1,0:T(8,128)S(1)}, f32[256,128]{1,0:T(8,128)S(1)}, u32[]{:S(2)}, u32[]{:S(2)}) collective-permute-start(f32[256,128]{1,0:T(8,128)S(1)} %get-tuple-element.25), channel_id=1, source_target_pairs={{0,0},{1,2},{2,1},{3,3},{4,4},{5,6},{6,5},{7,7},{8,8},{9,10},{10,9... | collective-permute-start | bytes 393224 | tf_op jit(solution)/shard_map/ppermute | solution.py:640
  18.7 2.4 %inner.1 = (f32[2352,128]{1,0:T(8,128)S(1)}, f32[2352,128]{1,0:T(8,128)S(1)}, f32[6,12,4,8,128]{4,3,2,1,0:T(8,128)S(1)}, f32[4,10,3,3,8,128]{5,4,3,2,1,0:T(8,128...) custom-call(f32[232,128]{1,0:T(8,128)S(1)} %get-tuple-element.20.own, ...), custom_call_target="tpu_custom_call" | custom-call | flops 4000000000 | bytes 2097152 | tf_op jit(solution)/shard_map/inner/pallas_call | solution.py:734
  21.0 0.0 collective-permute-done.4.from_core
  21.1 0.8 %collective-permute-done.5.from_chip = f32[256,128]{1,0:T(8,128)S(1)} collective-permute-done((f32[256,128]{1,0:T(8,128)S(1)}, f32[256,128]{1,0:T(8,128)S(1)}, u32[]{:S(2)}, u32[]{:S(2)}) %collective-permute-start.5) | collective-permute-done | bytes 131104 | tf_op jit(solution)/shard_map/ppermute | solution.py:640
  21.9 4.8 %galerkin.1 = (f32[125,1,256]{2,1,0:T(1,128)}, f32[2352,128]{1,0:T(8,128)S(1)}, f32[2352,128]{1,0:T(8,128)S(1)}, f32[6,12,4,8,128]{4,3,2,1,0:T(8,128)S(1)}, f32[...) custom-call(f32[256,128]{1,0:T(8,128)S(1)} %collective-permute-done., ...), custom_call_target="tpu_custom_call", output_to_operand_aliasing={{1}: (6, {}), {2}: (7, {}), {3}: (8, {}), {4}: (9, {}), {5}... | custom-call | tf_op jit(solution)/shard_map/galerkin/pallas_call | solution.py:749
  (1 shorter events, 0.0 us)
Async XLA Ops:
  0.0 3.8 %collective-permute-start.1 = (s32[1,1,512]{2,1,0:T(1,128)}, s32[1,1,512]{2,1,0:T(1,128)S(1)}, u32[]{:S(2)}, u32[]{:S(2)}) collective-permute-start(s32[1,1,512]{2,1,0:T(1,128)} %refs_2_.1), channel_id=1, source_target_pairs={{0,4},{4,0},{8,12},{12,8},{16,20},{20,16},{24,28},{28,24},{1,5},{5... | collective-permute-start | bytes 6152 | tf_op jit(solution)/shard_map/ppermute | solution.py:640
  3.7 9.4 %collective-permute-start = (f32[232,128]{1,0:T(8,128)S(1)}, f32[232,128]{1,0:T(8,128)S(1)}, u32[]{:S(2)}, u32[]{:S(2)}) collective-permute-start(f32[232,128]{1,0:T(8,128)S(1)} %get-tuple-element.20.own), channel_id=1, source_target_pairs={{0,4},{4,0},{8,12},{12,8},{16,20},{20,16},{24,28},{28,24},{1,5},{5... | collective-permute-start | bytes 356360 | tf_op jit(solution)/shard_map/ppermute | solution.py:640
  3.9 9.3 %collective-permute-start.2 = (f32[240,128]{1,0:T(8,128)S(1)}, f32[240,128]{1,0:T(8,128)S(1)}, u32[]{:S(2)}, u32[]{:S(2)}) collective-permute-start(f32[240,128]{1,0:T(8,128)S(1)} %join.1), channel_id=1, source_target_pairs={{0,0},{4,8},{8,4},{12,16},{16,12},{20,24},{24,20},{28,28},{1,1},{5... | collective-permute-start | bytes 368648 | tf_op jit(solution)/shard_map/ppermute | solution.py:640
  5.6 7.6 %collective-permute-start.3 = (f32[72,128]{1,0:T(8,128)S(1)}, f32[72,128]{1,0:T(8,128)S(1)}, u32[]{:S(2)}, u32[]{:S(2)}) collective-permute-start(f32[72,128]{1,0:T(8,128)S(1)} %get-tuple-element.22), channel_id=1, source_target_pairs={{0,8},{4,12},{8,16},{12,20},{16,24},{20,28},{24,0},{28,4},{1,9},{5... | collective-permute-start | bytes 110600 | tf_op jit(solution)/shard_map/ppermute | solution.py:640
  13.2 7.8 %collective-permute-start.4 = (f32[256,128]{1,0:T(8,128)S(1)}, f32[256,128]{1,0:T(8,128)S(1)}, u32[]{:S(2)}, u32[]{:S(2)}) collective-permute-start(f32[256,128]{1,0:T(8,128)S(1)} %get-tuple-element.24), channel_id=1, source_target_pairs={{0,1},{1,0},{2,3},{3,2},{4,5},{5,4},{6,7},{7,6},{8,9},{9,8},{10,11... | collective-permute-start | bytes 393224 | tf_op jit(solution)/shard_map/ppermute | solution.py:640
  15.6 6.3 %collective-permute-start.5 = (f32[256,128]{1,0:T(8,128)S(1)}, f32[256,128]{1,0:T(8,128)S(1)}, u32[]{:S(2)}, u32[]{:S(2)}) collective-permute-start(f32[256,128]{1,0:T(8,128)S(1)} %get-tuple-element.25), channel_id=1, source_target_pairs={{0,0},{1,2},{2,1},{3,3},{4,4},{5,6},{6,5},{7,7},{8,8},{9,10},{10,9... | collective-permute-start | bytes 393224 | tf_op jit(solution)/shard_map/ppermute | solution.py:640

commit v9 on v8

--- a/solution.py
+++ b/solution.py
@@ -33,10 +33,17 @@
 PER = 14
 COLBLOCK = 93
 THIRD = 2 * COLBLOCK
-FAULT_ROW, Y_ROWS = 232, 256
+FAULT_ROW = 225
+BAND_ROW, SUM_ROW, Y_ROWS = 237, 254, 280
+REACH = 8
+DIAGONALS = 2 * REACH + 1
 
 f32 = jnp.float32
 bf16 = jnp.bfloat16
+
+
+def dot_nt(a, b):
+    return lax.dot_general(a, b, (((1,), (1,)), ((), ())), preferred_element_type=f32)
 
 
 def dot_nn(a, b):
@@ -136,16 +143,9 @@
     return jnp.where(lax.rem(at, 2) == 0, at > 0, at < peers - 1)
 
 
-def column_kernel(peers, own, rp, ro, rs, cells, after, to_core, to_chip):
-    del after
+def column_kernel(peers, own, rp, ro, rs, band, sums, to_core, to_chip):
     ro = Masked(ro, has_other("gx", peers[0]))
     lo2 = Masked(rs, lax.axis_index("gx") >= 2)
-    tile = own[224:232, :]
-    other = ro[224:232, :]
-    parts = (tile[0:4], partner_rows(cells), tile[4:8], other[0:4], ro[232:236, :], other[4:8])
-    for out in (to_core, to_chip):
-        for k, part in enumerate(parts):
-            out[FAULT_ROW + 4 * k : FAULT_ROW + 4 * k + 4, :] = part
 
     def fill(out, lo, hi, first, third, runs):
         for c in range(2):
@@ -163,6 +163,14 @@
                 for o in runs:
                     out[at : at + 3, :] = ref[pl.ds((x * PER + o) * 8 + third, 3, stride=8), :]
                     at += 3
+        for k, start in enumerate((224, 232, 228)):
+            out[FAULT_ROW + 4 * k : FAULT_ROW + 4 * k + 4, :] = ro[start : start + 4, :]
+        out[BAND_ROW : BAND_ROW + DIAGONALS, :] = band[int(first > 0), 0:DIAGONALS, :]
+        for c in range(2):
+            for k in range(2):
+                at = SUM_ROW + (2 * c + k) * 6
+                out[at : at + 6, :] = sums[k, first + c, 0:6, :]
+        out[SUM_ROW + 24 : Y_ROWS, :] = jnp.zeros((Y_ROWS - SUM_ROW - 24, NZ), f32)
 
     def for_x(odd_x):
         lo, hi = (rp, ro) if odd_x else (ro, rp)
@@ -202,14 +210,30 @@
         far2[rows, NZ : 2 * NZ] = jnp.where(match, live[r] - high, 0.0).astype(bf16)
 
 
-def fill_tint(eo, beyond, live):
-    lane = lax.broadcasted_iota(jnp.int32, (NZ, NZ), 1)
-    for r in range(4):
-        tint = colour(beyond[r].astype(jnp.int32) & 127)
-        high = live[r].astype(bf16).astype(f32)
-        value = jnp.where((lane == tint) | (lane == 5), high, 0.0)
-        value = jnp.where((lane == tint + 8) | (lane == 13), live[r] - high, value)
-        eo[r * NZ : (r + 1) * NZ, :] = value.astype(bf16)
+def flat_rows(rows):
+    return jnp.concatenate([rows[r : r + 1] for r in range(4)], axis=1)
+
+
+def colour_sums(hot, beyond, live):
+    e16 = lax.broadcasted_iota(jnp.int32, (16, SLOTS), 0)
+    tint = colour(flat_rows(beyond).astype(jnp.int32) & 127)
+    live = flat_rows(live)
+    high = live.astype(bf16).astype(f32)
+    value = jnp.where((e16 == tint) | (e16 == 5), high, 0.0)
+    value = jnp.where((e16 == tint + 8) | (e16 == 13), live - high, value)
+    got = dot_nt(value.astype(bf16), hot)
+    return got[:8] + got[8:]
+
+
+def diagonals(hot, own, far, live):
+    d24 = lax.broadcasted_iota(jnp.int32, (24, SLOTS), 0)
+    step = (flat_rows(far).astype(jnp.int32) & 127) - (flat_rows(own).astype(jnp.int32) & 127)
+    live = flat_rows(live)
+    high = live.astype(bf16).astype(f32)
+    match = step + REACH == d24
+    both = [jnp.where(match, value, 0.0) for value in (high, live - high)]
+    got = dot_nt(jnp.concatenate(both, axis=0).astype(bf16), hot)
+    return got[:24] + got[24:]
 
 
 def fill_hot(hot, cells, columns):
@@ -230,14 +254,17 @@
     return f2, ft2, dot_nn(one2, ft2), dot_nn(one2, f2)
 
 
-def fault_kernel(own, plane, cells, f2, ft2, rf, plane_out, far2, hot, both):
-    plane_out[...] = plane[...]
+def fault_kernel(own, cells, f2, ft2, rf, band, far2, hot, both):
     partner, live = slot_columns([partner_rows(cells), own[228:232, :]])
     fill_far(far2, partner, live)
     fill_hot(hot, flat_cells(own[224:228, :]), range(CY))
     both[...] = dot_nn(hot[...], far2[...])
     for y in range(CY):
         f2[y], ft2[y], rf[0, y], rf[1, y] = pair_matrix(both[y * NZ : (y + 1) * NZ, :])
+    for k, y in enumerate((0, CY - 1)):
+        band[k] = diagonals(
+            hot[y * NZ : (y + 1) * NZ, :], own[224:228, :], partner_rows(cells), own[228:232, :]
+        )
 
 
 def through(value, matrix2):
@@ -412,6 +439,26 @@
             ap[plane - 1, c - 1, lx, ly] = ap[plane - 1, c - 1, lx, ly] - total[8 * lat : 8 * lat + 8]
 
 
+def fault_apply_band(here, qe, ap, c, band):
+    ly_oth = 2 * (c % 2)
+    to_own, to_far = [0.0] * 4, [0.0] * 4
+    for d in range(DIAGONALS):
+        weight = band[d : d + 1, :]
+        for lat in range(4):
+            ahead = pltpu.roll(qe[here.p_far, c, lat], (REACH - d) % NZ, 1)
+            to_own[lat] = to_own[lat] + weight * ahead
+            back = weight * qe[here.p_own, c, lat]
+            to_far[lat] = to_far[lat] + pltpu.roll(back, (d - REACH) % NZ, 1)
+    for plane, x_own, total in (
+        (here.p_own, 1 + here.sgn, to_own),
+        (here.p_far, 1 - here.sgn, to_far),
+    ):
+        for lat in range(4):
+            lx = 1 if lat >= 2 else x_own
+            ly = ly_oth if lat % 2 else 1
+            ap[plane - 1, c - 1, lx, ly] = ap[plane - 1, c - 1, lx, ly] - total[lat]
+
+
 def gather(here, qc, ap, tt, coarse_y, rows, add):
     shift = (-1, 0, 0, 1)
     for zk in range(2):
@@ -455,7 +502,7 @@
 
 
 def inner_kernel(
-    peers, own, rp, ro, rs, f2, ft2, rf_pair, w, wr, qe, ap, tt, rf_third, qc, inv, diag, fd, eo, hot, both
+    peers, own, rp, ro, rs, f2, ft2, rf_pair, w, wr, qe, ap, tt, rf_third, qc, inv, diag, fd, hot
 ):
     here = Place()
     ro = Masked(ro, has_other("gx", peers[0]))
@@ -474,14 +521,11 @@
     place(Masked(rs, here.gx >= 2), 9, 4)
     place(own, 28, 3 * PER)
 
-    beyond, live = slot_columns([ro[232:236, :], ro[228:232, :]])
-    fill_tint(eo, beyond, live)
     fill_hot(hot, flat_cells(ro[224:228, :]), range(CY))
-    both[...] = dot_nn(hot[...], eo[...])
+    got = colour_sums(hot[...], ro[232:236, :], ro[228:232, :])
     fd[...] = jnp.zeros_like(fd)
     for y in range(CY):
-        pieces = jnp.transpose(both[y * NZ : (y + 1) * NZ, :])
-        rf_third[y] = pieces[:8] + pieces[8:16]
+        rf_third[y] = got[:, y * NZ : (y + 1) * NZ]
         for plane, value in zip(here.p_fault, (rf_pair[0, y], rf_pair[1, y], rf_third[y])):
             fd[pl.ds(plane * 16 + y + 2, 1), :] = value[5:6, :]
 
@@ -531,10 +575,7 @@
     diag,
     fd,
     rf,
-    f2h,
-    ft2h,
-    far2,
-    eo,
+    band,
     hot,
 ):
     del w_in, wr_in, qe_in, ap_in, tt_in
@@ -568,32 +609,25 @@
         put(y + 2, 0, rf_pair[0, y])
         put(y + 2, 1, rf_pair[1, y])
         put(y + 2, 2, rf_third[y])
-    core_rows = from_core[FAULT_ROW : FAULT_ROW + 24, :]
-    chip_rows = from_chip[FAULT_ROW : FAULT_ROW + 24, :]
     odd_y = lax.rem(here.gy, 2) == 1
     for side, first, second, columns in (
-        (0, core_rows, chip_rows, ((0, 6), (1, 7))),
-        (1, chip_rows, core_rows, ((10, 0), (11, 1))),
+        (0, from_core, from_chip, ((0, 6), (1, 7))),
+        (1, from_chip, from_core, ((10, 0), (11, 1))),
     ):
-        rows = jnp.where(odd_y, first, second)
-        cells, far, weight, cells_o, far_o, weight_o = (rows[4 * k : 4 * k + 4] for k in range(6))
-        partner, live, beyond, live_o = slot_columns([far, weight, far_o, weight_o])
-        fill_far(far2.at[side], partner, live)
-        fill_tint(eo.at[side], beyond, live_o)
-        ys = [y for _, y in columns]
-        fill_hot(hot.at[side, 0], flat_cells(cells), ys)
-        fill_hot(hot.at[side, 1], flat_cells(cells_o), ys)
-        pair = dot_nn(hot[side, 0], far2[side])
-        third = dot_nn(hot[side, 1], eo[side])
-        for k, (column, y) in enumerate(columns):
-            near, near_t, at_own, at_far = pair_matrix(pair[k * NZ : (k + 1) * NZ])
-            if column in (1, 10):
-                f2h[side] = near
-                ft2h[side] = near_t
-            put(column, 0, at_own)
-            put(column, 1, at_far)
-            pieces = jnp.transpose(third[k * NZ : (k + 1) * NZ])
-            put(column, 2, pieces[:8] + pieces[8:16])
+
+        def rows(start, count):
+            here_rows = slice(start, start + count)
+            return jnp.where(odd_y, first[here_rows, :], second[here_rows, :])
+
+        band[side, 0:DIAGONALS, :] = rows(BAND_ROW, DIAGONALS)
+        lists = rows(FAULT_ROW, 12)
+        fill_hot(hot.at[side], flat_cells(lists[0:4]), [y for _, y in columns])
+        third = colour_sums(hot[side], lists[4:8], lists[8:12])
+        for c, (column, _) in enumerate(columns):
+            for k in range(2):
+                value = rows(SUM_ROW + (2 * c + k) * 6, 6)
+                put(column, k, jnp.concatenate([value, jnp.zeros((2, NZ), f32)], axis=0))
+            put(column, 2, third[:, c * NZ : (c + 1) * NZ])
 
     smooth(w, wr, fd, qc, inv, diag, 0, 16)
     spread(
@@ -612,8 +646,8 @@
     outer = [y for y in range(CY) if y not in INNER]
     for y in outer:
         fault_apply(here, qe, ap, y + 2, f2[y], ft2[y])
-    fault_apply(here, qe, ap, 1, f2h[0], ft2h[0])
-    fault_apply(here, qe, ap, 10, f2h[1], ft2h[1])
+    fault_apply_band(here, qe, ap, 1, band.at[0])
+    fault_apply_band(here, qe, ap, 10, band.at[1])
     for coarse_y in range(CY // 2):
         gather(here, qc, ap, tt, coarse_y, rows_of(coarse_y, False), True)
     for y in outer:
@@ -682,6 +716,7 @@
         compiler_params=params(16),
         name="pack",
     )(fault_count, *sources)
+    rs = send(plane, "gx", ahead_of)
     joined = pl.pallas_call(
         join_kernel,
         out_shape=sds(240, NZ),
@@ -693,10 +728,10 @@
     ro = send(joined, "gx", other_of)
     rp = send(own, "gx", partner_of)
     pieces = sds(CY, 2 * NZ, NZ, dtype=bf16)
-    f2, ft2, rf_pair, plane = pl.pallas_call(
+    f2, ft2, rf_pair, band = pl.pallas_call(
         fault_kernel,
-        out_shape=(pieces, pieces, sds(2, CY, 8, NZ), sds(72, NZ)),
-        in_specs=[VMEM] * 3,
+        out_shape=(pieces, pieces, sds(2, CY, 8, NZ), sds(2, 24, NZ)),
+        in_specs=[VMEM] * 2,
         out_specs=(VMEM,) * 4,
         scratch_shapes=[
             pltpu.VMEM((SLOTS, 2 * NZ), bf16),
@@ -706,8 +741,7 @@
         compiler_params=params(16),
         cost_estimate=pl.CostEstimate(flops=2 * 10**9, bytes_accessed=2**21, transcendentals=0),
         name="faults",
-    )(own, plane, cells)
-    rs = send(plane, "gx", ahead_of)
+    )(own, cells)
     to_core, to_chip = pl.pallas_call(
         functools.partial(column_kernel, peers),
         out_shape=(sds(Y_ROWS, NZ), sds(Y_ROWS, NZ)),
@@ -715,7 +749,7 @@
         out_specs=(VMEM,) * 2,
         compiler_params=params(16),
         name="columns",
-    )(own, rp, ro, rs, cells, rf_pair)
+    )(own, rp, ro, rs, band, rf_pair)
     from_chip = send(to_chip, "gy", other_of)
     from_core = send(to_core, "gy", partner_of)
     work = (
@@ -736,12 +770,7 @@
         out_shape=work + (sds(CY, 8, NZ),),
         in_specs=[VMEM] * 7,
         out_specs=(VMEM,) * 6,
-        scratch_shapes=fields
-        + [
-            pltpu.VMEM((SLOTS, NZ), bf16),
-            pltpu.VMEM((CY * NZ, SLOTS), bf16),
-            pltpu.VMEM((CY * NZ, NZ), f32),
-        ],
+        scratch_shapes=fields + [pltpu.VMEM((CY * NZ, SLOTS), bf16)],
         compiler_params=params(16),
         cost_estimate=pl.CostEstimate(flops=4 * 10**9, bytes_accessed=2**21, transcendentals=0),
         name="inner",
@@ -754,11 +783,8 @@
         scratch_shapes=fields
         + [
             pltpu.VMEM((3, 12, 8, NZ), f32),
-            pltpu.VMEM((2, 2 * NZ, NZ), bf16),
-            pltpu.VMEM((2, 2 * NZ, NZ), bf16),
-            pltpu.VMEM((2, SLOTS, 2 * NZ), bf16),
-            pltpu.VMEM((2, SLOTS, NZ), bf16),
-            pltpu.VMEM((2, 2, 2 * NZ, SLOTS), bf16),
+            pltpu.VMEM((2, 24, NZ), f32),
+            pltpu.VMEM((2, 2 * NZ, SLOTS), bf16),
         ],
         input_output_aliases={6 + k: 1 + k for k in range(5)},
         compiler_params=params(16),

time: 26.9 us -> 24.1 us (0.90)
  the two profiles are of different devices: /device:TPU:1 before, /device:TPU:9 now
where the time goes in v9:
time: 24.1 us; the launch traced here: 23.9 us
  starting transfers between devices  11.6 us (48%)
  Pallas kernels  7.83 us (32%)
  waiting for transfers between devices  3.75 us (16%)
  between operations  0.72 us (3%)
    ppermute x6, starting transfers between devices, send(): lax.ppermute(value, axis, [(i, target(i, peers)) for i in range(peers)])  11.6 us
    ppermute x6, waiting for transfers between devices, send(): lax.ppermute(value, axis, [(i, target(i, peers)) for i in range(peers)])  3.75 us
    pallas_call x1, Pallas kernels, per_device(): pl.pallas_call(functools.partial(main_kernel, peers), out_shape=(sds(125,...  3.63 us
    pallas_call x1, Pallas kernels, per_device(): pl.pallas_call(functools.partial(inner_kernel, peers), out_shape=work + (...  1.86 us
    pallas_call x1, Pallas kernels, per_device(): pl.pallas_call(fault_kernel, out_shape=(pieces, pieces, sds(2, CY, 8, NZ)...  1.23 us
    pallas_call x1, Pallas kernels, per_device(): pl.pallas_call(functools.partial(pack_kernel, peers), out_shape=(sds(232,...  1.05 us
  transfers between devices with their start and end apart: 6, of which 2 were waited for; matrix products, arithmetic and copies ran while one was open for 0% of the time, Pallas kernels for 17%

profile of v9, /device:TPU:9, one launch (start us, length us, event | category | flops | bytes accessed | tf_op | source)
XLA Modules:
  0.0 23.9 jit_solution(17083342590137679545)
XLA Ops:
  0.0 1.2 %collective-permute-start.1 = (s32[1,1,512]{2,1,0:T(1,128)}, s32[1,1,512]{2,1,0:T(1,128)S(1)}, u32[]{:S(2)}, u32[]{:S(2)}) collective-permute-start(s32[1,1,512]{2,1,0:T(1,128)} %refs_2_.1), channel_id=1, source_target_pairs={{0,4},{4,0},{8,12},{12,8},{16,20},{20,16},{24,28},{28,24},{1,5},{5... | collective-permute-start | bytes 6152 | tf_op jit(solution)/shard_map/ppermute | solution.py:674
  1.9 1.0 %pack.1 = (f32[232,128]{1,0:T(8,128)S(1)}, f32[72,128]{1,0:T(8,128)S(1)}) custom-call(s32[1,1]{1,0:T(1,128)S(6)} %copy.16.count, f32[13,2,1024]{2,1,0:T(2,128)} %refs_0_.1, f32[2,1024]{1,0:T(2,128)} %refs_1_.1, s32[1,1,512]{2,1,0:T(1,128)} %refs_2_.1, f32[1,1,512]{2,1,0:T(1,128)} %refs_3_.1), custom_call_target="tpu_custom_call" | custom-call | tf_op jit(solution)/shard_map/pack/pallas_call | solution.py:709
  2.9 1.3 %collective-permute-start.3 = (f32[72,128]{1,0:T(8,128)S(1)}, f32[72,128]{1,0:T(8,128)S(1)}, u32[]{:S(2)}, u32[]{:S(2)}) collective-permute-start(f32[72,128]{1,0:T(8,128)S(1)} %get-tuple-element.21), channel_id=1, source_target_pairs={{0,8},{4,12},{8,16},{12,20},{16,24},{20,28},{24,0},{28,4},{1,9},{5... | collective-permute-start | bytes 110600 | tf_op jit(solution)/shard_map/ppermute | solution.py:674
  4.3 0.3 %collective-permute-start = (f32[232,128]{1,0:T(8,128)S(1)}, f32[232,128]{1,0:T(8,128)S(1)}, u32[]{:S(2)}, u32[]{:S(2)}) collective-permute-start(f32[232,128]{1,0:T(8,128)S(1)} %get-tuple-element.20.own), channel_id=1, source_target_pairs={{0,4},{4,0},{8,12},{12,8},{16,20},{20,16},{24,28},{28,24},{1,5},{5... | collective-permute-start | bytes 356360 | tf_op jit(solution)/shard_map/ppermute | solution.py:674
  4.5 0.0 collective-permute-done.1.cells
  4.5 3.0 %collective-permute-start.2 = (f32[240,128]{1,0:T(8,128)S(1)}, f32[240,128]{1,0:T(8,128)S(1)}, u32[]{:S(2)}, u32[]{:S(2)}) collective-permute-start(f32[240,128]{1,0:T(8,128)S(1)} %join.1), channel_id=1, source_target_pairs={{0,0},{4,8},{8,4},{12,16},{16,12},{20,24},{24,20},{28,28},{1,1},{5... | collective-permute-start | bytes 368648 | tf_op jit(solution)/shard_map/ppermute | solution.py:674
  7.6 1.2 %faults.1 = (bf16[8,256,128]{2,1,0:T(8,128)(2,1)S(1)}, bf16[8,256,128]{2,1,0:T(8,128)(2,1)S(1)}, f32[2,8,8,128]{3,2,1,0:T(8,128)S(1)}, f32[2,24,128]{2,1,0:T(8,128)S(1)}) custom-call(f32[232,128]{1,0:T(8,128)S(1)} %get-tuple-element.20.own, s32[1,1,512]{2,1,0:T(1,128)S(1)} %collective-permute-done.1.cells), custom_call_target="tpu_custom_call" | custom-call | flops 2000000000 | bytes 2097152 | tf_op jit(solution)/shard_map/faults/pallas_call | solution.py:731
  8.8 0.0 collective-permute-done.3.rs
  8.8 0.0 collective-permute-done.rp
  8.8 2.2 %collective-permute-done.2.ro = f32[240,128]{1,0:T(8,128)S(1)} collective-permute-done((f32[240,128]{1,0:T(8,128)S(1)}, f32[240,128]{1,0:T(8,128)S(1)}, u32[]{:S(2)}, u32[]{:S(2)}) %collective-permute-start.2) | collective-permute-done | bytes 122912 | tf_op jit(solution)/shard_map/ppermute | solution.py:674
  11.1 0.1 columns.1
  11.1 2.7 %collective-permute-start.4 = (f32[280,128]{1,0:T(8,128)S(1)}, f32[280,128]{1,0:T(8,128)S(1)}, u32[]{:S(2)}, u32[]{:S(2)}) collective-permute-start(f32[280,128]{1,0:T(8,128)S(1)} %get-tuple-element.24), channel_id=1, source_target_pairs={{0,1},{1,0},{2,3},{3,2},{4,5},{5,4},{6,7},{7,6},{8,9},{9,8},{10,11... | collective-permute-start | bytes 430088 | tf_op jit(solution)/shard_map/ppermute | solution.py:674
  13.9 3.0 %collective-permute-start.5 = (f32[280,128]{1,0:T(8,128)S(1)}, f32[280,128]{1,0:T(8,128)S(1)}, u32[]{:S(2)}, u32[]{:S(2)}) collective-permute-start(f32[280,128]{1,0:T(8,128)S(1)} %get-tuple-element.25), channel_id=1, source_target_pairs={{0,0},{1,2},{2,1},{3,3},{4,4},{5,6},{6,5},{7,7},{8,8},{9,10},{10,9... | collective-permute-start | bytes 430088 | tf_op jit(solution)/shard_map/ppermute | solution.py:674
  16.9 1.9 %inner.1 = (f32[2352,128]{1,0:T(8,128)S(1)}, f32[2352,128]{1,0:T(8,128)S(1)}, f32[6,12,4,8,128]{4,3,2,1,0:T(8,128)S(1)}, f32[4,10,3,3,8,128]{5,4,3,2,1,0:T(8,128...) custom-call(f32[232,128]{1,0:T(8,128)S(1)} %get-tuple-element.20.own, ...), custom_call_target="tpu_custom_call" | custom-call | flops 4000000000 | bytes 2097152 | tf_op jit(solution)/shard_map/inner/pallas_call | solution.py:768
  18.8 0.0 collective-permute-done.4.from_core
  18.8 1.5 %collective-permute-done.5.from_chip = f32[280,128]{1,0:T(8,128)S(1)} collective-permute-done((f32[280,128]{1,0:T(8,128)S(1)}, f32[280,128]{1,0:T(8,128)S(1)}, u32[]{:S(2)}, u32[]{:S(2)}) %collective-permute-start.5) | collective-permute-done | bytes 143392 | tf_op jit(solution)/shard_map/ppermute | solution.py:674
  20.3 3.6 %galerkin.1 = (f32[125,1,256]{2,1,0:T(1,128)}, f32[2352,128]{1,0:T(8,128)S(1)}, f32[2352,128]{1,0:T(8,128)S(1)}, f32[6,12,4,8,128]{4,3,2,1,0:T(8,128)S(1)}, f32[...) custom-call(f32[280,128]{1,0:T(8,128)S(1)} %collective-permute-done., ...), custom_call_target="tpu_custom_call", output_to_operand_aliasing={{1}: (6, {}), {2}: (7, {}), {3}: (8, {}), {4}: (9, {}), {5}... | custom-call | tf_op jit(solution)/shard_map/galerkin/pallas_call | solution.py:778
  (1 shorter events, 0.0 us)
Async XLA Ops:
  0.0 4.5 %collective-permute-start.1 = (s32[1,1,512]{2,1,0:T(1,128)}, s32[1,1,512]{2,1,0:T(1,128)S(1)}, u32[]{:S(2)}, u32[]{:S(2)}) collective-permute-start(s32[1,1,512]{2,1,0:T(1,128)} %refs_2_.1), channel_id=1, source_target_pairs={{0,4},{4,0},{8,12},{12,8},{16,20},{20,16},{24,28},{28,24},{1,5},{5... | collective-permute-start | bytes 6152 | tf_op jit(solution)/shard_map/ppermute | solution.py:674
  2.9 5.9 %collective-permute-start.3 = (f32[72,128]{1,0:T(8,128)S(1)}, f32[72,128]{1,0:T(8,128)S(1)}, u32[]{:S(2)}, u32[]{:S(2)}) collective-permute-start(f32[72,128]{1,0:T(8,128)S(1)} %get-tuple-element.21), channel_id=1, source_target_pairs={{0,8},{4,12},{8,16},{12,20},{16,24},{20,28},{24,0},{28,4},{1,9},{5... | collective-permute-start | bytes 110600 | tf_op jit(solution)/shard_map/ppermute | solution.py:674
  4.3 4.6 %collective-permute-start = (f32[232,128]{1,0:T(8,128)S(1)}, f32[232,128]{1,0:T(8,128)S(1)}, u32[]{:S(2)}, u32[]{:S(2)}) collective-permute-start(f32[232,128]{1,0:T(8,128)S(1)} %get-tuple-element.20.own), channel_id=1, source_target_pairs={{0,4},{4,0},{8,12},{12,8},{16,20},{20,16},{24,28},{28,24},{1,5},{5... | collective-permute-start | bytes 356360 | tf_op jit(solution)/shard_map/ppermute | solution.py:674
  4.5 6.5 %collective-permute-start.2 = (f32[240,128]{1,0:T(8,128)S(1)}, f32[240,128]{1,0:T(8,128)S(1)}, u32[]{:S(2)}, u32[]{:S(2)}) collective-permute-start(f32[240,128]{1,0:T(8,128)S(1)} %join.1), channel_id=1, source_target_pairs={{0,0},{4,8},{8,4},{12,16},{16,12},{20,24},{24,20},{28,28},{1,1},{5... | collective-permute-start | bytes 368648 | tf_op jit(solution)/shard_map/ppermute | solution.py:674
  11.1 7.7 %collective-permute-start.4 = (f32[280,128]{1,0:T(8,128)S(1)}, f32[280,128]{1,0:T(8,128)S(1)}, u32[]{:S(2)}, u32[]{:S(2)}) collective-permute-start(f32[280,128]{1,0:T(8,128)S(1)} %get-tuple-element.24), channel_id=1, source_target_pairs={{0,1},{1,0},{2,3},{3,2},{4,5},{5,4},{6,7},{7,6},{8,9},{9,8},{10,11... | collective-permute-start | bytes 430088 | tf_op jit(solution)/shard_map/ppermute | solution.py:674
  13.9 6.4 %collective-permute-start.5 = (f32[280,128]{1,0:T(8,128)S(1)}, f32[280,128]{1,0:T(8,128)S(1)}, u32[]{:S(2)}, u32[]{:S(2)}) collective-permute-start(f32[280,128]{1,0:T(8,128)S(1)} %get-tuple-element.25), channel_id=1, source_target_pairs={{0,0},{1,2},{2,1},{3,3},{4,4},{5,6},{6,5},{7,7},{8,8},{9,10},{10,9... | collective-permute-start | bytes 430088 | tf_op jit(solution)/shard_map/ppermute | solution.py:674

commit v10 on v9

--- a/solution.py
+++ b/solution.py
@@ -382,15 +382,14 @@
     lax.fori_loop(0, count, one, 0)
 
 
-def apply_column(w, wr, diag, qe, ap, p, y, odd_y):
-    odd_x = p % 2
+def apply_column(w, wr, diag, qe, ap, p, y, odd_x, odd_y):
     acc = {}
     for dx in (-1, 0, 1):
         for dy in (-1, 0, 1):
             q = [qe[p + dx, y + dy, lat] for lat in range(4)]
             own_x = dx if (dx == 1 and odd_x) or (dx == -1 and not odd_x) else 0
             own_y = dy if (dy == 1 and odd_y) or (dy == -1 and not odd_y) else 0
-            oth_x = own_x + (1 if (p + dx) % 2 else -1)
+            oth_x = own_x + (1 if (odd_x + dx) % 2 else -1)
             oth_y = own_y + (1 if (odd_y + dy) % 2 else -1)
             for dz in (-1, 0, 1):
                 if (dx, dy, dz) == (0, 0, 0):
@@ -537,8 +536,8 @@
 
     def pair(k, carry):
         for p in range(1, 5):
-            apply_column(w, wr, diag, qe, ap, p, 2 * k + 4, 0)
-            apply_column(w, wr, diag, qe, ap, p, 2 * k + 5, 1)
+            apply_column(w, wr, diag, qe, ap, p, 2 * k + 4, p % 2, 0)
+            apply_column(w, wr, diag, qe, ap, p, 2 * k + 5, p % 2, 1)
         return carry
 
     lax.fori_loop(0, 2, pair, 0)
@@ -551,107 +550,91 @@
         gather_fault(here, inv, ap, tt, y, ft2[y])
 
 
-def main_kernel(
-    peers,
-    from_core,
-    from_chip,
-    f2,
-    ft2,
-    rf_pair,
-    rf_third,
-    w_in,
-    wr_in,
-    qe_in,
-    ap_in,
-    tt_in,
-    out,
-    w,
-    wr,
-    qe,
-    ap,
-    tt,
-    qc,
-    inv,
-    diag,
-    fd,
-    rf,
-    band,
-    hot,
-):
-    del w_in, wr_in, qe_in, ap_in, tt_in
+def side(high, halo, f2, ft2, rf_pair, rf_third, work, fields, rf, band, hot):
     here = Place()
-    from_chip = Masked(from_chip, has_other("gy", peers[1]))
-
-    def place_y(odd):
-        yl, yh = (from_core, from_chip) if odd else (from_chip, from_core)
-        for ref, row, third, runs in ((yl, 1, 0, (1, 10)), (yh, 11, 13, (4,))):
-            for c in range(2):
-                base = c * COLBLOCK
-                w[pl.ds(4 * ROWS + row + c, 9, stride=ROWS), :] = ref[base : base + 9, :]
-                w[pl.ds(PER * ROWS + row + c, 84, stride=ROWS), :] = ref[base + 9 : base + 93, :]
-            at = THIRD
-            for plane in range(7):
-                for o in runs[-1:] if plane == 0 else runs:
-                    start = (plane * PER + o) * ROWS + third
-                    w[pl.ds(start, 3, stride=ROWS), :] = ref[at : at + 3, :]
-                    at += 3
-
-    by_parity("gy", place_y)
-    roll_weights(w, wr, 0, 16)
+    w, wr, qe, ap, tt = work
+    qc, inv, diag, fd = fields
+    first = 6 if high else 0
+    columns = (10, 11) if high else (0, 1)
+    row, third, runs = (11, 13, (4,)) if high else (1, 0, (1, 10))
+
+    for c in range(2):
+        base = c * COLBLOCK
+        w[pl.ds(4 * ROWS + row + c, 9, stride=ROWS), :] = halo[base : base + 9, :]
+        w[pl.ds(PER * ROWS + row + c, 84, stride=ROWS), :] = halo[base + 9 : base + 93, :]
+    at = THIRD
+    for plane in range(7):
+        for o in runs[-1:] if plane == 0 else runs:
+            start = (plane * PER + o) * ROWS + third
+            w[pl.ds(start, 3, stride=ROWS), :] = halo[at : at + 3, :]
+            at += 3
+    roll_weights(w, wr, 8 if high else 0, 8)
 
     fd[...] = jnp.zeros_like(fd)
 
     def put(column, k, value):
-        rf[k, column] = value
+        rf[k, column - first] = value
         fd[pl.ds(here.p_fault[k] * 16 + column, 1), :] = value[5:6, :]
 
-    for y in range(CY):
-        put(y + 2, 0, rf_pair[0, y])
-        put(y + 2, 1, rf_pair[1, y])
-        put(y + 2, 2, rf_third[y])
-    odd_y = lax.rem(here.gy, 2) == 1
-    for side, first, second, columns in (
-        (0, from_core, from_chip, ((0, 6), (1, 7))),
-        (1, from_chip, from_core, ((10, 0), (11, 1))),
-    ):
-
-        def rows(start, count):
-            here_rows = slice(start, start + count)
-            return jnp.where(odd_y, first[here_rows, :], second[here_rows, :])
-
-        band[side, 0:DIAGONALS, :] = rows(BAND_ROW, DIAGONALS)
-        lists = rows(FAULT_ROW, 12)
-        fill_hot(hot.at[side], flat_cells(lists[0:4]), [y for _, y in columns])
-        third = colour_sums(hot[side], lists[4:8], lists[8:12])
-        for c, (column, _) in enumerate(columns):
-            for k in range(2):
-                value = rows(SUM_ROW + (2 * c + k) * 6, 6)
-                put(column, k, jnp.concatenate([value, jnp.zeros((2, NZ), f32)], axis=0))
-            put(column, 2, third[:, c * NZ : (c + 1) * NZ])
-
-    smooth(w, wr, fd, qc, inv, diag, 0, 16)
+    for column in range(first, first + 8):
+        y = column - 2
+        if 0 <= y < CY:
+            put(column, 0, rf_pair[0, y])
+            put(column, 1, rf_pair[1, y])
+            put(column, 2, rf_third[y])
+    band[0:DIAGONALS, :] = halo[BAND_ROW : BAND_ROW + DIAGONALS, :]
+    lists = halo[FAULT_ROW : FAULT_ROW + 12, :]
+    fill_hot(hot, flat_cells(lists[0:4]), (0, 1) if high else (CY - 2, CY - 1))
+    got = colour_sums(hot[...], lists[4:8], lists[8:12])
+    for c, column in enumerate(columns):
+        for k in range(2):
+            at = SUM_ROW + (2 * c + k) * 6
+            value = halo[at : at + 6, :]
+            put(column, k, jnp.concatenate([value, jnp.zeros((2, NZ), f32)], axis=0))
+        put(column, 2, got[:, c * NZ : (c + 1) * NZ])
+
+    smooth(w, wr, fd, qc, inv, diag, first, 8)
     spread(
-        here, qc, inv, qe, lambda k, c: rf[k, c], lambda k: jnp.where(k < 3, k, k + 6), 6
+        here, qc, inv, qe, lambda k, c: rf[k, c - first], lambda k: k + (9 if high else 0), 3
     )
 
-    def outer_pair(k, carry):
-        odd_y = 1 + 2 * k + 4 * (k // 2)
-        even_y = 2 + 6 * jnp.minimum(k, 1) + 2 * (k // 2)
-        for p in range(1, 5):
-            apply_column(w, wr, diag, qe, ap, p, odd_y, 1)
-            apply_column(w, wr, diag, qe, ap, p, even_y, 0)
+    def planes(k, carry):
+        for odd_x in (1, 0):
+            p = 2 * k + 2 - odd_x
+            for y in (8, 9, 10) if high else (1, 2, 3):
+                apply_column(w, wr, diag, qe, ap, p, y, odd_x, y % 2)
         return carry
 
-    lax.fori_loop(0, 3, outer_pair, 0)
-    outer = [y for y in range(CY) if y not in INNER]
-    for y in outer:
+    lax.fori_loop(0, 2, planes, 0)
+    own = (6, 7) if high else (0, 1)
+    for y in own:
         fault_apply(here, qe, ap, y + 2, f2[y], ft2[y])
-    fault_apply_band(here, qe, ap, 1, band.at[0])
-    fault_apply_band(here, qe, ap, 10, band.at[1])
-    for coarse_y in range(CY // 2):
-        gather(here, qc, ap, tt, coarse_y, rows_of(coarse_y, False), True)
-    for y in outer:
+    fault_apply_band(here, qe, ap, 10 if high else 1, band)
+    parts = ((3, (0, 1, 2)), (2, (2,))) if high else ((0, (-1, 0, 1)), (1, (-1,)))
+    for coarse_y, rows in parts:
+        gather(here, qc, ap, tt, coarse_y, rows, True)
+    for y in own:
         gather_fault(here, inv, ap, tt, y, ft2[y])
+
+
+def core_kernel(halo, f2, ft2, rf_pair, rf_third, *refs):
+    work, fields, rest = refs[5:10], refs[10:14], refs[14:]
+
+    def body(odd):
+        side(not odd, halo, f2, ft2, rf_pair, rf_third, work, fields, *rest)
+
+    by_parity("gy", body)
+
+
+def main_kernel(peers, halo, f2, ft2, rf_pair, rf_third, *refs):
+    out, work, fields, rest = refs[5], refs[6:11], refs[11:15], refs[15:]
+    halo = Masked(halo, has_other("gy", peers[1]))
+
+    def body(odd):
+        side(odd, halo, f2, ft2, rf_pair, rf_third, work, fields, *rest)
+
+    by_parity("gy", body)
+    tt = work[4]
 
     kz = lax.broadcasted_iota(jnp.int32, (512, NZ), 0)
     kout = lax.broadcasted_iota(jnp.int32, (512, NZ), 1)
@@ -775,21 +758,32 @@
         cost_estimate=pl.CostEstimate(flops=4 * 10**9, bytes_accessed=2**21, transcendentals=0),
         name="inner",
     )(own, rp, ro, rs, f2, ft2, rf_pair)
+    side_scratch = fields + [
+        pltpu.VMEM((3, 8, 8, NZ), f32),
+        pltpu.VMEM((24, NZ), f32),
+        pltpu.VMEM((2 * NZ, SLOTS), bf16),
+    ]
+    work_in = pl.pallas_call(
+        core_kernel,
+        out_shape=work,
+        in_specs=[VMEM] * 10,
+        out_specs=(VMEM,) * 5,
+        scratch_shapes=side_scratch,
+        input_output_aliases={5 + k: k for k in range(5)},
+        compiler_params=params(16),
+        cost_estimate=pl.CostEstimate(flops=2 * 10**9, bytes_accessed=2**20, transcendentals=0),
+        name="core_side",
+    )(from_core, f2, ft2, rf_pair, rf_third, *work_in)
     result, *_ = pl.pallas_call(
         functools.partial(main_kernel, peers),
         out_shape=(sds(125, 1, 256),) + work,
-        in_specs=[VMEM] * 11,
+        in_specs=[VMEM] * 10,
         out_specs=(VMEM,) * 6,
-        scratch_shapes=fields
-        + [
-            pltpu.VMEM((3, 12, 8, NZ), f32),
-            pltpu.VMEM((2, 24, NZ), f32),
-            pltpu.VMEM((2, 2 * NZ, SLOTS), bf16),
-        ],
-        input_output_aliases={6 + k: 1 + k for k in range(5)},
+        scratch_shapes=side_scratch,
+        input_output_aliases={5 + k: 1 + k for k in range(5)},
         compiler_params=params(16),
-        name="galerkin",
-    )(from_core, from_chip, f2, ft2, rf_pair, rf_third, *work_in)
+        name="chip_side",
+    )(from_chip, f2, ft2, rf_pair, rf_third, *work_in)
     return result
 
 

time: 24.1 us -> 23 us (0.954)
  waiting for transfers between devices: 3.75 us -> 2.27 us
  Pallas kernels: 7.83 us -> 8.2 us
    ppermute x6, waiting for transfers between devices: 3.75 us -> 2.27 us  [send(): lax.ppermute(value, axis, [(i, target(i, peers)) for i in range(peers)])]
    pallas_call x0 -> x1, Pallas kernels: none -> 1.43 us  [per_device(): pl.pallas_call(core_kernel, out_shape=work, in_specs=[VMEM] * 10, out_spe...]
    pallas_call x1, Pallas kernels: 3.63 us -> 2.59 us  [per_device(): pl.pallas_call(functools.partial(main_kernel, peers), out_shape=(sds(125,...]
  transfers between devices with their start and end apart: 6 -> 6, of which waited for: 2 -> 1; matrix products, arithmetic and copies ran while one was open for 0% -> 0% of each run, Pallas kernels for 17% -> 24%
where the time goes in v10:
time: 23 us; the launch traced here: 22.8 us
  starting transfers between devices  11.6 us (50%)
  Pallas kernels  8.2 us (36%)
  waiting for transfers between devices  2.27 us (10%)
  between operations  0.74 us (3%)
    ppermute x6, starting transfers between devices, send(): lax.ppermute(value, axis, [(i, target(i, peers)) for i in range(peers)])  11.6 us
    pallas_call x1, Pallas kernels, per_device(): pl.pallas_call(functools.partial(main_kernel, peers), out_shape=(sds(125,...  2.59 us
    ppermute x6, waiting for transfers between devices, send(): lax.ppermute(value, axis, [(i, target(i, peers)) for i in range(peers)])  2.27 us
    pallas_call x1, Pallas kernels, per_device(): pl.pallas_call(functools.partial(inner_kernel, peers), out_shape=work + (...  1.84 us
    pallas_call x1, Pallas kernels, per_device(): pl.pallas_call(core_kernel, out_shape=work, in_specs=[VMEM] * 10, out_spe...  1.43 us
    pallas_call x1, Pallas kernels, per_device(): pl.pallas_call(fault_kernel, out_shape=(pieces, pieces, sds(2, CY, 8, NZ)...  1.23 us
    pallas_call x1, Pallas kernels, per_device(): pl.pallas_call(functools.partial(pack_kernel, peers), out_shape=(sds(232,...  1.05 us
  transfers between devices with their start and end apart: 6, of which 1 were waited for; matrix products, arithmetic and copies ran while one was open for 0% of the time, Pallas kernels for 24%

profile of v10, /device:TPU:9, one launch (start us, length us, event | category | flops | bytes accessed | tf_op | source)
XLA Modules:
  0.0 22.8 jit_solution(1688531192803014567)
XLA Ops:
  0.0 1.2 %collective-permute-start.1 = (s32[1,1,512]{2,1,0:T(1,128)}, s32[1,1,512]{2,1,0:T(1,128)S(1)}, u32[]{:S(2)}, u32[]{:S(2)}) collective-permute-start(s32[1,1,512]{2,1,0:T(1,128)} %refs_2_.1), channel_id=1, source_target_pairs={{0,4},{4,0},{8,12},{12,8},{16,20},{20,16},{24,28},{28,24},{1,5},{5... | collective-permute-start | bytes 6152 | tf_op jit(solution)/shard_map/ppermute | solution.py:657
  1.9 1.0 %pack.1 = (f32[232,128]{1,0:T(8,128)S(1)}, f32[72,128]{1,0:T(8,128)S(1)}) custom-call(s32[1,1]{1,0:T(1,128)S(6)} %copy.26.count, f32[13,2,1024]{2,1,0:T(2,128)} %refs_0_.1, f32[2,1024]{1,0:T(2,128)} %refs_1_.1, s32[1,1,512]{2,1,0:T(1,128)} %refs_2_.1, f32[1,1,512]{2,1,0:T(1,128)} %refs_3_.1), custom_call_target="tpu_custom_call" | custom-call | tf_op jit(solution)/shard_map/pack/pallas_call | solution.py:692
  2.9 1.3 %collective-permute-start.3 = (f32[72,128]{1,0:T(8,128)S(1)}, f32[72,128]{1,0:T(8,128)S(1)}, u32[]{:S(2)}, u32[]{:S(2)}) collective-permute-start(f32[72,128]{1,0:T(8,128)S(1)} %get-tuple-element.26), channel_id=1, source_target_pairs={{0,8},{4,12},{8,16},{12,20},{16,24},{20,28},{24,0},{28,4},{1,9},{5... | collective-permute-start | bytes 110600 | tf_op jit(solution)/shard_map/ppermute | solution.py:657
  4.3 0.3 %collective-permute-start = (f32[232,128]{1,0:T(8,128)S(1)}, f32[232,128]{1,0:T(8,128)S(1)}, u32[]{:S(2)}, u32[]{:S(2)}) collective-permute-start(f32[232,128]{1,0:T(8,128)S(1)} %get-tuple-element.25.own), channel_id=1, source_target_pairs={{0,4},{4,0},{8,12},{12,8},{16,20},{20,16},{24,28},{28,24},{1,5},{5... | collective-permute-start | bytes 356360 | tf_op jit(solution)/shard_map/ppermute | solution.py:657
  4.5 0.0 collective-permute-done.1.cells
  4.5 3.0 %collective-permute-start.2 = (f32[240,128]{1,0:T(8,128)S(1)}, f32[240,128]{1,0:T(8,128)S(1)}, u32[]{:S(2)}, u32[]{:S(2)}) collective-permute-start(f32[240,128]{1,0:T(8,128)S(1)} %join.1), channel_id=1, source_target_pairs={{0,0},{4,8},{8,4},{12,16},{16,12},{20,24},{24,20},{28,28},{1,1},{5... | collective-permute-start | bytes 368648 | tf_op jit(solution)/shard_map/ppermute | solution.py:657
  7.6 1.2 %faults.1 = (bf16[8,256,128]{2,1,0:T(8,128)(2,1)S(1)}, bf16[8,256,128]{2,1,0:T(8,128)(2,1)S(1)}, f32[2,8,8,128]{3,2,1,0:T(8,128)S(1)}, f32[2,24,128]{2,1,0:T(8,128)S(1)}) custom-call(f32[232,128]{1,0:T(8,128)S(1)} %get-tuple-element.25.own, s32[1,1,512]{2,1,0:T(1,128)S(1)} %collective-permute-done.1.cells), custom_call_target="tpu_custom_call" | custom-call | flops 2000000000 | bytes 2097152 | tf_op jit(solution)/shard_map/faults/pallas_call | solution.py:714
  8.8 0.0 collective-permute-done.3.rs
  8.8 0.0 collective-permute-done.rp
  8.8 2.2 %collective-permute-done.2.ro = f32[240,128]{1,0:T(8,128)S(1)} collective-permute-done((f32[240,128]{1,0:T(8,128)S(1)}, f32[240,128]{1,0:T(8,128)S(1)}, u32[]{:S(2)}, u32[]{:S(2)}) %collective-permute-start.2) | collective-permute-done | bytes 122912 | tf_op jit(solution)/shard_map/ppermute | solution.py:657
  11.1 0.1 columns.1
  11.1 5.7 %collective-permute-start.4 = (f32[280,128]{1,0:T(8,128)S(1)}, f32[280,128]{1,0:T(8,128)S(1)}, u32[]{:S(2)}, u32[]{:S(2)}) collective-permute-start(f32[280,128]{1,0:T(8,128)S(1)} %get-tuple-element.29), channel_id=1, source_target_pairs={{0,0},{1,2},{2,1},{3,3},{4,4},{5,6},{6,5},{7,7},{8,8},{9,10},{10,9... | collective-permute-start | bytes 430088 | tf_op jit(solution)/shard_map/ppermute | solution.py:657
  16.8 0.1 collective-permute-start.5
  16.9 1.8 %inner.1 = (f32[2352,128]{1,0:T(8,128)S(1)}, f32[2352,128]{1,0:T(8,128)S(1)}, f32[6,12,4,8,128]{4,3,2,1,0:T(8,128)S(1)}, f32[4,10,3,3,8,128]{5,4,3,2,1,0:T(8,128...) custom-call(f32[232,128]{1,0:T(8,128)S(1)} %get-tuple-element.25.own, ...), custom_call_target="tpu_custom_call" | custom-call | flops 4000000000 | bytes 2097152 | tf_op jit(solution)/shard_map/inner/pallas_call | solution.py:751
  18.8 0.0 collective-permute-done.5.halo
  18.8 1.4 %core_side.1 = (f32[2352,128]{1,0:T(8,128)S(1)}, f32[2352,128]{1,0:T(8,128)S(1)}, f32[6,12,4,8,128]{4,3,2,1,0:T(8,128)S(1)}, f32[4,10,3,3,8,128]{5,4,3,2,1,0:T(8,128)S(1)}, f32[2,5,5,8,512]{4,3,2,1,0:T(8,128)S(1)}) custom-call(f32[280,128]{1,0:T(8,128)S(1)} %collective-permute-done.5.h, ...), custom_call_target="tpu_custom_call", output_to_operand_aliasing={{0}: (5, {}), {1}: (6, {}), {2}: (7, {}), {3}: (8, {}), {4}... | custom-call | flops 2000000000 | bytes 1048576 | tf_op jit(solution)/shard_map/core_side/pallas_call | solution.py:766
  20.2 0.0 collective-permute-done.4.halo
  20.2 2.6 %chip_side.1 = (f32[125,1,256]{2,1,0:T(1,128)}, f32[2352,128]{1,0:T(8,128)S(1)}, f32[2352,128]{1,0:T(8,128)S(1)}, f32[6,12,4,8,128]{4,3,2,1,0:T(8,128)S(1)}, f32...) custom-call(f32[280,128]{1,0:T(8,128)S(1)} %collective-permute-done., ...), custom_call_target="tpu_custom_call", output_to_operand_aliasing={{1}: (5, {}), {2}: (6, {}), {3}: (7, {}), {4}: (8, {}), {5}... | custom-call | tf_op jit(solution)/shard_map/chip_side/pallas_call | solution.py:777
  (1 shorter events, 0.0 us)
Async XLA Ops:
  0.0 4.5 %collective-permute-start.1 = (s32[1,1,512]{2,1,0:T(1,128)}, s32[1,1,512]{2,1,0:T(1,128)S(1)}, u32[]{:S(2)}, u32[]{:S(2)}) collective-permute-start(s32[1,1,512]{2,1,0:T(1,128)} %refs_2_.1), channel_id=1, source_target_pairs={{0,4},{4,0},{8,12},{12,8},{16,20},{20,16},{24,28},{28,24},{1,5},{5... | collective-permute-start | bytes 6152 | tf_op jit(solution)/shard_map/ppermute | solution.py:657
  2.9 5.9 %collective-permute-start.3 = (f32[72,128]{1,0:T(8,128)S(1)}, f32[72,128]{1,0:T(8,128)S(1)}, u32[]{:S(2)}, u32[]{:S(2)}) collective-permute-start(f32[72,128]{1,0:T(8,128)S(1)} %get-tuple-element.26), channel_id=1, source_target_pairs={{0,8},{4,12},{8,16},{12,20},{16,24},{20,28},{24,0},{28,4},{1,9},{5... | collective-permute-start | bytes 110600 | tf_op jit(solution)/shard_map/ppermute | solution.py:657
  4.3 4.6 %collective-permute-start = (f32[232,128]{1,0:T(8,128)S(1)}, f32[232,128]{1,0:T(8,128)S(1)}, u32[]{:S(2)}, u32[]{:S(2)}) collective-permute-start(f32[232,128]{1,0:T(8,128)S(1)} %get-tuple-element.25.own), channel_id=1, source_target_pairs={{0,4},{4,0},{8,12},{12,8},{16,20},{20,16},{24,28},{28,24},{1,5},{5... | collective-permute-start | bytes 356360 | tf_op jit(solution)/shard_map/ppermute | solution.py:657
  4.5 6.5 %collective-permute-start.2 = (f32[240,128]{1,0:T(8,128)S(1)}, f32[240,128]{1,0:T(8,128)S(1)}, u32[]{:S(2)}, u32[]{:S(2)}) collective-permute-start(f32[240,128]{1,0:T(8,128)S(1)} %join.1), channel_id=1, source_target_pairs={{0,0},{4,8},{8,4},{12,16},{16,12},{20,24},{24,20},{28,28},{1,1},{5... | collective-permute-start | bytes 368648 | tf_op jit(solution)/shard_map/ppermute | solution.py:657
  11.1 9.1 %collective-permute-start.4 = (f32[280,128]{1,0:T(8,128)S(1)}, f32[280,128]{1,0:T(8,128)S(1)}, u32[]{:S(2)}, u32[]{:S(2)}) collective-permute-start(f32[280,128]{1,0:T(8,128)S(1)} %get-tuple-element.29), channel_id=1, source_target_pairs={{0,0},{1,2},{2,1},{3,3},{4,4},{5,6},{6,5},{7,7},{8,8},{9,10},{10,9... | collective-permute-start | bytes 430088 | tf_op jit(solution)/shard_map/ppermute | solution.py:657
  16.8 1.9 %collective-permute-start.5 = (f32[280,128]{1,0:T(8,128)S(1)}, f32[280,128]{1,0:T(8,128)S(1)}, u32[]{:S(2)}, u32[]{:S(2)}) collective-permute-start(f32[280,128]{1,0:T(8,128)S(1)} %get-tuple-element.33), channel_id=1, source_target_pairs={{0,1},{1,0},{2,3},{3,2},{4,5},{5,4},{6,7},{7,6},{8,9},{9,8},{10,11... | collective-permute-start | bytes 430088 | tf_op jit(solution)/shard_map/ppermute | solution.py:657

commit v11 on v10

--- a/solution.py
+++ b/solution.py
@@ -254,7 +254,8 @@
     return f2, ft2, dot_nn(one2, ft2), dot_nn(one2, f2)
 
 
-def fault_kernel(own, cells, f2, ft2, rf, band, far2, hot, both):
+def fault_kernel(own, plane, cells, f2, ft2, rf, band, plane_out, far2, hot, both):
+    plane_out[...] = plane[...]
     partner, live = slot_columns([partner_rows(cells), own[228:232, :]])
     fill_far(far2, partner, live)
     fill_hot(hot, flat_cells(own[224:228, :]), range(CY))
@@ -617,25 +618,7 @@
         gather_fault(here, inv, ap, tt, y, ft2[y])
 
 
-def core_kernel(halo, f2, ft2, rf_pair, rf_third, *refs):
-    work, fields, rest = refs[5:10], refs[10:14], refs[14:]
-
-    def body(odd):
-        side(not odd, halo, f2, ft2, rf_pair, rf_third, work, fields, *rest)
-
-    by_parity("gy", body)
-
-
-def main_kernel(peers, halo, f2, ft2, rf_pair, rf_third, *refs):
-    out, work, fields, rest = refs[5], refs[6:11], refs[11:15], refs[15:]
-    halo = Masked(halo, has_other("gy", peers[1]))
-
-    def body(odd):
-        side(odd, halo, f2, ft2, rf_pair, rf_third, work, fields, *rest)
-
-    by_parity("gy", body)
-    tt = work[4]
-
+def finish(tt, pair, store):
     kz = lax.broadcasted_iota(jnp.int32, (512, NZ), 0)
     kout = lax.broadcasted_iota(jnp.int32, (512, NZ), 1)
     z_in = kz & 127
@@ -645,16 +628,47 @@
     )
     fits = (target == (kout & 63)) & ((kz >> 8) == (kout >> 6))
     collect = jnp.where(fits, 1.0, 0.0).astype(bf16)
-    for pair in range(2):
-        high, low = split(tt[pair].reshape(200, 512))
-        got = (dot_nn(high, collect) + dot_nn(low, collect)) * 0.125
-        for k in range(25):
-            out[5 * k : 5 * k + 5, 0, pair * NZ : (pair + 1) * NZ] = got[8 * k : 8 * k + 5]
+    high, low = split(tt[pair].reshape(200, 512))
+    got = (dot_nn(high, collect) + dot_nn(low, collect)) * 0.125
+    for k in range(25):
+        store(5 * k, got[8 * k : 8 * k + 5])
+
+
+def core_kernel(halo, f2, ft2, rf_pair, rf_third, *refs):
+    half, work, fields, rest = refs[5], refs[6:11], refs[11:15], refs[15:]
+
+    def body(odd):
+        side(not odd, halo, f2, ft2, rf_pair, rf_third, work, fields, *rest)
+
+        def store(row, value):
+            half[row : row + 5, :] = value
+
+        finish(work[4], 0 if odd else 1, store)
+
+    by_parity("gy", body)
+
+
+def main_kernel(peers, halo, f2, ft2, rf_pair, rf_third, half, *refs):
+    out, work, fields, rest = refs[5], refs[6:11], refs[11:15], refs[15:]
+    halo = Masked(halo, has_other("gy", peers[1]))
+
+    def body(odd):
+        side(odd, halo, f2, ft2, rf_pair, rf_third, work, fields, *rest)
+        lanes = [slice(0, NZ), slice(NZ, 2 * NZ)]
+
+        def store(row, value):
+            out[row : row + 5, 0, lanes[odd]] = value
+            out[row : row + 5, 0, lanes[1 - odd]] = half[row : row + 5, :]
+
+        finish(work[4], odd, store)
+
+    by_parity("gy", body)
 
 
 def send(value, axis, target):
     peers = lax.axis_size(axis)
-    return lax.ppermute(value, axis, [(i, target(i, peers)) for i in range(peers)])
+    pairs = [(i, target(i, peers)) for i in range(peers)]
+    return lax.ppermute(value, axis, [(i, j) for i, j in pairs if j < peers])
 
 
 def partner_of(i, peers):
@@ -667,7 +681,7 @@
 
 
 def ahead_of(i, peers):
-    return (i + 2) % peers
+    return i + 2
 
 
 VMEM = pl.BlockSpec(memory_space=pltpu.VMEM)
@@ -699,7 +713,6 @@
         compiler_params=params(16),
         name="pack",
     )(fault_count, *sources)
-    rs = send(plane, "gx", ahead_of)
     joined = pl.pallas_call(
         join_kernel,
         out_shape=sds(240, NZ),
@@ -711,11 +724,11 @@
     ro = send(joined, "gx", other_of)
     rp = send(own, "gx", partner_of)
     pieces = sds(CY, 2 * NZ, NZ, dtype=bf16)
-    f2, ft2, rf_pair, band = pl.pallas_call(
+    f2, ft2, rf_pair, band, plane = pl.pallas_call(
         fault_kernel,
-        out_shape=(pieces, pieces, sds(2, CY, 8, NZ), sds(2, 24, NZ)),
-        in_specs=[VMEM] * 2,
-        out_specs=(VMEM,) * 4,
+        out_shape=(pieces, pieces, sds(2, CY, 8, NZ), sds(2, 24, NZ), sds(72, NZ)),
+        in_specs=[VMEM] * 3,
+        out_specs=(VMEM,) * 5,
         scratch_shapes=[
             pltpu.VMEM((SLOTS, 2 * NZ), bf16),
             pltpu.VMEM((CY * NZ, SLOTS), bf16),
@@ -724,7 +737,8 @@
         compiler_params=params(16),
         cost_estimate=pl.CostEstimate(flops=2 * 10**9, bytes_accessed=2**21, transcendentals=0),
         name="faults",
-    )(own, cells)
+    )(own, plane, cells)
+    rs = send(plane, "gx", ahead_of)
     to_core, to_chip = pl.pallas_call(
         functools.partial(column_kernel, peers),
         out_shape=(sds(Y_ROWS, NZ), sds(Y_ROWS, NZ)),
@@ -763,13 +777,13 @@
         pltpu.VMEM((24, NZ), f32),
         pltpu.VMEM((2 * NZ, SLOTS), bf16),
     ]
-    work_in = pl.pallas_call(
+    half, *work_in = pl.pallas_call(
         core_kernel,
-        out_shape=work,
+        out_shape=(sds(125, NZ),) + work,
         in_specs=[VMEM] * 10,
-        out_specs=(VMEM,) * 5,
+        out_specs=(VMEM,) * 6,
         scratch_shapes=side_scratch,
-        input_output_aliases={5 + k: k for k in range(5)},
+        input_output_aliases={5 + k: 1 + k for k in range(5)},
         compiler_params=params(16),
         cost_estimate=pl.CostEstimate(flops=2 * 10**9, bytes_accessed=2**20, transcendentals=0),
         name="core_side",
@@ -777,13 +791,13 @@
     result, *_ = pl.pallas_call(
         functools.partial(main_kernel, peers),
         out_shape=(sds(125, 1, 256),) + work,
-        in_specs=[VMEM] * 10,
+        in_specs=[VMEM] * 11,
         out_specs=(VMEM,) * 6,
         scratch_shapes=side_scratch,
-        input_output_aliases={5 + k: 1 + k for k in range(5)},
+        input_output_aliases={6 + k: 1 + k for k in range(5)},
         compiler_params=params(16),
         name="chip_side",
-    )(from_chip, f2, ft2, rf_pair, rf_third, *work_in)
+    )(from_chip, f2, ft2, rf_pair, rf_third, half, *work_in)
     return result
 
 

time: 23 us -> 24.9 us (1.083)
  the two profiles are of different devices: /device:TPU:9 before, /device:TPU:0 now
where the time goes in v11:
time: 24.9 us; the launch traced here: 24.7 us
  starting transfers between devices  13.9 us (56%)
  Pallas kernels  8.44 us (34%)
  waiting for transfers between devices  1.63 us (7%)
  between operations  0.75 us (3%)
    ppermute x6, starting transfers between devices, send(): return lax.ppermute(value, axis, [(i, j) for i, j in pairs if j < peers])  13.9 us
    pallas_call x1, Pallas kernels, per_device(): pl.pallas_call(functools.partial(main_kernel, peers), out_shape=(sds(125,...  2.48 us
    pallas_call x1, Pallas kernels, per_device(): pl.pallas_call(functools.partial(inner_kernel, peers), out_shape=work + (...  1.82 us
    pallas_call x1, Pallas kernels, per_device(): pl.pallas_call(core_kernel, out_shape=(sds(125, NZ),) + work, in_specs=[V...  1.8 us
    ppermute x6, waiting for transfers between devices, send(): return lax.ppermute(value, axis, [(i, j) for i, j in pairs if j < peers])  1.63 us
    pallas_call x1, Pallas kernels, per_device(): pl.pallas_call(fault_kernel, out_shape=(pieces, pieces, sds(2, CY, 8, NZ)...  1.23 us
    pallas_call x1, Pallas kernels, per_device(): pl.pallas_call(functools.partial(pack_kernel, peers), out_shape=(sds(232,...  1.05 us
  transfers between devices with their start and end apart: 6, of which 1 were waited for; matrix products, arithmetic and copies ran while one was open for 0% of the time, Pallas kernels for 24%

profile of v11, /device:TPU:0, one launch (start us, length us, event | category | flops | bytes accessed | tf_op | source)
XLA Modules:
  0.0 24.7 jit_solution(14604691050214429001)
XLA Ops:
  0.0 2.9 %collective-permute-start.1 = (s32[1,1,512]{2,1,0:T(1,128)}, s32[1,1,512]{2,1,0:T(1,128)S(1)}, u32[]{:S(2)}, u32[]{:S(2)}) collective-permute-start(s32[1,1,512]{2,1,0:T(1,128)} %refs_2_.1), channel_id=1, source_target_pairs={{0,4},{4,0},{8,12},{12,8},{16,20},{20,16},{24,28},{28,24},{1,5},{5... | collective-permute-start | bytes 6152 | tf_op jit(solution)/shard_map/ppermute | solution.py:671
  3.6 1.0 %pack.1 = (f32[232,128]{1,0:T(8,128)S(1)}, f32[72,128]{1,0:T(8,128)S(1)}) custom-call(s32[1,1]{1,0:T(1,128)S(6)} %copy.26.count, f32[13,2,1024]{2,1,0:T(2,128)} %refs_0_.1, f32[2,1024]{1,0:T(2,128)} %refs_1_.1, s32[1,1,512]{2,1,0:T(1,128)} %refs_2_.1, f32[1,1,512]{2,1,0:T(1,128)} %refs_3_.1), custom_call_target="tpu_custom_call" | custom-call | tf_op jit(solution)/shard_map/pack/pallas_call | solution.py:706
  4.6 0.1 collective-permute-start
  4.7 0.0 collective-permute-done.1.cells
  4.8 0.7 %collective-permute-start.2 = (f32[240,128]{1,0:T(8,128)S(1)}, f32[240,128]{1,0:T(8,128)S(1)}, u32[]{:S(2)}, u32[]{:S(2)}) collective-permute-start(f32[240,128]{1,0:T(8,128)S(1)} %join.1), channel_id=1, source_target_pairs={{0,0},{4,8},{8,4},{12,16},{16,12},{20,24},{24,20},{28,28},{1,1},{5... | collective-permute-start | bytes 368648 | tf_op jit(solution)/shard_map/ppermute | solution.py:671
  5.4 1.2 %faults.1 = (bf16[8,256,128]{2,1,0:T(8,128)(2,1)S(1)}, bf16[8,256,128]{2,1,0:T(8,128)(2,1)S(1)}, f32[2,8,8,128]{3,2,1,0:T(8,128)S(1)}, f32[2,24,128]{2,1,0:T(8,128)S(1)}, f32[72,128]{1,0:T(8,128)S(1)}) custom-call(f32[232,128]{1,0:T(8,128)S(1)} %get-tuple-element.27.own, f32[72,128]{1,0:T(8,128)S(1)} %get-tuple-element.28.plane, ...), custom_call_target="tpu_custom_call" | custom-call | flops 2000000000 | bytes 2097152 | tf_op jit(solution)/shard_map/faults/pallas_call | solution.py:727
  6.7 6.6 %collective-permute-start.3 = (f32[72,128]{1,0:T(8,128)S(1)}, f32[72,128]{1,0:T(8,128)S(1)}, u32[]{:S(2)}, u32[]{:S(2)}) collective-permute-start(f32[72,128]{1,0:T(8,128)S(1)} %get-tuple-element.29), channel_id=1, source_target_pairs={{0,8},{4,12},{8,16},{12,20},{16,24},{20,28},{1,9},{5,13},{9,17},{1... | collective-permute-start | bytes 110600 | tf_op jit(solution)/shard_map/ppermute | solution.py:671
  13.3 1.6 %collective-permute-done.3.rs = f32[72,128]{1,0:T(8,128)S(1)} collective-permute-done((f32[72,128]{1,0:T(8,128)S(1)}, f32[72,128]{1,0:T(8,128)S(1)}, u32[]{:S(2)}, u32[]{:S(2)}) %collective-permute-start.3) | collective-permute-done | bytes 36896 | tf_op jit(solution)/shard_map/ppermute | solution.py:671
  14.9 0.0 collective-permute-done.rp
  14.9 0.0 collective-permute-done.2.ro
  14.9 0.1 columns.1
  15.0 0.7 %collective-permute-start.4 = (f32[280,128]{1,0:T(8,128)S(1)}, f32[280,128]{1,0:T(8,128)S(1)}, u32[]{:S(2)}, u32[]{:S(2)}) collective-permute-start(f32[280,128]{1,0:T(8,128)S(1)} %get-tuple-element.32), channel_id=1, source_target_pairs={{0,0},{1,2},{2,1},{3,3},{4,4},{5,6},{6,5},{7,7},{8,8},{9,10},{10,9... | collective-permute-start | bytes 430088 | tf_op jit(solution)/shard_map/ppermute | solution.py:671
  15.7 2.9 %collective-permute-start.5 = (f32[280,128]{1,0:T(8,128)S(1)}, f32[280,128]{1,0:T(8,128)S(1)}, u32[]{:S(2)}, u32[]{:S(2)}) collective-permute-start(f32[280,128]{1,0:T(8,128)S(1)} %get-tuple-element.36), channel_id=1, source_target_pairs={{0,1},{1,0},{2,3},{3,2},{4,5},{5,4},{6,7},{7,6},{8,9},{9,8},{10,11... | collective-permute-start | bytes 430088 | tf_op jit(solution)/shard_map/ppermute | solution.py:671
  18.6 1.8 %inner.1 = (f32[2352,128]{1,0:T(8,128)S(1)}, f32[2352,128]{1,0:T(8,128)S(1)}, f32[6,12,4,8,128]{4,3,2,1,0:T(8,128)S(1)}, f32[4,10,3,3,8,128]{5,4,3,2,1,0:T(8,128...) custom-call(f32[232,128]{1,0:T(8,128)S(1)} %get-tuple-element.27.own, ...), custom_call_target="tpu_custom_call" | custom-call | flops 4000000000 | bytes 2097152 | tf_op jit(solution)/shard_map/inner/pallas_call | solution.py:765
  20.4 0.0 collective-permute-done.5.halo
  20.5 1.8 %core_side.1 = (f32[125,128]{1,0:T(8,128)S(1)}, f32[2352,128]{1,0:T(8,128)S(1)}, f32[2352,128]{1,0:T(8,128)S(1)}, f32[6,12,4,8,128]{4,3,2,1,0:T(8,128)S(1)}, f32...) custom-call(f32[280,128]{1,0:T(8,128)S(1)} %collective-permute-done., ...), custom_call_target="tpu_custom_call", output_to_operand_aliasing={{1}: (5, {}), {2}: (6, {}), {3}: (7, {}), {4}: (8, {}), {5}... | custom-call | flops 2000000000 | bytes 1048576 | tf_op jit(solution)/shard_map/core_side/pallas_call | solution.py:780
  22.3 0.0 collective-permute-done.4.halo
  22.3 2.5 %chip_side.1 = (f32[125,1,256]{2,1,0:T(1,128)}, f32[2352,128]{1,0:T(8,128)S(1)}, f32[2352,128]{1,0:T(8,128)S(1)}, f32[6,12,4,8,128]{4,3,2,1,0:T(8,128)S(1)}, f32...) custom-call(f32[280,128]{1,0:T(8,128)S(1)} %collective-permute-done., ...), custom_call_target="tpu_custom_call", output_to_operand_aliasing={{1}: (6, {}), {2}: (7, {}), {3}: (8, {}), {4}: (9, {}), {5}... | custom-call | tf_op jit(solution)/shard_map/chip_side/pallas_call | solution.py:791
  (1 shorter events, 0.0 us)
Async XLA Ops:
  0.0 4.7 %collective-permute-start.1 = (s32[1,1,512]{2,1,0:T(1,128)}, s32[1,1,512]{2,1,0:T(1,128)S(1)}, u32[]{:S(2)}, u32[]{:S(2)}) collective-permute-start(s32[1,1,512]{2,1,0:T(1,128)} %refs_2_.1), channel_id=1, source_target_pairs={{0,4},{4,0},{8,12},{12,8},{16,20},{20,16},{24,28},{28,24},{1,5},{5... | collective-permute-start | bytes 6152 | tf_op jit(solution)/shard_map/ppermute | solution.py:671
  4.6 10.3 %collective-permute-start = (f32[232,128]{1,0:T(8,128)S(1)}, f32[232,128]{1,0:T(8,128)S(1)}, u32[]{:S(2)}, u32[]{:S(2)}) collective-permute-start(f32[232,128]{1,0:T(8,128)S(1)} %get-tuple-element.27.own), channel_id=1, source_target_pairs={{0,4},{4,0},{8,12},{12,8},{16,20},{20,16},{24,28},{28,24},{1,5},{5... | collective-permute-start | bytes 356360 | tf_op jit(solution)/shard_map/ppermute | solution.py:671
  4.8 10.2 %collective-permute-start.2 = (f32[240,128]{1,0:T(8,128)S(1)}, f32[240,128]{1,0:T(8,128)S(1)}, u32[]{:S(2)}, u32[]{:S(2)}) collective-permute-start(f32[240,128]{1,0:T(8,128)S(1)} %join.1), channel_id=1, source_target_pairs={{0,0},{4,8},{8,4},{12,16},{16,12},{20,24},{24,20},{28,28},{1,1},{5... | collective-permute-start | bytes 368648 | tf_op jit(solution)/shard_map/ppermute | solution.py:671
  6.7 8.3 %collective-permute-start.3 = (f32[72,128]{1,0:T(8,128)S(1)}, f32[72,128]{1,0:T(8,128)S(1)}, u32[]{:S(2)}, u32[]{:S(2)}) collective-permute-start(f32[72,128]{1,0:T(8,128)S(1)} %get-tuple-element.29), channel_id=1, source_target_pairs={{0,8},{4,12},{8,16},{12,20},{16,24},{20,28},{1,9},{5,13},{9,17},{1... | collective-permute-start | bytes 110600 | tf_op jit(solution)/shard_map/ppermute | solution.py:671
  15.0 7.3 %collective-permute-start.4 = (f32[280,128]{1,0:T(8,128)S(1)}, f32[280,128]{1,0:T(8,128)S(1)}, u32[]{:S(2)}, u32[]{:S(2)}) collective-permute-start(f32[280,128]{1,0:T(8,128)S(1)} %get-tuple-element.32), channel_id=1, source_target_pairs={{0,0},{1,2},{2,1},{3,3},{4,4},{5,6},{6,5},{7,7},{8,8},{9,10},{10,9... | collective-permute-start | bytes 430088 | tf_op jit(solution)/shard_map/ppermute | solution.py:671
  15.7 4.8 %collective-permute-start.5 = (f32[280,128]{1,0:T(8,128)S(1)}, f32[280,128]{1,0:T(8,128)S(1)}, u32[]{:S(2)}, u32[]{:S(2)}) collective-permute-start(f32[280,128]{1,0:T(8,128)S(1)} %get-tuple-element.36), channel_id=1, source_target_pairs={{0,1},{1,0},{2,3},{3,2},{4,5},{5,4},{6,7},{7,6},{8,9},{9,8},{10,11... | collective-permute-start | bytes 430088 | tf_op jit(solution)/shard_map/ppermute | solution.py:671

commit v12 on v11

--- a/solution.py
+++ b/solution.py
@@ -254,8 +254,7 @@
     return f2, ft2, dot_nn(one2, ft2), dot_nn(one2, f2)
 
 
-def fault_kernel(own, plane, cells, f2, ft2, rf, band, plane_out, far2, hot, both):
-    plane_out[...] = plane[...]
+def fault_kernel(own, cells, f2, ft2, rf, band, far2, hot, both):
     partner, live = slot_columns([partner_rows(cells), own[228:232, :]])
     fill_far(far2, partner, live)
     fill_hot(hot, flat_cells(own[224:228, :]), range(CY))
@@ -665,23 +664,42 @@
     by_parity("gy", body)
 
 
-def send(value, axis, target):
-    peers = lax.axis_size(axis)
-    pairs = [(i, target(i, peers)) for i in range(peers)]
-    return lax.ppermute(value, axis, [(i, j) for i, j in pairs if j < peers])
-
-
-def partner_of(i, peers):
-    return i ^ 1
-
-
-def other_of(i, peers):
-    j = i + 1 if i % 2 else i - 1
-    return j if 0 <= j < peers else i
-
-
-def ahead_of(i, peers):
-    return i + 2
+def send(value, target):
+    size_x, size_y = lax.axis_size("gx"), lax.axis_size("gy")
+    pairs = []
+    for x in range(size_x):
+        for y in range(size_y):
+            to_x, to_y = target(x, y)
+            pairs.append((x * size_y + y, to_x * size_y + to_y))
+    return lax.ppermute(value, ("gx", "gy"), pairs)
+
+
+def x_partner(x, y):
+    return x ^ 1, y
+
+
+def core_partner(x, y):
+    return x, y ^ 1
+
+
+def x_other(size_x):
+    def target(x, y):
+        other = x + 1 if x % 2 else x - 1
+        return (other, y) if 0 <= other < size_x else core_partner(x, y)
+
+    return target
+
+
+def chip_other(size_y):
+    def target(x, y):
+        other = y + 1 if y % 2 else y - 1
+        return (x, other) if 0 <= other < size_y else x_partner(x, y)
+
+    return target
+
+
+def x_ahead(size_x):
+    return lambda x, y: ((x + 2) % size_x, y)
 
 
 VMEM = pl.BlockSpec(memory_space=pltpu.VMEM)
@@ -698,7 +716,7 @@
 
 def per_device(trans, storage, fault_cells, fault_count, fault_trans):
     peers = (lax.axis_size("gx"), lax.axis_size("gy"))
-    cells = send(fault_cells, "gx", partner_of)
+    cells = send(fault_cells, x_partner)
     sources = [
         pltpu.with_memory_space_constraint(array, pltpu.HBM)
         for array in (trans, storage, fault_cells, fault_trans)
@@ -713,6 +731,7 @@
         compiler_params=params(16),
         name="pack",
     )(fault_count, *sources)
+    rs = send(plane, x_ahead(peers[0]))
     joined = pl.pallas_call(
         join_kernel,
         out_shape=sds(240, NZ),
@@ -721,14 +740,14 @@
         compiler_params=params(16),
         name="join",
     )(own, cells)
-    ro = send(joined, "gx", other_of)
-    rp = send(own, "gx", partner_of)
+    ro = send(joined, x_other(peers[0]))
+    rp = send(own, x_partner)
     pieces = sds(CY, 2 * NZ, NZ, dtype=bf16)
-    f2, ft2, rf_pair, band, plane = pl.pallas_call(
+    f2, ft2, rf_pair, band = pl.pallas_call(
         fault_kernel,
-        out_shape=(pieces, pieces, sds(2, CY, 8, NZ), sds(2, 24, NZ), sds(72, NZ)),
-        in_specs=[VMEM] * 3,
-        out_specs=(VMEM,) * 5,
+        out_shape=(pieces, pieces, sds(2, CY, 8, NZ), sds(2, 24, NZ)),
+        in_specs=[VMEM] * 2,
+        out_specs=(VMEM,) * 4,
         scratch_shapes=[
             pltpu.VMEM((SLOTS, 2 * NZ), bf16),
             pltpu.VMEM((CY * NZ, SLOTS), bf16),
@@ -737,8 +756,7 @@
         compiler_params=params(16),
         cost_estimate=pl.CostEstimate(flops=2 * 10**9, bytes_accessed=2**21, transcendentals=0),
         name="faults",
-    )(own, plane, cells)
-    rs = send(plane, "gx", ahead_of)
+    )(own, cells)
     to_core, to_chip = pl.pallas_call(
         functools.partial(column_kernel, peers),
         out_shape=(sds(Y_ROWS, NZ), sds(Y_ROWS, NZ)),
@@ -747,8 +765,8 @@
         compiler_params=params(16),
         name="columns",
     )(own, rp, ro, rs, band, rf_pair)
-    from_chip = send(to_chip, "gy", other_of)
-    from_core = send(to_core, "gy", partner_of)
+    from_chip = send(to_chip, chip_other(peers[1]))
+    from_core = send(to_core, core_partner)
     work = (
         sds(7 * PER * ROWS, NZ),
         sds(7 * PER * ROWS, NZ),

time: 24.9 us -> 20.7 us (0.83)
  the two profiles are of different devices: /device:TPU:0 before, /device:TPU:1 now
where the time goes in v12:
time: 20.7 us; the launch traced here: 20.6 us
  starting transfers between devices  10.8 us (52%)
  Pallas kernels  8.42 us (41%)
  between operations  0.71 us (3%)
  waiting for transfers between devices  0.62 us (3%)
    ppermute x6, starting transfers between devices, send(): return lax.ppermute(value, ('gx', 'gy'), pairs)  10.8 us
    pallas_call x1, Pallas kernels, per_device(): pl.pallas_call(functools.partial(main_kernel, peers), out_shape=(sds(125,...  2.46 us
    pallas_call x1, Pallas kernels, per_device(): pl.pallas_call(functools.partial(inner_kernel, peers), out_shape=work + (...  1.82 us
    pallas_call x1, Pallas kernels, per_device(): pl.pallas_call(core_kernel, out_shape=(sds(125, NZ),) + work, in_specs=[V...  1.81 us
    pallas_call x1, Pallas kernels, per_device(): pl.pallas_call(fault_kernel, out_shape=(pieces, pieces, sds(2, CY, 8, NZ)...  1.22 us
    pallas_call x1, Pallas kernels, per_device(): pl.pallas_call(functools.partial(pack_kernel, peers), out_shape=(sds(232,...  1.05 us
    ppermute x6, waiting for transfers between devices, send(): return lax.ppermute(value, ('gx', 'gy'), pairs)  0.62 us
  transfers between devices with their start and end apart: 6, of which 2 were waited for; matrix products, arithmetic and copies ran while one was open for 0% of the time, Pallas kernels for 29%

profile of v12, /device:TPU:1, one launch (start us, length us, event | category | flops | bytes accessed | tf_op | source)
XLA Modules:
  0.0 20.6 jit_solution(974616527584039232)
XLA Ops:
  0.0 2.0 %collective-permute-start.1 = (s32[1,1,512]{2,1,0:T(1,128)}, s32[1,1,512]{2,1,0:T(1,128)S(1)}, u32[]{:S(2)}, u32[]{:S(2)}) collective-permute-start(s32[1,1,512]{2,1,0:T(1,128)} %refs_2_.1), channel_id=1, source_target_pairs={{0,4},{1,5},{2,6},{3,7},{4,0},{5,1},{6,2},{7,3},{8,12},{9,13},{10,... | collective-permute-start | bytes 6152 | tf_op jit(solution)/shard_map/ppermute | solution.py:674
  2.7 1.0 %pack.1 = (f32[232,128]{1,0:T(8,128)S(1)}, f32[72,128]{1,0:T(8,128)S(1)}) custom-call(s32[1,1]{1,0:T(1,128)S(6)} %copy.26.count, f32[13,2,1024]{2,1,0:T(2,128)} %refs_0_.1, f32[2,1024]{1,0:T(2,128)} %refs_1_.1, s32[1,1,512]{2,1,0:T(1,128)} %refs_2_.1, f32[1,1,512]{2,1,0:T(1,128)} %refs_3_.1), custom_call_target="tpu_custom_call" | custom-call | tf_op jit(solution)/shard_map/pack/pallas_call | solution.py:724
  3.7 1.3 %collective-permute-start.3 = (f32[72,128]{1,0:T(8,128)S(1)}, f32[72,128]{1,0:T(8,128)S(1)}, u32[]{:S(2)}, u32[]{:S(2)}) collective-permute-start(f32[72,128]{1,0:T(8,128)S(1)} %get-tuple-element.27), channel_id=1, source_target_pairs={{0,8},{1,9},{2,10},{3,11},{4,12},{5,13},{6,14},{7,15},{8,16},{9,17... | collective-permute-start | bytes 110600 | tf_op jit(solution)/shard_map/ppermute | solution.py:674
  5.1 0.3 %collective-permute-start = (f32[232,128]{1,0:T(8,128)S(1)}, f32[232,128]{1,0:T(8,128)S(1)}, u32[]{:S(2)}, u32[]{:S(2)}) collective-permute-start(f32[232,128]{1,0:T(8,128)S(1)} %get-tuple-element.26.own), channel_id=1, source_target_pairs={{0,4},{1,5},{2,6},{3,7},{4,0},{5,1},{6,2},{7,3},{8,12},{9,13},{10,... | collective-permute-start | bytes 356360 | tf_op jit(solution)/shard_map/ppermute | solution.py:674
  5.4 0.0 collective-permute-done.1.cells
  5.4 1.6 %collective-permute-start.2 = (f32[240,128]{1,0:T(8,128)S(1)}, f32[240,128]{1,0:T(8,128)S(1)}, u32[]{:S(2)}, u32[]{:S(2)}) collective-permute-start(f32[240,128]{1,0:T(8,128)S(1)} %join.1), channel_id=1, source_target_pairs={{0,1},{1,0},{2,3},{3,2},{4,8},{5,9},{6,10},{7,11},{8,4},{9,5},{10,... | collective-permute-start | bytes 368648 | tf_op jit(solution)/shard_map/ppermute | solution.py:674
  7.0 1.2 %faults.1 = (bf16[8,256,128]{2,1,0:T(8,128)(2,1)S(1)}, bf16[8,256,128]{2,1,0:T(8,128)(2,1)S(1)}, f32[2,8,8,128]{3,2,1,0:T(8,128)S(1)}, f32[2,24,128]{2,1,0:T(8,128)S(1)}) custom-call(f32[232,128]{1,0:T(8,128)S(1)} %get-tuple-element.26.own, s32[1,1,512]{2,1,0:T(1,128)S(1)} %collective-permute-done.1.cells), custom_call_target="tpu_custom_call" | custom-call | flops 2000000000 | bytes 2097152 | tf_op jit(solution)/shard_map/faults/pallas_call | solution.py:746
  8.2 0.3 %collective-permute-done.3.rs = f32[72,128]{1,0:T(8,128)S(1)} collective-permute-done((f32[72,128]{1,0:T(8,128)S(1)}, f32[72,128]{1,0:T(8,128)S(1)}, u32[]{:S(2)}, u32[]{:S(2)}) %collective-permute-start.3) | collective-permute-done | bytes 36896 | tf_op jit(solution)/shard_map/ppermute | solution.py:674
  8.5 0.3 %collective-permute-done.rp = f32[232,128]{1,0:T(8,128)S(1)} collective-permute-done((f32[232,128]{1,0:T(8,128)S(1)}, f32[232,128]{1,0:T(8,128)S(1)}, u32[]{:S(2)}, u32[]{:S(2)}) %collective-permute-start) | collective-permute-done | bytes 118816 | tf_op jit(solution)/shard_map/ppermute | solution.py:674
  8.8 0.0 collective-permute-done.2.ro
  8.8 0.1 columns.1
  8.9 3.6 %collective-permute-start.4 = (f32[280,128]{1,0:T(8,128)S(1)}, f32[280,128]{1,0:T(8,128)S(1)}, u32[]{:S(2)}, u32[]{:S(2)}) collective-permute-start(f32[280,128]{1,0:T(8,128)S(1)} %get-tuple-element.30), channel_id=1, source_target_pairs={{0,4},{1,2},{2,1},{3,7},{4,0},{5,6},{6,5},{7,3},{8,12},{9,10},{10,... | collective-permute-start | bytes 430088 | tf_op jit(solution)/shard_map/ppermute | solution.py:674
  12.4 2.0 %collective-permute-start.5 = (f32[280,128]{1,0:T(8,128)S(1)}, f32[280,128]{1,0:T(8,128)S(1)}, u32[]{:S(2)}, u32[]{:S(2)}) collective-permute-start(f32[280,128]{1,0:T(8,128)S(1)} %get-tuple-element.34), channel_id=1, source_target_pairs={{0,1},{1,0},{2,3},{3,2},{4,5},{5,4},{6,7},{7,6},{8,9},{9,8},{10,11... | collective-permute-start | bytes 430088 | tf_op jit(solution)/shard_map/ppermute | solution.py:674
  14.5 1.8 %inner.1 = (f32[2352,128]{1,0:T(8,128)S(1)}, f32[2352,128]{1,0:T(8,128)S(1)}, f32[6,12,4,8,128]{4,3,2,1,0:T(8,128)S(1)}, f32[4,10,3,3,8,128]{5,4,3,2,1,0:T(8,128...) custom-call(f32[232,128]{1,0:T(8,128)S(1)} %get-tuple-element.26.own, ...), custom_call_target="tpu_custom_call" | custom-call | flops 4000000000 | bytes 2097152 | tf_op jit(solution)/shard_map/inner/pallas_call | solution.py:783
  16.3 0.0 collective-permute-done.5.halo
  16.3 1.8 %core_side.1 = (f32[125,128]{1,0:T(8,128)S(1)}, f32[2352,128]{1,0:T(8,128)S(1)}, f32[2352,128]{1,0:T(8,128)S(1)}, f32[6,12,4,8,128]{4,3,2,1,0:T(8,128)S(1)}, f32...) custom-call(f32[280,128]{1,0:T(8,128)S(1)} %collective-permute-done., ...), custom_call_target="tpu_custom_call", output_to_operand_aliasing={{1}: (5, {}), {2}: (6, {}), {3}: (7, {}), {4}: (8, {}), {5}... | custom-call | flops 2000000000 | bytes 1048576 | tf_op jit(solution)/shard_map/core_side/pallas_call | solution.py:798
  18.1 0.0 collective-permute-done.4.halo
  18.1 2.5 %chip_side.1 = (f32[125,1,256]{2,1,0:T(1,128)}, f32[2352,128]{1,0:T(8,128)S(1)}, f32[2352,128]{1,0:T(8,128)S(1)}, f32[6,12,4,8,128]{4,3,2,1,0:T(8,128)S(1)}, f32...) custom-call(f32[280,128]{1,0:T(8,128)S(1)} %collective-permute-done., ...), custom_call_target="tpu_custom_call", output_to_operand_aliasing={{1}: (6, {}), {2}: (7, {}), {3}: (8, {}), {4}: (9, {}), {5}... | custom-call | tf_op jit(solution)/shard_map/chip_side/pallas_call | solution.py:809
  (1 shorter events, 0.0 us)
Async XLA Ops:
  0.0 5.4 %collective-permute-start.1 = (s32[1,1,512]{2,1,0:T(1,128)}, s32[1,1,512]{2,1,0:T(1,128)S(1)}, u32[]{:S(2)}, u32[]{:S(2)}) collective-permute-start(s32[1,1,512]{2,1,0:T(1,128)} %refs_2_.1), channel_id=1, source_target_pairs={{0,4},{1,5},{2,6},{3,7},{4,0},{5,1},{6,2},{7,3},{8,12},{9,13},{10,... | collective-permute-start | bytes 6152 | tf_op jit(solution)/shard_map/ppermute | solution.py:674
  3.7 4.7 %collective-permute-start.3 = (f32[72,128]{1,0:T(8,128)S(1)}, f32[72,128]{1,0:T(8,128)S(1)}, u32[]{:S(2)}, u32[]{:S(2)}) collective-permute-start(f32[72,128]{1,0:T(8,128)S(1)} %get-tuple-element.27), channel_id=1, source_target_pairs={{0,8},{1,9},{2,10},{3,11},{4,12},{5,13},{6,14},{7,15},{8,16},{9,17... | collective-permute-start | bytes 110600 | tf_op jit(solution)/shard_map/ppermute | solution.py:674
  5.1 3.7 %collective-permute-start = (f32[232,128]{1,0:T(8,128)S(1)}, f32[232,128]{1,0:T(8,128)S(1)}, u32[]{:S(2)}, u32[]{:S(2)}) collective-permute-start(f32[232,128]{1,0:T(8,128)S(1)} %get-tuple-element.26.own), channel_id=1, source_target_pairs={{0,4},{1,5},{2,6},{3,7},{4,0},{5,1},{6,2},{7,3},{8,12},{9,13},{10,... | collective-permute-start | bytes 356360 | tf_op jit(solution)/shard_map/ppermute | solution.py:674
  5.4 3.4 %collective-permute-start.2 = (f32[240,128]{1,0:T(8,128)S(1)}, f32[240,128]{1,0:T(8,128)S(1)}, u32[]{:S(2)}, u32[]{:S(2)}) collective-permute-start(f32[240,128]{1,0:T(8,128)S(1)} %join.1), channel_id=1, source_target_pairs={{0,1},{1,0},{2,3},{3,2},{4,8},{5,9},{6,10},{7,11},{8,4},{9,5},{10,... | collective-permute-start | bytes 368648 | tf_op jit(solution)/shard_map/ppermute | solution.py:674
  8.9 9.3 %collective-permute-start.4 = (f32[280,128]{1,0:T(8,128)S(1)}, f32[280,128]{1,0:T(8,128)S(1)}, u32[]{:S(2)}, u32[]{:S(2)}) collective-permute-start(f32[280,128]{1,0:T(8,128)S(1)} %get-tuple-element.30), channel_id=1, source_target_pairs={{0,4},{1,2},{2,1},{3,7},{4,0},{5,6},{6,5},{7,3},{8,12},{9,10},{10,... | collective-permute-start | bytes 430088 | tf_op jit(solution)/shard_map/ppermute | solution.py:674
  12.4 3.9 %collective-permute-start.5 = (f32[280,128]{1,0:T(8,128)S(1)}, f32[280,128]{1,0:T(8,128)S(1)}, u32[]{:S(2)}, u32[]{:S(2)}) collective-permute-start(f32[280,128]{1,0:T(8,128)S(1)} %get-tuple-element.34), channel_id=1, source_target_pairs={{0,1},{1,0},{2,3},{3,2},{4,5},{5,4},{6,7},{7,6},{8,9},{9,8},{10,11... | collective-permute-start | bytes 430088 | tf_op jit(solution)/shard_map/ppermute | solution.py:674

commit v13 on v12

--- a/solution.py
+++ b/solution.py
@@ -56,7 +56,7 @@
 
 
 def pack_kernel(peers, count, *refs):
-    sources, (block, plane), targets, sems = refs[:4], refs[4:6], refs[6:10], refs[10]
+    sources, (block, plane, tile), targets, sems = refs[:4], refs[4:7], refs[7:11], refs[11]
     copies = [
         pltpu.make_async_copy(src, dst, sems.at[k])
         for k, (src, dst) in enumerate(zip(sources, targets))
@@ -102,11 +102,10 @@
                 block[base : base + 8, :] = jnp.where(keep, block[base : base + 8, :], 0.0)
     live = count[0, 0]
     lane = lax.broadcasted_iota(jnp.int32, (1, NZ), 1)
-    base = 2 * PER * 8
     for r in range(4):
         lanes = slice(r * NZ, (r + 1) * NZ)
-        block[base + r : base + r + 1, :] = cells[0, :, lanes].astype(f32)
-        block[base + 4 + r : base + 5 + r, :] = jnp.where(
+        tile[r : r + 1, :] = cells[0, :, lanes].astype(f32)
+        tile[4 + r : 5 + r, :] = jnp.where(
             lane + r * NZ < live, ftrans[0, :, lanes], 0.0
         )
     plane[...] = block[(PER + 4) * 8 : (PER + 13) * 8, :]
@@ -118,8 +117,9 @@
     ).astype(f32)
 
 
-def join_kernel(own, cells, joined):
-    joined[0:232, :] = own[...]
+def join_kernel(own, tile, cells, joined):
+    joined[0:224, :] = own[...]
+    joined[224:232, :] = tile[...]
     joined[232:236, :] = partner_rows(cells)
     joined[236:240, :] = jnp.zeros((4, NZ), f32)
 
@@ -138,14 +138,24 @@
         return jnp.where(self.due, self.ref[index], 0.0)
 
 
+class Behind:
+    def __init__(self, first, second):
+        self.refs, self.at = (first, second), lax.axis_index("gx")
+
+    def __getitem__(self, index):
+        first, second = (ref[index] for ref in self.refs)
+        value = jnp.where(lax.rem(self.at // 2, 2) == 1, first, second)
+        return jnp.where(self.at >= 2, value, 0.0)
+
+
 def has_other(axis, peers):
     at = lax.axis_index(axis)
     return jnp.where(lax.rem(at, 2) == 0, at > 0, at < peers - 1)
 
 
-def column_kernel(peers, own, rp, ro, rs, band, sums, to_core, to_chip):
+def column_kernel(peers, own, rp, ro, ra, rb, band, sums, to_core, to_chip):
     ro = Masked(ro, has_other("gx", peers[0]))
-    lo2 = Masked(rs, lax.axis_index("gx") >= 2)
+    lo2 = Behind(ra, rb)
 
     def fill(out, lo, hi, first, third, runs):
         for c in range(2):
@@ -254,16 +264,17 @@
     return f2, ft2, dot_nn(one2, ft2), dot_nn(one2, f2)
 
 
-def fault_kernel(own, cells, f2, ft2, rf, band, far2, hot, both):
-    partner, live = slot_columns([partner_rows(cells), own[228:232, :]])
+def fault_kernel(tile, plane, cells, f2, ft2, rf, band, plane_out, far2, hot, both):
+    plane_out[...] = plane[...]
+    partner, live = slot_columns([partner_rows(cells), tile[4:8, :]])
     fill_far(far2, partner, live)
-    fill_hot(hot, flat_cells(own[224:228, :]), range(CY))
+    fill_hot(hot, flat_cells(tile[0:4, :]), range(CY))
     both[...] = dot_nn(hot[...], far2[...])
     for y in range(CY):
         f2[y], ft2[y], rf[0, y], rf[1, y] = pair_matrix(both[y * NZ : (y + 1) * NZ, :])
     for k, y in enumerate((0, CY - 1)):
         band[k] = diagonals(
-            hot[y * NZ : (y + 1) * NZ, :], own[224:228, :], partner_rows(cells), own[228:232, :]
+            hot[y * NZ : (y + 1) * NZ, :], tile[0:4, :], partner_rows(cells), tile[4:8, :]
         )
 
 
@@ -501,7 +512,7 @@
 
 
 def inner_kernel(
-    peers, own, rp, ro, rs, f2, ft2, rf_pair, w, wr, qe, ap, tt, rf_third, qc, inv, diag, fd, hot
+    peers, own, rp, ro, ra, rb, f2, ft2, rf_pair, w, wr, qe, ap, tt, rf_third, qc, inv, diag, fd, hot
 ):
     here = Place()
     ro = Masked(ro, has_other("gx", peers[0]))
@@ -517,7 +528,7 @@
         place(hi, 28, 5 * PER)
 
     by_parity("gx", place_x)
-    place(Masked(rs, here.gx >= 2), 9, 4)
+    place(Behind(ra, rb), 9, 4)
     place(own, 28, 3 * PER)
 
     fill_hot(hot, flat_cells(ro[224:228, :]), range(CY))
@@ -698,8 +709,20 @@
     return target
 
 
-def x_ahead(size_x):
-    return lambda x, y: ((x + 2) % size_x, y)
+def z_partner(size_x):
+    def target(x, y):
+        other = x ^ 2
+        return (other, y) if other < size_x else x_partner(x, y)
+
+    return target
+
+
+def z_other(size_x):
+    def target(x, y):
+        other = x + 2 if x % 4 >= 2 else x - 2
+        return (other, y) if 0 <= other < size_x else x_partner(x, y)
+
+    return target
 
 
 VMEM = pl.BlockSpec(memory_space=pltpu.VMEM)
@@ -721,33 +744,32 @@
         pltpu.with_memory_space_constraint(array, pltpu.HBM)
         for array in (trans, storage, fault_cells, fault_trans)
     ]
-    own, plane = pl.pallas_call(
+    own, plane, tile = pl.pallas_call(
         functools.partial(pack_kernel, peers),
-        out_shape=(sds(232, NZ), sds(72, NZ)),
+        out_shape=(sds(224, NZ), sds(72, NZ), sds(8, NZ)),
         in_specs=[pl.BlockSpec(memory_space=pltpu.SMEM)] + [HBM] * 4,
-        out_specs=(VMEM,) * 2,
+        out_specs=(VMEM,) * 3,
         scratch_shapes=[pltpu.VMEM(array.shape, array.dtype) for array in sources]
         + [pltpu.SemaphoreType.DMA((4,))],
         compiler_params=params(16),
         name="pack",
     )(fault_count, *sources)
-    rs = send(plane, x_ahead(peers[0]))
     joined = pl.pallas_call(
         join_kernel,
         out_shape=sds(240, NZ),
-        in_specs=[VMEM] * 2,
+        in_specs=[VMEM] * 3,
         out_specs=VMEM,
         compiler_params=params(16),
         name="join",
-    )(own, cells)
+    )(own, tile, cells)
     ro = send(joined, x_other(peers[0]))
     rp = send(own, x_partner)
     pieces = sds(CY, 2 * NZ, NZ, dtype=bf16)
-    f2, ft2, rf_pair, band = pl.pallas_call(
+    f2, ft2, rf_pair, band, plane = pl.pallas_call(
         fault_kernel,
-        out_shape=(pieces, pieces, sds(2, CY, 8, NZ), sds(2, 24, NZ)),
-        in_specs=[VMEM] * 2,
-        out_specs=(VMEM,) * 4,
+        out_shape=(pieces, pieces, sds(2, CY, 8, NZ), sds(2, 24, NZ), sds(72, NZ)),
+        in_specs=[VMEM] * 3,
+        out_specs=(VMEM,) * 5,
         scratch_shapes=[
             pltpu.VMEM((SLOTS, 2 * NZ), bf16),
             pltpu.VMEM((CY * NZ, SLOTS), bf16),
@@ -756,15 +778,17 @@
         compiler_params=params(16),
         cost_estimate=pl.CostEstimate(flops=2 * 10**9, bytes_accessed=2**21, transcendentals=0),
         name="faults",
-    )(own, cells)
+    )(tile, plane, cells)
+    ra = send(plane, z_partner(peers[0]))
+    rb = send(plane, z_other(peers[0]))
     to_core, to_chip = pl.pallas_call(
         functools.partial(column_kernel, peers),
         out_shape=(sds(Y_ROWS, NZ), sds(Y_ROWS, NZ)),
-        in_specs=[VMEM] * 6,
+        in_specs=[VMEM] * 7,
         out_specs=(VMEM,) * 2,
         compiler_params=params(16),
         name="columns",
-    )(own, rp, ro, rs, band, rf_pair)
+    )(own, rp, ro, ra, rb, band, rf_pair)
     from_chip = send(to_chip, chip_other(peers[1]))
     from_core = send(to_core, core_partner)
     work = (
@@ -783,13 +807,13 @@
     *work_in, rf_third = pl.pallas_call(
         functools.partial(inner_kernel, peers),
         out_shape=work + (sds(CY, 8, NZ),),
-        in_specs=[VMEM] * 7,
+        in_specs=[VMEM] * 8,
         out_specs=(VMEM,) * 6,
         scratch_shapes=fields + [pltpu.VMEM((CY * NZ, SLOTS), bf16)],
         compiler_params=params(16),
         cost_estimate=pl.CostEstimate(flops=4 * 10**9, bytes_accessed=2**21, transcendentals=0),
         name="inner",
-    )(own, rp, ro, rs, f2, ft2, rf_pair)
+    )(own, rp, ro, ra, rb, f2, ft2, rf_pair)
     side_scratch = fields + [
         pltpu.VMEM((3, 8, 8, NZ), f32),
         pltpu.VMEM((24, NZ), f32),

time: 20.7 us -> 21.6 us (1.043)
  the two profiles are of different devices: /device:TPU:1 before, /device:TPU:0 now
where the time goes in v13:
time: 21.6 us; the launch traced here: 21.4 us
  starting transfers between devices  9.85 us (46%)
  Pallas kernels  8.36 us (39%)
  waiting for transfers between devices  2.48 us (11%)
  between operations  0.73 us (3%)
    ppermute x7, starting transfers between devices, send(): return lax.ppermute(value, ('gx', 'gy'), pairs)  9.85 us
    ppermute x7, waiting for transfers between devices, send(): return lax.ppermute(value, ('gx', 'gy'), pairs)  2.48 us
    pallas_call x1, Pallas kernels, per_device(): pl.pallas_call(functools.partial(main_kernel, peers), out_shape=(sds(125,...  2.45 us
    pallas_call x1, Pallas kernels, per_device(): pl.pallas_call(functools.partial(inner_kernel, peers), out_shape=work + (...  1.79 us
    pallas_call x1, Pallas kernels, per_device(): pl.pallas_call(core_kernel, out_shape=(sds(125, NZ),) + work, in_specs=[V...  1.77 us
    pallas_call x1, Pallas kernels, per_device(): pl.pallas_call(fault_kernel, out_shape=(pieces, pieces, sds(2, CY, 8, NZ)...  1.23 us
    pallas_call x1, Pallas kernels, per_device(): pl.pallas_call(functools.partial(pack_kernel, peers), out_shape=(sds(224,...  1.04 us
  transfers between devices with their start and end apart: 7, of which 2 were waited for; matrix products, arithmetic and copies ran while one was open for 0% of the time, Pallas kernels for 27%

profile of v13, /device:TPU:0, one launch (start us, length us, event | category | flops | bytes accessed | tf_op | source)
XLA Modules:
  0.0 21.4 jit_solution(9372110981253556374)
XLA Ops:
  0.0 2.9 %collective-permute-start.1 = (s32[1,1,512]{2,1,0:T(1,128)}, s32[1,1,512]{2,1,0:T(1,128)S(1)}, u32[]{:S(2)}, u32[]{:S(2)}) collective-permute-start(s32[1,1,512]{2,1,0:T(1,128)} %refs_2_.1), channel_id=1, source_target_pairs={{0,4},{1,5},{2,6},{3,7},{4,0},{5,1},{6,2},{7,3},{8,12},{9,13},{10,... | collective-permute-start | bytes 6152 | tf_op jit(solution)/shard_map/ppermute | solution.py:685
  3.6 1.0 %pack.1 = (f32[224,128]{1,0:T(8,128)S(1)}, f32[72,128]{1,0:T(8,128)S(1)}, f32[8,128]{1,0:T(8,128)S(1)}) custom-call(s32[1,1]{1,0:T(1,128)S(6)} %copy.26.count, f32[13,2,1024]{2,1,0:T(2,128)} %refs_0_.1, f32[2,1024]{1,0:T(2,128)} %refs_1_.1, s32[1,1,512]{2,1,0:T(1,128)} %refs_2_.1, f32[1,1,512]{2,1,0:T(1,128)} %refs_3_.1), custom_call_target="tpu_custom_call" | custom-call | tf_op jit(solution)/shard_map/pack/pallas_call | solution.py:747
  4.6 0.1 collective-permute-start
  4.7 0.0 collective-permute-done.1.cells
  4.7 0.1 collective-permute-start.2
  4.8 1.2 %faults.1 = (bf16[8,256,128]{2,1,0:T(8,128)(2,1)S(1)}, bf16[8,256,128]{2,1,0:T(8,128)(2,1)S(1)}, f32[2,8,8,128]{3,2,1,0:T(8,128)S(1)}, f32[2,24,128]{2,1,0:T(8,128)S(1)}, f32[72,128]{1,0:T(8,128)S(1)}) custom-call(f32[8,128]{1,0:T(8,128)S(1)} %get-tuple-element.29.tile, f32[72,128]{1,0:T(8,128)S(1)} %get-tuple-element.30.plane, ...), custom_call_target="tpu_custom_call" | custom-call | flops 2000000000 | bytes 2097152 | tf_op jit(solution)/shard_map/faults/pallas_call | solution.py:768
  6.1 3.6 %collective-permute-start.4 = (f32[72,128]{1,0:T(8,128)S(1)}, f32[72,128]{1,0:T(8,128)S(1)}, u32[]{:S(2)}, u32[]{:S(2)}) collective-permute-start(f32[72,128]{1,0:T(8,128)S(1)} %get-tuple-element.31), channel_id=1, source_target_pairs={{0,4},{1,5},{2,6},{3,7},{4,0},{5,1},{6,2},{7,3},{8,16},{9,17},{10,... | collective-permute-start | bytes 110600 | tf_op jit(solution)/shard_map/ppermute | solution.py:685
  9.6 1.5 %collective-permute-start.3 = (f32[72,128]{1,0:T(8,128)S(1)}, f32[72,128]{1,0:T(8,128)S(1)}, u32[]{:S(2)}, u32[]{:S(2)}) collective-permute-start(f32[72,128]{1,0:T(8,128)S(1)} %get-tuple-element.31), channel_id=1, source_target_pairs={{0,8},{1,9},{2,10},{3,11},{4,12},{5,13},{6,14},{7,15},{8,0},{9,1},... | collective-permute-start | bytes 110600 | tf_op jit(solution)/shard_map/ppermute | solution.py:685
  11.1 0.4 %collective-permute-done.4.rb = f32[72,128]{1,0:T(8,128)S(1)} collective-permute-done((f32[72,128]{1,0:T(8,128)S(1)}, f32[72,128]{1,0:T(8,128)S(1)}, u32[]{:S(2)}, u32[]{:S(2)}) %collective-permute-start.4) | collective-permute-done | bytes 36896 | tf_op jit(solution)/shard_map/ppermute | solution.py:685
  11.6 2.0 %collective-permute-done.3.ra = f32[72,128]{1,0:T(8,128)S(1)} collective-permute-done((f32[72,128]{1,0:T(8,128)S(1)}, f32[72,128]{1,0:T(8,128)S(1)}, u32[]{:S(2)}, u32[]{:S(2)}) %collective-permute-start.3) | collective-permute-done | bytes 36896 | tf_op jit(solution)/shard_map/ppermute | solution.py:685
  13.6 0.0 collective-permute-done.rp
  13.6 0.0 collective-permute-done.2.ro
  13.6 0.1 columns.1
  13.7 1.2 %collective-permute-start.5 = (f32[280,128]{1,0:T(8,128)S(1)}, f32[280,128]{1,0:T(8,128)S(1)}, u32[]{:S(2)}, u32[]{:S(2)}) collective-permute-start(f32[280,128]{1,0:T(8,128)S(1)} %get-tuple-element.34), channel_id=1, source_target_pairs={{0,4},{1,2},{2,1},{3,7},{4,0},{5,6},{6,5},{7,3},{8,12},{9,10},{10,... | collective-permute-start | bytes 430088 | tf_op jit(solution)/shard_map/ppermute | solution.py:685
  14.9 0.5 %collective-permute-start.6 = (f32[280,128]{1,0:T(8,128)S(1)}, f32[280,128]{1,0:T(8,128)S(1)}, u32[]{:S(2)}, u32[]{:S(2)}) collective-permute-start(f32[280,128]{1,0:T(8,128)S(1)} %get-tuple-element.38), channel_id=1, source_target_pairs={{0,1},{1,0},{2,3},{3,2},{4,5},{5,4},{6,7},{7,6},{8,9},{9,8},{10,11... | collective-permute-start | bytes 430088 | tf_op jit(solution)/shard_map/ppermute | solution.py:685
  15.4 1.8 %inner.1 = (f32[2352,128]{1,0:T(8,128)S(1)}, f32[2352,128]{1,0:T(8,128)S(1)}, f32[6,12,4,8,128]{4,3,2,1,0:T(8,128)S(1)}, f32[4,10,3,3,8,128]{5,4,3,2,1,0:T(8,128...) custom-call(f32[224,128]{1,0:T(8,128)S(1)} %get-tuple-element.28.own, ...), custom_call_target="tpu_custom_call" | custom-call | flops 4000000000 | bytes 2097152 | tf_op jit(solution)/shard_map/inner/pallas_call | solution.py:807
  17.2 0.0 collective-permute-done.6.halo
  17.2 1.8 %core_side.1 = (f32[125,128]{1,0:T(8,128)S(1)}, f32[2352,128]{1,0:T(8,128)S(1)}, f32[2352,128]{1,0:T(8,128)S(1)}, f32[6,12,4,8,128]{4,3,2,1,0:T(8,128)S(1)}, f32...) custom-call(f32[280,128]{1,0:T(8,128)S(1)} %collective-permute-done., ...), custom_call_target="tpu_custom_call", output_to_operand_aliasing={{1}: (5, {}), {2}: (6, {}), {3}: (7, {}), {4}: (8, {}), {5}... | custom-call | flops 2000000000 | bytes 1048576 | tf_op jit(solution)/shard_map/core_side/pallas_call | solution.py:822
  19.0 0.0 collective-permute-done.5.halo
  19.0 2.5 %chip_side.1 = (f32[125,1,256]{2,1,0:T(1,128)}, f32[2352,128]{1,0:T(8,128)S(1)}, f32[2352,128]{1,0:T(8,128)S(1)}, f32[6,12,4,8,128]{4,3,2,1,0:T(8,128)S(1)}, f32...) custom-call(f32[280,128]{1,0:T(8,128)S(1)} %collective-permute-done., ...), custom_call_target="tpu_custom_call", output_to_operand_aliasing={{1}: (6, {}), {2}: (7, {}), {3}: (8, {}), {4}: (9, {}), {5}... | custom-call | tf_op jit(solution)/shard_map/chip_side/pallas_call | solution.py:833
  (1 shorter events, 0.0 us)
Async XLA Ops:
  0.0 4.7 %collective-permute-start.1 = (s32[1,1,512]{2,1,0:T(1,128)}, s32[1,1,512]{2,1,0:T(1,128)S(1)}, u32[]{:S(2)}, u32[]{:S(2)}) collective-permute-start(s32[1,1,512]{2,1,0:T(1,128)} %refs_2_.1), channel_id=1, source_target_pairs={{0,4},{1,5},{2,6},{3,7},{4,0},{5,1},{6,2},{7,3},{8,12},{9,13},{10,... | collective-permute-start | bytes 6152 | tf_op jit(solution)/shard_map/ppermute | solution.py:685
  4.6 9.0 %collective-permute-start = (f32[224,128]{1,0:T(8,128)S(1)}, f32[224,128]{1,0:T(8,128)S(1)}, u32[]{:S(2)}, u32[]{:S(2)}) collective-permute-start(f32[224,128]{1,0:T(8,128)S(1)} %get-tuple-element.28.own), channel_id=1, source_target_pairs={{0,4},{1,5},{2,6},{3,7},{4,0},{5,1},{6,2},{7,3},{8,12},{9,13},{10,... | collective-permute-start | bytes 344072 | tf_op jit(solution)/shard_map/ppermute | solution.py:685
  4.7 8.9 %collective-permute-start.2 = (f32[240,128]{1,0:T(8,128)S(1)}, f32[240,128]{1,0:T(8,128)S(1)}, u32[]{:S(2)}, u32[]{:S(2)}) collective-permute-start(f32[240,128]{1,0:T(8,128)S(1)} %join.1), channel_id=1, source_target_pairs={{0,1},{1,0},{2,3},{3,2},{4,8},{5,9},{6,10},{7,11},{8,4},{9,5},{10,... | collective-permute-start | bytes 368648 | tf_op jit(solution)/shard_map/ppermute | solution.py:685
  6.1 5.5 %collective-permute-start.4 = (f32[72,128]{1,0:T(8,128)S(1)}, f32[72,128]{1,0:T(8,128)S(1)}, u32[]{:S(2)}, u32[]{:S(2)}) collective-permute-start(f32[72,128]{1,0:T(8,128)S(1)} %get-tuple-element.31), channel_id=1, source_target_pairs={{0,4},{1,5},{2,6},{3,7},{4,0},{5,1},{6,2},{7,3},{8,16},{9,17},{10,... | collective-permute-start | bytes 110600 | tf_op jit(solution)/shard_map/ppermute | solution.py:685
  9.6 4.0 %collective-permute-start.3 = (f32[72,128]{1,0:T(8,128)S(1)}, f32[72,128]{1,0:T(8,128)S(1)}, u32[]{:S(2)}, u32[]{:S(2)}) collective-permute-start(f32[72,128]{1,0:T(8,128)S(1)} %get-tuple-element.31), channel_id=1, source_target_pairs={{0,8},{1,9},{2,10},{3,11},{4,12},{5,13},{6,14},{7,15},{8,0},{9,1},... | collective-permute-start | bytes 110600 | tf_op jit(solution)/shard_map/ppermute | solution.py:685
  13.7 5.3 %collective-permute-start.5 = (f32[280,128]{1,0:T(8,128)S(1)}, f32[280,128]{1,0:T(8,128)S(1)}, u32[]{:S(2)}, u32[]{:S(2)}) collective-permute-start(f32[280,128]{1,0:T(8,128)S(1)} %get-tuple-element.34), channel_id=1, source_target_pairs={{0,4},{1,2},{2,1},{3,7},{4,0},{5,6},{6,5},{7,3},{8,12},{9,10},{10,... | collective-permute-start | bytes 430088 | tf_op jit(solution)/shard_map/ppermute | solution.py:685
  14.9 2.3 %collective-permute-start.6 = (f32[280,128]{1,0:T(8,128)S(1)}, f32[280,128]{1,0:T(8,128)S(1)}, u32[]{:S(2)}, u32[]{:S(2)}) collective-permute-start(f32[280,128]{1,0:T(8,128)S(1)} %get-tuple-element.38), channel_id=1, source_target_pairs={{0,1},{1,0},{2,3},{3,2},{4,5},{5,4},{6,7},{7,6},{8,9},{9,8},{10,11... | collective-permute-start | bytes 430088 | tf_op jit(solution)/shard_map/ppermute | solution.py:685

commit v14 on v12

--- a/solution.py
+++ b/solution.py
@@ -56,7 +56,7 @@
 
 
 def pack_kernel(peers, count, *refs):
-    sources, (block, plane), targets, sems = refs[:4], refs[4:6], refs[6:10], refs[10]
+    sources, (block, plane, tile), targets, sems = refs[:4], refs[4:7], refs[7:11], refs[11]
     copies = [
         pltpu.make_async_copy(src, dst, sems.at[k])
         for k, (src, dst) in enumerate(zip(sources, targets))
@@ -102,11 +102,10 @@
                 block[base : base + 8, :] = jnp.where(keep, block[base : base + 8, :], 0.0)
     live = count[0, 0]
     lane = lax.broadcasted_iota(jnp.int32, (1, NZ), 1)
-    base = 2 * PER * 8
     for r in range(4):
         lanes = slice(r * NZ, (r + 1) * NZ)
-        block[base + r : base + r + 1, :] = cells[0, :, lanes].astype(f32)
-        block[base + 4 + r : base + 5 + r, :] = jnp.where(
+        tile[r : r + 1, :] = cells[0, :, lanes].astype(f32)
+        tile[4 + r : 5 + r, :] = jnp.where(
             lane + r * NZ < live, ftrans[0, :, lanes], 0.0
         )
     plane[...] = block[(PER + 4) * 8 : (PER + 13) * 8, :]
@@ -118,8 +117,10 @@
     ).astype(f32)
 
 
-def join_kernel(own, cells, joined):
-    joined[0:232, :] = own[...]
+def join_kernel(own, tile, plane, cells, joined, plane_out):
+    plane_out[...] = plane[...]
+    joined[0:224, :] = own[...]
+    joined[224:232, :] = tile[...]
     joined[232:236, :] = partner_rows(cells)
     joined[236:240, :] = jnp.zeros((4, NZ), f32)
 
@@ -254,16 +255,16 @@
     return f2, ft2, dot_nn(one2, ft2), dot_nn(one2, f2)
 
 
-def fault_kernel(own, cells, f2, ft2, rf, band, far2, hot, both):
-    partner, live = slot_columns([partner_rows(cells), own[228:232, :]])
+def fault_kernel(tile, cells, f2, ft2, rf, band, far2, hot, both):
+    partner, live = slot_columns([partner_rows(cells), tile[4:8, :]])
     fill_far(far2, partner, live)
-    fill_hot(hot, flat_cells(own[224:228, :]), range(CY))
+    fill_hot(hot, flat_cells(tile[0:4, :]), range(CY))
     both[...] = dot_nn(hot[...], far2[...])
     for y in range(CY):
         f2[y], ft2[y], rf[0, y], rf[1, y] = pair_matrix(both[y * NZ : (y + 1) * NZ, :])
     for k, y in enumerate((0, CY - 1)):
         band[k] = diagonals(
-            hot[y * NZ : (y + 1) * NZ, :], own[224:228, :], partner_rows(cells), own[228:232, :]
+            hot[y * NZ : (y + 1) * NZ, :], tile[0:4, :], partner_rows(cells), tile[4:8, :]
         )
 
 
@@ -721,25 +722,25 @@
         pltpu.with_memory_space_constraint(array, pltpu.HBM)
         for array in (trans, storage, fault_cells, fault_trans)
     ]
-    own, plane = pl.pallas_call(
+    own, plane, tile = pl.pallas_call(
         functools.partial(pack_kernel, peers),
-        out_shape=(sds(232, NZ), sds(72, NZ)),
+        out_shape=(sds(224, NZ), sds(72, NZ), sds(8, NZ)),
         in_specs=[pl.BlockSpec(memory_space=pltpu.SMEM)] + [HBM] * 4,
-        out_specs=(VMEM,) * 2,
+        out_specs=(VMEM,) * 3,
         scratch_shapes=[pltpu.VMEM(array.shape, array.dtype) for array in sources]
         + [pltpu.SemaphoreType.DMA((4,))],
         compiler_params=params(16),
         name="pack",
     )(fault_count, *sources)
-    rs = send(plane, x_ahead(peers[0]))
-    joined = pl.pallas_call(
+    joined, plane = pl.pallas_call(
         join_kernel,
-        out_shape=sds(240, NZ),
-        in_specs=[VMEM] * 2,
-        out_specs=VMEM,
+        out_shape=(sds(240, NZ), sds(72, NZ)),
+        in_specs=[VMEM] * 4,
+        out_specs=(VMEM,) * 2,
         compiler_params=params(16),
         name="join",
-    )(own, cells)
+    )(own, tile, plane, cells)
+    rs = send(plane, x_ahead(peers[0]))
     ro = send(joined, x_other(peers[0]))
     rp = send(own, x_partner)
     pieces = sds(CY, 2 * NZ, NZ, dtype=bf16)
@@ -756,7 +757,7 @@
         compiler_params=params(16),
         cost_estimate=pl.CostEstimate(flops=2 * 10**9, bytes_accessed=2**21, transcendentals=0),
         name="faults",
-    )(own, cells)
+    )(tile, cells)
     to_core, to_chip = pl.pallas_call(
         functools.partial(column_kernel, peers),
         out_shape=(sds(Y_ROWS, NZ), sds(Y_ROWS, NZ)),

time: 20.7 us -> 20.6 us (level)
  transfers between devices with their start and end apart: 6 -> 6, of which waited for: 2 -> 1; matrix products, arithmetic and copies ran while one was open for 0% -> 0% of each run, Pallas kernels for 29% -> 29%
where the time goes in v14:
time: 20.6 us; the launch traced here: 20.5 us
  starting transfers between devices  10.7 us (52%)
  Pallas kernels  8.42 us (41%)
  between operations  0.72 us (3%)
  waiting for transfers between devices  0.64 us (3%)
    ppermute x6, starting transfers between devices, send(): return lax.ppermute(value, ('gx', 'gy'), pairs)  10.7 us
    pallas_call x1, Pallas kernels, per_device(): pl.pallas_call(functools.partial(main_kernel, peers), out_shape=(sds(125,...  2.46 us
    pallas_call x1, Pallas kernels, per_device(): pl.pallas_call(core_kernel, out_shape=(sds(125, NZ),) + work, in_specs=[V...  1.81 us
    pallas_call x1, Pallas kernels, per_device(): pl.pallas_call(functools.partial(inner_kernel, peers), out_shape=work + (...  1.81 us
    pallas_call x1, Pallas kernels, per_device(): pl.pallas_call(fault_kernel, out_shape=(pieces, pieces, sds(2, CY, 8, NZ)...  1.22 us
    pallas_call x1, Pallas kernels, per_device(): pl.pallas_call(functools.partial(pack_kernel, peers), out_shape=(sds(224,...  1.04 us
    ppermute x6, waiting for transfers between devices, send(): return lax.ppermute(value, ('gx', 'gy'), pairs)  0.64 us
  transfers between devices with their start and end apart: 6, of which 1 were waited for; matrix products, arithmetic and copies ran while one was open for 0% of the time, Pallas kernels for 29%

profile of v14, /device:TPU:1, one launch (start us, length us, event | category | flops | bytes accessed | tf_op | source)
XLA Modules:
  0.0 20.5 jit_solution(2959545609226127722)
XLA Ops:
  0.0 2.0 %collective-permute-start.1 = (s32[1,1,512]{2,1,0:T(1,128)}, s32[1,1,512]{2,1,0:T(1,128)S(1)}, u32[]{:S(2)}, u32[]{:S(2)}) collective-permute-start(s32[1,1,512]{2,1,0:T(1,128)} %refs_2_.1), channel_id=1, source_target_pairs={{0,4},{1,5},{2,6},{3,7},{4,0},{5,1},{6,2},{7,3},{8,12},{9,13},{10,... | collective-permute-start | bytes 6152 | tf_op jit(solution)/shard_map/ppermute | solution.py:675
  2.7 1.0 %pack.1 = (f32[224,128]{1,0:T(8,128)S(1)}, f32[72,128]{1,0:T(8,128)S(1)}, f32[8,128]{1,0:T(8,128)S(1)}) custom-call(s32[1,1]{1,0:T(1,128)S(6)} %copy.26.count, f32[13,2,1024]{2,1,0:T(2,128)} %refs_0_.1, f32[2,1024]{1,0:T(2,128)} %refs_1_.1, s32[1,1,512]{2,1,0:T(1,128)} %refs_2_.1, f32[1,1,512]{2,1,0:T(1,128)} %refs_3_.1), custom_call_target="tpu_custom_call" | custom-call | tf_op jit(solution)/shard_map/pack/pallas_call | solution.py:725
  3.7 0.1 collective-permute-start
  3.8 0.0 collective-permute-done.1.cells
  3.9 1.6 %collective-permute-start.3 = (f32[72,128]{1,0:T(8,128)S(1)}, f32[72,128]{1,0:T(8,128)S(1)}, u32[]{:S(2)}, u32[]{:S(2)}) collective-permute-start(f32[72,128]{1,0:T(8,128)S(1)} %get-tuple-element.33), channel_id=1, source_target_pairs={{0,8},{1,9},{2,10},{3,11},{4,12},{5,13},{6,14},{7,15},{8,16},{9,17... | collective-permute-start | bytes 110600 | tf_op jit(solution)/shard_map/ppermute | solution.py:675
  5.4 1.5 %collective-permute-start.2 = (f32[240,128]{1,0:T(8,128)S(1)}, f32[240,128]{1,0:T(8,128)S(1)}, u32[]{:S(2)}, u32[]{:S(2)}) collective-permute-start(f32[240,128]{1,0:T(8,128)S(1)} %get-tuple-element.32), channel_id=1, source_target_pairs={{0,1},{1,0},{2,3},{3,2},{4,8},{5,9},{6,10},{7,11},{8,4},{9,5},{10,... | collective-permute-start | bytes 368648 | tf_op jit(solution)/shard_map/ppermute | solution.py:675
  7.0 1.2 %faults.1 = (bf16[8,256,128]{2,1,0:T(8,128)(2,1)S(1)}, bf16[8,256,128]{2,1,0:T(8,128)(2,1)S(1)}, f32[2,8,8,128]{3,2,1,0:T(8,128)S(1)}, f32[2,24,128]{2,1,0:T(8,128)S(1)}) custom-call(f32[8,128]{1,0:T(8,128)S(1)} %get-tuple-element.30.tile, s32[1,1,512]{2,1,0:T(1,128)S(1)} %collective-permute-done.1.cells), custom_call_target="tpu_custom_call" | custom-call | flops 2000000000 | bytes 2097152 | tf_op jit(solution)/shard_map/faults/pallas_call | solution.py:747
  8.2 0.6 %collective-permute-done.3.rs = f32[72,128]{1,0:T(8,128)S(1)} collective-permute-done((f32[72,128]{1,0:T(8,128)S(1)}, f32[72,128]{1,0:T(8,128)S(1)}, u32[]{:S(2)}, u32[]{:S(2)}) %collective-permute-start.3) | collective-permute-done | bytes 36896 | tf_op jit(solution)/shard_map/ppermute | solution.py:675
  8.8 0.0 collective-permute-done.rp
  8.8 0.0 collective-permute-done.2.ro
  8.8 0.1 columns.1
  8.9 3.6 %collective-permute-start.4 = (f32[280,128]{1,0:T(8,128)S(1)}, f32[280,128]{1,0:T(8,128)S(1)}, u32[]{:S(2)}, u32[]{:S(2)}) collective-permute-start(f32[280,128]{1,0:T(8,128)S(1)} %get-tuple-element.36), channel_id=1, source_target_pairs={{0,4},{1,2},{2,1},{3,7},{4,0},{5,6},{6,5},{7,3},{8,12},{9,10},{10,... | collective-permute-start | bytes 430088 | tf_op jit(solution)/shard_map/ppermute | solution.py:675
  12.5 1.9 %collective-permute-start.5 = (f32[280,128]{1,0:T(8,128)S(1)}, f32[280,128]{1,0:T(8,128)S(1)}, u32[]{:S(2)}, u32[]{:S(2)}) collective-permute-start(f32[280,128]{1,0:T(8,128)S(1)} %get-tuple-element.40), channel_id=1, source_target_pairs={{0,1},{1,0},{2,3},{3,2},{4,5},{5,4},{6,7},{7,6},{8,9},{9,8},{10,11... | collective-permute-start | bytes 430088 | tf_op jit(solution)/shard_map/ppermute | solution.py:675
  14.4 1.8 %inner.1 = (f32[2352,128]{1,0:T(8,128)S(1)}, f32[2352,128]{1,0:T(8,128)S(1)}, f32[6,12,4,8,128]{4,3,2,1,0:T(8,128)S(1)}, f32[4,10,3,3,8,128]{5,4,3,2,1,0:T(8,128...) custom-call(f32[224,128]{1,0:T(8,128)S(1)} %get-tuple-element.29.own, ...), custom_call_target="tpu_custom_call" | custom-call | flops 4000000000 | bytes 2097152 | tf_op jit(solution)/shard_map/inner/pallas_call | solution.py:784
  16.2 0.0 collective-permute-done.5.halo
  16.2 1.8 %core_side.1 = (f32[125,128]{1,0:T(8,128)S(1)}, f32[2352,128]{1,0:T(8,128)S(1)}, f32[2352,128]{1,0:T(8,128)S(1)}, f32[6,12,4,8,128]{4,3,2,1,0:T(8,128)S(1)}, f32...) custom-call(f32[280,128]{1,0:T(8,128)S(1)} %collective-permute-done., ...), custom_call_target="tpu_custom_call", output_to_operand_aliasing={{1}: (5, {}), {2}: (6, {}), {3}: (7, {}), {4}: (8, {}), {5}... | custom-call | flops 2000000000 | bytes 1048576 | tf_op jit(solution)/shard_map/core_side/pallas_call | solution.py:799
  18.0 0.0 collective-permute-done.4.halo
  18.0 2.5 %chip_side.1 = (f32[125,1,256]{2,1,0:T(1,128)}, f32[2352,128]{1,0:T(8,128)S(1)}, f32[2352,128]{1,0:T(8,128)S(1)}, f32[6,12,4,8,128]{4,3,2,1,0:T(8,128)S(1)}, f32...) custom-call(f32[280,128]{1,0:T(8,128)S(1)} %collective-permute-done., ...), custom_call_target="tpu_custom_call", output_to_operand_aliasing={{1}: (6, {}), {2}: (7, {}), {3}: (8, {}), {4}: (9, {}), {5}... | custom-call | tf_op jit(solution)/shard_map/chip_side/pallas_call | solution.py:810
  (1 shorter events, 0.0 us)
Async XLA Ops:
  0.0 3.8 %collective-permute-start.1 = (s32[1,1,512]{2,1,0:T(1,128)}, s32[1,1,512]{2,1,0:T(1,128)S(1)}, u32[]{:S(2)}, u32[]{:S(2)}) collective-permute-start(s32[1,1,512]{2,1,0:T(1,128)} %refs_2_.1), channel_id=1, source_target_pairs={{0,4},{1,5},{2,6},{3,7},{4,0},{5,1},{6,2},{7,3},{8,12},{9,13},{10,... | collective-permute-start | bytes 6152 | tf_op jit(solution)/shard_map/ppermute | solution.py:675
  3.7 5.1 %collective-permute-start = (f32[224,128]{1,0:T(8,128)S(1)}, f32[224,128]{1,0:T(8,128)S(1)}, u32[]{:S(2)}, u32[]{:S(2)}) collective-permute-start(f32[224,128]{1,0:T(8,128)S(1)} %get-tuple-element.29.own), channel_id=1, source_target_pairs={{0,4},{1,5},{2,6},{3,7},{4,0},{5,1},{6,2},{7,3},{8,12},{9,13},{10,... | collective-permute-start | bytes 344072 | tf_op jit(solution)/shard_map/ppermute | solution.py:675
  3.9 4.9 %collective-permute-start.3 = (f32[72,128]{1,0:T(8,128)S(1)}, f32[72,128]{1,0:T(8,128)S(1)}, u32[]{:S(2)}, u32[]{:S(2)}) collective-permute-start(f32[72,128]{1,0:T(8,128)S(1)} %get-tuple-element.33), channel_id=1, source_target_pairs={{0,8},{1,9},{2,10},{3,11},{4,12},{5,13},{6,14},{7,15},{8,16},{9,17... | collective-permute-start | bytes 110600 | tf_op jit(solution)/shard_map/ppermute | solution.py:675
  5.4 3.4 %collective-permute-start.2 = (f32[240,128]{1,0:T(8,128)S(1)}, f32[240,128]{1,0:T(8,128)S(1)}, u32[]{:S(2)}, u32[]{:S(2)}) collective-permute-start(f32[240,128]{1,0:T(8,128)S(1)} %get-tuple-element.32), channel_id=1, source_target_pairs={{0,1},{1,0},{2,3},{3,2},{4,8},{5,9},{6,10},{7,11},{8,4},{9,5},{10,... | collective-permute-start | bytes 368648 | tf_op jit(solution)/shard_map/ppermute | solution.py:675
  8.9 9.1 %collective-permute-start.4 = (f32[280,128]{1,0:T(8,128)S(1)}, f32[280,128]{1,0:T(8,128)S(1)}, u32[]{:S(2)}, u32[]{:S(2)}) collective-permute-start(f32[280,128]{1,0:T(8,128)S(1)} %get-tuple-element.36), channel_id=1, source_target_pairs={{0,4},{1,2},{2,1},{3,7},{4,0},{5,6},{6,5},{7,3},{8,12},{9,10},{10,... | collective-permute-start | bytes 430088 | tf_op jit(solution)/shard_map/ppermute | solution.py:675
  12.5 3.7 %collective-permute-start.5 = (f32[280,128]{1,0:T(8,128)S(1)}, f32[280,128]{1,0:T(8,128)S(1)}, u32[]{:S(2)}, u32[]{:S(2)}) collective-permute-start(f32[280,128]{1,0:T(8,128)S(1)} %get-tuple-element.40), channel_id=1, source_target_pairs={{0,1},{1,0},{2,3},{3,2},{4,5},{5,4},{6,7},{7,6},{8,9},{9,8},{10,11... | collective-permute-start | bytes 430088 | tf_op jit(solution)/shard_map/ppermute | solution.py:675

commit v15 on v14

--- a/solution.py
+++ b/solution.py
@@ -255,7 +255,20 @@
     return f2, ft2, dot_nn(one2, ft2), dot_nn(one2, f2)
 
 
-def fault_kernel(tile, cells, f2, ft2, rf, band, far2, hot, both):
+def fill_collect(collect):
+    kz = lax.broadcasted_iota(jnp.int32, (512, NZ), 0)
+    kout = lax.broadcasted_iota(jnp.int32, (512, NZ), 1)
+    z_in = kz & 127
+    is_oth = ((kz >> 7) & 1) == 1
+    target = jnp.where(
+        is_oth, (z_in >> 1) + jnp.where((z_in & 1) == 0, -1, 1), z_in >> 1
+    )
+    fits = (target == (kout & 63)) & ((kz >> 8) == (kout >> 6))
+    collect[...] = jnp.where(fits, 1.0, 0.0).astype(bf16)
+
+
+def fault_kernel(tile, cells, f2, ft2, rf, band, collect, far2, hot, both):
+    fill_collect(collect)
     partner, live = slot_columns([partner_rows(cells), tile[4:8, :]])
     fill_far(far2, partner, live)
     fill_hot(hot, flat_cells(tile[0:4, :]), range(CY))
@@ -358,7 +371,7 @@
             qc[at : at + count, :] = value
 
 
-def spread(here, qc, inv, qe, rf_at, columns, count):
+def spread(here, qc, inv, qe, rf_at, columns):
     z8 = lax.broadcasted_iota(jnp.int32, (8, NZ), 1)
     e8 = lax.broadcasted_iota(jnp.int32, (8, NZ), 0)
     beside = jnp.where((z8 & 1) == 0, z8 - 1, z8 + 1)
@@ -366,24 +379,19 @@
     mask_oth = jnp.where(e8 == colour(beside + 10), 1.0, 0.0)
     rows5 = jnp.where(e8 < 5, 1.0, 0.0)
 
-    def one(k, carry):
-        c = columns(k)
+    for c in columns:
         for p in range(6):
             for lat in range(4):
                 at = (p * 8 + 2 * lat) * 16 + c
-                qe[p, c, lat] = (
-                    qc[pl.ds(at, 1), :] * mask_own + qc[pl.ds(at + 16, 1), :] * mask_oth
-                )
+                qe[p, c, lat] = qc[at : at + 1, :] * mask_own + qc[at + 16 : at + 17, :] * mask_oth
         for k, plane in enumerate(here.p_fault):
             qe[plane, c, 2] = qe[plane, c, 2] + rf_at(k, c) * (
                 inv[pl.ds(plane * 16 + c, 1), :] * rows5
             )
-        return carry
-
-    lax.fori_loop(0, count, one, 0)
-
-
-def apply_column(w, wr, diag, qe, ap, p, y, odd_x, odd_y):
+
+
+def apply_column(w, wr, diag, qe, ap, p, y):
+    odd_x, odd_y = p % 2, y % 2
     acc = {}
     for dx in (-1, 0, 1):
         for dy in (-1, 0, 1):
@@ -401,14 +409,14 @@
                 else:
                     at = ((p + 1 + dx) * PER + OFFSET[-dx, -dy, -dz]) * ROWS + y + 1 + dy
                     ref = w
-                wt = ref[pl.ds(at, 1), :]
+                wt = ref[at : at + 1, :]
                 for lat in range(4):
                     lx = oth_x if lat >= 2 else own_x
                     ly = oth_y if lat % 2 else own_y
                     value = wt * q[lat]
                     key = (lx, ly, dz)
                     acc[key] = acc[key] + value if key in acc else value
-    centre = diag[pl.ds(p * 16 + y, 1), :]
+    centre = diag[p * 16 + y : p * 16 + y + 1, :]
     for lx in (-1, 0, 1):
         for ly in (-1, 0, 1):
             total = acc[lx, ly, 0]
@@ -532,16 +540,11 @@
     roll_weights(w, wr, 3, 8)
     smooth(w, wr, fd, qc, inv, diag, 2, 8)
     spread(
-        here, qc, inv, qe, lambda k, c: rf_third[c - 2] if k == 2 else rf_pair[k, c - 2], lambda k: k + 3, 6
+        here, qc, inv, qe, lambda k, c: rf_third[c - 2] if k == 2 else rf_pair[k, c - 2], range(3, 9)
     )
-
-    def pair(k, carry):
-        for p in range(1, 5):
-            apply_column(w, wr, diag, qe, ap, p, 2 * k + 4, p % 2, 0)
-            apply_column(w, wr, diag, qe, ap, p, 2 * k + 5, p % 2, 1)
-        return carry
-
-    lax.fori_loop(0, 2, pair, 0)
+    for p in range(1, 5):
+        for y in INNER:
+            apply_column(w, wr, diag, qe, ap, p, y + 2)
     for y in INNER:
         fault_apply(here, qe, ap, y + 2, f2[y], ft2[y])
     tt[...] = jnp.zeros_like(tt)
@@ -577,12 +580,11 @@
         rf[k, column - first] = value
         fd[pl.ds(here.p_fault[k] * 16 + column, 1), :] = value[5:6, :]
 
-    for column in range(first, first + 8):
-        y = column - 2
-        if 0 <= y < CY:
-            put(column, 0, rf_pair[0, y])
-            put(column, 1, rf_pair[1, y])
-            put(column, 2, rf_third[y])
+    own = (6, 7) if high else (0, 1)
+    for y in own:
+        put(y + 2, 0, rf_pair[0, y])
+        put(y + 2, 1, rf_pair[1, y])
+        put(y + 2, 2, rf_third[y])
     band[0:DIAGONALS, :] = halo[BAND_ROW : BAND_ROW + DIAGONALS, :]
     lists = halo[FAULT_ROW : FAULT_ROW + 12, :]
     fill_hot(hot, flat_cells(lists[0:4]), (0, 1) if high else (CY - 2, CY - 1))
@@ -596,18 +598,11 @@
 
     smooth(w, wr, fd, qc, inv, diag, first, 8)
     spread(
-        here, qc, inv, qe, lambda k, c: rf[k, c - first], lambda k: k + (9 if high else 0), 3
+        here, qc, inv, qe, lambda k, c: rf[k, c - first], (9, 10, 11) if high else (0, 1, 2)
     )
-
-    def planes(k, carry):
-        for odd_x in (1, 0):
-            p = 2 * k + 2 - odd_x
-            for y in (8, 9, 10) if high else (1, 2, 3):
-                apply_column(w, wr, diag, qe, ap, p, y, odd_x, y % 2)
-        return carry
-
-    lax.fori_loop(0, 2, planes, 0)
-    own = (6, 7) if high else (0, 1)
+    for p in range(1, 5):
+        for y in (8, 9, 10) if high else (1, 2, 3):
+            apply_column(w, wr, diag, qe, ap, p, y)
     for y in own:
         fault_apply(here, qe, ap, y + 2, f2[y], ft2[y])
     fault_apply_band(here, qe, ap, 10 if high else 1, band)
@@ -618,23 +613,14 @@
         gather_fault(here, inv, ap, tt, y, ft2[y])
 
 
-def finish(tt, pair, store):
-    kz = lax.broadcasted_iota(jnp.int32, (512, NZ), 0)
-    kout = lax.broadcasted_iota(jnp.int32, (512, NZ), 1)
-    z_in = kz & 127
-    is_oth = ((kz >> 7) & 1) == 1
-    target = jnp.where(
-        is_oth, (z_in >> 1) + jnp.where((z_in & 1) == 0, -1, 1), z_in >> 1
-    )
-    fits = (target == (kout & 63)) & ((kz >> 8) == (kout >> 6))
-    collect = jnp.where(fits, 1.0, 0.0).astype(bf16)
+def finish(tt, pair, collect, store):
     high, low = split(tt[pair].reshape(200, 512))
-    got = (dot_nn(high, collect) + dot_nn(low, collect)) * 0.125
+    got = (dot_nn(high, collect[...]) + dot_nn(low, collect[...])) * 0.125
     for k in range(25):
         store(5 * k, got[8 * k : 8 * k + 5])
 
 
-def core_kernel(halo, f2, ft2, rf_pair, rf_third, *refs):
+def core_kernel(halo, f2, ft2, rf_pair, rf_third, collect, *refs):
     half, work, fields, rest = refs[5], refs[6:11], refs[11:15], refs[15:]
 
     def body(odd):
@@ -643,12 +629,12 @@
         def store(row, value):
             half[row : row + 5, :] = value
 
-        finish(work[4], 0 if odd else 1, store)
+        finish(work[4], 0 if odd else 1, collect, store)
 
     by_parity("gy", body)
 
 
-def main_kernel(peers, halo, f2, ft2, rf_pair, rf_third, half, *refs):
+def main_kernel(peers, halo, f2, ft2, rf_pair, rf_third, collect, half, *refs):
     out, work, fields, rest = refs[5], refs[6:11], refs[11:15], refs[15:]
     halo = Masked(halo, has_other("gy", peers[1]))
 
@@ -660,7 +646,7 @@
             out[row : row + 5, 0, lanes[odd]] = value
             out[row : row + 5, 0, lanes[1 - odd]] = half[row : row + 5, :]
 
-        finish(work[4], odd, store)
+        finish(work[4], odd, collect, store)
 
     by_parity("gy", body)
 
@@ -744,11 +730,17 @@
     ro = send(joined, x_other(peers[0]))
     rp = send(own, x_partner)
     pieces = sds(CY, 2 * NZ, NZ, dtype=bf16)
-    f2, ft2, rf_pair, band = pl.pallas_call(
+    f2, ft2, rf_pair, band, collect = pl.pallas_call(
         fault_kernel,
-        out_shape=(pieces, pieces, sds(2, CY, 8, NZ), sds(2, 24, NZ)),
+        out_shape=(
+            pieces,
+            pieces,
+            sds(2, CY, 8, NZ),
+            sds(2, 24, NZ),
+            sds(512, NZ, dtype=bf16),
+        ),
         in_specs=[VMEM] * 2,
-        out_specs=(VMEM,) * 4,
+        out_specs=(VMEM,) * 5,
         scratch_shapes=[
             pltpu.VMEM((SLOTS, 2 * NZ), bf16),
             pltpu.VMEM((CY * NZ, SLOTS), bf16),
@@ -799,24 +791,24 @@
     half, *work_in = pl.pallas_call(
         core_kernel,
         out_shape=(sds(125, NZ),) + work,
-        in_specs=[VMEM] * 10,
-        out_specs=(VMEM,) * 6,
-        scratch_shapes=side_scratch,
-        input_output_aliases={5 + k: 1 + k for k in range(5)},
-        compiler_params=params(16),
-        cost_estimate=pl.CostEstimate(flops=2 * 10**9, bytes_accessed=2**20, transcendentals=0),
-        name="core_side",
-    )(from_core, f2, ft2, rf_pair, rf_third, *work_in)
-    result, *_ = pl.pallas_call(
-        functools.partial(main_kernel, peers),
-        out_shape=(sds(125, 1, 256),) + work,
         in_specs=[VMEM] * 11,
         out_specs=(VMEM,) * 6,
         scratch_shapes=side_scratch,
         input_output_aliases={6 + k: 1 + k for k in range(5)},
         compiler_params=params(16),
+        cost_estimate=pl.CostEstimate(flops=2 * 10**9, bytes_accessed=2**20, transcendentals=0),
+        name="core_side",
+    )(from_core, f2, ft2, rf_pair, rf_third, collect, *work_in)
+    result, *_ = pl.pallas_call(
+        functools.partial(main_kernel, peers),
+        out_shape=(sds(125, 1, 256),) + work,
+        in_specs=[VMEM] * 12,
+        out_specs=(VMEM,) * 6,
+        scratch_shapes=side_scratch,
+        input_output_aliases={7 + k: 1 + k for k in range(5)},
+        compiler_params=params(16),
         name="chip_side",
-    )(from_chip, f2, ft2, rf_pair, rf_third, half, *work_in)
+    )(from_chip, f2, ft2, rf_pair, rf_third, collect, half, *work_in)
     return result
 
 

time: 20.6 us -> 19.8 us (0.961)
  Pallas kernels: 8.42 us -> 7.78 us
    pallas_call x1, Pallas kernels: 2.46 us -> 2.18 us  [per_device(): pl.pallas_call(functools.partial(main_kernel, peers), out_shape=(sds(125,...]
    pallas_call x1, Pallas kernels: 1.81 us -> 1.53 us  [per_device(): pl.pallas_call(core_kernel, out_shape=(sds(125, NZ),) + work, in_specs=[V...]
    pallas_call x1, Pallas kernels: 1.81 us -> 1.6 us  [per_device(): pl.pallas_call(functools.partial(inner_kernel, peers), out_shape=work + (...]
  transfers between devices with their start and end apart: 6 -> 6, of which waited for: 1 -> 1; matrix products, arithmetic and copies ran while one was open for 0% -> 0% of each run, Pallas kernels for 29% -> 28%
where the time goes in v15:
time: 19.8 us; the launch traced here: 19.7 us
  starting transfers between devices  10.7 us (54%)
  Pallas kernels  7.78 us (39%)
  between operations  0.71 us (4%)
  waiting for transfers between devices  0.5 us (3%)
    ppermute x6, starting transfers between devices, send(): return lax.ppermute(value, ('gx', 'gy'), pairs)  10.7 us
    pallas_call x1, Pallas kernels, per_device(): pl.pallas_call(functools.partial(main_kernel, peers), out_shape=(sds(125,...  2.18 us
    pallas_call x1, Pallas kernels, per_device(): pl.pallas_call(functools.partial(inner_kernel, peers), out_shape=work + (...  1.6 us
    pallas_call x1, Pallas kernels, per_device(): pl.pallas_call(core_kernel, out_shape=(sds(125, NZ),) + work, in_specs=[V...  1.53 us
    pallas_call x1, Pallas kernels, per_device(): pl.pallas_call(fault_kernel, out_shape=(pieces, pieces, sds(2, CY, 8, NZ)...  1.36 us
    pallas_call x1, Pallas kernels, per_device(): pl.pallas_call(functools.partial(pack_kernel, peers), out_shape=(sds(224,...  1.04 us
    ppermute x6, waiting for transfers between devices, send(): return lax.ppermute(value, ('gx', 'gy'), pairs)  0.5 us
  transfers between devices with their start and end apart: 6, of which 1 were waited for; matrix products, arithmetic and copies ran while one was open for 0% of the time, Pallas kernels for 28%

profile of v15, /device:TPU:1, one launch (start us, length us, event | category | flops | bytes accessed | tf_op | source)
XLA Modules:
  0.0 19.7 jit_solution(7165522408233391167)
XLA Ops:
  0.0 2.0 %collective-permute-start.1 = (s32[1,1,512]{2,1,0:T(1,128)}, s32[1,1,512]{2,1,0:T(1,128)S(1)}, u32[]{:S(2)}, u32[]{:S(2)}) collective-permute-start(s32[1,1,512]{2,1,0:T(1,128)} %refs_2_.1), channel_id=1, source_target_pairs={{0,4},{1,5},{2,6},{3,7},{4,0},{5,1},{6,2},{7,3},{8,12},{9,13},{10,... | collective-permute-start | bytes 6152 | tf_op jit(solution)/shard_map/ppermute | solution.py:661
  2.7 1.0 %pack.1 = (f32[224,128]{1,0:T(8,128)S(1)}, f32[72,128]{1,0:T(8,128)S(1)}, f32[8,128]{1,0:T(8,128)S(1)}) custom-call(s32[1,1]{1,0:T(1,128)S(6)} %copy.26.count, f32[13,2,1024]{2,1,0:T(2,128)} %refs_0_.1, f32[2,1024]{1,0:T(2,128)} %refs_1_.1, s32[1,1,512]{2,1,0:T(1,128)} %refs_2_.1, f32[1,1,512]{2,1,0:T(1,128)} %refs_3_.1), custom_call_target="tpu_custom_call" | custom-call | tf_op jit(solution)/shard_map/pack/pallas_call | solution.py:711
  3.7 0.1 collective-permute-start
  3.8 0.0 collective-permute-done.1.cells
  3.9 1.6 %collective-permute-start.3 = (f32[72,128]{1,0:T(8,128)S(1)}, f32[72,128]{1,0:T(8,128)S(1)}, u32[]{:S(2)}, u32[]{:S(2)}) collective-permute-start(f32[72,128]{1,0:T(8,128)S(1)} %get-tuple-element.34), channel_id=1, source_target_pairs={{0,8},{1,9},{2,10},{3,11},{4,12},{5,13},{6,14},{7,15},{8,16},{9,17... | collective-permute-start | bytes 110600 | tf_op jit(solution)/shard_map/ppermute | solution.py:661
  5.4 1.5 %collective-permute-start.2 = (f32[240,128]{1,0:T(8,128)S(1)}, f32[240,128]{1,0:T(8,128)S(1)}, u32[]{:S(2)}, u32[]{:S(2)}) collective-permute-start(f32[240,128]{1,0:T(8,128)S(1)} %get-tuple-element.33), channel_id=1, source_target_pairs={{0,1},{1,0},{2,3},{3,2},{4,8},{5,9},{6,10},{7,11},{8,4},{9,5},{10,... | collective-permute-start | bytes 368648 | tf_op jit(solution)/shard_map/ppermute | solution.py:661
  7.0 1.4 %faults.1 = (bf16[8,256,128]{2,1,0:T(8,128)(2,1)S(1)}, bf16[8,256,128]{2,1,0:T(8,128)(2,1)S(1)}, f32[2,8,8,128]{3,2,1,0:T(8,128)S(1)}, f32[2,24,128]{2,1,0:T(8,128)S(1)}, bf16[512,128]{1,0:T(8,128)(2,1)S(1)}) custom-call(f32[8,128]{1,0:T(8,128)S(1)} %get-tuple-element.31.tile, s32[1,1,512]{2,1,0:T(1,128)S(1)} %collective-permute-done.1.cells), custom_call_target="tpu_custom_call" | custom-call | flops 2000000000 | bytes 2097152 | tf_op jit(solution)/shard_map/faults/pallas_call | solution.py:733
  8.3 0.5 %collective-permute-done.3.rs = f32[72,128]{1,0:T(8,128)S(1)} collective-permute-done((f32[72,128]{1,0:T(8,128)S(1)}, f32[72,128]{1,0:T(8,128)S(1)}, u32[]{:S(2)}, u32[]{:S(2)}) %collective-permute-start.3) | collective-permute-done | bytes 36896 | tf_op jit(solution)/shard_map/ppermute | solution.py:661
  8.8 0.0 collective-permute-done.rp
  8.8 0.0 collective-permute-done.2.ro
  8.8 0.1 columns.1
  8.9 3.6 %collective-permute-start.4 = (f32[280,128]{1,0:T(8,128)S(1)}, f32[280,128]{1,0:T(8,128)S(1)}, u32[]{:S(2)}, u32[]{:S(2)}) collective-permute-start(f32[280,128]{1,0:T(8,128)S(1)} %get-tuple-element.37), channel_id=1, source_target_pairs={{0,4},{1,2},{2,1},{3,7},{4,0},{5,6},{6,5},{7,3},{8,12},{9,10},{10,... | collective-permute-start | bytes 430088 | tf_op jit(solution)/shard_map/ppermute | solution.py:661
  12.5 1.9 %collective-permute-start.5 = (f32[280,128]{1,0:T(8,128)S(1)}, f32[280,128]{1,0:T(8,128)S(1)}, u32[]{:S(2)}, u32[]{:S(2)}) collective-permute-start(f32[280,128]{1,0:T(8,128)S(1)} %get-tuple-element.42), channel_id=1, source_target_pairs={{0,1},{1,0},{2,3},{3,2},{4,5},{5,4},{6,7},{7,6},{8,9},{9,8},{10,11... | collective-permute-start | bytes 430088 | tf_op jit(solution)/shard_map/ppermute | solution.py:661
  14.4 1.6 %inner.1 = (f32[2352,128]{1,0:T(8,128)S(1)}, f32[2352,128]{1,0:T(8,128)S(1)}, f32[6,12,4,8,128]{4,3,2,1,0:T(8,128)S(1)}, f32[4,10,3,3,8,128]{5,4,3,2,1,0:T(8,128...) custom-call(f32[224,128]{1,0:T(8,128)S(1)} %get-tuple-element.30.own, ...), custom_call_target="tpu_custom_call" | custom-call | flops 4000000000 | bytes 2097152 | tf_op jit(solution)/shard_map/inner/pallas_call | solution.py:776
  15.9 0.0 collective-permute-done.5.halo
  16.0 1.5 %core_side.1 = (f32[125,128]{1,0:T(8,128)S(1)}, f32[2352,128]{1,0:T(8,128)S(1)}, f32[2352,128]{1,0:T(8,128)S(1)}, f32[6,12,4,8,128]{4,3,2,1,0:T(8,128)S(1)}, f32...) custom-call(f32[280,128]{1,0:T(8,128)S(1)} %collective-permute-done., ...), custom_call_target="tpu_custom_call", output_to_operand_aliasing={{1}: (6, {}), {2}: (7, {}), {3}: (8, {}), {4}: (9, {}), {5}... | custom-call | flops 2000000000 | bytes 1048576 | tf_op jit(solution)/shard_map/core_side/pallas_call | solution.py:791
  17.5 0.0 collective-permute-done.4.halo
  17.5 2.2 %chip_side.1 = (f32[125,1,256]{2,1,0:T(1,128)}, f32[2352,128]{1,0:T(8,128)S(1)}, f32[2352,128]{1,0:T(8,128)S(1)}, f32[6,12,4,8,128]{4,3,2,1,0:T(8,128)S(1)}, f32...) custom-call(f32[280,128]{1,0:T(8,128)S(1)} %collective-permute-done., ...), custom_call_target="tpu_custom_call", output_to_operand_aliasing={{1}: (7, {}), {2}: (8, {}), {3}: (9, {}), {4}: (10, {}), {5... | custom-call | tf_op jit(solution)/shard_map/chip_side/pallas_call | solution.py:802
  (1 shorter events, 0.0 us)
Async XLA Ops:
  0.0 3.8 %collective-permute-start.1 = (s32[1,1,512]{2,1,0:T(1,128)}, s32[1,1,512]{2,1,0:T(1,128)S(1)}, u32[]{:S(2)}, u32[]{:S(2)}) collective-permute-start(s32[1,1,512]{2,1,0:T(1,128)} %refs_2_.1), channel_id=1, source_target_pairs={{0,4},{1,5},{2,6},{3,7},{4,0},{5,1},{6,2},{7,3},{8,12},{9,13},{10,... | collective-permute-start | bytes 6152 | tf_op jit(solution)/shard_map/ppermute | solution.py:661
  3.7 5.1 %collective-permute-start = (f32[224,128]{1,0:T(8,128)S(1)}, f32[224,128]{1,0:T(8,128)S(1)}, u32[]{:S(2)}, u32[]{:S(2)}) collective-permute-start(f32[224,128]{1,0:T(8,128)S(1)} %get-tuple-element.30.own), channel_id=1, source_target_pairs={{0,4},{1,5},{2,6},{3,7},{4,0},{5,1},{6,2},{7,3},{8,12},{9,13},{10,... | collective-permute-start | bytes 344072 | tf_op jit(solution)/shard_map/ppermute | solution.py:661
  3.9 4.9 %collective-permute-start.3 = (f32[72,128]{1,0:T(8,128)S(1)}, f32[72,128]{1,0:T(8,128)S(1)}, u32[]{:S(2)}, u32[]{:S(2)}) collective-permute-start(f32[72,128]{1,0:T(8,128)S(1)} %get-tuple-element.34), channel_id=1, source_target_pairs={{0,8},{1,9},{2,10},{3,11},{4,12},{5,13},{6,14},{7,15},{8,16},{9,17... | collective-permute-start | bytes 110600 | tf_op jit(solution)/shard_map/ppermute | solution.py:661
  5.4 3.4 %collective-permute-start.2 = (f32[240,128]{1,0:T(8,128)S(1)}, f32[240,128]{1,0:T(8,128)S(1)}, u32[]{:S(2)}, u32[]{:S(2)}) collective-permute-start(f32[240,128]{1,0:T(8,128)S(1)} %get-tuple-element.33), channel_id=1, source_target_pairs={{0,1},{1,0},{2,3},{3,2},{4,8},{5,9},{6,10},{7,11},{8,4},{9,5},{10,... | collective-permute-start | bytes 368648 | tf_op jit(solution)/shard_map/ppermute | solution.py:661
  8.9 8.6 %collective-permute-start.4 = (f32[280,128]{1,0:T(8,128)S(1)}, f32[280,128]{1,0:T(8,128)S(1)}, u32[]{:S(2)}, u32[]{:S(2)}) collective-permute-start(f32[280,128]{1,0:T(8,128)S(1)} %get-tuple-element.37), channel_id=1, source_target_pairs={{0,4},{1,2},{2,1},{3,7},{4,0},{5,6},{6,5},{7,3},{8,12},{9,10},{10,... | collective-permute-start | bytes 430088 | tf_op jit(solution)/shard_map/ppermute | solution.py:661
  12.5 3.5 %collective-permute-start.5 = (f32[280,128]{1,0:T(8,128)S(1)}, f32[280,128]{1,0:T(8,128)S(1)}, u32[]{:S(2)}, u32[]{:S(2)}) collective-permute-start(f32[280,128]{1,0:T(8,128)S(1)} %get-tuple-element.42), channel_id=1, source_target_pairs={{0,1},{1,0},{2,3},{3,2},{4,5},{5,4},{6,7},{7,6},{8,9},{9,8},{10,11... | collective-permute-start | bytes 430088 | tf_op jit(solution)/shard_map/ppermute | solution.py:661

commit v16 on v15

--- a/solution.py
+++ b/solution.py
@@ -144,7 +144,8 @@
     return jnp.where(lax.rem(at, 2) == 0, at > 0, at < peers - 1)
 
 
-def column_kernel(peers, own, rp, ro, rs, band, sums, to_core, to_chip):
+def column_kernel(peers, own, rp, ro, rs, band, sums, after, to_core, to_chip):
+    del after
     ro = Masked(ro, has_other("gx", peers[0]))
     lo2 = Masked(rs, lax.axis_index("gx") >= 2)
 
@@ -509,7 +510,21 @@
     return [y for y in range(-1, 3) if (2 * coarse_y + y in INNER) == inner]
 
 
-def inner_kernel(
+def has_time(peers):
+    at = lax.axis_index("gx")
+    return (lax.rem(lax.axis_index("gy"), 2) == 1) | (at == 0) | (at == peers[0] - 1)
+
+
+def early_kernel(peers, *refs):
+    pl.when(has_time(peers))(functools.partial(inner_part, peers, *refs))
+
+
+def late_kernel(peers, *refs):
+    refs = refs[:7] + refs[13:]
+    pl.when(jnp.logical_not(has_time(peers)))(functools.partial(inner_part, peers, *refs))
+
+
+def inner_part(
     peers, own, rp, ro, rs, f2, ft2, rf_pair, w, wr, qe, ap, tt, rf_third, qc, inv, diag, fd, hot
 ):
     here = Place()
@@ -750,16 +765,6 @@
         cost_estimate=pl.CostEstimate(flops=2 * 10**9, bytes_accessed=2**21, transcendentals=0),
         name="faults",
     )(tile, cells)
-    to_core, to_chip = pl.pallas_call(
-        functools.partial(column_kernel, peers),
-        out_shape=(sds(Y_ROWS, NZ), sds(Y_ROWS, NZ)),
-        in_specs=[VMEM] * 6,
-        out_specs=(VMEM,) * 2,
-        compiler_params=params(16),
-        name="columns",
-    )(own, rp, ro, rs, band, rf_pair)
-    from_chip = send(to_chip, chip_other(peers[1]))
-    from_core = send(to_core, core_partner)
     work = (
         sds(7 * PER * ROWS, NZ),
         sds(7 * PER * ROWS, NZ),
@@ -767,22 +772,45 @@
         sds(4, 10, 3, 3, 8, NZ),
         sds(2, 5, 5, 8, 512),
     )
+    inner = work + (sds(CY, 8, NZ),)
     fields = [
         pltpu.VMEM((6 * 8 * 16, NZ), f32),
         pltpu.VMEM((6 * 16, NZ), f32),
         pltpu.VMEM((6 * 16, NZ), f32),
         pltpu.VMEM((6 * 16, NZ), f32),
     ]
-    *work_in, rf_third = pl.pallas_call(
-        functools.partial(inner_kernel, peers),
-        out_shape=work + (sds(CY, 8, NZ),),
+    inner_args = (own, rp, ro, rs, f2, ft2, rf_pair)
+    inner_scratch = fields + [pltpu.VMEM((CY * NZ, SLOTS), bf16)]
+    filled = pl.pallas_call(
+        functools.partial(early_kernel, peers),
+        out_shape=inner,
         in_specs=[VMEM] * 7,
         out_specs=(VMEM,) * 6,
-        scratch_shapes=fields + [pltpu.VMEM((CY * NZ, SLOTS), bf16)],
+        scratch_shapes=inner_scratch,
+        compiler_params=params(16),
+        name="inner_early",
+    )(*inner_args)
+    to_core, to_chip = pl.pallas_call(
+        functools.partial(column_kernel, peers),
+        out_shape=(sds(Y_ROWS, NZ), sds(Y_ROWS, NZ)),
+        in_specs=[VMEM] * 7,
+        out_specs=(VMEM,) * 2,
+        compiler_params=params(16),
+        name="columns",
+    )(own, rp, ro, rs, band, rf_pair, filled[5])
+    from_chip = send(to_chip, chip_other(peers[1]))
+    from_core = send(to_core, core_partner)
+    *work_in, rf_third = pl.pallas_call(
+        functools.partial(late_kernel, peers),
+        out_shape=inner,
+        in_specs=[VMEM] * 13,
+        out_specs=(VMEM,) * 6,
+        scratch_shapes=inner_scratch,
+        input_output_aliases={7 + k: k for k in range(6)},
         compiler_params=params(16),
         cost_estimate=pl.CostEstimate(flops=4 * 10**9, bytes_accessed=2**21, transcendentals=0),
-        name="inner",
-    )(own, rp, ro, rs, f2, ft2, rf_pair)
+        name="inner_late",
+    )(*inner_args, *filled)
     side_scratch = fields + [
         pltpu.VMEM((3, 8, 8, NZ), f32),
         pltpu.VMEM((24, NZ), f32),

time: 19.8 us -> 20.1 us (1.015)
  the two profiles are of different devices: /device:TPU:1 before, /device:TPU:0 now
where the time goes in v16:
time: 20.1 us; the launch traced here: 20 us
  Pallas kernels  7.75 us (39%)
  starting transfers between devices  7.06 us (35%)
  waiting for transfers between devices  4.48 us (22%)
  between operations  0.71 us (4%)
    ppermute x6, starting transfers between devices, send(): return lax.ppermute(value, ('gx', 'gy'), pairs)  7.06 us
    ppermute x6, waiting for transfers between devices, send(): return lax.ppermute(value, ('gx', 'gy'), pairs)  4.48 us
    pallas_call x1, Pallas kernels, per_device(): pl.pallas_call(functools.partial(main_kernel, peers), out_shape=(sds(125,...  2.19 us
    pallas_call x1, Pallas kernels, per_device(): pl.pallas_call(functools.partial(early_kernel, peers), out_shape=inner, i...  1.59 us
    pallas_call x1, Pallas kernels, per_device(): pl.pallas_call(core_kernel, out_shape=(sds(125, NZ),) + work, in_specs=[V...  1.47 us
    pallas_call x1, Pallas kernels, per_device(): pl.pallas_call(fault_kernel, out_shape=(pieces, pieces, sds(2, CY, 8, NZ)...  1.36 us
    pallas_call x1, Pallas kernels, per_device(): pl.pallas_call(functools.partial(pack_kernel, peers), out_shape=(sds(224,...  1.04 us
  transfers between devices with their start and end apart: 6, of which 3 were waited for; matrix products, arithmetic and copies ran while one was open for 0% of the time, Pallas kernels for 19%

profile of v16, /device:TPU:0, one launch (start us, length us, event | category | flops | bytes accessed | tf_op | source)
XLA Modules:
  0.0 20.0 jit_solution(11105686939587276019)
XLA Ops:
  0.0 2.9 %collective-permute-start.1 = (s32[1,1,512]{2,1,0:T(1,128)}, s32[1,1,512]{2,1,0:T(1,128)S(1)}, u32[]{:S(2)}, u32[]{:S(2)}) collective-permute-start(s32[1,1,512]{2,1,0:T(1,128)} %refs_2_.1), channel_id=1, source_target_pairs={{0,4},{1,5},{2,6},{3,7},{4,0},{5,1},{6,2},{7,3},{8,12},{9,13},{10,... | collective-permute-start | bytes 6152 | tf_op jit(solution)/shard_map/ppermute | solution.py:676
  3.6 1.0 %pack.1 = (f32[224,128]{1,0:T(8,128)S(1)}, f32[72,128]{1,0:T(8,128)S(1)}, f32[8,128]{1,0:T(8,128)S(1)}) custom-call(s32[1,1]{1,0:T(1,128)S(6)} %copy.38.count, f32[13,2,1024]{2,1,0:T(2,128)} %refs_0_.1, f32[2,1024]{1,0:T(2,128)} %refs_1_.1, s32[1,1,512]{2,1,0:T(1,128)} %refs_2_.1, f32[1,1,512]{2,1,0:T(1,128)} %refs_3_.1), custom_call_target="tpu_custom_call" | custom-call | tf_op jit(solution)/shard_map/pack/pallas_call | solution.py:726
  4.6 0.1 collective-permute-start
  4.7 0.0 collective-permute-done.1.cells
  4.8 2.1 %collective-permute-start.3 = (f32[72,128]{1,0:T(8,128)S(1)}, f32[72,128]{1,0:T(8,128)S(1)}, u32[]{:S(2)}, u32[]{:S(2)}) collective-permute-start(f32[72,128]{1,0:T(8,128)S(1)} %get-tuple-element.40), channel_id=1, source_target_pairs={{0,8},{1,9},{2,10},{3,11},{4,12},{5,13},{6,14},{7,15},{8,16},{9,17... | collective-permute-start | bytes 110600 | tf_op jit(solution)/shard_map/ppermute | solution.py:676
  6.9 0.0 collective-permute-start.2
  6.9 1.4 %faults.1 = (bf16[8,256,128]{2,1,0:T(8,128)(2,1)S(1)}, bf16[8,256,128]{2,1,0:T(8,128)(2,1)S(1)}, f32[2,8,8,128]{3,2,1,0:T(8,128)S(1)}, f32[2,24,128]{2,1,0:T(8,128)S(1)}, bf16[512,128]{1,0:T(8,128)(2,1)S(1)}) custom-call(f32[8,128]{1,0:T(8,128)S(1)} %get-tuple-element.37.tile, s32[1,1,512]{2,1,0:T(1,128)S(1)} %collective-permute-done.1.cells), custom_call_target="tpu_custom_call" | custom-call | flops 2000000000 | bytes 2097152 | tf_op jit(solution)/shard_map/faults/pallas_call | solution.py:748
  8.3 2.7 %collective-permute-done.3.refs_3_.rs = f32[72,128]{1,0:T(8,128)S(1)} collective-permute-done((f32[72,128]{1,0:T(8,128)S(1)}, f32[72,128]{1,0:T(8,128)S(1)}, u32[]{:S(2)}, u32[]{:S(2)}) %collective-permute-start.3) | collective-permute-done | bytes 36896 | tf_op jit(solution)/shard_map/ppermute | solution.py:676
  11.0 0.0 collective-permute-done.refs_1_.rp
  11.0 0.0 collective-permute-done.2.refs_2_.ro
  11.0 1.6 %inner_early.1 = (f32[2352,128]{1,0:T(8,128)S(1)}, f32[2352,128]{1,0:T(8,128)S(1)}, f32[6,12,4,8,128]{4,3,2,1,0:T(8,128)S(1)}, f32[4,10,3,3,8,128]{5,4,3,2,1,0:T...) custom-call(f32[224,128]{1,0:T(8,128)S(1)} %get-tuple-element.36.own.refs_0_, ...), custom_call_target="tpu_custom_call" | custom-call | tf_op jit(solution)/shard_map/inner_early/pallas_call | solution.py:784
  12.6 0.1 columns.1
  12.6 1.6 %collective-permute-start.4 = (f32[280,128]{1,0:T(8,128)S(1)}, f32[280,128]{1,0:T(8,128)S(1)}, u32[]{:S(2)}, u32[]{:S(2)}) collective-permute-start(f32[280,128]{1,0:T(8,128)S(1)} %get-tuple-element.46), channel_id=1, source_target_pairs={{0,4},{1,2},{2,1},{3,7},{4,0},{5,6},{6,5},{7,3},{8,12},{9,10},{10,... | collective-permute-start | bytes 430088 | tf_op jit(solution)/shard_map/ppermute | solution.py:676
  14.3 0.3 %collective-permute-start.5 = (f32[280,128]{1,0:T(8,128)S(1)}, f32[280,128]{1,0:T(8,128)S(1)}, u32[]{:S(2)}, u32[]{:S(2)}) collective-permute-start(f32[280,128]{1,0:T(8,128)S(1)} %get-tuple-element.54), channel_id=1, source_target_pairs={{0,1},{1,0},{2,3},{3,2},{4,5},{5,4},{6,7},{7,6},{8,9},{9,8},{10,11... | collective-permute-start | bytes 430088 | tf_op jit(solution)/shard_map/ppermute | solution.py:676
  14.6 1.1 %collective-permute-done.5.halo = f32[280,128]{1,0:T(8,128)S(1)} collective-permute-done((f32[280,128]{1,0:T(8,128)S(1)}, f32[280,128]{1,0:T(8,128)S(1)}, u32[]{:S(2)}, u32[]{:S(2)}) %collective-permute-start.5) | collective-permute-done | bytes 143392 | tf_op jit(solution)/shard_map/ppermute | solution.py:676
  15.7 1.5 %core_side.1 = (f32[125,128]{1,0:T(8,128)S(1)}, f32[2352,128]{1,0:T(8,128)S(1)}, f32[2352,128]{1,0:T(8,128)S(1)}, f32[6,12,4,8,128]{4,3,2,1,0:T(8,128)S(1)}, f32...) custom-call(f32[280,128]{1,0:T(8,128)S(1)} %collective-permute-done., ...), custom_call_target="tpu_custom_call", output_to_operand_aliasing={{1}: (6, {}), {2}: (7, {}), {3}: (8, {}), {4}: (9, {}), {5}... | custom-call | flops 2000000000 | bytes 1048576 | tf_op jit(solution)/shard_map/core_side/pallas_call | solution.py:819
  17.1 0.7 %collective-permute-done.4.halo = f32[280,128]{1,0:T(8,128)S(1)} collective-permute-done((f32[280,128]{1,0:T(8,128)S(1)}, f32[280,128]{1,0:T(8,128)S(1)}, u32[]{:S(2)}, u32[]{:S(2)}) %collective-permute-start.4) | collective-permute-done | bytes 143392 | tf_op jit(solution)/shard_map/ppermute | solution.py:676
  17.8 2.2 %chip_side.1 = (f32[125,1,256]{2,1,0:T(1,128)}, f32[2352,128]{1,0:T(8,128)S(1)}, f32[2352,128]{1,0:T(8,128)S(1)}, f32[6,12,4,8,128]{4,3,2,1,0:T(8,128)S(1)}, f32...) custom-call(f32[280,128]{1,0:T(8,128)S(1)} %collective-permute-done., ...), custom_call_target="tpu_custom_call", output_to_operand_aliasing={{1}: (7, {}), {2}: (8, {}), {3}: (9, {}), {4}: (10, {}), {5... | custom-call | tf_op jit(solution)/shard_map/chip_side/pallas_call | solution.py:830
  (2 shorter events, 0.0 us)
Async XLA Ops:
  0.0 4.7 %collective-permute-start.1 = (s32[1,1,512]{2,1,0:T(1,128)}, s32[1,1,512]{2,1,0:T(1,128)S(1)}, u32[]{:S(2)}, u32[]{:S(2)}) collective-permute-start(s32[1,1,512]{2,1,0:T(1,128)} %refs_2_.1), channel_id=1, source_target_pairs={{0,4},{1,5},{2,6},{3,7},{4,0},{5,1},{6,2},{7,3},{8,12},{9,13},{10,... | collective-permute-start | bytes 6152 | tf_op jit(solution)/shard_map/ppermute | solution.py:676
  4.6 6.3 %collective-permute-start = (f32[224,128]{1,0:T(8,128)S(1)}, f32[224,128]{1,0:T(8,128)S(1)}, u32[]{:S(2)}, u32[]{:S(2)}) collective-permute-start(f32[224,128]{1,0:T(8,128)S(1)} %get-tuple-element.36.own.refs_0_), channel_id=1, source_target_pairs={{0,4},{1,5},{2,6},{3,7},{4,0},{5,1},{6,2},{7,3},{8,12},{9,13},{10,... | collective-permute-start | bytes 344072 | tf_op jit(solution)/shard_map/ppermute | solution.py:676
  4.8 6.2 %collective-permute-start.3 = (f32[72,128]{1,0:T(8,128)S(1)}, f32[72,128]{1,0:T(8,128)S(1)}, u32[]{:S(2)}, u32[]{:S(2)}) collective-permute-start(f32[72,128]{1,0:T(8,128)S(1)} %get-tuple-element.40), channel_id=1, source_target_pairs={{0,8},{1,9},{2,10},{3,11},{4,12},{5,13},{6,14},{7,15},{8,16},{9,17... | collective-permute-start | bytes 110600 | tf_op jit(solution)/shard_map/ppermute | solution.py:676
  6.9 4.1 %collective-permute-start.2 = (f32[240,128]{1,0:T(8,128)S(1)}, f32[240,128]{1,0:T(8,128)S(1)}, u32[]{:S(2)}, u32[]{:S(2)}) collective-permute-start(f32[240,128]{1,0:T(8,128)S(1)} %get-tuple-element.39), channel_id=1, source_target_pairs={{0,1},{1,0},{2,3},{3,2},{4,8},{5,9},{6,10},{7,11},{8,4},{9,5},{10,... | collective-permute-start | bytes 368648 | tf_op jit(solution)/shard_map/ppermute | solution.py:676
  12.6 5.2 %collective-permute-start.4 = (f32[280,128]{1,0:T(8,128)S(1)}, f32[280,128]{1,0:T(8,128)S(1)}, u32[]{:S(2)}, u32[]{:S(2)}) collective-permute-start(f32[280,128]{1,0:T(8,128)S(1)} %get-tuple-element.46), channel_id=1, source_target_pairs={{0,4},{1,2},{2,1},{3,7},{4,0},{5,6},{6,5},{7,3},{8,12},{9,10},{10,... | collective-permute-start | bytes 430088 | tf_op jit(solution)/shard_map/ppermute | solution.py:676
  14.3 1.4 %collective-permute-start.5 = (f32[280,128]{1,0:T(8,128)S(1)}, f32[280,128]{1,0:T(8,128)S(1)}, u32[]{:S(2)}, u32[]{:S(2)}) collective-permute-start(f32[280,128]{1,0:T(8,128)S(1)} %get-tuple-element.54), channel_id=1, source_target_pairs={{0,1},{1,0},{2,3},{3,2},{4,5},{5,4},{6,7},{7,6},{8,9},{9,8},{10,11... | collective-permute-start | bytes 430088 | tf_op jit(solution)/shard_map/ppermute | solution.py:676

commit v17 on v16

--- a/solution.py
+++ b/solution.py
@@ -56,7 +56,7 @@
 
 
 def pack_kernel(peers, count, *refs):
-    sources, (block, plane, tile), targets, sems = refs[:4], refs[4:7], refs[7:11], refs[11]
+    sources, (block, plane), targets, sems = refs[:4], refs[4:6], refs[6:10], refs[10]
     copies = [
         pltpu.make_async_copy(src, dst, sems.at[k])
         for k, (src, dst) in enumerate(zip(sources, targets))
@@ -104,25 +104,18 @@
     lane = lax.broadcasted_iota(jnp.int32, (1, NZ), 1)
     for r in range(4):
         lanes = slice(r * NZ, (r + 1) * NZ)
-        tile[r : r + 1, :] = cells[0, :, lanes].astype(f32)
-        tile[4 + r : 5 + r, :] = jnp.where(
+        at = 2 * PER * 8 + r
+        block[at : at + 1, :] = cells[0, :, lanes].astype(f32)
+        block[at + 4 : at + 5, :] = jnp.where(
             lane + r * NZ < live, ftrans[0, :, lanes], 0.0
         )
-    plane[...] = block[(PER + 4) * 8 : (PER + 13) * 8, :]
-
-
-def partner_rows(cells):
-    return jnp.concatenate(
-        [cells[0, :, r * NZ : (r + 1) * NZ] for r in range(4)], axis=0
-    ).astype(f32)
-
-
-def join_kernel(own, tile, plane, cells, joined, plane_out):
+    plane[0:72, :] = block[(PER + 4) * 8 : (PER + 13) * 8, :]
+    plane[72:80, :] = block[224:232, :]
+
+
+def pass_kernel(own, plane, own_out, plane_out):
+    own_out[...] = own[...]
     plane_out[...] = plane[...]
-    joined[0:224, :] = own[...]
-    joined[224:232, :] = tile[...]
-    joined[232:236, :] = partner_rows(cells)
-    joined[236:240, :] = jnp.zeros((4, NZ), f32)
 
 
 def by_parity(axis, body):
@@ -139,15 +132,25 @@
         return jnp.where(self.due, self.ref[index], 0.0)
 
 
+class Behind:
+    def __init__(self, rd, re):
+        self.refs, self.at = (rd, re), lax.axis_index("gx")
+
+    def __getitem__(self, index):
+        even, odd = (ref[index] for ref in self.refs)
+        value = jnp.where(lax.rem(self.at, 2) == 0, even, odd)
+        return jnp.where(self.at >= 2, value, 0.0)
+
+
 def has_other(axis, peers):
     at = lax.axis_index(axis)
     return jnp.where(lax.rem(at, 2) == 0, at > 0, at < peers - 1)
 
 
-def column_kernel(peers, own, rp, ro, rs, band, sums, after, to_core, to_chip):
+def column_kernel(peers, own, rp, ro, rd, re, band, sums, after, to_core, to_chip):
     del after
     ro = Masked(ro, has_other("gx", peers[0]))
-    lo2 = Masked(rs, lax.axis_index("gx") >= 2)
+    lo2 = Behind(rd, re)
 
     def fill(out, lo, hi, first, third, runs):
         for c in range(2):
@@ -165,8 +168,8 @@
                 for o in runs:
                     out[at : at + 3, :] = ref[pl.ds((x * PER + o) * 8 + third, 3, stride=8), :]
                     at += 3
-        for k, start in enumerate((224, 232, 228)):
-            out[FAULT_ROW + 4 * k : FAULT_ROW + 4 * k + 4, :] = ro[start : start + 4, :]
+        for k, rows in enumerate((ro[224:228, :], rd[72:76, :], ro[228:232, :])):
+            out[FAULT_ROW + 4 * k : FAULT_ROW + 4 * k + 4, :] = rows
         out[BAND_ROW : BAND_ROW + DIAGONALS, :] = band[int(first > 0), 0:DIAGONALS, :]
         for c in range(2):
             for k in range(2):
@@ -268,17 +271,17 @@
     collect[...] = jnp.where(fits, 1.0, 0.0).astype(bf16)
 
 
-def fault_kernel(tile, cells, f2, ft2, rf, band, collect, far2, hot, both):
+def fault_kernel(own, rp, f2, ft2, rf, band, collect, far2, hot, both):
     fill_collect(collect)
-    partner, live = slot_columns([partner_rows(cells), tile[4:8, :]])
+    partner, live = slot_columns([rp[224:228, :], own[228:232, :]])
     fill_far(far2, partner, live)
-    fill_hot(hot, flat_cells(tile[0:4, :]), range(CY))
+    fill_hot(hot, flat_cells(own[224:228, :]), range(CY))
     both[...] = dot_nn(hot[...], far2[...])
     for y in range(CY):
         f2[y], ft2[y], rf[0, y], rf[1, y] = pair_matrix(both[y * NZ : (y + 1) * NZ, :])
     for k, y in enumerate((0, CY - 1)):
         band[k] = diagonals(
-            hot[y * NZ : (y + 1) * NZ, :], tile[0:4, :], partner_rows(cells), tile[4:8, :]
+            hot[y * NZ : (y + 1) * NZ, :], own[224:228, :], rp[224:228, :], own[228:232, :]
         )
 
 
@@ -520,12 +523,12 @@
 
 
 def late_kernel(peers, *refs):
-    refs = refs[:7] + refs[13:]
+    refs = refs[:8] + refs[14:]
     pl.when(jnp.logical_not(has_time(peers)))(functools.partial(inner_part, peers, *refs))
 
 
 def inner_part(
-    peers, own, rp, ro, rs, f2, ft2, rf_pair, w, wr, qe, ap, tt, rf_third, qc, inv, diag, fd, hot
+    peers, own, rp, ro, rd, re, f2, ft2, rf_pair, w, wr, qe, ap, tt, rf_third, qc, inv, diag, fd, hot
 ):
     here = Place()
     ro = Masked(ro, has_other("gx", peers[0]))
@@ -541,11 +544,11 @@
         place(hi, 28, 5 * PER)
 
     by_parity("gx", place_x)
-    place(Masked(rs, here.gx >= 2), 9, 4)
+    place(Behind(rd, re), 9, 4)
     place(own, 28, 3 * PER)
 
     fill_hot(hot, flat_cells(ro[224:228, :]), range(CY))
-    got = colour_sums(hot[...], ro[232:236, :], ro[228:232, :])
+    got = colour_sums(hot[...], rd[72:76, :], ro[228:232, :])
     fd[...] = jnp.zeros_like(fd)
     for y in range(CY):
         rf_third[y] = got[:, y * NZ : (y + 1) * NZ]
@@ -692,16 +695,23 @@
     return target
 
 
-def chip_other(size_y):
+def chip_other(size_x, size_y):
     def target(x, y):
         other = y + 1 if y % 2 else y - 1
-        return (x, other) if 0 <= other < size_y else x_partner(x, y)
+        if 0 <= other < size_y:
+            return x, other
+        beside = x + 1 if x % 2 else x - 1
+        return (beside, y) if 0 <= beside < size_x else (x, size_y - 1 - y)
 
     return target
 
 
-def x_ahead(size_x):
-    return lambda x, y: ((x + 2) % size_x, y)
+def x_two(size_x, up):
+    def target(x, y):
+        other = x + 2 if x % 2 == up else x - 2
+        return (other, y) if 0 <= other < size_x else x_partner(x, y)
+
+    return target
 
 
 VMEM = pl.BlockSpec(memory_space=pltpu.VMEM)
@@ -718,32 +728,32 @@
 
 def per_device(trans, storage, fault_cells, fault_count, fault_trans):
     peers = (lax.axis_size("gx"), lax.axis_size("gy"))
-    cells = send(fault_cells, x_partner)
     sources = [
         pltpu.with_memory_space_constraint(array, pltpu.HBM)
         for array in (trans, storage, fault_cells, fault_trans)
     ]
-    own, plane, tile = pl.pallas_call(
+    own, plane = pl.pallas_call(
         functools.partial(pack_kernel, peers),
-        out_shape=(sds(224, NZ), sds(72, NZ), sds(8, NZ)),
+        out_shape=(sds(232, NZ), sds(80, NZ)),
         in_specs=[pl.BlockSpec(memory_space=pltpu.SMEM)] + [HBM] * 4,
-        out_specs=(VMEM,) * 3,
+        out_specs=(VMEM,) * 2,
         scratch_shapes=[pltpu.VMEM(array.shape, array.dtype) for array in sources]
         + [pltpu.SemaphoreType.DMA((4,))],
         compiler_params=params(16),
         name="pack",
     )(fault_count, *sources)
-    joined, plane = pl.pallas_call(
-        join_kernel,
-        out_shape=(sds(240, NZ), sds(72, NZ)),
-        in_specs=[VMEM] * 4,
+    rp = send(own, x_partner)
+    own_again, plane = pl.pallas_call(
+        pass_kernel,
+        out_shape=(sds(232, NZ), sds(80, NZ)),
+        in_specs=[VMEM] * 2,
         out_specs=(VMEM,) * 2,
         compiler_params=params(16),
-        name="join",
-    )(own, tile, plane, cells)
-    rs = send(plane, x_ahead(peers[0]))
-    ro = send(joined, x_other(peers[0]))
-    rp = send(own, x_partner)
+        name="pass",
+    )(own, plane)
+    rd = send(plane, x_two(peers[0], 0))
+    re = send(plane, x_two(peers[0], 1))
+    ro = send(own_again, x_other(peers[0]))
     pieces = sds(CY, 2 * NZ, NZ, dtype=bf16)
     f2, ft2, rf_pair, band, collect = pl.pallas_call(
         fault_kernel,
@@ -764,7 +774,7 @@
         compiler_params=params(16),
         cost_estimate=pl.CostEstimate(flops=2 * 10**9, bytes_accessed=2**21, transcendentals=0),
         name="faults",
-    )(tile, cells)
+    )(own, rp)
     work = (
         sds(7 * PER * ROWS, NZ),
         sds(7 * PER * ROWS, NZ),
@@ -779,12 +789,12 @@
         pltpu.VMEM((6 * 16, NZ), f32),
         pltpu.VMEM((6 * 16, NZ), f32),
     ]
-    inner_args = (own, rp, ro, rs, f2, ft2, rf_pair)
+    inner_args = (own, rp, ro, rd, re, f2, ft2, rf_pair)
     inner_scratch = fields + [pltpu.VMEM((CY * NZ, SLOTS), bf16)]
     filled = pl.pallas_call(
         functools.partial(early_kernel, peers),
         out_shape=inner,
-        in_specs=[VMEM] * 7,
+        in_specs=[VMEM] * 8,
         out_specs=(VMEM,) * 6,
         scratch_shapes=inner_scratch,
         compiler_params=params(16),
@@ -793,20 +803,20 @@
     to_core, to_chip = pl.pallas_call(
         functools.partial(column_kernel, peers),
         out_shape=(sds(Y_ROWS, NZ), sds(Y_ROWS, NZ)),
-        in_specs=[VMEM] * 7,
+        in_specs=[VMEM] * 8,
         out_specs=(VMEM,) * 2,
         compiler_params=params(16),
         name="columns",
-    )(own, rp, ro, rs, band, rf_pair, filled[5])
-    from_chip = send(to_chip, chip_other(peers[1]))
+    )(own, rp, ro, rd, re, band, rf_pair, filled[5])
+    from_chip = send(to_chip, chip_other(*peers))
     from_core = send(to_core, core_partner)
     *work_in, rf_third = pl.pallas_call(
         functools.partial(late_kernel, peers),
         out_shape=inner,
-        in_specs=[VMEM] * 13,
+        in_specs=[VMEM] * 14,
         out_specs=(VMEM,) * 6,
         scratch_shapes=inner_scratch,
-        input_output_aliases={7 + k: k for k in range(6)},
+        input_output_aliases={8 + k: k for k in range(6)},
         compiler_params=params(16),
         cost_estimate=pl.CostEstimate(flops=4 * 10**9, bytes_accessed=2**21, transcendentals=0),
         name="inner_late",

time: 20.1 us -> 20.3 us (level)
  waiting for transfers between devices: 4.48 us -> 5.49 us
  starting transfers between devices: 7.06 us -> 6.2 us
    ppermute x6, waiting for transfers between devices: 4.48 us -> 5.49 us  [send(): return lax.ppermute(value, ('gx', 'gy'), pairs)]
    ppermute x6, starting transfers between devices: 7.06 us -> 6.2 us  [send(): return lax.ppermute(value, ('gx', 'gy'), pairs)]
  transfers between devices with their start and end apart: 6 -> 6, of which waited for: 3 -> 4; matrix products, arithmetic and copies ran while one was open for 0% -> 0% of each run, Pallas kernels for 19% -> 14%
where the time goes in v17:
time: 20.3 us; the launch traced here: 20.2 us
  Pallas kernels  7.82 us (39%)
  starting transfers between devices  6.2 us (31%)
  waiting for transfers between devices  5.49 us (27%)
  between operations  0.69 us (3%)
    ppermute x6, starting transfers between devices, send(): return lax.ppermute(value, ('gx', 'gy'), pairs)  6.2 us
    ppermute x6, waiting for transfers between devices, send(): return lax.ppermute(value, ('gx', 'gy'), pairs)  5.49 us
    pallas_call x1, Pallas kernels, per_device(): pl.pallas_call(functools.partial(main_kernel, peers), out_shape=(sds(125,...  2.19 us
    pallas_call x1, Pallas kernels, per_device(): pl.pallas_call(functools.partial(early_kernel, peers), out_shape=inner, i...  1.63 us
    pallas_call x1, Pallas kernels, per_device(): pl.pallas_call(core_kernel, out_shape=(sds(125, NZ),) + work, in_specs=[V...  1.5 us
    pallas_call x1, Pallas kernels, per_device(): pl.pallas_call(fault_kernel, out_shape=(pieces, pieces, sds(2, CY, 8, NZ)...  1.36 us
    pallas_call x1, Pallas kernels, per_device(): pl.pallas_call(functools.partial(pack_kernel, peers), out_shape=(sds(232,...  1.05 us
  transfers between devices with their start and end apart: 6, of which 4 were waited for; matrix products, arithmetic and copies ran while one was open for 0% of the time, Pallas kernels for 14%

profile of v17, /device:TPU:0, one launch (start us, length us, event | category | flops | bytes accessed | tf_op | source)
XLA Modules:
  0.0 20.2 jit_solution(1659261222342571374)
XLA Ops:
  0.7 1.0 %pack.1 = (f32[232,128]{1,0:T(8,128)S(1)}, f32[80,128]{1,0:T(8,128)S(1)}) custom-call(s32[1,1]{1,0:T(1,128)S(6)} %copy.38.count, f32[13,2,1024]{2,1,0:T(2,128)} %refs_0_.1, f32[2,1024]{1,0:T(2,128)} %refs_1_.1, s32[1,1,512]{2,1,0:T(1,128)} %refs_2_.1, f32[1,1,512]{2,1,0:T(1,128)} %refs_3_.1), custom_call_target="tpu_custom_call" | custom-call | tf_op jit(solution)/shard_map/pack/pallas_call | solution.py:735
  1.7 3.0 %collective-permute-start = (f32[232,128]{1,0:T(8,128)S(1)}, f32[232,128]{1,0:T(8,128)S(1)}, u32[]{:S(2)}, u32[]{:S(2)}) collective-permute-start(f32[232,128]{1,0:T(8,128)S(1)} %get-tuple-element.35.own.refs_0_), channel_id=1, source_target_pairs={{0,4},{1,5},{2,6},{3,7},{4,0},{5,1},{6,2},{7,3},{8,12},{9,13},{10,... | collective-permute-start | bytes 356360 | tf_op jit(solution)/shard_map/ppermute | solution.py:679
  4.7 0.1 collective-permute-start.3
  4.8 2.0 %collective-permute-start.2 = (f32[80,128]{1,0:T(8,128)S(1)}, f32[80,128]{1,0:T(8,128)S(1)}, u32[]{:S(2)}, u32[]{:S(2)}) collective-permute-start(f32[80,128]{1,0:T(8,128)S(1)} %get-tuple-element.38), channel_id=1, source_target_pairs={{0,8},{1,9},{2,10},{3,11},{4,0},{5,1},{6,2},{7,3},{8,16},{9,17},{1... | collective-permute-start | bytes 122888 | tf_op jit(solution)/shard_map/ppermute | solution.py:679
  6.8 0.0 collective-permute-start.1
  6.8 1.6 %collective-permute-done.rp.refs_1_ = f32[232,128]{1,0:T(8,128)S(1)} collective-permute-done((f32[232,128]{1,0:T(8,128)S(1)}, f32[232,128]{1,0:T(8,128)S(1)}, u32[]{:S(2)}, u32[]{:S(2)}) %collective-permute-start) | collective-permute-done | bytes 118816 | tf_op jit(solution)/shard_map/ppermute | solution.py:679
  8.4 1.4 %faults.1 = (bf16[8,256,128]{2,1,0:T(8,128)(2,1)S(1)}, bf16[8,256,128]{2,1,0:T(8,128)(2,1)S(1)}, f32[2,8,8,128]{3,2,1,0:T(8,128)S(1)}, f32[2,24,128]{2,1,0:T(8,128)S(1)}, bf16[512,128]{1,0:T(8,128)(2,1)S(1)}) custom-call(f32[232,128]{1,0:T(8,128)S(1)} %get-tuple-element.35.own.refs_0_, f32[232,128]{1,0:T(8,128)S(1)} %collective-permute-done.rp.refs_1_), custom_call_target="tpu_custom_call" | custom-call | flops 2000000000 | bytes 2097152 | tf_op jit(solution)/shard_map/faults/pallas_call | solution.py:758
  9.7 0.9 %collective-permute-done.3.refs_4_.re = f32[80,128]{1,0:T(8,128)S(1)} collective-permute-done((f32[80,128]{1,0:T(8,128)S(1)}, f32[80,128]{1,0:T(8,128)S(1)}, u32[]{:S(2)}, u32[]{:S(2)}) %collective-permute-start.3) | collective-permute-done | bytes 40992 | tf_op jit(solution)/shard_map/ppermute | solution.py:679
  10.7 0.0 collective-permute-done.2.refs_3_.rd
  10.7 0.0 collective-permute-done.1.refs_2_.ro
  10.7 1.6 %inner_early.1 = (f32[2352,128]{1,0:T(8,128)S(1)}, f32[2352,128]{1,0:T(8,128)S(1)}, f32[6,12,4,8,128]{4,3,2,1,0:T(8,128)S(1)}, f32[4,10,3,3,8,128]{5,4,3,2,1,0:T...) custom-call(f32[232,128]{1,0:T(8,128)S(1)} %get-tuple-element.35.own.refs_0_, ...), custom_call_target="tpu_custom_call" | custom-call | tf_op jit(solution)/shard_map/inner_early/pallas_call | solution.py:794
  12.3 0.1 columns.1
  12.4 0.1 collective-permute-start.4
  12.5 1.0 %collective-permute-start.5 = (f32[280,128]{1,0:T(8,128)S(1)}, f32[280,128]{1,0:T(8,128)S(1)}, u32[]{:S(2)}, u32[]{:S(2)}) collective-permute-start(f32[280,128]{1,0:T(8,128)S(1)} %get-tuple-element.52), channel_id=1, source_target_pairs={{0,1},{1,0},{2,3},{3,2},{4,5},{5,4},{6,7},{7,6},{8,9},{9,8},{10,11... | collective-permute-start | bytes 430088 | tf_op jit(solution)/shard_map/ppermute | solution.py:679
  13.5 1.0 %collective-permute-done.5.halo = f32[280,128]{1,0:T(8,128)S(1)} collective-permute-done((f32[280,128]{1,0:T(8,128)S(1)}, f32[280,128]{1,0:T(8,128)S(1)}, u32[]{:S(2)}, u32[]{:S(2)}) %collective-permute-start.5) | collective-permute-done | bytes 143392 | tf_op jit(solution)/shard_map/ppermute | solution.py:679
  14.5 1.5 %core_side.1 = (f32[125,128]{1,0:T(8,128)S(1)}, f32[2352,128]{1,0:T(8,128)S(1)}, f32[2352,128]{1,0:T(8,128)S(1)}, f32[6,12,4,8,128]{4,3,2,1,0:T(8,128)S(1)}, f32...) custom-call(f32[280,128]{1,0:T(8,128)S(1)} %collective-permute-done., ...), custom_call_target="tpu_custom_call", output_to_operand_aliasing={{1}: (6, {}), {2}: (7, {}), {3}: (8, {}), {4}: (9, {}), {5}... | custom-call | flops 2000000000 | bytes 1048576 | tf_op jit(solution)/shard_map/core_side/pallas_call | solution.py:829
  16.0 2.0 %collective-permute-done.4.halo = f32[280,128]{1,0:T(8,128)S(1)} collective-permute-done((f32[280,128]{1,0:T(8,128)S(1)}, f32[280,128]{1,0:T(8,128)S(1)}, u32[]{:S(2)}, u32[]{:S(2)}) %collective-permute-start.4) | collective-permute-done | bytes 143392 | tf_op jit(solution)/shard_map/ppermute | solution.py:679
  18.0 2.2 %chip_side.1 = (f32[125,1,256]{2,1,0:T(1,128)}, f32[2352,128]{1,0:T(8,128)S(1)}, f32[2352,128]{1,0:T(8,128)S(1)}, f32[6,12,4,8,128]{4,3,2,1,0:T(8,128)S(1)}, f32...) custom-call(f32[280,128]{1,0:T(8,128)S(1)} %collective-permute-done., ...), custom_call_target="tpu_custom_call", output_to_operand_aliasing={{1}: (7, {}), {2}: (8, {}), {3}: (9, {}), {4}: (10, {}), {5... | custom-call | tf_op jit(solution)/shard_map/chip_side/pallas_call | solution.py:840
  (2 shorter events, 0.0 us)
Async XLA Ops:
  1.7 6.7 %collective-permute-start = (f32[232,128]{1,0:T(8,128)S(1)}, f32[232,128]{1,0:T(8,128)S(1)}, u32[]{:S(2)}, u32[]{:S(2)}) collective-permute-start(f32[232,128]{1,0:T(8,128)S(1)} %get-tuple-element.35.own.refs_0_), channel_id=1, source_target_pairs={{0,4},{1,5},{2,6},{3,7},{4,0},{5,1},{6,2},{7,3},{8,12},{9,13},{10,... | collective-permute-start | bytes 356360 | tf_op jit(solution)/shard_map/ppermute | solution.py:679
  4.7 5.9 %collective-permute-start.3 = (f32[80,128]{1,0:T(8,128)S(1)}, f32[80,128]{1,0:T(8,128)S(1)}, u32[]{:S(2)}, u32[]{:S(2)}) collective-permute-start(f32[80,128]{1,0:T(8,128)S(1)} %get-tuple-element.38), channel_id=1, source_target_pairs={{0,4},{1,5},{2,6},{3,7},{4,12},{5,13},{6,14},{7,15},{8,0},{9,1},{1... | collective-permute-start | bytes 122888 | tf_op jit(solution)/shard_map/ppermute | solution.py:679
  4.8 5.9 %collective-permute-start.2 = (f32[80,128]{1,0:T(8,128)S(1)}, f32[80,128]{1,0:T(8,128)S(1)}, u32[]{:S(2)}, u32[]{:S(2)}) collective-permute-start(f32[80,128]{1,0:T(8,128)S(1)} %get-tuple-element.38), channel_id=1, source_target_pairs={{0,8},{1,9},{2,10},{3,11},{4,0},{5,1},{6,2},{7,3},{8,16},{9,17},{1... | collective-permute-start | bytes 122888 | tf_op jit(solution)/shard_map/ppermute | solution.py:679
  6.8 3.9 %collective-permute-start.1 = (f32[232,128]{1,0:T(8,128)S(1)}, f32[232,128]{1,0:T(8,128)S(1)}, u32[]{:S(2)}, u32[]{:S(2)}) collective-permute-start(f32[232,128]{1,0:T(8,128)S(1)} %get-tuple-element.37), channel_id=1, source_target_pairs={{0,1},{1,0},{2,3},{3,2},{4,8},{5,9},{6,10},{7,11},{8,4},{9,5},{10,... | collective-permute-start | bytes 356360 | tf_op jit(solution)/shard_map/ppermute | solution.py:679
  12.4 5.6 %collective-permute-start.4 = (f32[280,128]{1,0:T(8,128)S(1)}, f32[280,128]{1,0:T(8,128)S(1)}, u32[]{:S(2)}, u32[]{:S(2)}) collective-permute-start(f32[280,128]{1,0:T(8,128)S(1)} %get-tuple-element.44), channel_id=1, source_target_pairs={{0,3},{1,2},{2,1},{3,0},{4,8},{5,6},{6,5},{7,11},{8,4},{9,10},{10,... | collective-permute-start | bytes 430088 | tf_op jit(solution)/shard_map/ppermute | solution.py:679
  12.5 2.0 %collective-permute-start.5 = (f32[280,128]{1,0:T(8,128)S(1)}, f32[280,128]{1,0:T(8,128)S(1)}, u32[]{:S(2)}, u32[]{:S(2)}) collective-permute-start(f32[280,128]{1,0:T(8,128)S(1)} %get-tuple-element.52), channel_id=1, source_target_pairs={{0,1},{1,0},{2,3},{3,2},{4,5},{5,4},{6,7},{7,6},{8,9},{9,8},{10,11... | collective-permute-start | bytes 430088 | tf_op jit(solution)/shard_map/ppermute | solution.py:679

commit v18 on v17

--- a/solution.py
+++ b/solution.py
@@ -55,7 +55,7 @@
     return high, (value - high.astype(f32)).astype(bf16)
 
 
-def pack_kernel(peers, count, *refs):
+def pack_kernel(peers, *refs):
     sources, (block, plane), targets, sems = refs[:4], refs[4:6], refs[6:10], refs[10]
     copies = [
         pltpu.make_async_copy(src, dst, sems.at[k])
@@ -100,22 +100,20 @@
                 keep = inside if keep is None else keep & inside
             if keep is not None:
                 block[base : base + 8, :] = jnp.where(keep, block[base : base + 8, :], 0.0)
-    live = count[0, 0]
-    lane = lax.broadcasted_iota(jnp.int32, (1, NZ), 1)
     for r in range(4):
         lanes = slice(r * NZ, (r + 1) * NZ)
         at = 2 * PER * 8 + r
         block[at : at + 1, :] = cells[0, :, lanes].astype(f32)
-        block[at + 4 : at + 5, :] = jnp.where(
-            lane + r * NZ < live, ftrans[0, :, lanes], 0.0
-        )
+        block[at + 4 : at + 5, :] = ftrans[0, :, lanes]
     plane[0:72, :] = block[(PER + 4) * 8 : (PER + 13) * 8, :]
     plane[72:80, :] = block[224:232, :]
 
 
-def pass_kernel(own, plane, own_out, plane_out):
-    own_out[...] = own[...]
-    plane_out[...] = plane[...]
+def live_kernel(count, own, own_out):
+    own_out[0:228, :] = own[0:228, :]
+    slot = lax.broadcasted_iota(jnp.int32, (4, NZ), 0) * NZ
+    slot = slot + lax.broadcasted_iota(jnp.int32, (4, NZ), 1)
+    own_out[228:232, :] = jnp.where(slot < count[0, 0], own[228:232, :], 0.0)
 
 
 def by_parity(axis, body):
@@ -735,25 +733,25 @@
     own, plane = pl.pallas_call(
         functools.partial(pack_kernel, peers),
         out_shape=(sds(232, NZ), sds(80, NZ)),
-        in_specs=[pl.BlockSpec(memory_space=pltpu.SMEM)] + [HBM] * 4,
+        in_specs=[HBM] * 4,
         out_specs=(VMEM,) * 2,
         scratch_shapes=[pltpu.VMEM(array.shape, array.dtype) for array in sources]
         + [pltpu.SemaphoreType.DMA((4,))],
         compiler_params=params(16),
         name="pack",
-    )(fault_count, *sources)
+    )(*sources)
     rp = send(own, x_partner)
-    own_again, plane = pl.pallas_call(
-        pass_kernel,
-        out_shape=(sds(232, NZ), sds(80, NZ)),
-        in_specs=[VMEM] * 2,
-        out_specs=(VMEM,) * 2,
-        compiler_params=params(16),
-        name="pass",
-    )(own, plane)
     rd = send(plane, x_two(peers[0], 0))
     re = send(plane, x_two(peers[0], 1))
-    ro = send(own_again, x_other(peers[0]))
+    live = pl.pallas_call(
+        live_kernel,
+        out_shape=sds(232, NZ),
+        in_specs=[pl.BlockSpec(memory_space=pltpu.SMEM), VMEM],
+        out_specs=VMEM,
+        compiler_params=params(16),
+        name="live",
+    )(fault_count, own)
+    ro = send(live, x_other(peers[0]))
     pieces = sds(CY, 2 * NZ, NZ, dtype=bf16)
     f2, ft2, rf_pair, band, collect = pl.pallas_call(
         fault_kernel,
@@ -774,7 +772,7 @@
         compiler_params=params(16),
         cost_estimate=pl.CostEstimate(flops=2 * 10**9, bytes_accessed=2**21, transcendentals=0),
         name="faults",
-    )(own, rp)
+    )(live, rp)
     work = (
         sds(7 * PER * ROWS, NZ),
         sds(7 * PER * ROWS, NZ),

time: 20.3 us -> 19.6 us (0.966)
  the two profiles are of different devices: /device:TPU:0 before, /device:TPU:16 now
where the time goes in v18:
time: 19.6 us; the launch traced here: 19.4 us
  Pallas kernels  7.81 us (40%)
  starting transfers between devices  5.77 us (29%)
  waiting for transfers between devices  5.15 us (26%)
  between operations  0.71 us (4%)
    ppermute x6, starting transfers between devices, send(): return lax.ppermute(value, ('gx', 'gy'), pairs)  5.77 us
    ppermute x6, waiting for transfers between devices, send(): return lax.ppermute(value, ('gx', 'gy'), pairs)  5.15 us
    pallas_call x1, Pallas kernels, per_device(): pl.pallas_call(functools.partial(main_kernel, peers), out_shape=(sds(125,...  2.19 us
    pallas_call x1, Pallas kernels, per_device(): pl.pallas_call(functools.partial(late_kernel, peers), out_shape=inner, in...  1.63 us
    pallas_call x1, Pallas kernels, per_device(): pl.pallas_call(core_kernel, out_shape=(sds(125, NZ),) + work, in_specs=[V...  1.51 us
    pallas_call x1, Pallas kernels, per_device(): pl.pallas_call(fault_kernel, out_shape=(pieces, pieces, sds(2, CY, 8, NZ)...  1.36 us
    pallas_call x1, Pallas kernels, per_device(): pl.pallas_call(functools.partial(pack_kernel, peers), out_shape=(sds(232,...  1.04 us
  transfers between devices with their start and end apart: 6, of which 3 were waited for; matrix products, arithmetic and copies ran while one was open for 0% of the time, Pallas kernels for 23%

profile of v18, /device:TPU:16, one launch (start us, length us, event | category | flops | bytes accessed | tf_op | source)
XLA Modules:
  0.0 19.4 jit_solution(15350286178346437883)
XLA Ops:
  0.0 1.0 %pack.1 = (f32[232,128]{1,0:T(8,128)S(1)}, f32[80,128]{1,0:T(8,128)S(1)}) custom-call(f32[13,2,1024]{2,1,0:T(2,128)} %refs_0_.1, f32[2,1024]{1,0:T(2,128)} %refs_1_.1, s32[1,1,512]{2,1,0:T(1,128)} %refs_2_.1, f32[1,1,512]{2,1,0:T(1,128)} %refs_3_.1), custom_call_target="tpu_custom_call" | custom-call | tf_op jit(solution)/shard_map/pack/pallas_call | solution.py:733
  1.1 1.6 %collective-permute-start = (f32[232,128]{1,0:T(8,128)S(1)}, f32[232,128]{1,0:T(8,128)S(1)}, u32[]{:S(2)}, u32[]{:S(2)}) collective-permute-start(f32[232,128]{1,0:T(8,128)S(1)} %get-tuple-element.33.own.refs_0_), channel_id=1, source_target_pairs={{0,4},{1,5},{2,6},{3,7},{4,0},{5,1},{6,2},{7,3},{8,12},{9,13},{10,... | collective-permute-start | bytes 356360 | tf_op jit(solution)/shard_map/ppermute | solution.py:677
  2.6 0.4 %collective-permute-start.3 = (f32[80,128]{1,0:T(8,128)S(1)}, f32[80,128]{1,0:T(8,128)S(1)}, u32[]{:S(2)}, u32[]{:S(2)}) collective-permute-start(f32[80,128]{1,0:T(8,128)S(1)} %get-tuple-element.34), channel_id=1, source_target_pairs={{0,4},{1,5},{2,6},{3,7},{4,12},{5,13},{6,14},{7,15},{8,0},{9,1},{1... | collective-permute-start | bytes 122888 | tf_op jit(solution)/shard_map/ppermute | solution.py:677
  3.1 1.6 %collective-permute-start.2 = (f32[80,128]{1,0:T(8,128)S(1)}, f32[80,128]{1,0:T(8,128)S(1)}, u32[]{:S(2)}, u32[]{:S(2)}) collective-permute-start(f32[80,128]{1,0:T(8,128)S(1)} %get-tuple-element.34), channel_id=1, source_target_pairs={{0,8},{1,9},{2,10},{3,11},{4,0},{5,1},{6,2},{7,3},{8,16},{9,17},{1... | collective-permute-start | bytes 122888 | tf_op jit(solution)/shard_map/ppermute | solution.py:677
  5.3 0.5 %collective-permute-start.1 = (f32[232,128]{1,0:T(8,128)S(1)}, f32[232,128]{1,0:T(8,128)S(1)}, u32[]{:S(2)}, u32[]{:S(2)}) collective-permute-start(f32[232,128]{1,0:T(8,128)S(1)} %live.1.own), channel_id=1, source_target_pairs={{0,1},{1,0},{2,3},{3,2},{4,8},{5,9},{6,10},{7,11},{8,4},{9,5},{10,... | collective-permute-start | bytes 356360 | tf_op jit(solution)/shard_map/ppermute | solution.py:677
  5.8 0.3 %collective-permute-done.rp.refs_1_ = f32[232,128]{1,0:T(8,128)S(1)} collective-permute-done((f32[232,128]{1,0:T(8,128)S(1)}, f32[232,128]{1,0:T(8,128)S(1)}, u32[]{:S(2)}, u32[]{:S(2)}) %collective-permute-start) | collective-permute-done | bytes 118816 | tf_op jit(solution)/shard_map/ppermute | solution.py:677
  6.1 1.4 %faults.1 = (bf16[8,256,128]{2,1,0:T(8,128)(2,1)S(1)}, bf16[8,256,128]{2,1,0:T(8,128)(2,1)S(1)}, f32[2,8,8,128]{3,2,1,0:T(8,128)S(1)}, f32[2,24,128]{2,1,0:T(8,128)S(1)}, bf16[512,128]{1,0:T(8,128)(2,1)S(1)}) custom-call(f32[232,128]{1,0:T(8,128)S(1)} %live.1.own, f32[232,128]{1,0:T(8,128)S(1)} %collective-permute-done.rp.refs_1_), custom_call_target="tpu_custom_call" | custom-call | flops 2000000000 | bytes 2097152 | tf_op jit(solution)/shard_map/faults/pallas_call | solution.py:756
  7.5 0.0 collective-permute-done.3.refs_4_.re
  7.5 0.0 collective-permute-done.2.refs_3_.rd
  7.5 3.6 %collective-permute-done.1.refs_2_.ro = f32[232,128]{1,0:T(8,128)S(1)} collective-permute-done((f32[232,128]{1,0:T(8,128)S(1)}, f32[232,128]{1,0:T(8,128)S(1)}, u32[]{:S(2)}, u32[]{:S(2)}) %collective-permute-start.1) | collective-permute-done | bytes 118816 | tf_op jit(solution)/shard_map/ppermute | solution.py:677
  11.1 0.1 columns.1
  11.2 0.5 %collective-permute-start.4 = (f32[280,128]{1,0:T(8,128)S(1)}, f32[280,128]{1,0:T(8,128)S(1)}, u32[]{:S(2)}, u32[]{:S(2)}) collective-permute-start(f32[280,128]{1,0:T(8,128)S(1)} %get-tuple-element.40), channel_id=1, source_target_pairs={{0,3},{1,2},{2,1},{3,0},{4,8},{5,6},{6,5},{7,11},{8,4},{9,10},{10,... | collective-permute-start | bytes 430088 | tf_op jit(solution)/shard_map/ppermute | solution.py:677
  11.7 1.2 %collective-permute-start.5 = (f32[280,128]{1,0:T(8,128)S(1)}, f32[280,128]{1,0:T(8,128)S(1)}, u32[]{:S(2)}, u32[]{:S(2)}) collective-permute-start(f32[280,128]{1,0:T(8,128)S(1)} %get-tuple-element.48), channel_id=1, source_target_pairs={{0,1},{1,0},{2,3},{3,2},{4,5},{5,4},{6,7},{7,6},{8,9},{9,8},{10,11... | collective-permute-start | bytes 430088 | tf_op jit(solution)/shard_map/ppermute | solution.py:677
  12.9 1.6 %inner_late.1 = (f32[2352,128]{1,0:T(8,128)S(1)}, f32[2352,128]{1,0:T(8,128)S(1)}, f32[6,12,4,8,128]{4,3,2,1,0:T(8,128)S(1)}, f32[4,10,3,3,8,128]{5,4,3,2,1,0:T(...) custom-call(f32[232,128]{1,0:T(8,128)S(1)} %get-tuple-element.33.own, ...), custom_call_target="tpu_custom_call", output_to_operand_aliasing={{0}: (8, {}), {1}: (9, {}), {2}: (10, {}), {3}: (11, {}), {... | custom-call | flops 4000000000 | bytes 2097152 | tf_op jit(solution)/shard_map/inner_late/pallas_call | solution.py:811
  14.5 0.0 collective-permute-done.5.halo
  14.5 1.5 %core_side.1 = (f32[125,128]{1,0:T(8,128)S(1)}, f32[2352,128]{1,0:T(8,128)S(1)}, f32[2352,128]{1,0:T(8,128)S(1)}, f32[6,12,4,8,128]{4,3,2,1,0:T(8,128)S(1)}, f32...) custom-call(f32[280,128]{1,0:T(8,128)S(1)} %collective-permute-done., ...), custom_call_target="tpu_custom_call", output_to_operand_aliasing={{1}: (6, {}), {2}: (7, {}), {3}: (8, {}), {4}: (9, {}), {5}... | custom-call | flops 2000000000 | bytes 1048576 | tf_op jit(solution)/shard_map/core_side/pallas_call | solution.py:827
  16.0 1.2 %collective-permute-done.4.halo = f32[280,128]{1,0:T(8,128)S(1)} collective-permute-done((f32[280,128]{1,0:T(8,128)S(1)}, f32[280,128]{1,0:T(8,128)S(1)}, u32[]{:S(2)}, u32[]{:S(2)}) %collective-permute-start.4) | collective-permute-done | bytes 143392 | tf_op jit(solution)/shard_map/ppermute | solution.py:677
  17.2 2.2 %chip_side.1 = (f32[125,1,256]{2,1,0:T(1,128)}, f32[2352,128]{1,0:T(8,128)S(1)}, f32[2352,128]{1,0:T(8,128)S(1)}, f32[6,12,4,8,128]{4,3,2,1,0:T(8,128)S(1)}, f32...) custom-call(f32[280,128]{1,0:T(8,128)S(1)} %collective-permute-done., ...), custom_call_target="tpu_custom_call", output_to_operand_aliasing={{1}: (7, {}), {2}: (8, {}), {3}: (9, {}), {4}: (10, {}), {5... | custom-call | tf_op jit(solution)/shard_map/chip_side/pallas_call | solution.py:838
  (2 shorter events, 0.0 us)
Async XLA Ops:
  1.1 5.0 %collective-permute-start = (f32[232,128]{1,0:T(8,128)S(1)}, f32[232,128]{1,0:T(8,128)S(1)}, u32[]{:S(2)}, u32[]{:S(2)}) collective-permute-start(f32[232,128]{1,0:T(8,128)S(1)} %get-tuple-element.33.own.refs_0_), channel_id=1, source_target_pairs={{0,4},{1,5},{2,6},{3,7},{4,0},{5,1},{6,2},{7,3},{8,12},{9,13},{10,... | collective-permute-start | bytes 356360 | tf_op jit(solution)/shard_map/ppermute | solution.py:677
  2.6 4.9 %collective-permute-start.3 = (f32[80,128]{1,0:T(8,128)S(1)}, f32[80,128]{1,0:T(8,128)S(1)}, u32[]{:S(2)}, u32[]{:S(2)}) collective-permute-start(f32[80,128]{1,0:T(8,128)S(1)} %get-tuple-element.34), channel_id=1, source_target_pairs={{0,4},{1,5},{2,6},{3,7},{4,12},{5,13},{6,14},{7,15},{8,0},{9,1},{1... | collective-permute-start | bytes 122888 | tf_op jit(solution)/shard_map/ppermute | solution.py:677
  3.1 4.4 %collective-permute-start.2 = (f32[80,128]{1,0:T(8,128)S(1)}, f32[80,128]{1,0:T(8,128)S(1)}, u32[]{:S(2)}, u32[]{:S(2)}) collective-permute-start(f32[80,128]{1,0:T(8,128)S(1)} %get-tuple-element.34), channel_id=1, source_target_pairs={{0,8},{1,9},{2,10},{3,11},{4,0},{5,1},{6,2},{7,3},{8,16},{9,17},{1... | collective-permute-start | bytes 122888 | tf_op jit(solution)/shard_map/ppermute | solution.py:677
  5.3 5.8 %collective-permute-start.1 = (f32[232,128]{1,0:T(8,128)S(1)}, f32[232,128]{1,0:T(8,128)S(1)}, u32[]{:S(2)}, u32[]{:S(2)}) collective-permute-start(f32[232,128]{1,0:T(8,128)S(1)} %live.1.own), channel_id=1, source_target_pairs={{0,1},{1,0},{2,3},{3,2},{4,8},{5,9},{6,10},{7,11},{8,4},{9,5},{10,... | collective-permute-start | bytes 356360 | tf_op jit(solution)/shard_map/ppermute | solution.py:677
  11.2 6.1 %collective-permute-start.4 = (f32[280,128]{1,0:T(8,128)S(1)}, f32[280,128]{1,0:T(8,128)S(1)}, u32[]{:S(2)}, u32[]{:S(2)}) collective-permute-start(f32[280,128]{1,0:T(8,128)S(1)} %get-tuple-element.40), channel_id=1, source_target_pairs={{0,3},{1,2},{2,1},{3,0},{4,8},{5,6},{6,5},{7,11},{8,4},{9,10},{10,... | collective-permute-start | bytes 430088 | tf_op jit(solution)/shard_map/ppermute | solution.py:677
  11.7 2.8 %collective-permute-start.5 = (f32[280,128]{1,0:T(8,128)S(1)}, f32[280,128]{1,0:T(8,128)S(1)}, u32[]{:S(2)}, u32[]{:S(2)}) collective-permute-start(f32[280,128]{1,0:T(8,128)S(1)} %get-tuple-element.48), channel_id=1, source_target_pairs={{0,1},{1,0},{2,3},{3,2},{4,5},{5,4},{6,7},{7,6},{8,9},{9,8},{10,11... | collective-permute-start | bytes 430088 | tf_op jit(solution)/shard_map/ppermute | solution.py:677
